TPU v7x, 32 devices: a whole 2x2x4 slice. The times are simulated.
32 devices in a mesh: parts: 2 (over y), train: 8 (over z, core), layer: 2 (over x), query: 1.
Axes of the slice: x: 2, y: 2, z: 4, core: 2. Of those that a mesh axis runs over, the one named last changes fastest.
Arguments:
- train_grads: bfloat16 [4096, 4, 4096], P(('parts', 'train'), 'layer'), parts along dimension 0, may hold values from -0.046875 to 0.046875
- queries: bfloat16 [4, 1, 128, 4096], P('layer', 'query', 'train'), may hold values from -6 to 6
- left_factor: float32 [4, 64, 64], P('layer'), may hold values from -1 to 2
- right_factor: float32 [4, 64, 64], P('layer'), may hold values from -1 to 2
Outputs:
- scores: float32 [4096, 128], P(('parts', 'train', 'layer'), 'query'), parts along dimension 0
There are 2 independent parts, one for each index of `parts`. A program takes and returns all parts, laid end to end along the dimension named above; an argument that names none is the same for every part. Nothing has to cross between parts.
All inputs are finite; a program needn't handle non-finite values.
Results may differ from a plain program's by a relative error of at most 0.0029.
Values may be sent and summed in bfloat16 or wider, within the bound.
No kernel may reach another device: no remote copies, remote signals or barrier semaphores. Data moves between devices by JAX's collectives and lax.ppermute only.
A program may use at most 128 MiB of HBM per device.

v0:
```python
import jax
import jax.numpy as jnp
from jax import lax
from jax.sharding import PartitionSpec as P


def body(train_grads, queries, left_factor, right_factor):
    rows_out = left_factor.shape[1]
    rows_in = right_factor.shape[1]
    block = lax.all_gather(queries, "train", axis=2, tiled=True)[:, 0]
    layer_count, count, width = block.shape
    grid = block.astype(jnp.float32).reshape(layer_count, count, rows_out, rows_in)
    left_part = jnp.einsum("lab,lnbc->lnac", left_factor, grid, precision=lax.Precision.HIGHEST)
    both = jnp.einsum("lnac,lcd->lnad", left_part, right_factor, precision=lax.Precision.HIGHEST)
    partial_value = jnp.einsum(
        "fkm,krm->fr",
        train_grads,
        both.reshape(layer_count, count, width).astype(jnp.bfloat16),
        preferred_element_type=jnp.float32,
    )
    summed = lax.psum(partial_value, "layer")
    share = summed.shape[0] // lax.axis_size("layer")
    scores = lax.dynamic_slice_in_dim(summed, lax.axis_index("layer") * share, share, 0)
    return scores


def solution(mesh):
    return jax.shard_map(
        body,
        mesh=mesh,
        in_specs=(
            P(("parts", "train"), "layer", None),
            P("layer", "query", "train", None),
            P("layer", None, None),
            P("layer", None, None),
        ),
        out_specs=P(("parts", "train", "layer"), "query"),
        check_vma=False,
    )
```

profile of v0, /device:TPU:0, one launch (start us, length us, event | category | flops | bytes accessed | tf_op | source)
XLA Modules:
  0.0 87.1 jit_solution(2216941142772894710)
XLA Ops:
  6.5 0.0 copy-start
  6.5 0.0 all-gather.2.cloned.1.call-start
  6.5 2.0 %copy.14 = bf16[2,1,16,4096]{3,0,1,2:T(2,128)(2,1)} copy(bf16[2,1,16,4096]{3,2,1,0:T(8,128)(2,1)} %param.5) | data formatting | bytes 524288 | tf_op args[1]
  8.5 0.0 all-gather.2.cloned.1.call-update
  8.5 0.0 all-reduce.2.cloned.1.call-start
  8.6 32.2 %all-gather.2.cloned.1.call-done = bf16[2,1,128,4096]{3,0,1,2:T(2,128)(2,1)} async-done(((bf16[2,1,16,4096]{3,0,1,2:T(2,128)(2,1)}), bf16[2,1,128,4096]{3,0,1,2:T(2,128)(2,1)}) %all-gather.2.cloned.1.call-update) | async-done | bytes 2097168 | tf_op jit(solution)/shard_map/all_gather | solution.py:10
  40.8 4.9 %copy.15 = bf16[2,1,128,4096]{2,3,0,1:T(8,128)(2,1)S(1)} copy(bf16[2,1,128,4096]{3,0,1,2:T(2,128)(2,1)} %all-gather.2.cloned.1.call-done) | data formatting | bytes 4194304 | tf_op jit(solution)/shard_map/all_gather | solution.py:10
  45.7 0.0 copy-start.1
  45.7 0.0 copy-done
  45.7 2.6 %convolution_bitcast_fusion = f32[2,128,64,64]{1,2,3,0:T(8,128)S(1)} fusion(bf16[2,128,64,64]{1,3,2,0:T(8,128)(2,1)S(1)} %bitcast.19, f32[2,64,64]{2,1,0:T(8,128)S(1)} %copy-done), kind=kOutput, calls=%fused_computation.4 | convolution fusion | flops 805306368 | bytes 6324224 | tf_op jit(solution)/shard_map/lab,lnbc->lnac/dot_general | solution.py:13
  48.3 0.0 copy-done.1
  48.4 0.0 copy-start.2
  48.4 5.9 %fusion.5 = bf16[2,128,64,64]{1,3,2,0:T(8,128)(2,1)S(1)} fusion(f32[2,128,64,64]{1,2,3,0:T(8,128)S(1)} %convolution_bitcast_fusion, f32[2,64,64]{2,1,0:T(8,128)S(1)} %copy-done.1), kind=kOutput, calls=%fused_computation.6 | convolution fusion | flops 806354944 | bytes 6324224 | tf_op jit(solution)/shard_map/lnac,lcd->lnad/dot_general | solution.py:14
  54.2 0.0 copy-done.2
  54.2 3.4 %fusion.8 = f32[256,128]{0,1:T(8,128)} fusion(bf16[2,128,4096]{1,2,0:T(8,128)(2,1)S(1)} %bitcast.20, bf16[256,2,4096]{2,1,0:T(2,128)(2,1)S(1)} %copy-done.2), kind=kOutput, calls=%fused_computation.7 | convolution fusion | flops 536870912 | bytes 6422528 | tf_op jit(solution)/shard_map/fkm,krm->fr/dot_general | solution.py:15
  57.6 0.0 all-reduce.2.cloned.1.call-update
  57.6 21.1 %all-reduce.2.cloned.1.call-done = f32[256,128]{0,1:T(8,128)} async-done(((f32[256,128]{0,1:T(8,128)}), f32[256,128]{0,1:T(8,128)}) %all-reduce.2.cloned.1.call-update) | async-done | bytes 131088 | tf_op jit(solution)/shard_map/psum | solution.py:21
  78.7 0.8 constant_dynamic-slice_fusion
  79.6 0.7 copy.21
Async XLA Ops:
  6.5 39.2 %copy-start = (f32[2,64,64]{2,1,0:T(8,128)S(1)}, f32[2,64,64]{2,1,0:T(8,128)}, u32[]{:S(2)}) copy-start(f32[2,64,64]{2,1,0:T(8,128)} %param.6) | copy-start | bytes 98308
  6.5 34.3 %all-gather.2.cloned.1.call-start = ((), (), s32[]{:S(2)}) async-start(), calls=%async_computation | async-start | bytes 2359296 | tf_op jit(solution)/shard_map/all_gather | solution.py:10
  8.5 70.2 %all-reduce.2.cloned.1.call-start = ((), (), s32[]{:S(2)}) async-start(), calls=%async_computation.1 | async-start | bytes 262144 | tf_op jit(solution)/shard_map/psum | solution.py:21
  45.7 2.7 %copy-start.1 = (f32[2,64,64]{2,1,0:T(8,128)S(1)}, f32[2,64,64]{2,1,0:T(8,128)}, u32[]{:S(2)}) copy-start(f32[2,64,64]{2,1,0:T(8,128)} %param.7) | copy-start | bytes 98308
  48.4 5.9 %copy-start.2 = (bf16[256,2,4096]{2,1,0:T(2,128)(2,1)S(1)}, bf16[256,2,4096]{2,1,0:T(2,128)(2,1)}, u32[]{:S(2)}) copy-start(bf16[256,2,4096]{2,1,0:T(2,128)(2,1)} %param.4) | copy-start | bytes 12582916
Sparse Core Ops, SparseCore 0:
  9.0 31.7 all-gather.1
  57.8 20.9 all-reduce.1
where the time goes:
time: 87.4 us; the launch traced here: 87.1 us
  waiting for transfers between devices  53.3 us (61%)
  between operations  13.5 us (15%)
  matrix products  11.9 us (14%)
  local copies, waits for them, and re-layouts  8.42 us (10%)
    all_gather x1, waiting for transfers between devices, body(): block = lax.all_gather(queries, 'train', axis=2, tiled=True)[:, 0]  32.2 us
    psum x1, waiting for transfers between devices, body(): summed = lax.psum(partial_value, 'layer')  21.1 us
    dot_general x1, matrix products, body(): jnp.einsum('lnac,lcd->lnad', left_part, right_factor, precision=lax.Preci...  5.86 us
    all_gather x1, local copies, waits for them, and re-layouts, body(): block = lax.all_gather(queries, 'train', axis=2, tiled=True)[:, 0]  4.88 us
    dot_general x1, matrix products, body(): jnp.einsum('fkm,krm->fr', train_grads, both.reshape(layer_count, count, w...  3.37 us
    dot_general x1, matrix products, body(): jnp.einsum('lab,lnbc->lnac', left_factor, grid, precision=lax.Precision.H...  2.63 us
    unnamed x7, local copies, waits for them, and re-layouts  1.97 us
  transfers between devices with their start and end apart: 2, of which 2 were waited for; matrix products, arithmetic and copies ran while one was open for 0% of the time, Pallas kernels for 0%

commit v1 on v0

v1 whole, which is shorter than its diff:
```python
import jax
import jax.numpy as jnp
from jax import lax
from jax.sharding import PartitionSpec as P


def swap_parts(value, parts):
    return lax.ppermute(value, "parts", [(p, (p + 1) % parts) for p in range(parts)])


def gather_blocks(own, parts, pair, columns):
    train = pair * columns

    def along_columns(value, step):
        return lax.ppermute(
            value,
            "train",
            [(k, (k // pair - step) % columns * pair + k % pair) for k in range(train)],
        )

    def along_pair(value):
        return lax.ppermute(value, "train", [(k, k ^ 1) for k in range(train)])

    me = lax.axis_index("parts")
    mine = lax.dynamic_index_in_dim(own, me, 0, keepdims=False)
    got = [along_columns(mine, step) for step in range(1, columns)]
    blocks = [own]
    for piece in got:
        other = swap_parts(piece, parts)
        blocks.append(jnp.where(me == 0, jnp.stack([piece, other]), jnp.stack([other, piece])))
    ordered = []
    for block in blocks:
        ordered.append(block)
        ordered.append(along_pair(block))
    return jnp.concatenate(ordered, axis=1)


def body(shape, train_grads, queries, left_factor, right_factor):
    rows_out = left_factor.shape[1]
    rows_in = right_factor.shape[1]
    own = queries[:, 0]
    layer_count, count, width = own.shape
    grid = own.astype(jnp.float32).reshape(layer_count, count, rows_out, rows_in)
    left_part = jnp.einsum("lab,lnbc->lnac", left_factor, grid, precision=lax.Precision.HIGHEST)
    both = jnp.einsum("lnac,lcd->lnad", left_part, right_factor, precision=lax.Precision.HIGHEST)
    ready = both.reshape(layer_count, count, width).astype(jnp.bfloat16)

    train, parts, layers = shape["train"], shape["parts"], shape["layer"]
    pair = 2
    columns = train // pair
    direct = shape["query"] == 1 and train % pair == 0 and columns <= 4 and parts == layer_count == 2
    if direct:
        block = gather_blocks(ready, parts, pair, columns)
    else:
        block = lax.all_gather(ready, "train", axis=1, tiled=True)

    share = train_grads.shape[0] // layers
    here = lax.axis_index("layer")

    def terms(step):
        rows = lax.dynamic_slice_in_dim(train_grads, (here + step) % layers * share, share, 0)
        return jnp.einsum("fkm,krm->fr", rows, block, preferred_element_type=jnp.float32)

    scores = None
    for step in range(1, layers):
        sent = lax.ppermute(terms(step), "layer", [(k, (k + step) % layers) for k in range(layers)])
        scores = sent if scores is None else scores + sent
    own_terms = terms(0)
    scores = own_terms if scores is None else scores + own_terms
    if direct:
        place = lax.axis_index("train")
        scores = scores.reshape(share, columns, pair, count)
        scores = jnp.roll(scores, place // pair, axis=1)
        scores = jnp.where(place % pair == 0, scores, scores[:, :, ::-1])
        scores = scores.reshape(share, train * count)
    return scores


def solution(mesh):
    shape = dict(mesh.shape)
    return jax.shard_map(
        lambda *arrays: body(shape, *arrays),
        mesh=mesh,
        in_specs=(
            P(("parts", "train"), "layer", None),
            P("layer", "query", "train", None),
            P("layer", None, None),
            P("layer", None, None),
        ),
        out_specs=P(("parts", "train", "layer"), "query"),
        check_vma=False,
    )
```

time: 87.4 us -> 65.5 us (0.75)
  waiting for transfers between devices: 53.3 us -> 31.1 us
  between operations: 13.5 us -> 0.17 us
  starting transfers between devices: 0.04 us -> 13 us
  matrix products: 11.9 us -> 6.96 us
  local copies, waits for them, and re-layouts: 8.42 us -> 13.2 us
  other arithmetic: 0 us -> 0.88 us
    all_gather x1 -> x0, waiting for transfers between devices: 32.2 us -> none  [body(): block = lax.all_gather(queries, 'train', axis=2, tiled=True)[:, 0]]
    ppermute x0 -> x11, waiting for transfers between devices: none -> 31.1 us  [the longest x3 19.1 us: along_columns(): lax.ppermute(value, 'train', [(k, (k // pair - step) % columns * pair + k...]
    psum x1 -> x0, waiting for transfers between devices: 21.1 us -> none  [body(): summed = lax.psum(partial_value, 'layer')]
    ppermute x0 -> x11, starting transfers between devices: none -> 13 us  [the longest x3 6.27 us: along_columns(): lax.ppermute(value, 'train', [(k, (k // pair - step) % columns * pair + k...]
    dynamic_slice x2 -> x1, local copies, waits for them, and re-layouts: 1.57 us -> 9.55 us  [terms(): lax.dynamic_slice_in_dim(train_grads, (here + step) % layers * share, sha...]
    all_gather x1 -> x0, local copies, waits for them, and re-layouts: 4.88 us -> none  [body(): block = lax.all_gather(queries, 'train', axis=2, tiled=True)[:, 0]]
    dot_general x1, matrix products: 5.86 us -> 1.02 us  [body(): jnp.einsum('lnac,lcd->lnad', left_part, right_factor, precision=lax.Preci...]
    reshape x0 -> x2, local copies, waits for them, and re-layouts: none -> 2.23 us  [the longest x1 1.5 us: body(): own.astype(jnp.float32).reshape(layer_count, count, rows_out, rows_in)]
  transfers between devices with their start and end apart: 2 -> 11, of which waited for: 2 -> 7; matrix products, arithmetic and copies ran while one was open for 0% -> 17% of each run, Pallas kernels for 0% -> 0%
where the time goes in v1:
time: 65.5 us; the launch traced here: 65.3 us
  waiting for transfers between devices  31.1 us (47%)
  local copies, waits for them, and re-layouts  13.2 us (20%)
  starting transfers between devices  13 us (20%)
  matrix products  6.96 us (11%)
  other arithmetic  0.88 us (1%)
    ppermute x3, waiting for transfers between devices, along_columns(): lax.ppermute(value, 'train', [(k, (k // pair - step) % columns * pair + k...  19.1 us
    ppermute x3, waiting for transfers between devices, swap_parts(): lax.ppermute(value, 'parts', [(p, (p + 1) % parts) for p in range(parts)])  10.6 us
    dynamic_slice x1, local copies, waits for them, and re-layouts, terms(): lax.dynamic_slice_in_dim(train_grads, (here + step) % layers * share, sha...  9.55 us
    ppermute x3, starting transfers between devices, along_columns(): lax.ppermute(value, 'train', [(k, (k // pair - step) % columns * pair + k...  6.27 us
    dot_general x2, matrix products, terms(): jnp.einsum('fkm,krm->fr', rows, block, preferred_element_type=jnp.float32)  5.39 us
    ppermute x3, starting transfers between devices, swap_parts(): lax.ppermute(value, 'parts', [(p, (p + 1) % parts) for p in range(parts)])  4.56 us
    ppermute x1, starting transfers between devices, body(): lax.ppermute(terms(step), 'layer', [(k, (k + step) % layers) for k in ran...  1.55 us
    reshape x1, local copies, waits for them, and re-layouts, body(): own.astype(jnp.float32).reshape(layer_count, count, rows_out, rows_in)  1.5 us
  transfers between devices with their start and end apart: 11, of which 7 were waited for; matrix products, arithmetic and copies ran while one was open for 17% of the time, Pallas kernels for 0%

profile of v1, /device:TPU:0, one launch (start us, length us, event | category | flops | bytes accessed | tf_op | source)
XLA Modules:
  0.0 65.3 jit_solution(8911473782890897961)
XLA Ops:
  0.0 0.0 copy-start
  0.0 0.0 copy-start.1
  0.0 1.5 %reshape.12 = bf16[2,16,64,64]{3,2,1,0:T(8,128)(2,1)S(1)} reshape(bf16[2,1,16,4096]{3,2,1,0:T(8,128)(2,1)} %param.5) | data formatting | bytes 524288 | tf_op jit(solution)/shard_map/reshape | solution.py:43
  1.5 0.0 copy-done
  1.5 0.6 convolution_bitcast_fusion
  2.1 0.0 copy-done.1
  2.1 1.0 %convolution_convert_fusion = bf16[2,16,64,64]{3,2,1,0:T(8,128)(2,1)S(1)} fusion(f32[2,16,64,64]{3,2,1,0:T(8,128)S(1)} %convolution_bitcast_fusion, f32[2,64,64]{2,1,0:T(8,128)S(1)} %copy-done.1), kind=kOutput, calls=%fused_computation.5 | convolution fusion | flops 100794368 | bytes 819200 | tf_op jit(solution)/shard_map/lnac,lcd->lnad/dot_general | solution.py:45
  3.1 0.5 convert_element_type.8
  3.6 0.5 collective-permute-start
  4.1 4.7 %collective-permute-start.1 = (bf16[16,4096]{1,0:T(8,128)(2,1)S(1)}, bf16[16,4096]{1,0:T(8,128)(2,1)S(1)}, u32[]{:S(2)}, u32[]{:S(2)}) collective-permute-start(bf16[16,4096]{1,0:T(8,128)(2,1)S(1)} %dynamic-slice_bitcast_fusion), channel_id=1, source_target_pairs={{0,12},{2,14},{4,0},{6,2},{8,4},{10,6},{12,8},{14,10},{1,13},{3,15... | collective-permute-start | bytes 393224 | tf_op jit(solution)/shard_map/ppermute | solution.py:15
  8.8 3.4 %collective-permute-done.1 = bf16[16,4096]{1,0:T(8,128)(2,1)S(1)} collective-permute-done((bf16[16,4096]{1,0:T(8,128)(2,1)S(1)}, bf16[16,4096]{1,0:T(8,128)(2,1)S(1)}, u32[]{:S(2)}, u32[]{:S(2)}) %collective-permute-start.1) | collective-permute-done | bytes 131104 | tf_op jit(solution)/shard_map/ppermute | solution.py:15
  12.2 1.5 %collective-permute-start.2 = (bf16[16,4096]{1,0:T(8,128)(2,1)S(1)}, bf16[16,4096]{1,0:T(8,128)(2,1)S(1)}, u32[]{:S(2)}, u32[]{:S(2)}) collective-permute-start(bf16[16,4096]{1,0:T(8,128)(2,1)S(1)} %collective-permute-done.1), channel_id=1, source_target_pairs={{0,16},{16,0},{1,17},{17,1},{2,18},{18,2},{3,19},{19,3},{4,20},{20... | collective-permute-start | bytes 393224 | tf_op jit(solution)/shard_map/ppermute | solution.py:8
  13.7 0.0 collective-permute-done
  13.7 3.6 %collective-permute-done.2 = bf16[16,4096]{1,0:T(8,128)(2,1)S(1)} collective-permute-done((bf16[16,4096]{1,0:T(8,128)(2,1)S(1)}, bf16[16,4096]{1,0:T(8,128)(2,1)S(1)}, u32[]{:S(2)}, u32[]{:S(2)}) %collective-permute-start.2) | collective-permute-done | bytes 131104 | tf_op jit(solution)/shard_map/ppermute | solution.py:8
  17.3 0.1 collective-permute-start.3
  17.4 1.5 %collective-permute-start.4 = (bf16[16,4096]{1,0:T(8,128)(2,1)S(1)}, bf16[16,4096]{1,0:T(8,128)(2,1)S(1)}, u32[]{:S(2)}, u32[]{:S(2)}) collective-permute-start(bf16[16,4096]{1,0:T(8,128)(2,1)S(1)} %dynamic-slice_bitcast_fusion), channel_id=1, source_target_pairs={{0,8},{2,10},{4,12},{6,14},{8,0},{10,2},{12,4},{14,6},{1,9},{3,11}... | collective-permute-start | bytes 393224 | tf_op jit(solution)/shard_map/ppermute | solution.py:15
  18.9 8.1 %collective-permute-done.4 = bf16[16,4096]{1,0:T(8,128)(2,1)S(1)} collective-permute-done((bf16[16,4096]{1,0:T(8,128)(2,1)S(1)}, bf16[16,4096]{1,0:T(8,128)(2,1)S(1)}, u32[]{:S(2)}, u32[]{:S(2)}) %collective-permute-start.4) | collective-permute-done | bytes 131104 | tf_op jit(solution)/shard_map/ppermute | solution.py:15
  27.0 1.5 %collective-permute-start.5 = (bf16[16,4096]{1,0:T(8,128)(2,1)S(1)}, bf16[16,4096]{1,0:T(8,128)(2,1)S(1)}, u32[]{:S(2)}, u32[]{:S(2)}) collective-permute-start(bf16[16,4096]{1,0:T(8,128)(2,1)S(1)} %collective-permute-done.4), channel_id=1, source_target_pairs={{0,16},{16,0},{1,17},{17,1},{2,18},{18,2},{3,19},{19,3},{4,20},{20... | collective-permute-start | bytes 393224 | tf_op jit(solution)/shard_map/ppermute | solution.py:8
  28.5 0.0 collective-permute-done.3
  28.6 3.5 %collective-permute-done.5 = bf16[16,4096]{1,0:T(8,128)(2,1)S(1)} collective-permute-done((bf16[16,4096]{1,0:T(8,128)(2,1)S(1)}, bf16[16,4096]{1,0:T(8,128)(2,1)S(1)}, u32[]{:S(2)}, u32[]{:S(2)}) %collective-permute-start.5) | collective-permute-done | bytes 131104 | tf_op jit(solution)/shard_map/ppermute | solution.py:8
  32.1 0.1 collective-permute-start.6
  32.2 0.1 collective-permute-start.7
  32.3 7.6 %collective-permute-done.7 = bf16[16,4096]{1,0:T(8,128)(2,1)S(1)} collective-permute-done((bf16[16,4096]{1,0:T(8,128)(2,1)S(1)}, bf16[16,4096]{1,0:T(8,128)(2,1)S(1)}, u32[]{:S(2)}, u32[]{:S(2)}) %collective-permute-start.7) | collective-permute-done | bytes 131104 | tf_op jit(solution)/shard_map/ppermute | solution.py:15
  39.9 1.5 %collective-permute-start.8 = (bf16[16,4096]{1,0:T(8,128)(2,1)S(1)}, bf16[16,4096]{1,0:T(8,128)(2,1)S(1)}, u32[]{:S(2)}, u32[]{:S(2)}) collective-permute-start(bf16[16,4096]{1,0:T(8,128)(2,1)S(1)} %collective-permute-done.7), channel_id=1, source_target_pairs={{0,16},{16,0},{1,17},{17,1},{2,18},{18,2},{3,19},{19,3},{4,20},{20... | collective-permute-start | bytes 393224 | tf_op jit(solution)/shard_map/ppermute | solution.py:8
  41.4 0.0 collective-permute-done.6
  41.5 0.0 copy-start.2
  41.5 3.5 %collective-permute-done.8 = bf16[16,4096]{1,0:T(8,128)(2,1)S(1)} collective-permute-done((bf16[16,4096]{1,0:T(8,128)(2,1)S(1)}, bf16[16,4096]{1,0:T(8,128)(2,1)S(1)}, u32[]{:S(2)}, u32[]{:S(2)}) %collective-permute-start.8) | collective-permute-done | bytes 131104 | tf_op jit(solution)/shard_map/ppermute | solution.py:8
  45.0 0.0 copy-done.2
  45.0 0.7 %constant_dynamic-update-slice_fusion.1 = (bf16[2,128,4096]{2,1,0:T(8,128)(2,1)}, bf16[2,16,4096]{2,1,0:T(8,128)(2,1)S(1)}) fusion(bf16[2,128,4096]{2,1,0:T(8,128)(2,1)} %copy-done.2, bf16[1,16,4096]{2,1,0:T(8,128)(2,1)S(1)} %bitcast.36, bf16[1,16,4096]{2,1,0:T(8,128)(2,1)S(1)} %bitcast.39, pred[]{:T(512)S(6)} %eq.16), kind=kLoop, calls=%fused_computation.19 | loop fusion | flops 1179648 | bytes 786433
  45.7 0.0 collective-permute-start.9
  45.7 9.6 %constant_dynamic-slice_fusion = (bf16[128,2,4096]{2,1,0:T(2,128)(2,1)S(1)}, bf16[128,2,4096]{2,1,0:T(2,128)(2,1)}) fusion(bf16[256,2,4096]{2,1,0:T(2,128)(2,1)} %param.4, s32[]{:T(128)S(6)} %select_n.75, s32[]{:T(128)S(6)} %select_n.68), kind=kLoop, calls=%fused_computation.26 | loop fusion | bytes 8388616 | tf_op jit(solution)/shard_map/dynamic_slice | solution.py:61
  55.3 0.0 collective-permute-done.9
  55.3 0.7 %constant_dynamic-update-slice_fusion = bf16[2,128,4096]{2,1,0:T(8,128)(2,1)} fusion(bf16[2,128,4096]{2,1,0:T(8,128)(2,1)} %get-tuple-element.5, bf16[2,16,4096]{2,1,0:T(8,128)(2,1)S(1)} %collective-permute-done.9), kind=kLoop, calls=%fused_computation.18 | loop fusion | bytes 524288 | tf_op jit(solution)/shard_map/concatenate | solution.py:35
  56.0 0.0 copy-start.3
  56.0 3.9 %fusion.4 = f32[128,128]{1,0:T(8,128)S(1)} fusion(bf16[2,128,4096]{2,1,0:T(8,128)(2,1)} %constant_dynamic-update-slice_fusion, bf16[128,2,4096]{2,1,0:T(2,128)(2,1)} %get-tuple-element.12), kind=kOutput, calls=%fused_computation.6 | convolution fusion | flops 268435456 | bytes 4259840 | tf_op jit(solution)/shard_map/fkm,krm->fr/dot_general | solution.py:62
  59.9 1.5 %collective-permute-start.10 = (f32[128,128]{1,0:T(8,128)S(1)}, f32[128,128]{1,0:T(8,128)S(1)}, u32[]{:S(2)}, u32[]{:S(2)}) collective-permute-start(f32[128,128]{1,0:T(8,128)S(1)} %fusion.4), channel_id=1, source_target_pairs={{0,1},{1,0},{2,3},{3,2},{4,5},{5,4},{6,7},{7,6},{8,9},{9,8},{10,11... | collective-permute-start | bytes 196616 | tf_op jit(solution)/shard_map/ppermute | solution.py:66
  61.4 0.0 copy-done.3
  61.4 1.5 %fusion.7 = f32[128,128]{1,0:T(8,128)S(1)} fusion(bf16[2,128,4096]{2,1,0:T(8,128)(2,1)S(1)} %copy-done.3, bf16[128,2,4096]{2,1,0:T(2,128)(2,1)S(1)} %get-tuple-element.11), kind=kOutput, calls=%fused_computation.7 | convolution fusion | flops 268435456 | bytes 4259840 | tf_op jit(solution)/shard_map/fkm,krm->fr/dot_general | solution.py:62
  63.0 1.5 %collective-permute-done.10 = f32[128,128]{1,0:T(8,128)S(1)} collective-permute-done((f32[128,128]{1,0:T(8,128)S(1)}, f32[128,128]{1,0:T(8,128)S(1)}, u32[]{:S(2)}, u32[]{:S(2)}) %collective-permute-start.10) | collective-permute-done | bytes 65568 | tf_op jit(solution)/shard_map/ppermute | solution.py:66
  64.5 0.1 copy.11
  64.6 0.7 %copy.12 = f32[128,128]{1,0:T(8,128)} copy(f32[128,128]{0,1:T(8,128)S(1)} %bitcast.35) | data formatting | bytes 131072 | tf_op jit(solution)/shard_map/reshape | solution.py:75
  (10 shorter events, 0.2 us)
Async XLA Ops:
  0.0 1.5 %copy-start = (f32[2,64,64]{2,1,0:T(8,128)S(1)}, f32[2,64,64]{2,1,0:T(8,128)}, u32[]{:S(2)}) copy-start(f32[2,64,64]{2,1,0:T(8,128)} %param.6) | copy-start | bytes 98308
  0.0 2.1 %copy-start.1 = (f32[2,64,64]{2,1,0:T(8,128)S(1)}, f32[2,64,64]{2,1,0:T(8,128)}, u32[]{:S(2)}) copy-start(f32[2,64,64]{2,1,0:T(8,128)} %param.7) | copy-start | bytes 98308
  3.6 10.1 %collective-permute-start = (bf16[2,16,4096]{2,1,0:T(8,128)(2,1)S(1)}, bf16[2,16,4096]{2,1,0:T(8,128)(2,1)S(1)}, u32[]{:S(2)}, u32[]{:S(2)}) collective-permute-start(bf16[2,16,4096]{2,1,0:T(8,128)(2,1)S(1)} %convert_element_type.8), channel_id=1, source_target_pairs={{0,2},{2,0},{4,6},{6,4},{8,10},{10,8},{12,14},{14,12},{1,3},{3,1},... | collective-permute-start | bytes 786440 | tf_op jit(solution)/shard_map/ppermute | solution.py:22
  4.1 8.1 %collective-permute-start.1 = (bf16[16,4096]{1,0:T(8,128)(2,1)S(1)}, bf16[16,4096]{1,0:T(8,128)(2,1)S(1)}, u32[]{:S(2)}, u32[]{:S(2)}) collective-permute-start(bf16[16,4096]{1,0:T(8,128)(2,1)S(1)} %dynamic-slice_bitcast_fusion), channel_id=1, source_target_pairs={{0,12},{2,14},{4,0},{6,2},{8,4},{10,6},{12,8},{14,10},{1,13},{3,15... | collective-permute-start | bytes 393224 | tf_op jit(solution)/shard_map/ppermute | solution.py:15
  12.2 5.1 %collective-permute-start.2 = (bf16[16,4096]{1,0:T(8,128)(2,1)S(1)}, bf16[16,4096]{1,0:T(8,128)(2,1)S(1)}, u32[]{:S(2)}, u32[]{:S(2)}) collective-permute-start(bf16[16,4096]{1,0:T(8,128)(2,1)S(1)} %collective-permute-done.1), channel_id=1, source_target_pairs={{0,16},{16,0},{1,17},{17,1},{2,18},{18,2},{3,19},{19,3},{4,20},{20... | collective-permute-start | bytes 393224 | tf_op jit(solution)/shard_map/ppermute | solution.py:8
  17.3 11.2 %collective-permute-start.3 = (bf16[2,16,4096]{2,1,0:T(8,128)(2,1)S(1)}, bf16[2,16,4096]{2,1,0:T(8,128)(2,1)S(1)}, u32[]{:S(2)}, u32[]{:S(2)}) collective-permute-start(bf16[2,16,4096]{2,1,0:T(8,128)(2,1)S(1)} %get-tuple-element.10), channel_id=1, source_target_pairs={{0,2},{2,0},{4,6},{6,4},{8,10},{10,8},{12,14},{14,12},{1,3},{3,1},... | collective-permute-start | bytes 786440 | tf_op jit(solution)/shard_map/ppermute | solution.py:22
  17.4 9.6 %collective-permute-start.4 = (bf16[16,4096]{1,0:T(8,128)(2,1)S(1)}, bf16[16,4096]{1,0:T(8,128)(2,1)S(1)}, u32[]{:S(2)}, u32[]{:S(2)}) collective-permute-start(bf16[16,4096]{1,0:T(8,128)(2,1)S(1)} %dynamic-slice_bitcast_fusion), channel_id=1, source_target_pairs={{0,8},{2,10},{4,12},{6,14},{8,0},{10,2},{12,4},{14,6},{1,9},{3,11}... | collective-permute-start | bytes 393224 | tf_op jit(solution)/shard_map/ppermute | solution.py:15
  27.0 5.1 %collective-permute-start.5 = (bf16[16,4096]{1,0:T(8,128)(2,1)S(1)}, bf16[16,4096]{1,0:T(8,128)(2,1)S(1)}, u32[]{:S(2)}, u32[]{:S(2)}) collective-permute-start(bf16[16,4096]{1,0:T(8,128)(2,1)S(1)} %collective-permute-done.4), channel_id=1, source_target_pairs={{0,16},{16,0},{1,17},{17,1},{2,18},{18,2},{3,19},{19,3},{4,20},{20... | collective-permute-start | bytes 393224 | tf_op jit(solution)/shard_map/ppermute | solution.py:8
  32.1 9.3 %collective-permute-start.6 = (bf16[2,16,4096]{2,1,0:T(8,128)(2,1)S(1)}, bf16[2,16,4096]{2,1,0:T(8,128)(2,1)S(1)}, u32[]{:S(2)}, u32[]{:S(2)}) collective-permute-start(bf16[2,16,4096]{2,1,0:T(8,128)(2,1)S(1)} %get-tuple-element.8), channel_id=1, source_target_pairs={{0,2},{2,0},{4,6},{6,4},{8,10},{10,8},{12,14},{14,12},{1,3},{3,1},... | collective-permute-start | bytes 786440 | tf_op jit(solution)/shard_map/ppermute | solution.py:22
  32.2 7.7 %collective-permute-start.7 = (bf16[16,4096]{1,0:T(8,128)(2,1)S(1)}, bf16[16,4096]{1,0:T(8,128)(2,1)S(1)}, u32[]{:S(2)}, u32[]{:S(2)}) collective-permute-start(bf16[16,4096]{1,0:T(8,128)(2,1)S(1)} %dynamic-slice_bitcast_fusion), channel_id=1, source_target_pairs={{0,4},{2,6},{4,8},{6,10},{8,12},{10,14},{12,0},{14,2},{1,5},{3,7},... | collective-permute-start | bytes 393224 | tf_op jit(solution)/shard_map/ppermute | solution.py:15
  39.9 5.1 %collective-permute-start.8 = (bf16[16,4096]{1,0:T(8,128)(2,1)S(1)}, bf16[16,4096]{1,0:T(8,128)(2,1)S(1)}, u32[]{:S(2)}, u32[]{:S(2)}) collective-permute-start(bf16[16,4096]{1,0:T(8,128)(2,1)S(1)} %collective-permute-done.7), channel_id=1, source_target_pairs={{0,16},{16,0},{1,17},{17,1},{2,18},{18,2},{3,19},{19,3},{4,20},{20... | collective-permute-start | bytes 393224 | tf_op jit(solution)/shard_map/ppermute | solution.py:8
  41.5 3.5 %copy-start.2 = (bf16[2,128,4096]{2,1,0:T(8,128)(2,1)}, bf16[2,128,4096]{2,1,0:T(8,128)(2,1)S(1)}, u32[]{:S(2)}) copy-start(bf16[2,128,4096]{2,1,0:T(8,128)(2,1)S(1)} %constant_dynamic-update-slice_fusion.2) | copy-start | bytes 6291460
  45.7 9.6 %collective-permute-start.9 = (bf16[2,16,4096]{2,1,0:T(8,128)(2,1)S(1)}, bf16[2,16,4096]{2,1,0:T(8,128)(2,1)S(1)}, u32[]{:S(2)}, u32[]{:S(2)}) collective-permute-start(bf16[2,16,4096]{2,1,0:T(8,128)(2,1)S(1)} %get-tuple-element.6), channel_id=1, source_target_pairs={{0,2},{2,0},{4,6},{6,4},{8,10},{10,8},{12,14},{14,12},{1,3},{3,1},... | collective-permute-start | bytes 786440 | tf_op jit(solution)/shard_map/ppermute | solution.py:22
  56.0 5.4 %copy-start.3 = (bf16[2,128,4096]{2,1,0:T(8,128)(2,1)S(1)}, bf16[2,128,4096]{2,1,0:T(8,128)(2,1)}, u32[]{:S(2)}) copy-start(bf16[2,128,4096]{2,1,0:T(8,128)(2,1)} %constant_dynamic-update-slice_fusion) | copy-start | bytes 6291460
  59.9 4.6 %collective-permute-start.10 = (f32[128,128]{1,0:T(8,128)S(1)}, f32[128,128]{1,0:T(8,128)S(1)}, u32[]{:S(2)}, u32[]{:S(2)}) collective-permute-start(f32[128,128]{1,0:T(8,128)S(1)} %fusion.4), channel_id=1, source_target_pairs={{0,1},{1,0},{2,3},{3,2},{4,5},{5,4},{6,7},{7,6},{8,9},{9,8},{10,11... | collective-permute-start | bytes 196616 | tf_op jit(solution)/shard_map/ppermute | solution.py:66

commit v2 on v0

v2 whole, which is shorter than its diff:
```python
import functools

import jax
import jax.numpy as jnp
from jax import lax
from jax.experimental import pallas as pl
from jax.experimental.pallas import tpu as pltpu
from jax.sharding import PartitionSpec as P

PAIR = 2
COLUMNS = 4
LANES_LAST = (((1,), (1,)), ((), ()))


def condition(own, left_factor, right_factor):
    layer_count, count, width = own.shape
    rows_out, rows_in = left_factor.shape[1], right_factor.shape[1]
    grid = own.astype(jnp.float32).reshape(layer_count, count, rows_out, rows_in)
    left_part = jnp.einsum("lab,lnbc->lnac", left_factor, grid, precision=lax.Precision.HIGHEST)
    both = jnp.einsum("lnac,lcd->lnad", left_part, right_factor, precision=lax.Precision.HIGHEST)
    return both.reshape(layer_count, count, width).astype(jnp.bfloat16)


def along_columns(value, step):
    pairs = [
        (((k + step) % COLUMNS) * PAIR + c, k * PAIR + c)
        for k in range(COLUMNS)
        for c in range(PAIR)
    ]
    return lax.ppermute(value, "train", pairs)


def relay(value):
    pairs = [(a * PAIR + c, b * PAIR + c) for a, b in ((0, 2), (2, 3), (3, 1), (1, 0)) for c in range(PAIR)]
    return lax.ppermute(value, "train", pairs)


def other_core(value):
    return lax.ppermute(value, "train", [(k, k ^ 1) for k in range(COLUMNS * PAIR)])


def other_part(value):
    return lax.ppermute(value, "parts", [(0, 1), (1, 0)])


def score_kernel(
    train, own, own_c, s1, s1_c, s3, s3_c, y1, y1_c, y3, y3_c, r2, r2_c, d2, d2_c, sent, kept, table, terms
):
    part = lax.axis_index("parts")
    place = lax.axis_index("train")
    here = lax.axis_index("layer")
    column, core = place // PAIR, lax.rem(place, PAIR)
    count = own.shape[1]

    def put(layer, step, twin, block):
        member = lax.rem(column + step, COLUMNS) * PAIR + (1 - core if twin else core)
        table[layer, pl.ds(pl.multiple_of(member * count, count), count), :] = block

    for twin, (a, b, c, d, e, f, g) in enumerate(
        ((own, s1, s3, y1, y3, r2, d2), (own_c, s1_c, s3_c, y1_c, y3_c, r2_c, d2_c))
    ):
        put(0, 0, twin, a[0])
        put(1, 0, twin, a[1])
        put(part, 1, twin, b[...])
        put(part, 3, twin, c[...])
        put(1 - part, 1, twin, d[...])
        put(1 - part, 3, twin, e[...])
        put(part, 2, twin, f[...])
        put(1 - part, 2, twin, g[...])

    rows, layer_count, width = train.shape
    queries = table.shape[1]
    both = lax.dot_general(
        train.reshape(rows * layer_count, width)[...],
        table[...].reshape(layer_count * queries, width),
        LANES_LAST,
        preferred_element_type=jnp.float32,
    )
    for layer in range(layer_count):
        terms[layer] = both[:, layer * queries : (layer + 1) * queries]
    share = kept.shape[0]
    for out, owner in ((sent, 1 - here), (kept, here)):
        first = pl.multiple_of(owner * share * layer_count, share * layer_count)
        out[...] = sum(
            terms[layer, pl.ds(first + layer, share, stride=layer_count), :] for layer in range(layer_count)
        )


def direct(train_grads, queries, left_factor, right_factor):
    own = condition(queries[:, 0], left_factor, right_factor)
    me = lax.axis_index("parts")
    column = lax.axis_index("train") // PAIR
    mine = lax.dynamic_index_in_dim(own, me, 0, keepdims=False)
    theirs = lax.dynamic_index_in_dim(own, 1 - me, 0, keepdims=False)
    s1 = along_columns(mine, 1)
    s3 = along_columns(mine, 3)
    d2 = along_columns(theirs, 2)
    s1, s3 = lax.optimization_barrier((s1, s3))
    passed = jnp.where(column == 1, s1, jnp.where(column == 2, s3, mine))
    r2 = relay(passed)
    d2, r2 = lax.optimization_barrier((d2, r2))
    y1 = other_part(s1)
    y3 = other_part(s3)
    blocks = []
    for block in (own, s1, s3, y1, y3, r2, d2):
        blocks += [block, other_core(block)]

    rows, layer_count, width = train_grads.shape
    total = queries.shape[2] * COLUMNS * PAIR
    share = rows // 2
    spec = pl.BlockSpec(memory_space=pltpu.VMEM)
    flops = 4 * rows * layer_count * width * total
    sent, kept = pl.pallas_call(
        score_kernel,
        out_shape=[jax.ShapeDtypeStruct((share, total), jnp.float32)] * 2,
        in_specs=[spec] * (1 + len(blocks)),
        out_specs=[spec] * 2,
        scratch_shapes=[
            pltpu.VMEM((layer_count, total, width), jnp.bfloat16),
            pltpu.VMEM((layer_count, rows * layer_count, total), jnp.float32),
        ],
        compiler_params=pltpu.CompilerParams(vmem_limit_bytes=24 * 2**20),
        cost_estimate=pl.CostEstimate(flops=flops, bytes_accessed=6 * 2**20, transcendentals=0),
        name="scores",
    )(train_grads, *blocks)
    return kept + lax.ppermute(sent, "layer", [(0, 1), (1, 0)])


def general(shape, train_grads, queries, left_factor, right_factor):
    layers = shape["layer"]
    own = condition(queries[:, 0], left_factor, right_factor)
    block = lax.all_gather(own, "train", axis=1, tiled=True)
    share = train_grads.shape[0] // layers
    here = lax.axis_index("layer")

    def terms(step):
        rows = lax.dynamic_slice_in_dim(train_grads, (here + step) % layers * share, share, 0)
        return jnp.einsum("fkm,krm->fr", rows, block, preferred_element_type=jnp.float32)

    scores = terms(0)
    for step in range(1, layers):
        scores += lax.ppermute(terms(step), "layer", [(k, (k + step) % layers) for k in range(layers)])
    return scores


def body(shape, train_grads, queries, left_factor, right_factor):
    fits = (
        shape["train"] == COLUMNS * PAIR
        and shape["parts"] == shape["layer"] == 2
        and shape["query"] == 1
        and train_grads.shape[0] % 32 == 0
        and train_grads.shape[1:] == (2, 4096)
        and queries.shape[1:] == (1, 16, 4096)
    )
    if fits:
        return direct(train_grads, queries, left_factor, right_factor)
    return general(shape, train_grads, queries, left_factor, right_factor)


def solution(mesh):
    return jax.shard_map(
        functools.partial(body, dict(mesh.shape)),
        mesh=mesh,
        in_specs=(
            P(("parts", "train"), "layer", None),
            P("layer", "query", "train", None),
            P("layer", None, None),
            P("layer", None, None),
        ),
        out_specs=P(("parts", "train", "layer"), "query"),
        check_vma=False,
    )
```

time: 87.4 us -> 39.8 us (0.46)
  waiting for transfers between devices: 53.3 us -> 12.7 us
  starting transfers between devices: 0.04 us -> 17.9 us
  between operations: 13.5 us -> 0.06 us
  matrix products: 11.9 us -> 2.41 us
  local copies, waits for them, and re-layouts: 8.42 us -> 4.18 us
  Pallas kernels: 0 us -> 1.64 us
    all_gather x1 -> x0, waiting for transfers between devices: 32.2 us -> none  [body(): block = lax.all_gather(queries, 'train', axis=2, tiled=True)[:, 0]]
    psum x1 -> x0, waiting for transfers between devices: 21.1 us -> none  [body(): summed = lax.psum(partial_value, 'layer')]
    ppermute x0 -> x14, starting transfers between devices: none -> 17.9 us  [the longest x3 6.13 us: along_columns(): return lax.ppermute(value, 'train', pairs)]
    ppermute x0 -> x14, waiting for transfers between devices: none -> 12.7 us  [the longest x3 4.73 us: along_columns(): return lax.ppermute(value, 'train', pairs)]
    dot_general x3 -> x2, matrix products: 11.9 us -> 2.41 us  [the longest x1 1.86 us: condition(): jnp.einsum('lnac,lcd->lnad', left_part, right_factor, precision=lax.Preci...]
    all_gather x1 -> x0, local copies, waits for them, and re-layouts: 4.88 us -> none  [body(): block = lax.all_gather(queries, 'train', axis=2, tiled=True)[:, 0]]
    pallas_call x0 -> x1, Pallas kernels: none -> 1.64 us  [direct(): pl.pallas_call(score_kernel, out_shape=[jax.ShapeDtypeStruct((share, tota...]
    dynamic_slice x2 -> x0, local copies, waits for them, and re-layouts: 1.57 us -> none  [body(): lax.dynamic_slice_in_dim(summed, lax.axis_index('layer') * share, share, 0)]
  transfers between devices with their start and end apart: 2 -> 14, of which waited for: 2 -> 7; matrix products, arithmetic and copies ran while one was open for 0% -> 0% of each run, Pallas kernels for 0% -> 0%
where the time goes in v2:
time: 39.8 us; the launch traced here: 39.6 us
  starting transfers between devices  17.9 us (45%)
  waiting for transfers between devices  12.7 us (32%)
  local copies, waits for them, and re-layouts  4.18 us (11%)
  matrix products  2.41 us (6%)
  Pallas kernels  1.64 us (4%)
  other arithmetic  0.66 us (2%)
    ppermute x3, starting transfers between devices, along_columns(): return lax.ppermute(value, 'train', pairs)  6.13 us
    ppermute x1, starting transfers between devices, relay(): return lax.ppermute(value, 'train', pairs)  6.1 us
    ppermute x3, waiting for transfers between devices, along_columns(): return lax.ppermute(value, 'train', pairs)  4.73 us
    ppermute x2, waiting for transfers between devices, other_part(): return lax.ppermute(value, 'parts', [(0, 1), (1, 0)])  4.13 us
    ppermute x1, waiting for transfers between devices, direct(): return kept + lax.ppermute(sent, 'layer', [(0, 1), (1, 0)])  2.85 us
    ppermute x2, starting transfers between devices, other_part(): return lax.ppermute(value, 'parts', [(0, 1), (1, 0)])  2.61 us
    unnamed x4, local copies, waits for them, and re-layouts  2.19 us
    dot_general x1, matrix products, condition(): jnp.einsum('lnac,lcd->lnad', left_part, right_factor, precision=lax.Preci...  1.86 us
  transfers between devices with their start and end apart: 14, of which 7 were waited for; matrix products, arithmetic and copies ran while one was open for 0% of the time, Pallas kernels for 0%

profile of v2, /device:TPU:0, one launch (start us, length us, event | category | flops | bytes accessed | tf_op | source)
XLA Modules:
  0.0 39.6 jit_solution(13557259927695059110)
XLA Ops:
  0.0 0.0 copy-start
  0.0 1.5 %reshape.6 = bf16[2,16,64,64]{3,2,1,0:T(8,128)(2,1)S(1)} reshape(bf16[2,1,16,4096]{3,2,1,0:T(8,128)(2,1)} %param.5) | data formatting | bytes 524288 | tf_op jit(solution)/shard_map/reshape | solution.py:18
  1.5 0.0 copy-done
  1.5 0.5 %convolution_bitcast_fusion = f32[2,16,64,64]{3,2,1,0:T(8,128)S(1)} fusion(bf16[2,16,64,64]{3,2,1,0:T(8,128)(2,1)S(1)} %reshape.6, f32[2,64,64]{2,1,0:T(8,128)S(1)} %copy-done), kind=kOutput, calls=%fused_computation | convolution fusion | flops 100663296 | bytes 819200 | tf_op jit(solution)/shard_map/lab,lnbc->lnac/dot_general | solution.py:19
  2.1 1.9 %convolution_convert_fusion = bf16[2,16,64,64]{3,2,1,0:T(8,128)(2,1)S(1)} fusion(f32[2,16,64,64]{3,2,1,0:T(8,128)S(1)} %convolution_bitcast_fusion, f32[2,64,64]{2,1,0:T(8,128)} %param.7), kind=kOutput, calls=%fused_computation.1 | convolution fusion | flops 100794368 | bytes 819200 | tf_op jit(solution)/shard_map/lnac,lcd->lnad/dot_general | solution.py:20
  3.9 0.5 %convert_element_type.7.own = bf16[2,16,4096]{2,1,0:T(8,128)(2,1)S(1)} reshape(bf16[2,16,64,64]{3,2,1,0:T(8,128)(2,1)S(1)} %convolution_convert_fusion) | data formatting | bytes 524288 | tf_op jit(solution)/shard_map/convert_element_type | solution.py:21
  4.4 3.1 %collective-permute-start.2 = (bf16[16,4096]{1,0:T(8,128)(2,1)S(1)}, bf16[16,4096]{1,0:T(8,128)(2,1)S(1)}, u32[]{:S(2)}, u32[]{:S(2)}) collective-permute-start(bf16[16,4096]{1,0:T(8,128)(2,1)S(1)} %get-tuple-element.18), channel_id=1, source_target_pairs={{12,0},{14,2},{0,4},{2,6},{4,8},{6,10},{8,12},{10,14},{13,1},{15,3... | collective-permute-start | bytes 393224 | tf_op jit(solution)/shard_map/ppermute | solution.py:30
  7.5 2.1 %collective-permute-start.1 = (bf16[16,4096]{1,0:T(8,128)(2,1)S(1)}, bf16[16,4096]{1,0:T(8,128)(2,1)S(1)}, u32[]{:S(2)}, u32[]{:S(2)}) collective-permute-start(bf16[16,4096]{1,0:T(8,128)(2,1)S(1)} %get-tuple-element.18), channel_id=1, source_target_pairs={{4,0},{6,2},{8,4},{10,6},{12,8},{14,10},{0,12},{2,14},{5,1},{7,3},... | collective-permute-start | bytes 393224 | tf_op jit(solution)/shard_map/ppermute | solution.py:30
  9.6 0.9 %collective-permute-start.9 = (bf16[16,4096]{1,0:T(8,128)(2,1)S(1)}, bf16[16,4096]{1,0:T(8,128)(2,1)S(1)}, u32[]{:S(2)}, u32[]{:S(2)}) collective-permute-start(bf16[16,4096]{1,0:T(8,128)(2,1)S(1)} %get-tuple-element.17), channel_id=1, source_target_pairs={{8,0},{10,2},{12,4},{14,6},{0,8},{2,10},{4,12},{6,14},{9,1},{11,3}... | collective-permute-start | bytes 393224 | tf_op jit(solution)/shard_map/ppermute | solution.py:30
  10.6 3.3 %collective-permute-done.2.s3 = bf16[16,4096]{1,0:T(8,128)(2,1)S(1)} collective-permute-done((bf16[16,4096]{1,0:T(8,128)(2,1)S(1)}, bf16[16,4096]{1,0:T(8,128)(2,1)S(1)}, u32[]{:S(2)}, u32[]{:S(2)}) %collective-permute-start.2) | collective-permute-done | bytes 131104 | tf_op jit(solution)/shard_map/ppermute | solution.py:30
  13.9 1.4 %collective-permute-done.1.s1 = bf16[16,4096]{1,0:T(8,128)(2,1)S(1)} collective-permute-done((bf16[16,4096]{1,0:T(8,128)(2,1)S(1)}, bf16[16,4096]{1,0:T(8,128)(2,1)S(1)}, u32[]{:S(2)}, u32[]{:S(2)}) %collective-permute-start.1) | collective-permute-done | bytes 131104 | tf_op jit(solution)/shard_map/ppermute | solution.py:30
  15.3 6.1 %collective-permute-start.10 = (bf16[16,4096]{1,0:T(8,128)(2,1)S(1)}, bf16[16,4096]{1,0:T(8,128)(2,1)S(1)}, u32[]{:S(2)}, u32[]{:S(2)}) collective-permute-start(bf16[16,4096]{1,0:T(8,128)(2,1)S(1)} %select_select_fusion), channel_id=1, source_target_pairs={{0,8},{2,10},{8,12},{10,14},{12,4},{14,6},{4,0},{6,2},{1,9},{3,11}... | collective-permute-start | bytes 393224 | tf_op jit(solution)/shard_map/ppermute | solution.py:35
  21.4 1.5 %collective-permute-start.5 = (bf16[16,4096]{1,0:T(8,128)(2,1)S(1)}, bf16[16,4096]{1,0:T(8,128)(2,1)S(1)}, u32[]{:S(2)}, u32[]{:S(2)}) collective-permute-start(bf16[16,4096]{1,0:T(8,128)(2,1)S(1)} %collective-permute-done.1.s1), channel_id=1, source_target_pairs={{0,16},{16,0},{1,17},{17,1},{2,18},{18,2},{3,19},{19,3},{4,20},{20... | collective-permute-start | bytes 393224 | tf_op jit(solution)/shard_map/ppermute | solution.py:43
  22.9 0.0 collective-permute-start.3
  22.9 0.5 %collective-permute-start = (bf16[2,16,4096]{2,1,0:T(8,128)(2,1)S(1)}, bf16[2,16,4096]{2,1,0:T(8,128)(2,1)S(1)}, u32[]{:S(2)}, u32[]{:S(2)}) collective-permute-start(bf16[2,16,4096]{2,1,0:T(8,128)(2,1)S(1)} %convert_element_type.7.own), channel_id=1, source_target_pairs={{0,2},{2,0},{4,6},{6,4},{8,10},{10,8},{12,14},{14,12},{1,3},{3,1},... | collective-permute-start | bytes 786440 | tf_op jit(solution)/shard_map/ppermute | solution.py:39
  23.4 0.0 collective-permute-done.9.d2
  23.5 1.1 %collective-permute-start.7 = (bf16[16,4096]{1,0:T(8,128)(2,1)S(1)}, bf16[16,4096]{1,0:T(8,128)(2,1)S(1)}, u32[]{:S(2)}, u32[]{:S(2)}) collective-permute-start(bf16[16,4096]{1,0:T(8,128)(2,1)S(1)} %collective-permute-done.2.s3), channel_id=1, source_target_pairs={{0,16},{16,0},{1,17},{17,1},{2,18},{18,2},{3,19},{19,3},{4,20},{20... | collective-permute-start | bytes 393224 | tf_op jit(solution)/shard_map/ppermute | solution.py:43
  24.5 0.0 collective-permute-done.10.r2
  24.5 0.0 collective-permute-start.4
  24.5 2.1 %collective-permute-done.5.y1 = bf16[16,4096]{1,0:T(8,128)(2,1)S(1)} collective-permute-done((bf16[16,4096]{1,0:T(8,128)(2,1)S(1)}, bf16[16,4096]{1,0:T(8,128)(2,1)S(1)}, u32[]{:S(2)}, u32[]{:S(2)}) %collective-permute-start.5) | collective-permute-done | bytes 131104 | tf_op jit(solution)/shard_map/ppermute | solution.py:43
  26.7 0.0 collective-permute-start.11
  26.7 0.0 collective-permute-done.3.s1_c
  26.7 0.5 %collective-permute-start.12 = (bf16[16,4096]{1,0:T(8,128)(2,1)S(1)}, bf16[16,4096]{1,0:T(8,128)(2,1)S(1)}, u32[]{:S(2)}, u32[]{:S(2)}) collective-permute-start(bf16[16,4096]{1,0:T(8,128)(2,1)S(1)} %collective-permute-done.9.d2), channel_id=1, source_target_pairs={{0,2},{2,0},{4,6},{6,4},{8,10},{10,8},{12,14},{14,12},{1,3},{3,1},... | collective-permute-start | bytes 393224 | tf_op jit(solution)/shard_map/ppermute | solution.py:39
  27.2 2.0 %collective-permute-done.7.y3 = bf16[16,4096]{1,0:T(8,128)(2,1)S(1)} collective-permute-done((bf16[16,4096]{1,0:T(8,128)(2,1)S(1)}, bf16[16,4096]{1,0:T(8,128)(2,1)S(1)}, u32[]{:S(2)}, u32[]{:S(2)}) %collective-permute-start.7) | collective-permute-done | bytes 131104 | tf_op jit(solution)/shard_map/ppermute | solution.py:43
  29.2 0.0 collective-permute-start.6
  29.2 0.0 collective-permute-done.4.s3_c
  29.2 0.5 %collective-permute-start.8 = (bf16[16,4096]{1,0:T(8,128)(2,1)S(1)}, bf16[16,4096]{1,0:T(8,128)(2,1)S(1)}, u32[]{:S(2)}, u32[]{:S(2)}) collective-permute-start(bf16[16,4096]{1,0:T(8,128)(2,1)S(1)} %collective-permute-done.7.y3), channel_id=1, source_target_pairs={{0,2},{2,0},{4,6},{6,4},{8,10},{10,8},{12,14},{14,12},{1,3},{3,1},... | collective-permute-start | bytes 393224 | tf_op jit(solution)/shard_map/ppermute | solution.py:39
  29.7 0.0 collective-permute-done.own_c
  29.7 0.0 collective-permute-done.11.r2_c
  29.7 0.0 collective-permute-done.12.d2_c
  29.7 0.8 %collective-permute-done.6.y1_c = bf16[16,4096]{1,0:T(8,128)(2,1)S(1)} collective-permute-done((bf16[16,4096]{1,0:T(8,128)(2,1)S(1)}, bf16[16,4096]{1,0:T(8,128)(2,1)S(1)}, u32[]{:S(2)}, u32[]{:S(2)}) %collective-permute-start.6) | collective-permute-done | bytes 131104 | tf_op jit(solution)/shard_map/ppermute | solution.py:39
  30.5 0.2 collective-permute-done.8.y3_c
  30.7 0.0 copy-start.1
  30.7 2.2 %copy-done.1 = bf16[256,2,4096]{2,1,0:T(2,128)(2,1)S(1)} copy-done((bf16[256,2,4096]{2,1,0:T(2,128)(2,1)S(1)}, bf16[256,2,4096]{2,1,0:T(2,128)(2,1)}, u32[]{:S(2)}) %copy-start.1) | copy-done | bytes 4194328
  32.9 1.6 %scores.1 = (f32[128,128]{1,0:T(8,128)S(1)}, f32[128,128]{1,0:T(8,128)S(1)}) custom-call(bf16[256,2,4096]{2,1,0:T(2,128)(2,1)S(1)} %copy-done.1, bf16[2,16,4096]{2,1,0:T(8,128)(2,1)S(1)} %convert_element_type.7.own, bf16[2,16,4096]{2,1,0:T(8,128)(2,1)S(1)} %collective-permute-done.own_c, bf16[16,4096]{1,0:T(8,128)(2,1)S(1)} %collective-permute-done.1.s1, ...), custom_call_target="tpu_custom_call" | custom-call | flops 1073741824 | bytes 6291456 | tf_op jit(solution)/shard_map/scores/pallas_call | solution.py:113
  34.6 1.5 %collective-permute-start.13 = (f32[128,128]{1,0:T(8,128)S(1)}, f32[128,128]{1,0:T(8,128)S(1)}, u32[]{:S(2)}, u32[]{:S(2)}) collective-permute-start(f32[128,128]{1,0:T(8,128)S(1)} %get-tuple-element.16), channel_id=1, source_target_pairs={{0,1},{1,0},{2,3},{3,2},{4,5},{5,4},{6,7},{7,6},{8,9},{9,8},{10,11... | collective-permute-start | bytes 196616 | tf_op jit(solution)/shard_map/ppermute | solution.py:126
  36.1 2.8 %collective-permute-done.13 = f32[128,128]{1,0:T(8,128)S(1)} collective-permute-done((f32[128,128]{1,0:T(8,128)S(1)}, f32[128,128]{1,0:T(8,128)S(1)}, u32[]{:S(2)}, u32[]{:S(2)}) %collective-permute-start.13) | collective-permute-done | bytes 65568 | tf_op jit(solution)/shard_map/ppermute | solution.py:126
  38.9 0.6 %add.14 = f32[128,128]{1,0:T(8,128)} add(f32[128,128]{1,0:T(8,128)S(1)} %get-tuple-element.15, f32[128,128]{1,0:T(8,128)S(1)} %collective-permute-done.13) | non-fusion elementwise | flops 16384 | bytes 196608 | tf_op jit(solution)/shard_map/add | solution.py:126
  (2 shorter events, 0.0 us)
Async XLA Ops:
  0.0 1.5 %copy-start = (f32[2,64,64]{2,1,0:T(8,128)S(1)}, f32[2,64,64]{2,1,0:T(8,128)}, u32[]{:S(2)}) copy-start(f32[2,64,64]{2,1,0:T(8,128)} %param.6) | copy-start | bytes 98308
  4.4 9.4 %collective-permute-start.2 = (bf16[16,4096]{1,0:T(8,128)(2,1)S(1)}, bf16[16,4096]{1,0:T(8,128)(2,1)S(1)}, u32[]{:S(2)}, u32[]{:S(2)}) collective-permute-start(bf16[16,4096]{1,0:T(8,128)(2,1)S(1)} %get-tuple-element.18), channel_id=1, source_target_pairs={{12,0},{14,2},{0,4},{2,6},{4,8},{6,10},{8,12},{10,14},{13,1},{15,3... | collective-permute-start | bytes 393224 | tf_op jit(solution)/shard_map/ppermute | solution.py:30
  7.5 7.8 %collective-permute-start.1 = (bf16[16,4096]{1,0:T(8,128)(2,1)S(1)}, bf16[16,4096]{1,0:T(8,128)(2,1)S(1)}, u32[]{:S(2)}, u32[]{:S(2)}) collective-permute-start(bf16[16,4096]{1,0:T(8,128)(2,1)S(1)} %get-tuple-element.18), channel_id=1, source_target_pairs={{4,0},{6,2},{8,4},{10,6},{12,8},{14,10},{0,12},{2,14},{5,1},{7,3},... | collective-permute-start | bytes 393224 | tf_op jit(solution)/shard_map/ppermute | solution.py:30
  9.6 13.8 %collective-permute-start.9 = (bf16[16,4096]{1,0:T(8,128)(2,1)S(1)}, bf16[16,4096]{1,0:T(8,128)(2,1)S(1)}, u32[]{:S(2)}, u32[]{:S(2)}) collective-permute-start(bf16[16,4096]{1,0:T(8,128)(2,1)S(1)} %get-tuple-element.17), channel_id=1, source_target_pairs={{8,0},{10,2},{12,4},{14,6},{0,8},{2,10},{4,12},{6,14},{9,1},{11,3}... | collective-permute-start | bytes 393224 | tf_op jit(solution)/shard_map/ppermute | solution.py:30
  15.3 9.2 %collective-permute-start.10 = (bf16[16,4096]{1,0:T(8,128)(2,1)S(1)}, bf16[16,4096]{1,0:T(8,128)(2,1)S(1)}, u32[]{:S(2)}, u32[]{:S(2)}) collective-permute-start(bf16[16,4096]{1,0:T(8,128)(2,1)S(1)} %select_select_fusion), channel_id=1, source_target_pairs={{0,8},{2,10},{8,12},{10,14},{12,4},{14,6},{4,0},{6,2},{1,9},{3,11}... | collective-permute-start | bytes 393224 | tf_op jit(solution)/shard_map/ppermute | solution.py:35
  21.4 5.3 %collective-permute-start.5 = (bf16[16,4096]{1,0:T(8,128)(2,1)S(1)}, bf16[16,4096]{1,0:T(8,128)(2,1)S(1)}, u32[]{:S(2)}, u32[]{:S(2)}) collective-permute-start(bf16[16,4096]{1,0:T(8,128)(2,1)S(1)} %collective-permute-done.1.s1), channel_id=1, source_target_pairs={{0,16},{16,0},{1,17},{17,1},{2,18},{18,2},{3,19},{19,3},{4,20},{20... | collective-permute-start | bytes 393224 | tf_op jit(solution)/shard_map/ppermute | solution.py:43
  22.9 3.7 %collective-permute-start.3 = (bf16[16,4096]{1,0:T(8,128)(2,1)S(1)}, bf16[16,4096]{1,0:T(8,128)(2,1)S(1)}, u32[]{:S(2)}, u32[]{:S(2)}) collective-permute-start(bf16[16,4096]{1,0:T(8,128)(2,1)S(1)} %collective-permute-done.1.s1), channel_id=1, source_target_pairs={{0,2},{2,0},{4,6},{6,4},{8,10},{10,8},{12,14},{14,12},{1,3},{3,1},... | collective-permute-start | bytes 393224 | tf_op jit(solution)/shard_map/ppermute | solution.py:39
  22.9 6.8 %collective-permute-start = (bf16[2,16,4096]{2,1,0:T(8,128)(2,1)S(1)}, bf16[2,16,4096]{2,1,0:T(8,128)(2,1)S(1)}, u32[]{:S(2)}, u32[]{:S(2)}) collective-permute-start(bf16[2,16,4096]{2,1,0:T(8,128)(2,1)S(1)} %convert_element_type.7.own), channel_id=1, source_target_pairs={{0,2},{2,0},{4,6},{6,4},{8,10},{10,8},{12,14},{14,12},{1,3},{3,1},... | collective-permute-start | bytes 786440 | tf_op jit(solution)/shard_map/ppermute | solution.py:39
  23.5 5.7 %collective-permute-start.7 = (bf16[16,4096]{1,0:T(8,128)(2,1)S(1)}, bf16[16,4096]{1,0:T(8,128)(2,1)S(1)}, u32[]{:S(2)}, u32[]{:S(2)}) collective-permute-start(bf16[16,4096]{1,0:T(8,128)(2,1)S(1)} %collective-permute-done.2.s3), channel_id=1, source_target_pairs={{0,16},{16,0},{1,17},{17,1},{2,18},{18,2},{3,19},{19,3},{4,20},{20... | collective-permute-start | bytes 393224 | tf_op jit(solution)/shard_map/ppermute | solution.py:43
  24.5 4.7 %collective-permute-start.4 = (bf16[16,4096]{1,0:T(8,128)(2,1)S(1)}, bf16[16,4096]{1,0:T(8,128)(2,1)S(1)}, u32[]{:S(2)}, u32[]{:S(2)}) collective-permute-start(bf16[16,4096]{1,0:T(8,128)(2,1)S(1)} %collective-permute-done.2.s3), channel_id=1, source_target_pairs={{0,2},{2,0},{4,6},{6,4},{8,10},{10,8},{12,14},{14,12},{1,3},{3,1},... | collective-permute-start | bytes 393224 | tf_op jit(solution)/shard_map/ppermute | solution.py:39
  26.7 3.0 %collective-permute-start.11 = (bf16[16,4096]{1,0:T(8,128)(2,1)S(1)}, bf16[16,4096]{1,0:T(8,128)(2,1)S(1)}, u32[]{:S(2)}, u32[]{:S(2)}) collective-permute-start(bf16[16,4096]{1,0:T(8,128)(2,1)S(1)} %collective-permute-done.10.r2), channel_id=1, source_target_pairs={{0,2},{2,0},{4,6},{6,4},{8,10},{10,8},{12,14},{14,12},{1,3},{3,1},... | collective-permute-start | bytes 393224 | tf_op jit(solution)/shard_map/ppermute | solution.py:39
  26.7 3.0 %collective-permute-start.12 = (bf16[16,4096]{1,0:T(8,128)(2,1)S(1)}, bf16[16,4096]{1,0:T(8,128)(2,1)S(1)}, u32[]{:S(2)}, u32[]{:S(2)}) collective-permute-start(bf16[16,4096]{1,0:T(8,128)(2,1)S(1)} %collective-permute-done.9.d2), channel_id=1, source_target_pairs={{0,2},{2,0},{4,6},{6,4},{8,10},{10,8},{12,14},{14,12},{1,3},{3,1},... | collective-permute-start | bytes 393224 | tf_op jit(solution)/shard_map/ppermute | solution.py:39
  29.2 1.3 %collective-permute-start.6 = (bf16[16,4096]{1,0:T(8,128)(2,1)S(1)}, bf16[16,4096]{1,0:T(8,128)(2,1)S(1)}, u32[]{:S(2)}, u32[]{:S(2)}) collective-permute-start(bf16[16,4096]{1,0:T(8,128)(2,1)S(1)} %collective-permute-done.5.y1), channel_id=1, source_target_pairs={{0,2},{2,0},{4,6},{6,4},{8,10},{10,8},{12,14},{14,12},{1,3},{3,1},... | collective-permute-start | bytes 393224 | tf_op jit(solution)/shard_map/ppermute | solution.py:39
  29.2 1.5 %collective-permute-start.8 = (bf16[16,4096]{1,0:T(8,128)(2,1)S(1)}, bf16[16,4096]{1,0:T(8,128)(2,1)S(1)}, u32[]{:S(2)}, u32[]{:S(2)}) collective-permute-start(bf16[16,4096]{1,0:T(8,128)(2,1)S(1)} %collective-permute-done.7.y3), channel_id=1, source_target_pairs={{0,2},{2,0},{4,6},{6,4},{8,10},{10,8},{12,14},{14,12},{1,3},{3,1},... | collective-permute-start | bytes 393224 | tf_op jit(solution)/shard_map/ppermute | solution.py:39
  30.7 2.2 %copy-start.1 = (bf16[256,2,4096]{2,1,0:T(2,128)(2,1)S(1)}, bf16[256,2,4096]{2,1,0:T(2,128)(2,1)}, u32[]{:S(2)}) copy-start(bf16[256,2,4096]{2,1,0:T(2,128)(2,1)} %train.1) | copy-start | bytes 12582916
  34.6 4.4 %collective-permute-start.13 = (f32[128,128]{1,0:T(8,128)S(1)}, f32[128,128]{1,0:T(8,128)S(1)}, u32[]{:S(2)}, u32[]{:S(2)}) collective-permute-start(f32[128,128]{1,0:T(8,128)S(1)} %get-tuple-element.16), channel_id=1, source_target_pairs={{0,1},{1,0},{2,3},{3,2},{4,5},{5,4},{6,7},{7,6},{8,9},{9,8},{10,11... | collective-permute-start | bytes 196616 | tf_op jit(solution)/shard_map/ppermute | solution.py:126

commit v3 on v2

--- a/solution.py
+++ b/solution.py
@@ -30,11 +30,6 @@
     return lax.ppermute(value, "train", pairs)
 
 
-def relay(value):
-    pairs = [(a * PAIR + c, b * PAIR + c) for a, b in ((0, 2), (2, 3), (3, 1), (1, 0)) for c in range(PAIR)]
-    return lax.ppermute(value, "train", pairs)
-
-
 def other_core(value):
     return lax.ppermute(value, "train", [(k, k ^ 1) for k in range(COLUMNS * PAIR)])
 
@@ -43,8 +38,27 @@
     return lax.ppermute(value, "parts", [(0, 1), (1, 0)])
 
 
+def copy_kernel(source, target, done):
+    copy = pltpu.make_async_copy(source, target, done)
+    copy.start()
+    copy.wait()
+
+
+def copy_near(value):
+    return pl.pallas_call(
+        copy_kernel,
+        out_shape=jax.ShapeDtypeStruct(value.shape, value.dtype),
+        in_specs=[pl.BlockSpec(memory_space=pltpu.HBM)],
+        out_specs=pl.BlockSpec(memory_space=pltpu.VMEM),
+        scratch_shapes=[pltpu.SemaphoreType.DMA],
+        compiler_params=pltpu.CompilerParams(vmem_limit_bytes=6 * 2**20),
+        cost_estimate=pl.CostEstimate(flops=0, bytes_accessed=2 * value.size * 2, transcendentals=0),
+        name="near",
+    )(value)
+
+
 def score_kernel(
-    train, own, own_c, s1, s1_c, s3, s3_c, y1, y1_c, y3, y3_c, r2, r2_c, d2, d2_c, sent, kept, table, terms
+    train, own, own_c, s2, s2_c, s1, s1_c, s3, s3_c, y2, y2_c, y1, y1_c, y3, y3_c, sent, kept, table, terms
 ):
     part = lax.axis_index("parts")
     place = lax.axis_index("train")
@@ -56,17 +70,14 @@
         member = lax.rem(column + step, COLUMNS) * PAIR + (1 - core if twin else core)
         table[layer, pl.ds(pl.multiple_of(member * count, count), count), :] = block
 
-    for twin, (a, b, c, d, e, f, g) in enumerate(
-        ((own, s1, s3, y1, y3, r2, d2), (own_c, s1_c, s3_c, y1_c, y3_c, r2_c, d2_c))
+    for twin, (both, here_steps, there_steps) in enumerate(
+        ((own, (s1, s2, s3), (y1, y2, y3)), (own_c, (s1_c, s2_c, s3_c), (y1_c, y2_c, y3_c)))
     ):
-        put(0, 0, twin, a[0])
-        put(1, 0, twin, a[1])
-        put(part, 1, twin, b[...])
-        put(part, 3, twin, c[...])
-        put(1 - part, 1, twin, d[...])
-        put(1 - part, 3, twin, e[...])
-        put(part, 2, twin, f[...])
-        put(1 - part, 2, twin, g[...])
+        put(0, 0, twin, both[0])
+        put(1, 0, twin, both[1])
+        for step in range(1, COLUMNS):
+            put(part, step, twin, here_steps[step - 1][...])
+            put(1 - part, step, twin, there_steps[step - 1][...])
 
     rows, layer_count, width = train.shape
     queries = table.shape[1]
@@ -88,21 +99,16 @@
 
 def direct(train_grads, queries, left_factor, right_factor):
     own = condition(queries[:, 0], left_factor, right_factor)
-    me = lax.axis_index("parts")
-    column = lax.axis_index("train") // PAIR
-    mine = lax.dynamic_index_in_dim(own, me, 0, keepdims=False)
-    theirs = lax.dynamic_index_in_dim(own, 1 - me, 0, keepdims=False)
+    mine = lax.dynamic_index_in_dim(own, lax.axis_index("parts"), 0, keepdims=False)
+    near = copy_near(train_grads)
+    s2 = along_columns(mine, 2)
     s1 = along_columns(mine, 1)
     s3 = along_columns(mine, 3)
-    d2 = along_columns(theirs, 2)
-    s1, s3 = lax.optimization_barrier((s1, s3))
-    passed = jnp.where(column == 1, s1, jnp.where(column == 2, s3, mine))
-    r2 = relay(passed)
-    d2, r2 = lax.optimization_barrier((d2, r2))
+    y2 = other_part(s2)
     y1 = other_part(s1)
     y3 = other_part(s3)
     blocks = []
-    for block in (own, s1, s3, y1, y3, r2, d2):
+    for block in (own, s2, s1, s3, y2, y1, y3):
         blocks += [block, other_core(block)]
 
     rows, layer_count, width = train_grads.shape
@@ -122,7 +128,7 @@
         compiler_params=pltpu.CompilerParams(vmem_limit_bytes=24 * 2**20),
         cost_estimate=pl.CostEstimate(flops=flops, bytes_accessed=6 * 2**20, transcendentals=0),
         name="scores",
-    )(train_grads, *blocks)
+    )(near, *blocks)
     return kept + lax.ppermute(sent, "layer", [(0, 1), (1, 0)])
 
 

time: 39.8 us -> 37 us (0.930)
  starting transfers between devices: 17.9 us -> 12.9 us
  waiting for transfers between devices: 12.7 us -> 14.7 us
    ppermute x1 -> x0, starting transfers between devices: 6.1 us -> none  [relay(): return lax.ppermute(value, 'train', pairs)]
    ppermute x3, waiting for transfers between devices: 4.73 us -> 7.98 us  [along_columns(): return lax.ppermute(value, 'train', pairs)]
    ppermute x2 -> x3, starting transfers between devices: 2.61 us -> 3.92 us  [other_part(): return lax.ppermute(value, 'parts', [(0, 1), (1, 0)])]
    ppermute x7, waiting for transfers between devices: 1.02 us -> 0.02 us  [other_core(): lax.ppermute(value, 'train', [(k, k ^ 1) for k in range(COLUMNS * PAIR)])]
    ppermute x2 -> x3, waiting for transfers between devices: 4.13 us -> 3.64 us  [other_part(): return lax.ppermute(value, 'parts', [(0, 1), (1, 0)])]
  transfers between devices with their start and end apart: 14 -> 14, of which waited for: 7 -> 4; matrix products, arithmetic and copies ran while one was open for 0% -> 0% of each run, Pallas kernels for 0% -> 1%
where the time goes in v3:
time: 37 us; the launch traced here: 36.8 us
  waiting for transfers between devices  14.7 us (40%)
  starting transfers between devices  12.9 us (35%)
  local copies, waits for them, and re-layouts  4.17 us (11%)
  matrix products  2.41 us (7%)
  Pallas kernels  1.94 us (5%)
  other arithmetic  0.64 us (2%)
    ppermute x3, waiting for transfers between devices, along_columns(): return lax.ppermute(value, 'train', pairs)  7.98 us
    ppermute x3, starting transfers between devices, along_columns(): return lax.ppermute(value, 'train', pairs)  6.13 us
    ppermute x3, starting transfers between devices, other_part(): return lax.ppermute(value, 'parts', [(0, 1), (1, 0)])  3.92 us
    ppermute x3, waiting for transfers between devices, other_part(): return lax.ppermute(value, 'parts', [(0, 1), (1, 0)])  3.64 us
    ppermute x1, waiting for transfers between devices, direct(): return kept + lax.ppermute(sent, 'layer', [(0, 1), (1, 0)])  3.02 us
    unnamed x4, local copies, waits for them, and re-layouts  2.19 us
    dot_general x1, matrix products, condition(): jnp.einsum('lnac,lcd->lnad', left_part, right_factor, precision=lax.Preci...  1.86 us
    pallas_call x1, Pallas kernels, direct(): pl.pallas_call(score_kernel, out_shape=[jax.ShapeDtypeStruct((share, tota...  1.66 us
  transfers between devices with their start and end apart: 14, of which 4 were waited for; matrix products, arithmetic and copies ran while one was open for 0% of the time, Pallas kernels for 1%

profile of v3, /device:TPU:0, one launch (start us, length us, event | category | flops | bytes accessed | tf_op | source)
XLA Modules:
  0.0 36.8 jit_solution(12753920671637532497)
XLA Ops:
  0.0 0.0 copy-start
  0.0 1.5 %reshape.6 = bf16[2,16,64,64]{3,2,1,0:T(8,128)(2,1)S(1)} reshape(bf16[2,1,16,4096]{3,2,1,0:T(8,128)(2,1)} %param.5) | data formatting | bytes 524288 | tf_op jit(solution)/shard_map/reshape | solution.py:18
  1.5 0.0 copy-done
  1.5 0.5 %convolution_bitcast_fusion = f32[2,16,64,64]{3,2,1,0:T(8,128)S(1)} fusion(bf16[2,16,64,64]{3,2,1,0:T(8,128)(2,1)S(1)} %reshape.6, f32[2,64,64]{2,1,0:T(8,128)S(1)} %copy-done), kind=kOutput, calls=%fused_computation | convolution fusion | flops 100663296 | bytes 819200 | tf_op jit(solution)/shard_map/lab,lnbc->lnac/dot_general | solution.py:19
  2.1 1.9 %convolution_convert_fusion = bf16[2,16,64,64]{3,2,1,0:T(8,128)(2,1)S(1)} fusion(f32[2,16,64,64]{3,2,1,0:T(8,128)S(1)} %convolution_bitcast_fusion, f32[2,64,64]{2,1,0:T(8,128)} %param.7), kind=kOutput, calls=%fused_computation.1 | convolution fusion | flops 100794368 | bytes 819200 | tf_op jit(solution)/shard_map/lnac,lcd->lnad/dot_general | solution.py:20
  3.9 0.5 %convert_element_type.7.own = bf16[2,16,4096]{2,1,0:T(8,128)(2,1)S(1)} reshape(bf16[2,16,64,64]{3,2,1,0:T(8,128)(2,1)S(1)} %convolution_convert_fusion) | data formatting | bytes 524288 | tf_op jit(solution)/shard_map/convert_element_type | solution.py:21
  4.4 3.1 %collective-permute-start.5 = (bf16[16,4096]{1,0:T(8,128)(2,1)S(1)}, bf16[16,4096]{1,0:T(8,128)(2,1)S(1)}, u32[]{:S(2)}, u32[]{:S(2)}) collective-permute-start(bf16[16,4096]{1,0:T(8,128)(2,1)S(1)} %dynamic-slice_bitcast_fusion), channel_id=1, source_target_pairs={{12,0},{14,2},{0,4},{2,6},{4,8},{6,10},{8,12},{10,14},{13,1},{15,3... | collective-permute-start | bytes 393224 | tf_op jit(solution)/shard_map/ppermute | solution.py:30
  7.5 2.1 %collective-permute-start.3 = (bf16[16,4096]{1,0:T(8,128)(2,1)S(1)}, bf16[16,4096]{1,0:T(8,128)(2,1)S(1)}, u32[]{:S(2)}, u32[]{:S(2)}) collective-permute-start(bf16[16,4096]{1,0:T(8,128)(2,1)S(1)} %dynamic-slice_bitcast_fusion), channel_id=1, source_target_pairs={{4,0},{6,2},{8,4},{10,6},{12,8},{14,10},{0,12},{2,14},{5,1},{7,3},... | collective-permute-start | bytes 393224 | tf_op jit(solution)/shard_map/ppermute | solution.py:30
  9.6 0.9 %collective-permute-start.1 = (bf16[16,4096]{1,0:T(8,128)(2,1)S(1)}, bf16[16,4096]{1,0:T(8,128)(2,1)S(1)}, u32[]{:S(2)}, u32[]{:S(2)}) collective-permute-start(bf16[16,4096]{1,0:T(8,128)(2,1)S(1)} %dynamic-slice_bitcast_fusion), channel_id=1, source_target_pairs={{8,0},{10,2},{12,4},{14,6},{0,8},{2,10},{4,12},{6,14},{9,1},{11,3}... | collective-permute-start | bytes 393224 | tf_op jit(solution)/shard_map/ppermute | solution.py:30
  10.5 3.3 %collective-permute-done.5.s3 = bf16[16,4096]{1,0:T(8,128)(2,1)S(1)} collective-permute-done((bf16[16,4096]{1,0:T(8,128)(2,1)S(1)}, bf16[16,4096]{1,0:T(8,128)(2,1)S(1)}, u32[]{:S(2)}, u32[]{:S(2)}) %collective-permute-start.5) | collective-permute-done | bytes 131104 | tf_op jit(solution)/shard_map/ppermute | solution.py:30
  13.9 1.8 %collective-permute-start.11 = (bf16[16,4096]{1,0:T(8,128)(2,1)S(1)}, bf16[16,4096]{1,0:T(8,128)(2,1)S(1)}, u32[]{:S(2)}, u32[]{:S(2)}) collective-permute-start(bf16[16,4096]{1,0:T(8,128)(2,1)S(1)} %collective-permute-done.5.s3), channel_id=1, source_target_pairs={{0,16},{16,0},{1,17},{17,1},{2,18},{18,2},{3,19},{19,3},{4,20},{20... | collective-permute-start | bytes 393224 | tf_op jit(solution)/shard_map/ppermute | solution.py:38
  15.6 0.0 collective-permute-start
  15.6 0.5 %collective-permute-start.6 = (bf16[16,4096]{1,0:T(8,128)(2,1)S(1)}, bf16[16,4096]{1,0:T(8,128)(2,1)S(1)}, u32[]{:S(2)}, u32[]{:S(2)}) collective-permute-start(bf16[16,4096]{1,0:T(8,128)(2,1)S(1)} %collective-permute-done.5.s3), channel_id=1, source_target_pairs={{0,2},{2,0},{4,6},{6,4},{8,10},{10,8},{12,14},{14,12},{1,3},{3,1},... | collective-permute-start | bytes 393224 | tf_op jit(solution)/shard_map/ppermute | solution.py:34
  16.1 0.0 collective-permute-done.3.s1
  16.1 0.7 %collective-permute-start.9 = (bf16[16,4096]{1,0:T(8,128)(2,1)S(1)}, bf16[16,4096]{1,0:T(8,128)(2,1)S(1)}, u32[]{:S(2)}, u32[]{:S(2)}) collective-permute-start(bf16[16,4096]{1,0:T(8,128)(2,1)S(1)} %collective-permute-done.3.s1), channel_id=1, source_target_pairs={{0,16},{16,0},{1,17},{17,1},{2,18},{18,2},{3,19},{19,3},{4,20},{20... | collective-permute-start | bytes 393224 | tf_op jit(solution)/shard_map/ppermute | solution.py:38
  16.8 4.7 %collective-permute-done.1.s2 = bf16[16,4096]{1,0:T(8,128)(2,1)S(1)} collective-permute-done((bf16[16,4096]{1,0:T(8,128)(2,1)S(1)}, bf16[16,4096]{1,0:T(8,128)(2,1)S(1)}, u32[]{:S(2)}, u32[]{:S(2)}) %collective-permute-start.1) | collective-permute-done | bytes 131104 | tf_op jit(solution)/shard_map/ppermute | solution.py:30
  21.4 0.0 collective-permute-start.4
  21.5 0.0 collective-permute-done.11.y3
  21.5 1.5 %collective-permute-start.7 = (bf16[16,4096]{1,0:T(8,128)(2,1)S(1)}, bf16[16,4096]{1,0:T(8,128)(2,1)S(1)}, u32[]{:S(2)}, u32[]{:S(2)}) collective-permute-start(bf16[16,4096]{1,0:T(8,128)(2,1)S(1)} %collective-permute-done.1.s2), channel_id=1, source_target_pairs={{0,16},{16,0},{1,17},{17,1},{2,18},{18,2},{3,19},{19,3},{4,20},{20... | collective-permute-start | bytes 393224 | tf_op jit(solution)/shard_map/ppermute | solution.py:38
  23.0 0.0 collective-permute-done.6.s3_c
  23.0 0.2 collective-permute-start.2
  23.2 0.0 collective-permute-done.9.y1
  23.2 0.3 collective-permute-start.12
  23.5 0.0 collective-permute-done.4.s1_c
  23.5 0.2 collective-permute-start.10
  23.7 3.6 %collective-permute-done.7.y2 = bf16[16,4096]{1,0:T(8,128)(2,1)S(1)} collective-permute-done((bf16[16,4096]{1,0:T(8,128)(2,1)S(1)}, bf16[16,4096]{1,0:T(8,128)(2,1)S(1)}, u32[]{:S(2)}, u32[]{:S(2)}) %collective-permute-start.7) | collective-permute-done | bytes 131104 | tf_op jit(solution)/shard_map/ppermute | solution.py:38
  27.4 0.0 collective-permute-start.8
  27.4 0.0 copy-start.1
  27.4 2.2 %copy-done.1 = bf16[256,2,4096]{2,1,0:T(2,128)(2,1)S(1)} copy-done((bf16[256,2,4096]{2,1,0:T(2,128)(2,1)S(1)}, bf16[256,2,4096]{2,1,0:T(2,128)(2,1)}, u32[]{:S(2)}) %copy-start.1) | copy-done | bytes 4194328
  29.6 0.3 near.1.train
  29.9 0.0 collective-permute-done.2.s2_c
  29.9 0.0 collective-permute-done.own_c
  29.9 0.0 collective-permute-done.12.y3_c
  29.9 0.0 collective-permute-done.10.y1_c
  29.9 0.0 collective-permute-done.8.y2_c
  29.9 1.7 %scores.1 = (f32[128,128]{1,0:T(8,128)S(1)}, f32[128,128]{1,0:T(8,128)S(1)}) custom-call(bf16[256,2,4096]{2,1,0:T(2,128)(2,1)S(1)} %near.1.train, bf16[2,16,4096]{2,1,0:T(8,128)(2,1)S(1)} %convert_element_type.7.own, bf16[2,16,4096]{2,1,0:T(8,128)(2,1)S(1)} %collective-permute-done.own_c, bf16[16,4096]{1,0:T(8,128)(2,1)S(1)} %collective-permute-done.1.s2, ...), custom_call_target="tpu_custom_call" | custom-call | flops 1073741824 | bytes 6291456 | tf_op jit(solution)/shard_map/scores/pallas_call | solution.py:119
  31.6 1.6 %collective-permute-start.13 = (f32[128,128]{1,0:T(8,128)S(1)}, f32[128,128]{1,0:T(8,128)S(1)}, u32[]{:S(2)}, u32[]{:S(2)}) collective-permute-start(f32[128,128]{1,0:T(8,128)S(1)} %get-tuple-element.8), channel_id=1, source_target_pairs={{0,1},{1,0},{2,3},{3,2},{4,5},{5,4},{6,7},{7,6},{8,9},{9,8},{10,11... | collective-permute-start | bytes 196616 | tf_op jit(solution)/shard_map/ppermute | solution.py:132
  33.1 3.0 %collective-permute-done.13 = f32[128,128]{1,0:T(8,128)S(1)} collective-permute-done((f32[128,128]{1,0:T(8,128)S(1)}, f32[128,128]{1,0:T(8,128)S(1)}, u32[]{:S(2)}, u32[]{:S(2)}) %collective-permute-start.13) | collective-permute-done | bytes 65568 | tf_op jit(solution)/shard_map/ppermute | solution.py:132
  36.1 0.6 %add.8 = f32[128,128]{1,0:T(8,128)} add(f32[128,128]{1,0:T(8,128)S(1)} %get-tuple-element.7, f32[128,128]{1,0:T(8,128)S(1)} %collective-permute-done.13) | non-fusion elementwise | flops 16384 | bytes 196608 | tf_op jit(solution)/shard_map/add | solution.py:132
  (1 shorter events, 0.0 us)
Async XLA Ops:
  0.0 1.5 %copy-start = (f32[2,64,64]{2,1,0:T(8,128)S(1)}, f32[2,64,64]{2,1,0:T(8,128)}, u32[]{:S(2)}) copy-start(f32[2,64,64]{2,1,0:T(8,128)} %param.6) | copy-start | bytes 98308
  4.4 9.4 %collective-permute-start.5 = (bf16[16,4096]{1,0:T(8,128)(2,1)S(1)}, bf16[16,4096]{1,0:T(8,128)(2,1)S(1)}, u32[]{:S(2)}, u32[]{:S(2)}) collective-permute-start(bf16[16,4096]{1,0:T(8,128)(2,1)S(1)} %dynamic-slice_bitcast_fusion), channel_id=1, source_target_pairs={{12,0},{14,2},{0,4},{2,6},{4,8},{6,10},{8,12},{10,14},{13,1},{15,3... | collective-permute-start | bytes 393224 | tf_op jit(solution)/shard_map/ppermute | solution.py:30
  7.5 8.6 %collective-permute-start.3 = (bf16[16,4096]{1,0:T(8,128)(2,1)S(1)}, bf16[16,4096]{1,0:T(8,128)(2,1)S(1)}, u32[]{:S(2)}, u32[]{:S(2)}) collective-permute-start(bf16[16,4096]{1,0:T(8,128)(2,1)S(1)} %dynamic-slice_bitcast_fusion), channel_id=1, source_target_pairs={{4,0},{6,2},{8,4},{10,6},{12,8},{14,10},{0,12},{2,14},{5,1},{7,3},... | collective-permute-start | bytes 393224 | tf_op jit(solution)/shard_map/ppermute | solution.py:30
  9.6 11.8 %collective-permute-start.1 = (bf16[16,4096]{1,0:T(8,128)(2,1)S(1)}, bf16[16,4096]{1,0:T(8,128)(2,1)S(1)}, u32[]{:S(2)}, u32[]{:S(2)}) collective-permute-start(bf16[16,4096]{1,0:T(8,128)(2,1)S(1)} %dynamic-slice_bitcast_fusion), channel_id=1, source_target_pairs={{8,0},{10,2},{12,4},{14,6},{0,8},{2,10},{4,12},{6,14},{9,1},{11,3}... | collective-permute-start | bytes 393224 | tf_op jit(solution)/shard_map/ppermute | solution.py:30
  13.9 7.6 %collective-permute-start.11 = (bf16[16,4096]{1,0:T(8,128)(2,1)S(1)}, bf16[16,4096]{1,0:T(8,128)(2,1)S(1)}, u32[]{:S(2)}, u32[]{:S(2)}) collective-permute-start(bf16[16,4096]{1,0:T(8,128)(2,1)S(1)} %collective-permute-done.5.s3), channel_id=1, source_target_pairs={{0,16},{16,0},{1,17},{17,1},{2,18},{18,2},{3,19},{19,3},{4,20},{20... | collective-permute-start | bytes 393224 | tf_op jit(solution)/shard_map/ppermute | solution.py:38
  15.6 14.2 %collective-permute-start = (bf16[2,16,4096]{2,1,0:T(8,128)(2,1)S(1)}, bf16[2,16,4096]{2,1,0:T(8,128)(2,1)S(1)}, u32[]{:S(2)}, u32[]{:S(2)}) collective-permute-start(bf16[2,16,4096]{2,1,0:T(8,128)(2,1)S(1)} %convert_element_type.7.own), channel_id=1, source_target_pairs={{0,2},{2,0},{4,6},{6,4},{8,10},{10,8},{12,14},{14,12},{1,3},{3,1},... | collective-permute-start | bytes 786440 | tf_op jit(solution)/shard_map/ppermute | solution.py:34
  15.6 7.4 %collective-permute-start.6 = (bf16[16,4096]{1,0:T(8,128)(2,1)S(1)}, bf16[16,4096]{1,0:T(8,128)(2,1)S(1)}, u32[]{:S(2)}, u32[]{:S(2)}) collective-permute-start(bf16[16,4096]{1,0:T(8,128)(2,1)S(1)} %collective-permute-done.5.s3), channel_id=1, source_target_pairs={{0,2},{2,0},{4,6},{6,4},{8,10},{10,8},{12,14},{14,12},{1,3},{3,1},... | collective-permute-start | bytes 393224 | tf_op jit(solution)/shard_map/ppermute | solution.py:34
  16.1 7.1 %collective-permute-start.9 = (bf16[16,4096]{1,0:T(8,128)(2,1)S(1)}, bf16[16,4096]{1,0:T(8,128)(2,1)S(1)}, u32[]{:S(2)}, u32[]{:S(2)}) collective-permute-start(bf16[16,4096]{1,0:T(8,128)(2,1)S(1)} %collective-permute-done.3.s1), channel_id=1, source_target_pairs={{0,16},{16,0},{1,17},{17,1},{2,18},{18,2},{3,19},{19,3},{4,20},{20... | collective-permute-start | bytes 393224 | tf_op jit(solution)/shard_map/ppermute | solution.py:38
  21.4 2.1 %collective-permute-start.4 = (bf16[16,4096]{1,0:T(8,128)(2,1)S(1)}, bf16[16,4096]{1,0:T(8,128)(2,1)S(1)}, u32[]{:S(2)}, u32[]{:S(2)}) collective-permute-start(bf16[16,4096]{1,0:T(8,128)(2,1)S(1)} %collective-permute-done.3.s1), channel_id=1, source_target_pairs={{0,2},{2,0},{4,6},{6,4},{8,10},{10,8},{12,14},{14,12},{1,3},{3,1},... | collective-permute-start | bytes 393224 | tf_op jit(solution)/shard_map/ppermute | solution.py:34
  21.5 5.9 %collective-permute-start.7 = (bf16[16,4096]{1,0:T(8,128)(2,1)S(1)}, bf16[16,4096]{1,0:T(8,128)(2,1)S(1)}, u32[]{:S(2)}, u32[]{:S(2)}) collective-permute-start(bf16[16,4096]{1,0:T(8,128)(2,1)S(1)} %collective-permute-done.1.s2), channel_id=1, source_target_pairs={{0,16},{16,0},{1,17},{17,1},{2,18},{18,2},{3,19},{19,3},{4,20},{20... | collective-permute-start | bytes 393224 | tf_op jit(solution)/shard_map/ppermute | solution.py:38
  23.0 6.9 %collective-permute-start.2 = (bf16[16,4096]{1,0:T(8,128)(2,1)S(1)}, bf16[16,4096]{1,0:T(8,128)(2,1)S(1)}, u32[]{:S(2)}, u32[]{:S(2)}) collective-permute-start(bf16[16,4096]{1,0:T(8,128)(2,1)S(1)} %collective-permute-done.1.s2), channel_id=1, source_target_pairs={{0,2},{2,0},{4,6},{6,4},{8,10},{10,8},{12,14},{14,12},{1,3},{3,1},... | collective-permute-start | bytes 393224 | tf_op jit(solution)/shard_map/ppermute | solution.py:34
  23.2 6.7 %collective-permute-start.12 = (bf16[16,4096]{1,0:T(8,128)(2,1)S(1)}, bf16[16,4096]{1,0:T(8,128)(2,1)S(1)}, u32[]{:S(2)}, u32[]{:S(2)}) collective-permute-start(bf16[16,4096]{1,0:T(8,128)(2,1)S(1)} %collective-permute-done.11.y3), channel_id=1, source_target_pairs={{0,2},{2,0},{4,6},{6,4},{8,10},{10,8},{12,14},{14,12},{1,3},{3,1},... | collective-permute-start | bytes 393224 | tf_op jit(solution)/shard_map/ppermute | solution.py:34
  23.5 6.4 %collective-permute-start.10 = (bf16[16,4096]{1,0:T(8,128)(2,1)S(1)}, bf16[16,4096]{1,0:T(8,128)(2,1)S(1)}, u32[]{:S(2)}, u32[]{:S(2)}) collective-permute-start(bf16[16,4096]{1,0:T(8,128)(2,1)S(1)} %collective-permute-done.9.y1), channel_id=1, source_target_pairs={{0,2},{2,0},{4,6},{6,4},{8,10},{10,8},{12,14},{14,12},{1,3},{3,1},... | collective-permute-start | bytes 393224 | tf_op jit(solution)/shard_map/ppermute | solution.py:34
  27.4 2.5 %collective-permute-start.8 = (bf16[16,4096]{1,0:T(8,128)(2,1)S(1)}, bf16[16,4096]{1,0:T(8,128)(2,1)S(1)}, u32[]{:S(2)}, u32[]{:S(2)}) collective-permute-start(bf16[16,4096]{1,0:T(8,128)(2,1)S(1)} %collective-permute-done.7.y2), channel_id=1, source_target_pairs={{0,2},{2,0},{4,6},{6,4},{8,10},{10,8},{12,14},{14,12},{1,3},{3,1},... | collective-permute-start | bytes 393224 | tf_op jit(solution)/shard_map/ppermute | solution.py:34
  27.4 2.2 %copy-start.1 = (bf16[256,2,4096]{2,1,0:T(2,128)(2,1)S(1)}, bf16[256,2,4096]{2,1,0:T(2,128)(2,1)}, u32[]{:S(2)}) copy-start(bf16[256,2,4096]{2,1,0:T(2,128)(2,1)} %source.1) | copy-start | bytes 12582916
  31.6 4.6 %collective-permute-start.13 = (f32[128,128]{1,0:T(8,128)S(1)}, f32[128,128]{1,0:T(8,128)S(1)}, u32[]{:S(2)}, u32[]{:S(2)}) collective-permute-start(f32[128,128]{1,0:T(8,128)S(1)} %get-tuple-element.8), channel_id=1, source_target_pairs={{0,1},{1,0},{2,3},{3,2},{4,5},{5,4},{6,7},{7,6},{8,9},{9,8},{10,11... | collective-permute-start | bytes 196616 | tf_op jit(solution)/shard_map/ppermute | solution.py:132

commit v4 on v3

--- a/solution.py
+++ b/solution.py
@@ -7,9 +7,19 @@
 from jax.experimental.pallas import tpu as pltpu
 from jax.sharding import PartitionSpec as P
 
+LANES = 128
 PAIR = 2
 COLUMNS = 4
 LANES_LAST = (((1,), (1,)), ((), ()))
+
+
+def split(value, parts):
+    pieces = []
+    for _ in range(parts):
+        piece = value.astype(jnp.bfloat16)
+        pieces.append(piece)
+        value = value - piece.astype(jnp.float32)
+    return pieces
 
 
 def condition(own, left_factor, right_factor):
@@ -19,6 +29,114 @@
     left_part = jnp.einsum("lab,lnbc->lnac", left_factor, grid, precision=lax.Precision.HIGHEST)
     both = jnp.einsum("lnac,lcd->lnad", left_part, right_factor, precision=lax.Precision.HIGHEST)
     return both.reshape(layer_count, count, width).astype(jnp.bfloat16)
+
+
+def condition_block(block, left, right, put, spread, stacked, placed):
+    count, width = block.shape
+    inner = right.shape[0]
+    pairs = width // LANES
+    first_half = lax.broadcasted_iota(jnp.int32, (pairs, LANES), 1) < inner
+
+    empty = jnp.zeros((inner, LANES), jnp.float32)
+    twice = jnp.concatenate([right, right], axis=1)
+    weight = jnp.concatenate(
+        [jnp.concatenate([twice, empty], axis=1), jnp.concatenate([empty, twice], axis=1)], axis=0
+    )
+    high, middle, low = split(weight, 3)
+    rows = jnp.concatenate([block[:, k * LANES : (k + 1) * LANES] for k in range(pairs)], axis=0)
+    right_part = jnp.dot(
+        jnp.concatenate([rows, rows], axis=1),
+        jnp.concatenate([high, middle], axis=0),
+        preferred_element_type=jnp.float32,
+    ) + jnp.dot(rows, low, preferred_element_type=jnp.float32)
+    spread[0] = right_part[:, :LANES]
+    spread[1] = right_part[:, LANES:]
+
+    for q in range(0, count, 2):
+        for j in range(2):
+            even = spread[j, pl.ds(q, pairs, stride=count), :]
+            odd = spread[j, pl.ds(q + 1, pairs, stride=count), :]
+            stacked[q // 2, pl.ds(j, pairs, stride=2), :] = jnp.where(first_half, even, odd)
+
+    left_high, left_low = split(left, 2)
+    moved = jnp.concatenate([stacked[k] for k in range(count // 2)], axis=1)
+    moved_high, moved_low = split(moved, 2)
+    done = jnp.dot(
+        jnp.concatenate([left_high, left_high, left_low], axis=1),
+        jnp.concatenate([moved_high, moved_low, moved_high], axis=0),
+        preferred_element_type=jnp.float32,
+    )
+    for k in range(count // 2):
+        stacked[k] = done[:, k * LANES : (k + 1) * LANES]
+
+    for q in range(0, count, 2):
+        upper = stacked[q // 2, pl.ds(0, pairs, stride=2), :]
+        lower = stacked[q // 2, pl.ds(1, pairs, stride=2), :]
+        placed[pl.ds(q, pairs, stride=count), :] = jnp.where(first_half, upper, pltpu.roll(lower, inner, 1))
+        placed[pl.ds(q + 1, pairs, stride=count), :] = jnp.where(
+            first_half, pltpu.roll(upper, inner, 1), lower
+        )
+    for k in range(pairs):
+        put(k, placed[k * count : (k + 1) * count, :].astype(jnp.bfloat16))
+
+
+def condition_scratch(layers, count, width):
+    pairs = width // LANES
+    return [
+        pltpu.VMEM((layers, 2, pairs * count, LANES), jnp.float32),
+        pltpu.VMEM((layers, count // 2, 2 * pairs, LANES), jnp.float32),
+        pltpu.VMEM((layers, pairs * count, LANES), jnp.float32),
+    ]
+
+
+def condition_kernel(queries, left, right, own, mine, block_in, left_in, right_in, spread, stacked, placed, arrived):
+    layers = queries.shape[0]
+    copies = []
+    for k, (source, target) in enumerate(((left, left_in), (right, right_in), (queries.at[:, 0], block_in))):
+        copies.append(pltpu.make_async_copy(source, target, arrived.at[k]))
+        copies[-1].start()
+    for copy in copies:
+        copy.wait()
+    for layer in range(layers):
+
+        def put(k, tile):
+            own[layer, :, k * LANES : (k + 1) * LANES] = tile
+
+        condition_block(
+            block_in[layer],
+            left_in[layer],
+            right_in[layer],
+            put,
+            spread.at[layer],
+            stacked.at[layer],
+            placed.at[layer],
+        )
+    mine[...] = own[lax.axis_index("parts")]
+
+
+def condition_near(queries, left_factor, right_factor):
+    layers, _, count, width = queries.shape
+    spec = pl.BlockSpec(memory_space=pltpu.VMEM)
+    far = pl.BlockSpec(memory_space=pltpu.HBM)
+    return pl.pallas_call(
+        condition_kernel,
+        out_shape=[
+            jax.ShapeDtypeStruct((layers, count, width), jnp.bfloat16),
+            jax.ShapeDtypeStruct((count, width), jnp.bfloat16),
+        ],
+        in_specs=[far] * 3,
+        out_specs=[spec] * 2,
+        scratch_shapes=[
+            pltpu.VMEM((layers, count, width), jnp.bfloat16),
+            pltpu.VMEM(left_factor.shape, jnp.float32),
+            pltpu.VMEM(right_factor.shape, jnp.float32),
+            *condition_scratch(layers, count, width),
+            pltpu.SemaphoreType.DMA((3,)),
+        ],
+        compiler_params=pltpu.CompilerParams(vmem_limit_bytes=8 * 2**20),
+        cost_estimate=pl.CostEstimate(flops=2**28, bytes_accessed=2**20, transcendentals=0),
+        name="condition",
+    )(*(pltpu.with_memory_space_constraint(x, pltpu.HBM) for x in (queries, left_factor, right_factor)))
 
 
 def along_columns(value, step):
@@ -54,7 +172,7 @@
         compiler_params=pltpu.CompilerParams(vmem_limit_bytes=6 * 2**20),
         cost_estimate=pl.CostEstimate(flops=0, bytes_accessed=2 * value.size * 2, transcendentals=0),
         name="near",
-    )(value)
+    )(pltpu.with_memory_space_constraint(value, pltpu.HBM))
 
 
 def score_kernel(
@@ -98,8 +216,7 @@
 
 
 def direct(train_grads, queries, left_factor, right_factor):
-    own = condition(queries[:, 0], left_factor, right_factor)
-    mine = lax.dynamic_index_in_dim(own, lax.axis_index("parts"), 0, keepdims=False)
+    own, mine = condition_near(queries, left_factor, right_factor)
     near = copy_near(train_grads)
     s2 = along_columns(mine, 2)
     s1 = along_columns(mine, 1)
@@ -107,6 +224,7 @@
     y2 = other_part(s2)
     y1 = other_part(s1)
     y3 = other_part(s3)
+    y1, near = lax.optimization_barrier((y1, near))
     blocks = []
     for block in (own, s2, s1, s3, y2, y1, y3):
         blocks += [block, other_core(block)]
@@ -157,6 +275,7 @@
         and train_grads.shape[0] % 32 == 0
         and train_grads.shape[1:] == (2, 4096)
         and queries.shape[1:] == (1, 16, 4096)
+        and left_factor.shape[1:] == right_factor.shape[1:] == (64, 64)
     )
     if fits:
         return direct(train_grads, queries, left_factor, right_factor)

time: 37 us -> 32.5 us (0.88)
  Pallas kernels: 1.94 us -> 6.41 us
  local copies, waits for them, and re-layouts: 4.17 us -> 0 us
  waiting for transfers between devices: 14.7 us -> 11.3 us
  matrix products: 2.41 us -> 0 us
  starting transfers between devices: 12.9 us -> 13.9 us
    ppermute x3, waiting for transfers between devices: 3.64 us -> 0.56 us  [other_part(): return lax.ppermute(value, 'parts', [(0, 1), (1, 0)])]
    pallas_call x0 -> x1, Pallas kernels: none -> 2.58 us  [condition_near(): pl.pallas_call(condition_kernel, out_shape=[jax.ShapeDtypeStruct((layers,...]
    dot_general x2 -> x0, matrix products: 2.41 us -> none  [the longest x1 1.86 us: condition(): jnp.einsum('lnac,lcd->lnad', left_part, right_factor, precision=lax.Preci...]
    unnamed x4 -> x0, local copies, waits for them, and re-layouts: 2.19 us -> none
    pallas_call x1, Pallas kernels: 0.29 us -> 2.2 us  [copy_near(): pl.pallas_call(copy_kernel, out_shape=jax.ShapeDtypeStruct(value.shape, v...]
    reshape x1 -> x0, local copies, waits for them, and re-layouts: 1.5 us -> none  [condition(): own.astype(jnp.float32).reshape(layer_count, count, rows_out, rows_in)]
    ppermute x3, waiting for transfers between devices: 7.98 us -> 6.89 us  [along_columns(): return lax.ppermute(value, 'train', pairs)]
    ppermute x7, waiting for transfers between devices: 0.02 us -> 1.02 us  [other_core(): lax.ppermute(value, 'train', [(k, k ^ 1) for k in range(COLUMNS * PAIR)])]
  transfers between devices with their start and end apart: 14 -> 14, of which waited for: 4 -> 8; matrix products, arithmetic and copies ran while one was open for 0% -> 0% of each run, Pallas kernels for 1% -> 7%
where the time goes in v4:
time: 32.5 us; the launch traced here: 32.3 us
  starting transfers between devices  13.9 us (43%)
  waiting for transfers between devices  11.3 us (35%)
  Pallas kernels  6.41 us (20%)
  other arithmetic  0.64 us (2%)
    ppermute x3, waiting for transfers between devices, along_columns(): return lax.ppermute(value, 'train', pairs)  6.89 us
    ppermute x3, starting transfers between devices, along_columns(): return lax.ppermute(value, 'train', pairs)  6.11 us
    ppermute x3, starting transfers between devices, other_part(): return lax.ppermute(value, 'parts', [(0, 1), (1, 0)])  4.59 us
    ppermute x1, waiting for transfers between devices, direct(): return kept + lax.ppermute(sent, 'layer', [(0, 1), (1, 0)])  2.84 us
    pallas_call x1, Pallas kernels, condition_near(): pl.pallas_call(condition_kernel, out_shape=[jax.ShapeDtypeStruct((layers,...  2.58 us
    pallas_call x1, Pallas kernels, copy_near(): pl.pallas_call(copy_kernel, out_shape=jax.ShapeDtypeStruct(value.shape, v...  2.2 us
    ppermute x7, starting transfers between devices, other_core(): lax.ppermute(value, 'train', [(k, k ^ 1) for k in range(COLUMNS * PAIR)])  1.68 us
    pallas_call x1, Pallas kernels, direct(): pl.pallas_call(score_kernel, out_shape=[jax.ShapeDtypeStruct((share, tota...  1.64 us
  transfers between devices with their start and end apart: 14, of which 8 were waited for; matrix products, arithmetic and copies ran while one was open for 0% of the time, Pallas kernels for 7%

profile of v4, /device:TPU:0, one launch (start us, length us, event | category | flops | bytes accessed | tf_op | source)
XLA Modules:
  0.0 32.3 jit_solution(3610401595063652917)
XLA Ops:
  0.0 2.6 %condition.1 = (bf16[2,16,4096]{2,1,0:T(8,128)(2,1)S(1)}, bf16[16,4096]{1,0:T(8,128)(2,1)S(1)}) custom-call(bf16[2,1,16,4096]{3,2,1,0:T(8,128)(2,1)} %queries.1, f32[2,64,64]{2,1,0:T(8,128)} %left.1, f32[2,64,64]{2,1,0:T(8,128)} %right.1), custom_call_target="tpu_custom_call" | custom-call | flops 268435456 | bytes 1048576 | tf_op jit(solution)/shard_map/condition/pallas_call | solution.py:121
  2.6 5.1 %collective-permute-start = (bf16[16,4096]{1,0:T(8,128)(2,1)S(1)}, bf16[16,4096]{1,0:T(8,128)(2,1)S(1)}, u32[]{:S(2)}, u32[]{:S(2)}) collective-permute-start(bf16[16,4096]{1,0:T(8,128)(2,1)S(1)} %get-tuple-element.11), channel_id=1, source_target_pairs={{4,0},{6,2},{8,4},{10,6},{12,8},{14,10},{0,12},{2,14},{5,1},{7,3},... | collective-permute-start | bytes 393224 | tf_op jit(solution)/shard_map/ppermute | solution.py:148
  7.7 0.0 collective-permute-start.6
  7.7 1.0 %collective-permute-start.3 = (bf16[16,4096]{1,0:T(8,128)(2,1)S(1)}, bf16[16,4096]{1,0:T(8,128)(2,1)S(1)}, u32[]{:S(2)}, u32[]{:S(2)}) collective-permute-start(bf16[16,4096]{1,0:T(8,128)(2,1)S(1)} %get-tuple-element.11), channel_id=1, source_target_pairs={{8,0},{10,2},{12,4},{14,6},{0,8},{2,10},{4,12},{6,14},{9,1},{11,3}... | collective-permute-start | bytes 393224 | tf_op jit(solution)/shard_map/ppermute | solution.py:148
  8.7 2.9 %collective-permute-done.s1 = bf16[16,4096]{1,0:T(8,128)(2,1)S(1)} collective-permute-done((bf16[16,4096]{1,0:T(8,128)(2,1)S(1)}, bf16[16,4096]{1,0:T(8,128)(2,1)S(1)}, u32[]{:S(2)}, u32[]{:S(2)}) %collective-permute-start) | collective-permute-done | bytes 131104 | tf_op jit(solution)/shard_map/ppermute | solution.py:148
  11.6 1.5 %collective-permute-start.1 = (bf16[16,4096]{1,0:T(8,128)(2,1)S(1)}, bf16[16,4096]{1,0:T(8,128)(2,1)S(1)}, u32[]{:S(2)}, u32[]{:S(2)}) collective-permute-start(bf16[16,4096]{1,0:T(8,128)(2,1)S(1)} %collective-permute-done.s1), channel_id=1, source_target_pairs={{0,16},{16,0},{1,17},{17,1},{2,18},{18,2},{3,19},{19,3},{4,20},{20... | collective-permute-start | bytes 393224 | tf_op jit(solution)/shard_map/ppermute | solution.py:156
  13.1 2.8 %collective-permute-done.6.s3 = bf16[16,4096]{1,0:T(8,128)(2,1)S(1)} collective-permute-done((bf16[16,4096]{1,0:T(8,128)(2,1)S(1)}, bf16[16,4096]{1,0:T(8,128)(2,1)S(1)}, u32[]{:S(2)}, u32[]{:S(2)}) %collective-permute-start.6) | collective-permute-done | bytes 131104 | tf_op jit(solution)/shard_map/ppermute | solution.py:148
  15.9 1.5 %collective-permute-start.11 = (bf16[16,4096]{1,0:T(8,128)(2,1)S(1)}, bf16[16,4096]{1,0:T(8,128)(2,1)S(1)}, u32[]{:S(2)}, u32[]{:S(2)}) collective-permute-start(bf16[16,4096]{1,0:T(8,128)(2,1)S(1)} %collective-permute-done.6.s3), channel_id=1, source_target_pairs={{0,16},{16,0},{1,17},{17,1},{2,18},{18,2},{3,19},{19,3},{4,20},{20... | collective-permute-start | bytes 393224 | tf_op jit(solution)/shard_map/ppermute | solution.py:156
  17.5 0.0 collective-permute-start.2
  17.5 0.5 %collective-permute-start.7 = (bf16[16,4096]{1,0:T(8,128)(2,1)S(1)}, bf16[16,4096]{1,0:T(8,128)(2,1)S(1)}, u32[]{:S(2)}, u32[]{:S(2)}) collective-permute-start(bf16[16,4096]{1,0:T(8,128)(2,1)S(1)} %collective-permute-done.6.s3), channel_id=1, source_target_pairs={{0,2},{2,0},{4,6},{6,4},{8,10},{10,8},{12,14},{14,12},{1,3},{3,1},... | collective-permute-start | bytes 393224 | tf_op jit(solution)/shard_map/ppermute | solution.py:152
  18.0 1.2 %collective-permute-done.3.s2 = bf16[16,4096]{1,0:T(8,128)(2,1)S(1)} collective-permute-done((bf16[16,4096]{1,0:T(8,128)(2,1)S(1)}, bf16[16,4096]{1,0:T(8,128)(2,1)S(1)}, u32[]{:S(2)}, u32[]{:S(2)}) %collective-permute-start.3) | collective-permute-done | bytes 131104 | tf_op jit(solution)/shard_map/ppermute | solution.py:148
  19.2 1.5 %collective-permute-start.8 = (bf16[16,4096]{1,0:T(8,128)(2,1)S(1)}, bf16[16,4096]{1,0:T(8,128)(2,1)S(1)}, u32[]{:S(2)}, u32[]{:S(2)}) collective-permute-start(bf16[16,4096]{1,0:T(8,128)(2,1)S(1)} %collective-permute-done.3.s2), channel_id=1, source_target_pairs={{0,16},{16,0},{1,17},{17,1},{2,18},{18,2},{3,19},{19,3},{4,20},{20... | collective-permute-start | bytes 393224 | tf_op jit(solution)/shard_map/ppermute | solution.py:156
  20.7 0.0 collective-permute-done.1.y1
  20.7 0.0 collective-permute-start.4
  20.7 2.2 %near.1.train = bf16[256,2,4096]{2,1,0:T(2,128)(2,1)S(1)} custom-call(bf16[256,2,4096]{2,1,0:T(2,128)(2,1)} %source.1), custom_call_target="tpu_custom_call" | custom-call | bytes 8388608 | tf_op jit(solution)/shard_map/near/pallas_call | solution.py:166
  22.9 0.0 collective-permute-done.11.y3
  22.9 0.6 %collective-permute-start.5 = (bf16[16,4096]{1,0:T(8,128)(2,1)S(1)}, bf16[16,4096]{1,0:T(8,128)(2,1)S(1)}, u32[]{:S(2)}, u32[]{:S(2)}) collective-permute-start(bf16[16,4096]{1,0:T(8,128)(2,1)S(1)} %collective-permute-done.s1), channel_id=1, source_target_pairs={{0,2},{2,0},{4,6},{6,4},{8,10},{10,8},{12,14},{14,12},{1,3},{3,1},... | collective-permute-start | bytes 393224 | tf_op jit(solution)/shard_map/ppermute | solution.py:152
  23.5 0.0 collective-permute-done.7.s3_c
  23.5 0.1 collective-permute-start.12
  23.6 0.6 %collective-permute-done.8.y2 = bf16[16,4096]{1,0:T(8,128)(2,1)S(1)} collective-permute-done((bf16[16,4096]{1,0:T(8,128)(2,1)S(1)}, bf16[16,4096]{1,0:T(8,128)(2,1)S(1)}, u32[]{:S(2)}, u32[]{:S(2)}) %collective-permute-start.8) | collective-permute-done | bytes 131104 | tf_op jit(solution)/shard_map/ppermute | solution.py:156
  24.1 0.0 collective-permute-start.9
  24.1 0.0 collective-permute-done.4.s2_c
  24.1 0.5 %collective-permute-start.10 = (bf16[16,4096]{1,0:T(8,128)(2,1)S(1)}, bf16[16,4096]{1,0:T(8,128)(2,1)S(1)}, u32[]{:S(2)}, u32[]{:S(2)}) collective-permute-start(bf16[16,4096]{1,0:T(8,128)(2,1)S(1)} %collective-permute-done.1.y1), channel_id=1, source_target_pairs={{0,2},{2,0},{4,6},{6,4},{8,10},{10,8},{12,14},{14,12},{1,3},{3,1},... | collective-permute-start | bytes 393224 | tf_op jit(solution)/shard_map/ppermute | solution.py:152
  24.6 0.0 collective-permute-done.5.s1_c
  24.7 0.0 collective-permute-done.2.own_c
  24.7 0.2 collective-permute-done.12.y3_c
  24.8 0.6 %collective-permute-done.9.y2_c = bf16[16,4096]{1,0:T(8,128)(2,1)S(1)} collective-permute-done((bf16[16,4096]{1,0:T(8,128)(2,1)S(1)}, bf16[16,4096]{1,0:T(8,128)(2,1)S(1)}, u32[]{:S(2)}, u32[]{:S(2)}) %collective-permute-start.9) | collective-permute-done | bytes 131104 | tf_op jit(solution)/shard_map/ppermute | solution.py:152
  25.5 0.2 collective-permute-done.10.y1_c
  25.7 1.6 %scores.1 = (f32[128,128]{1,0:T(8,128)S(1)}, f32[128,128]{1,0:T(8,128)S(1)}) custom-call(bf16[256,2,4096]{2,1,0:T(2,128)(2,1)S(1)} %near.1.train, bf16[2,16,4096]{2,1,0:T(8,128)(2,1)S(1)} %get-tuple-element.13.own, bf16[2,16,4096]{2,1,0:T(8,128)(2,1)S(1)} %collective-permute-done.2.own_c, bf16[16,4096]{1,0:T(8,128)(2,1)S(1)} %collective-permute-done.3.s2, ...), custom_call_target="tpu_custom_call" | custom-call | flops 1073741824 | bytes 6291456 | tf_op jit(solution)/shard_map/scores/pallas_call | solution.py:237
  27.3 1.5 %collective-permute-start.13 = (f32[128,128]{1,0:T(8,128)S(1)}, f32[128,128]{1,0:T(8,128)S(1)}, u32[]{:S(2)}, u32[]{:S(2)}) collective-permute-start(f32[128,128]{1,0:T(8,128)S(1)} %get-tuple-element.16), channel_id=1, source_target_pairs={{0,1},{1,0},{2,3},{3,2},{4,5},{5,4},{6,7},{7,6},{8,9},{9,8},{10,11... | collective-permute-start | bytes 196616 | tf_op jit(solution)/shard_map/ppermute | solution.py:250
  28.9 2.8 %collective-permute-done.13 = f32[128,128]{1,0:T(8,128)S(1)} collective-permute-done((f32[128,128]{1,0:T(8,128)S(1)}, f32[128,128]{1,0:T(8,128)S(1)}, u32[]{:S(2)}, u32[]{:S(2)}) %collective-permute-start.13) | collective-permute-done | bytes 65568 | tf_op jit(solution)/shard_map/ppermute | solution.py:250
  31.7 0.6 %add.3 = f32[128,128]{1,0:T(8,128)} add(f32[128,128]{1,0:T(8,128)S(1)} %get-tuple-element.15, f32[128,128]{1,0:T(8,128)S(1)} %collective-permute-done.13) | non-fusion elementwise | flops 16384 | bytes 196608 | tf_op jit(solution)/shard_map/add | solution.py:250
Async XLA Ops:
  2.6 9.0 %collective-permute-start = (bf16[16,4096]{1,0:T(8,128)(2,1)S(1)}, bf16[16,4096]{1,0:T(8,128)(2,1)S(1)}, u32[]{:S(2)}, u32[]{:S(2)}) collective-permute-start(bf16[16,4096]{1,0:T(8,128)(2,1)S(1)} %get-tuple-element.11), channel_id=1, source_target_pairs={{4,0},{6,2},{8,4},{10,6},{12,8},{14,10},{0,12},{2,14},{5,1},{7,3},... | collective-permute-start | bytes 393224 | tf_op jit(solution)/shard_map/ppermute | solution.py:148
  7.7 8.3 %collective-permute-start.6 = (bf16[16,4096]{1,0:T(8,128)(2,1)S(1)}, bf16[16,4096]{1,0:T(8,128)(2,1)S(1)}, u32[]{:S(2)}, u32[]{:S(2)}) collective-permute-start(bf16[16,4096]{1,0:T(8,128)(2,1)S(1)} %get-tuple-element.11), channel_id=1, source_target_pairs={{12,0},{14,2},{0,4},{2,6},{4,8},{6,10},{8,12},{10,14},{13,1},{15,3... | collective-permute-start | bytes 393224 | tf_op jit(solution)/shard_map/ppermute | solution.py:148
  7.7 11.5 %collective-permute-start.3 = (bf16[16,4096]{1,0:T(8,128)(2,1)S(1)}, bf16[16,4096]{1,0:T(8,128)(2,1)S(1)}, u32[]{:S(2)}, u32[]{:S(2)}) collective-permute-start(bf16[16,4096]{1,0:T(8,128)(2,1)S(1)} %get-tuple-element.11), channel_id=1, source_target_pairs={{8,0},{10,2},{12,4},{14,6},{0,8},{2,10},{4,12},{6,14},{9,1},{11,3}... | collective-permute-start | bytes 393224 | tf_op jit(solution)/shard_map/ppermute | solution.py:148
  11.6 9.1 %collective-permute-start.1 = (bf16[16,4096]{1,0:T(8,128)(2,1)S(1)}, bf16[16,4096]{1,0:T(8,128)(2,1)S(1)}, u32[]{:S(2)}, u32[]{:S(2)}) collective-permute-start(bf16[16,4096]{1,0:T(8,128)(2,1)S(1)} %collective-permute-done.s1), channel_id=1, source_target_pairs={{0,16},{16,0},{1,17},{17,1},{2,18},{18,2},{3,19},{19,3},{4,20},{20... | collective-permute-start | bytes 393224 | tf_op jit(solution)/shard_map/ppermute | solution.py:156
  15.9 7.0 %collective-permute-start.11 = (bf16[16,4096]{1,0:T(8,128)(2,1)S(1)}, bf16[16,4096]{1,0:T(8,128)(2,1)S(1)}, u32[]{:S(2)}, u32[]{:S(2)}) collective-permute-start(bf16[16,4096]{1,0:T(8,128)(2,1)S(1)} %collective-permute-done.6.s3), channel_id=1, source_target_pairs={{0,16},{16,0},{1,17},{17,1},{2,18},{18,2},{3,19},{19,3},{4,20},{20... | collective-permute-start | bytes 393224 | tf_op jit(solution)/shard_map/ppermute | solution.py:156
  17.5 7.2 %collective-permute-start.2 = (bf16[2,16,4096]{2,1,0:T(8,128)(2,1)S(1)}, bf16[2,16,4096]{2,1,0:T(8,128)(2,1)S(1)}, u32[]{:S(2)}, u32[]{:S(2)}) collective-permute-start(bf16[2,16,4096]{2,1,0:T(8,128)(2,1)S(1)} %get-tuple-element.13.own), channel_id=1, source_target_pairs={{0,2},{2,0},{4,6},{6,4},{8,10},{10,8},{12,14},{14,12},{1,3},{3,1},... | collective-permute-start | bytes 786440 | tf_op jit(solution)/shard_map/ppermute | solution.py:152
  17.5 6.0 %collective-permute-start.7 = (bf16[16,4096]{1,0:T(8,128)(2,1)S(1)}, bf16[16,4096]{1,0:T(8,128)(2,1)S(1)}, u32[]{:S(2)}, u32[]{:S(2)}) collective-permute-start(bf16[16,4096]{1,0:T(8,128)(2,1)S(1)} %collective-permute-done.6.s3), channel_id=1, source_target_pairs={{0,2},{2,0},{4,6},{6,4},{8,10},{10,8},{12,14},{14,12},{1,3},{3,1},... | collective-permute-start | bytes 393224 | tf_op jit(solution)/shard_map/ppermute | solution.py:152
  19.2 5.0 %collective-permute-start.8 = (bf16[16,4096]{1,0:T(8,128)(2,1)S(1)}, bf16[16,4096]{1,0:T(8,128)(2,1)S(1)}, u32[]{:S(2)}, u32[]{:S(2)}) collective-permute-start(bf16[16,4096]{1,0:T(8,128)(2,1)S(1)} %collective-permute-done.3.s2), channel_id=1, source_target_pairs={{0,16},{16,0},{1,17},{17,1},{2,18},{18,2},{3,19},{19,3},{4,20},{20... | collective-permute-start | bytes 393224 | tf_op jit(solution)/shard_map/ppermute | solution.py:156
  20.7 3.4 %collective-permute-start.4 = (bf16[16,4096]{1,0:T(8,128)(2,1)S(1)}, bf16[16,4096]{1,0:T(8,128)(2,1)S(1)}, u32[]{:S(2)}, u32[]{:S(2)}) collective-permute-start(bf16[16,4096]{1,0:T(8,128)(2,1)S(1)} %collective-permute-done.3.s2), channel_id=1, source_target_pairs={{0,2},{2,0},{4,6},{6,4},{8,10},{10,8},{12,14},{14,12},{1,3},{3,1},... | collective-permute-start | bytes 393224 | tf_op jit(solution)/shard_map/ppermute | solution.py:152
  22.9 1.7 %collective-permute-start.5 = (bf16[16,4096]{1,0:T(8,128)(2,1)S(1)}, bf16[16,4096]{1,0:T(8,128)(2,1)S(1)}, u32[]{:S(2)}, u32[]{:S(2)}) collective-permute-start(bf16[16,4096]{1,0:T(8,128)(2,1)S(1)} %collective-permute-done.s1), channel_id=1, source_target_pairs={{0,2},{2,0},{4,6},{6,4},{8,10},{10,8},{12,14},{14,12},{1,3},{3,1},... | collective-permute-start | bytes 393224 | tf_op jit(solution)/shard_map/ppermute | solution.py:152
  23.5 1.3 %collective-permute-start.12 = (bf16[16,4096]{1,0:T(8,128)(2,1)S(1)}, bf16[16,4096]{1,0:T(8,128)(2,1)S(1)}, u32[]{:S(2)}, u32[]{:S(2)}) collective-permute-start(bf16[16,4096]{1,0:T(8,128)(2,1)S(1)} %collective-permute-done.11.y3), channel_id=1, source_target_pairs={{0,2},{2,0},{4,6},{6,4},{8,10},{10,8},{12,14},{14,12},{1,3},{3,1},... | collective-permute-start | bytes 393224 | tf_op jit(solution)/shard_map/ppermute | solution.py:152
  24.1 1.3 %collective-permute-start.9 = (bf16[16,4096]{1,0:T(8,128)(2,1)S(1)}, bf16[16,4096]{1,0:T(8,128)(2,1)S(1)}, u32[]{:S(2)}, u32[]{:S(2)}) collective-permute-start(bf16[16,4096]{1,0:T(8,128)(2,1)S(1)} %collective-permute-done.8.y2), channel_id=1, source_target_pairs={{0,2},{2,0},{4,6},{6,4},{8,10},{10,8},{12,14},{14,12},{1,3},{3,1},... | collective-permute-start | bytes 393224 | tf_op jit(solution)/shard_map/ppermute | solution.py:152
  24.1 1.5 %collective-permute-start.10 = (bf16[16,4096]{1,0:T(8,128)(2,1)S(1)}, bf16[16,4096]{1,0:T(8,128)(2,1)S(1)}, u32[]{:S(2)}, u32[]{:S(2)}) collective-permute-start(bf16[16,4096]{1,0:T(8,128)(2,1)S(1)} %collective-permute-done.1.y1), channel_id=1, source_target_pairs={{0,2},{2,0},{4,6},{6,4},{8,10},{10,8},{12,14},{14,12},{1,3},{3,1},... | collective-permute-start | bytes 393224 | tf_op jit(solution)/shard_map/ppermute | solution.py:152
  27.3 4.4 %collective-permute-start.13 = (f32[128,128]{1,0:T(8,128)S(1)}, f32[128,128]{1,0:T(8,128)S(1)}, u32[]{:S(2)}, u32[]{:S(2)}) collective-permute-start(f32[128,128]{1,0:T(8,128)S(1)} %get-tuple-element.16), channel_id=1, source_target_pairs={{0,1},{1,0},{2,3},{3,2},{4,5},{5,4},{6,7},{7,6},{8,9},{9,8},{10,11... | collective-permute-start | bytes 196616 | tf_op jit(solution)/shard_map/ppermute | solution.py:250

commit v5 on v4

--- a/solution.py
+++ b/solution.py
@@ -80,62 +80,47 @@
         put(k, placed[k * count : (k + 1) * count, :].astype(jnp.bfloat16))
 
 
-def condition_scratch(layers, count, width):
-    pairs = width // LANES
-    return [
-        pltpu.VMEM((layers, 2, pairs * count, LANES), jnp.float32),
-        pltpu.VMEM((layers, count // 2, 2 * pairs, LANES), jnp.float32),
-        pltpu.VMEM((layers, pairs * count, LANES), jnp.float32),
+def condition_kernel(other, queries, left, right, out, block_in, left_in, right_in, spread, stacked, placed, arrived):
+    part = lax.axis_index("parts")
+    layer = 1 - part if other else part
+    copies = [
+        pltpu.make_async_copy(source, target, arrived.at[k])
+        for k, (source, target) in enumerate(
+            ((queries.at[layer, 0], block_in), (right.at[layer], right_in), (left.at[layer], left_in))
+        )
     ]
-
-
-def condition_kernel(queries, left, right, own, mine, block_in, left_in, right_in, spread, stacked, placed, arrived):
-    layers = queries.shape[0]
-    copies = []
-    for k, (source, target) in enumerate(((left, left_in), (right, right_in), (queries.at[:, 0], block_in))):
-        copies.append(pltpu.make_async_copy(source, target, arrived.at[k]))
-        copies[-1].start()
+    for copy in copies:
+        copy.start()
     for copy in copies:
         copy.wait()
-    for layer in range(layers):
-
-        def put(k, tile):
-            own[layer, :, k * LANES : (k + 1) * LANES] = tile
-
-        condition_block(
-            block_in[layer],
-            left_in[layer],
-            right_in[layer],
-            put,
-            spread.at[layer],
-            stacked.at[layer],
-            placed.at[layer],
-        )
-    mine[...] = own[lax.axis_index("parts")]
-
-
-def condition_near(queries, left_factor, right_factor):
-    layers, _, count, width = queries.shape
-    spec = pl.BlockSpec(memory_space=pltpu.VMEM)
+
+    def put(k, tile):
+        out[:, k * LANES : (k + 1) * LANES] = tile
+
+    condition_block(block_in[...], left_in[...], right_in[...], put, spread, stacked, placed)
+
+
+def condition_layer(other, queries, left_factor, right_factor):
+    _, _, count, width = queries.shape
+    pairs = width // LANES
     far = pl.BlockSpec(memory_space=pltpu.HBM)
     return pl.pallas_call(
-        condition_kernel,
-        out_shape=[
-            jax.ShapeDtypeStruct((layers, count, width), jnp.bfloat16),
-            jax.ShapeDtypeStruct((count, width), jnp.bfloat16),
-        ],
+        functools.partial(condition_kernel, other),
+        out_shape=jax.ShapeDtypeStruct((count, width), jnp.bfloat16),
         in_specs=[far] * 3,
-        out_specs=[spec] * 2,
+        out_specs=pl.BlockSpec(memory_space=pltpu.VMEM),
         scratch_shapes=[
-            pltpu.VMEM((layers, count, width), jnp.bfloat16),
-            pltpu.VMEM(left_factor.shape, jnp.float32),
-            pltpu.VMEM(right_factor.shape, jnp.float32),
-            *condition_scratch(layers, count, width),
+            pltpu.VMEM((count, width), jnp.bfloat16),
+            pltpu.VMEM(left_factor.shape[1:], jnp.float32),
+            pltpu.VMEM(right_factor.shape[1:], jnp.float32),
+            pltpu.VMEM((2, pairs * count, LANES), jnp.float32),
+            pltpu.VMEM((count // 2, 2 * pairs, LANES), jnp.float32),
+            pltpu.VMEM((pairs * count, LANES), jnp.float32),
             pltpu.SemaphoreType.DMA((3,)),
         ],
         compiler_params=pltpu.CompilerParams(vmem_limit_bytes=8 * 2**20),
-        cost_estimate=pl.CostEstimate(flops=2**28, bytes_accessed=2**20, transcendentals=0),
-        name="condition",
+        cost_estimate=pl.CostEstimate(flops=2**27, bytes_accessed=2**19, transcendentals=0),
+        name="condition_other" if other else "condition_mine",
     )(*(pltpu.with_memory_space_constraint(x, pltpu.HBM) for x in (queries, left_factor, right_factor)))
 
 
@@ -175,39 +160,44 @@
     )(pltpu.with_memory_space_constraint(value, pltpu.HBM))
 
 
-def score_kernel(
-    train, own, own_c, s2, s2_c, s1, s1_c, s3, s3_c, y2, y2_c, y1, y1_c, y3, y3_c, sent, kept, table, terms
-):
-    part = lax.axis_index("parts")
-    place = lax.axis_index("train")
-    here = lax.axis_index("layer")
-    column, core = place // PAIR, lax.rem(place, PAIR)
-    count = own.shape[1]
+def place():
+    member = lax.axis_index("train")
+    return member // PAIR, lax.rem(member, PAIR)
+
+
+def both_products(train, table):
+    rows, layer_count, width = train.shape
+    return lax.dot_general(
+        train.reshape(rows * layer_count, width)[...],
+        table[...].reshape(table.shape[0] * table.shape[1], width),
+        LANES_LAST,
+        preferred_element_type=jnp.float32,
+    )
+
+
+def early_kernel(train, *refs):
+    blocks, (sent, kept, table, terms) = refs[:-4], refs[-4:]
+    part, here = lax.axis_index("parts"), lax.axis_index("layer")
+    column, core = place()
+    count, width = blocks[0].shape
+    layer_count, queries = table.shape[:2]
+    share = kept.shape[0]
 
     def put(layer, step, twin, block):
         member = lax.rem(column + step, COLUMNS) * PAIR + (1 - core if twin else core)
         table[layer, pl.ds(pl.multiple_of(member * count, count), count), :] = block
 
-    for twin, (both, here_steps, there_steps) in enumerate(
-        ((own, (s1, s2, s3), (y1, y2, y3)), (own_c, (s1_c, s2_c, s3_c), (y1_c, y2_c, y3_c)))
-    ):
-        put(0, 0, twin, both[0])
-        put(1, 0, twin, both[1])
-        for step in range(1, COLUMNS):
-            put(part, step, twin, here_steps[step - 1][...])
-            put(1 - part, step, twin, there_steps[step - 1][...])
-
-    rows, layer_count, width = train.shape
-    queries = table.shape[1]
-    both = lax.dot_general(
-        train.reshape(rows * layer_count, width)[...],
-        table[...].reshape(layer_count * queries, width),
-        LANES_LAST,
-        preferred_element_type=jnp.float32,
-    )
+    nothing = jnp.zeros((count, width), jnp.bfloat16)
+    for twin in range(PAIR):
+        for k, step in enumerate((0, 1, 3)):
+            put(part, step, twin, blocks[4 * k + twin][...])
+            put(1 - part, step, twin, blocks[4 * k + 2 + twin][...])
+        for layer in range(layer_count):
+            put(layer, 2, twin, nothing)
+
+    both = both_products(train, table)
     for layer in range(layer_count):
         terms[layer] = both[:, layer * queries : (layer + 1) * queries]
-    share = kept.shape[0]
     for out, owner in ((sent, 1 - here), (kept, here)):
         first = pl.multiple_of(owner * share * layer_count, share * layer_count)
         out[...] = sum(
@@ -215,39 +205,116 @@
         )
 
 
+def late_kernel(train, s2, s2_c, y2, y2_c, sent, kept, table, terms):
+    part, here = lax.axis_index("parts"), lax.axis_index("layer")
+    _, core = place()
+    count = s2.shape[0]
+    layer_count = table.shape[0]
+    late, share = kept.shape
+
+    for layer, block, twin in ((part, s2, core), (part, s2_c, 1 - core), (1 - part, y2, core), (1 - part, y2_c, 1 - core)):
+        table[layer, pl.ds(pl.multiple_of(twin * count, count), count), :] = block[...]
+    both = both_products(train, table)
+    terms[:, : layer_count * late] = both
+    for out, owner in ((sent, 1 - here), (kept, here)):
+        first = pl.multiple_of(owner * share * layer_count, share * layer_count)
+        total = terms[pl.ds(first, share, stride=layer_count), :]
+        for layer in range(1, layer_count):
+            more = terms[pl.ds(first + layer, share, stride=layer_count), :]
+            total = total + pltpu.roll(more, LANES - layer * late, 1)
+        out[...] = jnp.transpose(total)[:late]
+
+
+def sum_kernel(kept, received, late_kept, late_received, scores, late):
+    column, _ = place()
+    count = late_kept.shape[0]
+    late[...] = jnp.zeros_like(late)
+    first = pl.multiple_of(lax.rem(column + 2, COLUMNS) * count, count)
+    late[pl.ds(first, count), :] = late_kept[...] + late_received[...]
+    scores[...] = kept[...] + received[...] + jnp.transpose(late[...])
+
+
+def local_call(kernel, name, out_shape, scratch_shapes, flops, moved, *operands):
+    spec = pl.BlockSpec(memory_space=pltpu.VMEM)
+    return pl.pallas_call(
+        kernel,
+        out_shape=out_shape,
+        in_specs=[spec] * len(operands),
+        out_specs=jax.tree.map(lambda _: spec, out_shape),
+        scratch_shapes=scratch_shapes,
+        compiler_params=pltpu.CompilerParams(vmem_limit_bytes=24 * 2**20),
+        cost_estimate=pl.CostEstimate(flops=flops, bytes_accessed=moved, transcendentals=0),
+        name=name,
+    )(*operands)
+
+
 def direct(train_grads, queries, left_factor, right_factor):
-    own, mine = condition_near(queries, left_factor, right_factor)
+    rows, layer_count, width = train_grads.shape
+    count = queries.shape[2]
+    total = count * COLUMNS * PAIR
+    late = count * PAIR
+    share = rows // 2
+
+    mine = condition_layer(False, queries, left_factor, right_factor)
+    other = condition_layer(True, queries, left_factor, right_factor)
     near = copy_near(train_grads)
     s2 = along_columns(mine, 2)
     s1 = along_columns(mine, 1)
     s3 = along_columns(mine, 3)
+    s1, other = lax.optimization_barrier((s1, other))
+    y1 = other_part(s1)
+    s3, near = lax.optimization_barrier((s3, near))
+    y3 = other_part(s3)
     y2 = other_part(s2)
-    y1 = other_part(s1)
-    y3 = other_part(s3)
-    y1, near = lax.optimization_barrier((y1, near))
+
     blocks = []
-    for block in (own, s2, s1, s3, y2, y1, y3):
+    for block in (mine, other, s1, y1, s3, y3):
         blocks += [block, other_core(block)]
-
-    rows, layer_count, width = train_grads.shape
-    total = queries.shape[2] * COLUMNS * PAIR
-    share = rows // 2
-    spec = pl.BlockSpec(memory_space=pltpu.VMEM)
-    flops = 4 * rows * layer_count * width * total
-    sent, kept = pl.pallas_call(
-        score_kernel,
-        out_shape=[jax.ShapeDtypeStruct((share, total), jnp.float32)] * 2,
-        in_specs=[spec] * (1 + len(blocks)),
-        out_specs=[spec] * 2,
-        scratch_shapes=[
+    f32 = functools.partial(jax.ShapeDtypeStruct, dtype=jnp.float32)
+    sent, kept = local_call(
+        early_kernel,
+        "early_scores",
+        [f32((share, total))] * 2,
+        [
             pltpu.VMEM((layer_count, total, width), jnp.bfloat16),
             pltpu.VMEM((layer_count, rows * layer_count, total), jnp.float32),
         ],
-        compiler_params=pltpu.CompilerParams(vmem_limit_bytes=24 * 2**20),
-        cost_estimate=pl.CostEstimate(flops=flops, bytes_accessed=6 * 2**20, transcendentals=0),
-        name="scores",
-    )(near, *blocks)
-    return kept + lax.ppermute(sent, "layer", [(0, 1), (1, 0)])
+        4 * rows * layer_count * width * total,
+        6 * 2**20,
+        near,
+        *blocks,
+    )
+    y2, sent = lax.optimization_barrier((y2, sent))
+    received = lax.ppermute(sent, "layer", [(0, 1), (1, 0)])
+    late_sent, late_kept = local_call(
+        late_kernel,
+        "late_scores",
+        [f32((late, share))] * 2,
+        [
+            pltpu.VMEM((layer_count, late, width), jnp.bfloat16),
+            pltpu.VMEM((rows * layer_count, LANES), jnp.float32),
+        ],
+        4 * rows * layer_count * width * late,
+        5 * 2**20,
+        near,
+        s2,
+        other_core(s2),
+        y2,
+        other_core(y2),
+    )
+    late_received = lax.ppermute(late_sent, "layer", [(0, 1), (1, 0)])
+    return local_call(
+        sum_kernel,
+        "sum_scores",
+        f32((share, total)),
+        [pltpu.VMEM((total, share), jnp.float32)],
+        3 * share * total,
+        2**18,
+        kept,
+        received,
+        late_kept,
+        late_received,
+    )
 
 
 def general(shape, train_grads, queries, left_factor, right_factor):
@@ -272,7 +339,7 @@
         shape["train"] == COLUMNS * PAIR
         and shape["parts"] == shape["layer"] == 2
         and shape["query"] == 1
-        and train_grads.shape[0] % 32 == 0
+        and train_grads.shape[0] == 2 * LANES
         and train_grads.shape[1:] == (2, 4096)
         and queries.shape[1:] == (1, 16, 4096)
         and left_factor.shape[1:] == right_factor.shape[1:] == (64, 64)

time: 32.5 us -> 34.1 us (1.049)
  Pallas kernels: 6.41 us -> 9.71 us
  waiting for transfers between devices: 11.3 us -> 10.1 us
  other arithmetic: 0.64 us -> 0 us
    pallas_call x2 -> x5, Pallas kernels: 4.22 us -> 7.52 us  [the longest x3 3.97 us: local_call(): pl.pallas_call(kernel, out_shape=out_shape, in_specs=[spec] * len(operand...]
    ppermute x3, waiting for transfers between devices: 0.56 us -> 3.57 us  [other_part(): return lax.ppermute(value, 'parts', [(0, 1), (1, 0)])]
    ppermute x3, waiting for transfers between devices: 6.89 us -> 4.15 us  [along_columns(): return lax.ppermute(value, 'train', pairs)]
    ppermute x1 -> x2, starting transfers between devices: 1.55 us -> 2.86 us  [the longest x1 1.49 us: direct(): received = lax.ppermute(sent, 'layer', [(0, 1), (1, 0)])]
    ppermute x7 -> x8, waiting for transfers between devices: 1.02 us -> 0.02 us  [other_core(): lax.ppermute(value, 'train', [(k, k ^ 1) for k in range(COLUMNS * PAIR)])]
    ppermute x3, starting transfers between devices: 4.59 us -> 3.76 us  [other_part(): return lax.ppermute(value, 'parts', [(0, 1), (1, 0)])]
    add x1 -> x0, other arithmetic: 0.64 us -> none  [direct(): return kept + lax.ppermute(sent, 'layer', [(0, 1), (1, 0)])]
    ppermute x1 -> x2, waiting for transfers between devices: 2.84 us -> 2.41 us  [the longest x1 2.32 us: direct(): late_received = lax.ppermute(late_sent, 'layer', [(0, 1), (1, 0)])]
  transfers between devices with their start and end apart: 14 -> 16, of which waited for: 8 -> 5; matrix products, arithmetic and copies ran while one was open for 0% -> 0% of each run, Pallas kernels for 7% -> 21%
where the time goes in v5:
time: 34.1 us; the launch traced here: 33.9 us
  starting transfers between devices  14 us (41%)
  waiting for transfers between devices  10.1 us (30%)
  Pallas kernels  9.71 us (28%)
    ppermute x3, starting transfers between devices, along_columns(): return lax.ppermute(value, 'train', pairs)  6.11 us
    ppermute x3, waiting for transfers between devices, along_columns(): return lax.ppermute(value, 'train', pairs)  4.15 us
    pallas_call x3, Pallas kernels, local_call(): pl.pallas_call(kernel, out_shape=out_shape, in_specs=[spec] * len(operand...  3.97 us
    ppermute x3, starting transfers between devices, other_part(): return lax.ppermute(value, 'parts', [(0, 1), (1, 0)])  3.76 us
    ppermute x3, waiting for transfers between devices, other_part(): return lax.ppermute(value, 'parts', [(0, 1), (1, 0)])  3.57 us
    pallas_call x2, Pallas kernels, condition_layer(): pl.pallas_call(functools.partial(condition_kernel, other), out_shape=jax....  3.55 us
    ppermute x1, waiting for transfers between devices, direct(): late_received = lax.ppermute(late_sent, 'layer', [(0, 1), (1, 0)])  2.32 us
    pallas_call x1, Pallas kernels, copy_near(): pl.pallas_call(copy_kernel, out_shape=jax.ShapeDtypeStruct(value.shape, v...  2.2 us
  transfers between devices with their start and end apart: 16, of which 5 were waited for; matrix products, arithmetic and copies ran while one was open for 0% of the time, Pallas kernels for 21%

profile of v5, /device:TPU:0, one launch (start us, length us, event | category | flops | bytes accessed | tf_op | source)
XLA Modules:
  0.0 33.9 jit_solution(4234888590451571821)
XLA Ops:
  0.0 1.8 %condition_mine.1.refs_0_ = bf16[16,4096]{1,0:T(8,128)(2,1)S(1)} custom-call(bf16[2,1,16,4096]{3,2,1,0:T(8,128)(2,1)} %queries.3, f32[2,64,64]{2,1,0:T(8,128)} %left.3, f32[2,64,64]{2,1,0:T(8,128)} %right.3), custom_call_target="tpu_custom_call" | custom-call | flops 134217728 | bytes 524288 | tf_op jit(solution)/shard_map/condition_mine/pallas_call | solution.py:107
  1.8 3.1 %collective-permute-start = (bf16[16,4096]{1,0:T(8,128)(2,1)S(1)}, bf16[16,4096]{1,0:T(8,128)(2,1)S(1)}, u32[]{:S(2)}, u32[]{:S(2)}) collective-permute-start(bf16[16,4096]{1,0:T(8,128)(2,1)S(1)} %condition_mine.1.refs_0_), channel_id=1, source_target_pairs={{12,0},{14,2},{0,4},{2,6},{4,8},{6,10},{8,12},{10,14},{13,1},{15,3... | collective-permute-start | bytes 393224 | tf_op jit(solution)/shard_map/ppermute | solution.py:133
  4.9 2.1 %collective-permute-start.2 = (bf16[16,4096]{1,0:T(8,128)(2,1)S(1)}, bf16[16,4096]{1,0:T(8,128)(2,1)S(1)}, u32[]{:S(2)}, u32[]{:S(2)}) collective-permute-start(bf16[16,4096]{1,0:T(8,128)(2,1)S(1)} %condition_mine.1.refs_0_), channel_id=1, source_target_pairs={{4,0},{6,2},{8,4},{10,6},{12,8},{14,10},{0,12},{2,14},{5,1},{7,3},... | collective-permute-start | bytes 393224 | tf_op jit(solution)/shard_map/ppermute | solution.py:133
  6.9 0.0 collective-permute-start.1
  6.9 0.9 %collective-permute-start.10 = (bf16[16,4096]{1,0:T(8,128)(2,1)S(1)}, bf16[16,4096]{1,0:T(8,128)(2,1)S(1)}, u32[]{:S(2)}, u32[]{:S(2)}) collective-permute-start(bf16[16,4096]{1,0:T(8,128)(2,1)S(1)} %condition_mine.1.refs_0_), channel_id=1, source_target_pairs={{8,0},{10,2},{12,4},{14,6},{0,8},{2,10},{4,12},{6,14},{9,1},{11,3}... | collective-permute-start | bytes 393224 | tf_op jit(solution)/shard_map/ppermute | solution.py:133
  7.9 2.2 %near.1.train = bf16[256,2,4096]{2,1,0:T(2,128)(2,1)S(1)} custom-call(bf16[256,2,4096]{2,1,0:T(2,128)(2,1)} %source.1), custom_call_target="tpu_custom_call" | custom-call | bytes 8388608 | tf_op jit(solution)/shard_map/near/pallas_call | solution.py:151
  10.1 1.8 %condition_other.1.refs_2_ = bf16[16,4096]{1,0:T(8,128)(2,1)S(1)} custom-call(bf16[2,1,16,4096]{3,2,1,0:T(8,128)(2,1)} %queries.3, f32[2,64,64]{2,1,0:T(8,128)} %left.3, f32[2,64,64]{2,1,0:T(8,128)} %right.3), custom_call_target="tpu_custom_call" | custom-call | flops 134217728 | bytes 524288 | tf_op jit(solution)/shard_map/condition_other/pallas_call | solution.py:107
  11.9 0.0 collective-permute-done.refs_8_
  11.9 1.6 %collective-permute-start.8 = (bf16[16,4096]{1,0:T(8,128)(2,1)S(1)}, bf16[16,4096]{1,0:T(8,128)(2,1)S(1)}, u32[]{:S(2)}, u32[]{:S(2)}) collective-permute-start(bf16[16,4096]{1,0:T(8,128)(2,1)S(1)} %collective-permute-done.refs_8_), channel_id=1, source_target_pairs={{0,16},{16,0},{1,17},{17,1},{2,18},{18,2},{3,19},{19,3},{4,20},{20... | collective-permute-start | bytes 393224 | tf_op jit(solution)/shard_map/ppermute | solution.py:141
  13.5 0.0 collective-permute-done.2.refs_4_
  13.5 0.7 %collective-permute-start.5 = (bf16[16,4096]{1,0:T(8,128)(2,1)S(1)}, bf16[16,4096]{1,0:T(8,128)(2,1)S(1)}, u32[]{:S(2)}, u32[]{:S(2)}) collective-permute-start(bf16[16,4096]{1,0:T(8,128)(2,1)S(1)} %collective-permute-done.2.refs_4_), channel_id=1, source_target_pairs={{0,16},{16,0},{1,17},{17,1},{2,18},{18,2},{3,19},{19,3},{4,20},{20... | collective-permute-start | bytes 393224 | tf_op jit(solution)/shard_map/ppermute | solution.py:141
  14.1 0.0 collective-permute-start.7
  14.1 0.0 collective-permute-done.1.refs_1_
  14.1 0.5 %collective-permute-start.4 = (bf16[16,4096]{1,0:T(8,128)(2,1)S(1)}, bf16[16,4096]{1,0:T(8,128)(2,1)S(1)}, u32[]{:S(2)}, u32[]{:S(2)}) collective-permute-start(bf16[16,4096]{1,0:T(8,128)(2,1)S(1)} %collective-permute-done.2.refs_4_), channel_id=1, source_target_pairs={{0,2},{2,0},{4,6},{6,4},{8,10},{10,8},{12,14},{14,12},{1,3},{3,1},... | collective-permute-start | bytes 393224 | tf_op jit(solution)/shard_map/ppermute | solution.py:137
  14.7 4.1 %collective-permute-done.10.s2 = bf16[16,4096]{1,0:T(8,128)(2,1)S(1)} collective-permute-done((bf16[16,4096]{1,0:T(8,128)(2,1)S(1)}, bf16[16,4096]{1,0:T(8,128)(2,1)S(1)}, u32[]{:S(2)}, u32[]{:S(2)}) %collective-permute-start.10) | collective-permute-done | bytes 131104 | tf_op jit(solution)/shard_map/ppermute | solution.py:133
  18.8 0.0 collective-permute-start.3
  18.8 0.0 collective-permute-done.8.refs_10_
  18.8 0.5 %collective-permute-start.9 = (bf16[16,4096]{1,0:T(8,128)(2,1)S(1)}, bf16[16,4096]{1,0:T(8,128)(2,1)S(1)}, u32[]{:S(2)}, u32[]{:S(2)}) collective-permute-start(bf16[16,4096]{1,0:T(8,128)(2,1)S(1)} %collective-permute-done.8.refs_10_), channel_id=1, source_target_pairs={{0,2},{2,0},{4,6},{6,4},{8,10},{10,8},{12,14},{14,12},{1,3},{3,1},... | collective-permute-start | bytes 393224 | tf_op jit(solution)/shard_map/ppermute | solution.py:137
  19.3 1.1 %collective-permute-done.5.refs_6_ = bf16[16,4096]{1,0:T(8,128)(2,1)S(1)} collective-permute-done((bf16[16,4096]{1,0:T(8,128)(2,1)S(1)}, bf16[16,4096]{1,0:T(8,128)(2,1)S(1)}, u32[]{:S(2)}, u32[]{:S(2)}) %collective-permute-start.5) | collective-permute-done | bytes 131104 | tf_op jit(solution)/shard_map/ppermute | solution.py:141
  20.4 0.0 collective-permute-start.6
  20.4 0.0 collective-permute-done.7.refs_9_
  20.4 1.5 %collective-permute-start.11 = (bf16[16,4096]{1,0:T(8,128)(2,1)S(1)}, bf16[16,4096]{1,0:T(8,128)(2,1)S(1)}, u32[]{:S(2)}, u32[]{:S(2)}) collective-permute-start(bf16[16,4096]{1,0:T(8,128)(2,1)S(1)} %collective-permute-done.10.s2), channel_id=1, source_target_pairs={{0,16},{16,0},{1,17},{17,1},{2,18},{18,2},{3,19},{19,3},{4,20},{20... | collective-permute-start | bytes 393224 | tf_op jit(solution)/shard_map/ppermute | solution.py:141
  21.9 0.0 collective-permute-done.4.refs_5_
  21.9 0.2 collective-permute-start.13
  22.2 0.0 collective-permute-done.3.refs_3_
  22.2 0.0 collective-permute-done.9.refs_11_
  22.2 0.0 collective-permute-done.6.refs_7_
  22.2 1.7 %early_scores.1 = (f32[128,128]{1,0:T(8,128)S(1)}, f32[128,128]{1,0:T(8,128)S(1)}) custom-call(bf16[256,2,4096]{2,1,0:T(2,128)(2,1)S(1)} %near.1.train, bf16[16,4096]{1,0:T(8,128)(2,1)S(1)} %condition_mine.1.refs_0_, bf16[16,4096]{1,0:T(8,128)(2,1)S(1)} %collective-permute-done.1.refs_1_, bf16[16,4096]{1,0:T(8,128)(2,1)S(1)} %condition_other.1.refs_2_, ...), custom_call_target="tpu_custom_call" | custom-call | flops 1073741824 | bytes 6291456 | tf_op jit(solution)/shard_map/early_scores/pallas_call | solution.py:239
  23.8 2.5 %collective-permute-done.11.y2 = bf16[16,4096]{1,0:T(8,128)(2,1)S(1)} collective-permute-done((bf16[16,4096]{1,0:T(8,128)(2,1)S(1)}, bf16[16,4096]{1,0:T(8,128)(2,1)S(1)}, u32[]{:S(2)}, u32[]{:S(2)}) %collective-permute-start.11) | collective-permute-done | bytes 131104 | tf_op jit(solution)/shard_map/ppermute | solution.py:141
  26.3 0.0 collective-permute-start.14
  26.3 1.5 %collective-permute-start.12 = (f32[128,128]{1,0:T(8,128)S(1)}, f32[128,128]{1,0:T(8,128)S(1)}, u32[]{:S(2)}, u32[]{:S(2)}) collective-permute-start(f32[128,128]{1,0:T(8,128)S(1)} %get-tuple-element.21), channel_id=1, source_target_pairs={{0,1},{1,0},{2,3},{3,2},{4,5},{5,4},{6,7},{7,6},{8,9},{9,8},{10,11... | collective-permute-start | bytes 196616 | tf_op jit(solution)/shard_map/ppermute | solution.py:288
  27.8 0.0 collective-permute-done.13.s2_c
  27.8 0.0 collective-permute-done.14.y2_c
  27.8 1.6 %late_scores.1 = (f32[32,128]{1,0:T(8,128)S(1)}, f32[32,128]{1,0:T(8,128)S(1)}) custom-call(bf16[256,2,4096]{2,1,0:T(2,128)(2,1)S(1)} %near.1.train, bf16[16,4096]{1,0:T(8,128)(2,1)S(1)} %collective-permute-done.10.s2, bf16[16,4096]{1,0:T(8,128)(2,1)S(1)} %collective-permute-done.13.s2_c, bf16[16,4096]{1,0:T(8,128)(2,1)S(1)} %collective-permute-done.11.y2, ...), custom_call_target="tpu_custom_call" | custom-call | flops 268435456 | bytes 5242880 | tf_op jit(solution)/shard_map/late_scores/pallas_call | solution.py:239
  29.4 1.4 %collective-permute-start.15 = (f32[32,128]{1,0:T(8,128)S(1)}, f32[32,128]{1,0:T(8,128)S(1)}, u32[]{:S(2)}, u32[]{:S(2)}) collective-permute-start(f32[32,128]{1,0:T(8,128)S(1)} %get-tuple-element.24), channel_id=1, source_target_pairs={{0,1},{1,0},{2,3},{3,2},{4,5},{5,4},{6,7},{7,6},{8,9},{9,8},{10,11... | collective-permute-start | bytes 49160 | tf_op jit(solution)/shard_map/ppermute | solution.py:305
  30.7 0.1 collective-permute-done.12.received
  30.8 2.3 %collective-permute-done.15.late_received = f32[32,128]{1,0:T(8,128)S(1)} collective-permute-done((f32[32,128]{1,0:T(8,128)S(1)}, f32[32,128]{1,0:T(8,128)S(1)}, u32[]{:S(2)}, u32[]{:S(2)}) %collective-permute-start.15) | collective-permute-done | bytes 16416 | tf_op jit(solution)/shard_map/ppermute | solution.py:305
  33.2 0.8 %sum_scores.1 = f32[128,128]{1,0:T(8,128)} custom-call(f32[128,128]{1,0:T(8,128)S(1)} %get-tuple-element.19.kept, f32[128,128]{1,0:T(8,128)S(1)} %collective-permute-done.12.received, f32[32,128]{1,0:T(8,128)S(1)} %get-tuple-element.23.late_kept, f32[32,128]{1,0:T(8,128)S(1)} %collective-permute-done.15.late_received), custom_call_target="tpu_custom_call" | custom-call | flops 49152 | bytes 262144 | tf_op jit(solution)/shard_map/sum_scores/pallas_call | solution.py:239
Async XLA Ops:
  1.8 10.1 %collective-permute-start = (bf16[16,4096]{1,0:T(8,128)(2,1)S(1)}, bf16[16,4096]{1,0:T(8,128)(2,1)S(1)}, u32[]{:S(2)}, u32[]{:S(2)}) collective-permute-start(bf16[16,4096]{1,0:T(8,128)(2,1)S(1)} %condition_mine.1.refs_0_), channel_id=1, source_target_pairs={{12,0},{14,2},{0,4},{2,6},{4,8},{6,10},{8,12},{10,14},{13,1},{15,3... | collective-permute-start | bytes 393224 | tf_op jit(solution)/shard_map/ppermute | solution.py:133
  4.9 8.6 %collective-permute-start.2 = (bf16[16,4096]{1,0:T(8,128)(2,1)S(1)}, bf16[16,4096]{1,0:T(8,128)(2,1)S(1)}, u32[]{:S(2)}, u32[]{:S(2)}) collective-permute-start(bf16[16,4096]{1,0:T(8,128)(2,1)S(1)} %condition_mine.1.refs_0_), channel_id=1, source_target_pairs={{4,0},{6,2},{8,4},{10,6},{12,8},{14,10},{0,12},{2,14},{5,1},{7,3},... | collective-permute-start | bytes 393224 | tf_op jit(solution)/shard_map/ppermute | solution.py:133
  6.9 7.2 %collective-permute-start.1 = (bf16[16,4096]{1,0:T(8,128)(2,1)S(1)}, bf16[16,4096]{1,0:T(8,128)(2,1)S(1)}, u32[]{:S(2)}, u32[]{:S(2)}) collective-permute-start(bf16[16,4096]{1,0:T(8,128)(2,1)S(1)} %condition_mine.1.refs_0_), channel_id=1, source_target_pairs={{0,2},{2,0},{4,6},{6,4},{8,10},{10,8},{12,14},{14,12},{1,3},{3,1},... | collective-permute-start | bytes 393224 | tf_op jit(solution)/shard_map/ppermute | solution.py:137
  6.9 11.9 %collective-permute-start.10 = (bf16[16,4096]{1,0:T(8,128)(2,1)S(1)}, bf16[16,4096]{1,0:T(8,128)(2,1)S(1)}, u32[]{:S(2)}, u32[]{:S(2)}) collective-permute-start(bf16[16,4096]{1,0:T(8,128)(2,1)S(1)} %condition_mine.1.refs_0_), channel_id=1, source_target_pairs={{8,0},{10,2},{12,4},{14,6},{0,8},{2,10},{4,12},{6,14},{9,1},{11,3}... | collective-permute-start | bytes 393224 | tf_op jit(solution)/shard_map/ppermute | solution.py:133
  11.9 6.9 %collective-permute-start.8 = (bf16[16,4096]{1,0:T(8,128)(2,1)S(1)}, bf16[16,4096]{1,0:T(8,128)(2,1)S(1)}, u32[]{:S(2)}, u32[]{:S(2)}) collective-permute-start(bf16[16,4096]{1,0:T(8,128)(2,1)S(1)} %collective-permute-done.refs_8_), channel_id=1, source_target_pairs={{0,16},{16,0},{1,17},{17,1},{2,18},{18,2},{3,19},{19,3},{4,20},{20... | collective-permute-start | bytes 393224 | tf_op jit(solution)/shard_map/ppermute | solution.py:141
  13.5 6.9 %collective-permute-start.5 = (bf16[16,4096]{1,0:T(8,128)(2,1)S(1)}, bf16[16,4096]{1,0:T(8,128)(2,1)S(1)}, u32[]{:S(2)}, u32[]{:S(2)}) collective-permute-start(bf16[16,4096]{1,0:T(8,128)(2,1)S(1)} %collective-permute-done.2.refs_4_), channel_id=1, source_target_pairs={{0,16},{16,0},{1,17},{17,1},{2,18},{18,2},{3,19},{19,3},{4,20},{20... | collective-permute-start | bytes 393224 | tf_op jit(solution)/shard_map/ppermute | solution.py:141
  14.1 6.3 %collective-permute-start.7 = (bf16[16,4096]{1,0:T(8,128)(2,1)S(1)}, bf16[16,4096]{1,0:T(8,128)(2,1)S(1)}, u32[]{:S(2)}, u32[]{:S(2)}) collective-permute-start(bf16[16,4096]{1,0:T(8,128)(2,1)S(1)} %collective-permute-done.refs_8_), channel_id=1, source_target_pairs={{0,2},{2,0},{4,6},{6,4},{8,10},{10,8},{12,14},{14,12},{1,3},{3,1},... | collective-permute-start | bytes 393224 | tf_op jit(solution)/shard_map/ppermute | solution.py:137
  14.1 7.8 %collective-permute-start.4 = (bf16[16,4096]{1,0:T(8,128)(2,1)S(1)}, bf16[16,4096]{1,0:T(8,128)(2,1)S(1)}, u32[]{:S(2)}, u32[]{:S(2)}) collective-permute-start(bf16[16,4096]{1,0:T(8,128)(2,1)S(1)} %collective-permute-done.2.refs_4_), channel_id=1, source_target_pairs={{0,2},{2,0},{4,6},{6,4},{8,10},{10,8},{12,14},{14,12},{1,3},{3,1},... | collective-permute-start | bytes 393224 | tf_op jit(solution)/shard_map/ppermute | solution.py:137
  18.8 3.4 %collective-permute-start.3 = (bf16[16,4096]{1,0:T(8,128)(2,1)S(1)}, bf16[16,4096]{1,0:T(8,128)(2,1)S(1)}, u32[]{:S(2)}, u32[]{:S(2)}) collective-permute-start(bf16[16,4096]{1,0:T(8,128)(2,1)S(1)} %condition_other.1.refs_2_), channel_id=1, source_target_pairs={{0,2},{2,0},{4,6},{6,4},{8,10},{10,8},{12,14},{14,12},{1,3},{3,1},... | collective-permute-start | bytes 393224 | tf_op jit(solution)/shard_map/ppermute | solution.py:137
  18.8 3.3 %collective-permute-start.9 = (bf16[16,4096]{1,0:T(8,128)(2,1)S(1)}, bf16[16,4096]{1,0:T(8,128)(2,1)S(1)}, u32[]{:S(2)}, u32[]{:S(2)}) collective-permute-start(bf16[16,4096]{1,0:T(8,128)(2,1)S(1)} %collective-permute-done.8.refs_10_), channel_id=1, source_target_pairs={{0,2},{2,0},{4,6},{6,4},{8,10},{10,8},{12,14},{14,12},{1,3},{3,1},... | collective-permute-start | bytes 393224 | tf_op jit(solution)/shard_map/ppermute | solution.py:137
  20.4 1.8 %collective-permute-start.6 = (bf16[16,4096]{1,0:T(8,128)(2,1)S(1)}, bf16[16,4096]{1,0:T(8,128)(2,1)S(1)}, u32[]{:S(2)}, u32[]{:S(2)}) collective-permute-start(bf16[16,4096]{1,0:T(8,128)(2,1)S(1)} %collective-permute-done.5.refs_6_), channel_id=1, source_target_pairs={{0,2},{2,0},{4,6},{6,4},{8,10},{10,8},{12,14},{14,12},{1,3},{3,1},... | collective-permute-start | bytes 393224 | tf_op jit(solution)/shard_map/ppermute | solution.py:137
  20.4 5.9 %collective-permute-start.11 = (bf16[16,4096]{1,0:T(8,128)(2,1)S(1)}, bf16[16,4096]{1,0:T(8,128)(2,1)S(1)}, u32[]{:S(2)}, u32[]{:S(2)}) collective-permute-start(bf16[16,4096]{1,0:T(8,128)(2,1)S(1)} %collective-permute-done.10.s2), channel_id=1, source_target_pairs={{0,16},{16,0},{1,17},{17,1},{2,18},{18,2},{3,19},{19,3},{4,20},{20... | collective-permute-start | bytes 393224 | tf_op jit(solution)/shard_map/ppermute | solution.py:141
  21.9 5.9 %collective-permute-start.13 = (bf16[16,4096]{1,0:T(8,128)(2,1)S(1)}, bf16[16,4096]{1,0:T(8,128)(2,1)S(1)}, u32[]{:S(2)}, u32[]{:S(2)}) collective-permute-start(bf16[16,4096]{1,0:T(8,128)(2,1)S(1)} %collective-permute-done.10.s2), channel_id=1, source_target_pairs={{0,2},{2,0},{4,6},{6,4},{8,10},{10,8},{12,14},{14,12},{1,3},{3,1},... | collective-permute-start | bytes 393224 | tf_op jit(solution)/shard_map/ppermute | solution.py:137
  26.3 1.5 %collective-permute-start.14 = (bf16[16,4096]{1,0:T(8,128)(2,1)S(1)}, bf16[16,4096]{1,0:T(8,128)(2,1)S(1)}, u32[]{:S(2)}, u32[]{:S(2)}) collective-permute-start(bf16[16,4096]{1,0:T(8,128)(2,1)S(1)} %collective-permute-done.11.y2), channel_id=1, source_target_pairs={{0,2},{2,0},{4,6},{6,4},{8,10},{10,8},{12,14},{14,12},{1,3},{3,1},... | collective-permute-start | bytes 393224 | tf_op jit(solution)/shard_map/ppermute | solution.py:137
  26.3 4.5 %collective-permute-start.12 = (f32[128,128]{1,0:T(8,128)S(1)}, f32[128,128]{1,0:T(8,128)S(1)}, u32[]{:S(2)}, u32[]{:S(2)}) collective-permute-start(f32[128,128]{1,0:T(8,128)S(1)} %get-tuple-element.21), channel_id=1, source_target_pairs={{0,1},{1,0},{2,3},{3,2},{4,5},{5,4},{6,7},{7,6},{8,9},{9,8},{10,11... | collective-permute-start | bytes 196616 | tf_op jit(solution)/shard_map/ppermute | solution.py:288
  29.4 3.8 %collective-permute-start.15 = (f32[32,128]{1,0:T(8,128)S(1)}, f32[32,128]{1,0:T(8,128)S(1)}, u32[]{:S(2)}, u32[]{:S(2)}) collective-permute-start(f32[32,128]{1,0:T(8,128)S(1)} %get-tuple-element.24), channel_id=1, source_target_pairs={{0,1},{1,0},{2,3},{3,2},{4,5},{5,4},{6,7},{7,6},{8,9},{9,8},{10,11... | collective-permute-start | bytes 49160 | tf_op jit(solution)/shard_map/ppermute | solution.py:305

commit v6 on v5

--- a/solution.py
+++ b/solution.py
@@ -165,76 +165,45 @@
     return member // PAIR, lax.rem(member, PAIR)
 
 
-def both_products(train, table):
+def row_scores(train, table, owner, terms, scores):
+    share = scores.shape[0]
     rows, layer_count, width = train.shape
-    return lax.dot_general(
-        train.reshape(rows * layer_count, width)[...],
-        table[...].reshape(table.shape[0] * table.shape[1], width),
+    queries = table.shape[1]
+    first = pl.multiple_of(owner * share * layer_count, share * layer_count)
+    both = lax.dot_general(
+        train.reshape(rows * layer_count, width)[pl.ds(first, share * layer_count), :],
+        table[...].reshape(layer_count * queries, width),
         LANES_LAST,
         preferred_element_type=jnp.float32,
     )
-
-
-def early_kernel(train, *refs):
-    blocks, (sent, kept, table, terms) = refs[:-4], refs[-4:]
-    part, here = lax.axis_index("parts"), lax.axis_index("layer")
+    for layer in range(layer_count):
+        terms[layer] = both[:, layer * queries : (layer + 1) * queries]
+    scores[...] = sum(terms[layer, pl.ds(layer, share, stride=layer_count), :] for layer in range(layer_count))
+
+
+def sent_kernel(train, *refs):
+    blocks, (scores, table, terms) = refs[:-3], refs[-3:]
+    part = lax.axis_index("parts")
     column, core = place()
-    count, width = blocks[0].shape
-    layer_count, queries = table.shape[:2]
-    share = kept.shape[0]
+    count = blocks[0].shape[0]
 
     def put(layer, step, twin, block):
         member = lax.rem(column + step, COLUMNS) * PAIR + (1 - core if twin else core)
         table[layer, pl.ds(pl.multiple_of(member * count, count), count), :] = block
 
-    nothing = jnp.zeros((count, width), jnp.bfloat16)
     for twin in range(PAIR):
-        for k, step in enumerate((0, 1, 3)):
-            put(part, step, twin, blocks[4 * k + twin][...])
-            put(1 - part, step, twin, blocks[4 * k + 2 + twin][...])
-        for layer in range(layer_count):
-            put(layer, 2, twin, nothing)
-
-    both = both_products(train, table)
-    for layer in range(layer_count):
-        terms[layer] = both[:, layer * queries : (layer + 1) * queries]
-    for out, owner in ((sent, 1 - here), (kept, here)):
-        first = pl.multiple_of(owner * share * layer_count, share * layer_count)
-        out[...] = sum(
-            terms[layer, pl.ds(first + layer, share, stride=layer_count), :] for layer in range(layer_count)
-        )
-
-
-def late_kernel(train, s2, s2_c, y2, y2_c, sent, kept, table, terms):
-    part, here = lax.axis_index("parts"), lax.axis_index("layer")
-    _, core = place()
-    count = s2.shape[0]
-    layer_count = table.shape[0]
-    late, share = kept.shape
-
-    for layer, block, twin in ((part, s2, core), (part, s2_c, 1 - core), (1 - part, y2, core), (1 - part, y2_c, 1 - core)):
-        table[layer, pl.ds(pl.multiple_of(twin * count, count), count), :] = block[...]
-    both = both_products(train, table)
-    terms[:, : layer_count * late] = both
-    for out, owner in ((sent, 1 - here), (kept, here)):
-        first = pl.multiple_of(owner * share * layer_count, share * layer_count)
-        total = terms[pl.ds(first, share, stride=layer_count), :]
-        for layer in range(1, layer_count):
-            more = terms[pl.ds(first + layer, share, stride=layer_count), :]
-            total = total + pltpu.roll(more, LANES - layer * late, 1)
-        out[...] = jnp.transpose(total)[:late]
-
-
-def sum_kernel(kept, received, late_kept, late_received, scores, late):
-    column, _ = place()
-    count = late_kept.shape[0]
-    late[...] = jnp.zeros_like(late)
-    first = pl.multiple_of(lax.rem(column + 2, COLUMNS) * count, count)
-    late[pl.ds(first, count), :] = late_kept[...] + late_received[...]
-    scores[...] = kept[...] + received[...] + jnp.transpose(late[...])
-
-
-def local_call(kernel, name, out_shape, scratch_shapes, flops, moved, *operands):
+        for k, (layer, step) in enumerate(
+            ((part, 0), (1 - part, 0), (part, 2), (part, 1), (part, 3), (1 - part, 2), (1 - part, 1), (1 - part, 3))
+        ):
+            put(layer, step, twin, blocks[PAIR * k + twin][...])
+    row_scores(train, table, 1 - lax.axis_index("layer"), terms, scores)
+
+
+def kept_kernel(train, table, scores, terms):
+    row_scores(train, table, lax.axis_index("layer"), terms, scores)
+
+
+def local_call(kernel, name, out_shape, scratch_shapes, *operands):
     spec = pl.BlockSpec(memory_space=pltpu.VMEM)
     return pl.pallas_call(
         kernel,
@@ -243,7 +212,7 @@
         out_specs=jax.tree.map(lambda _: spec, out_shape),
         scratch_shapes=scratch_shapes,
         compiler_params=pltpu.CompilerParams(vmem_limit_bytes=24 * 2**20),
-        cost_estimate=pl.CostEstimate(flops=flops, bytes_accessed=moved, transcendentals=0),
+        cost_estimate=pl.CostEstimate(flops=2**29, bytes_accessed=2**22, transcendentals=0),
         name=name,
     )(*operands)
 
@@ -252,7 +221,6 @@
     rows, layer_count, width = train_grads.shape
     count = queries.shape[2]
     total = count * COLUMNS * PAIR
-    late = count * PAIR
     share = rows // 2
 
     mine = condition_layer(False, queries, left_factor, right_factor)
@@ -262,59 +230,28 @@
     s1 = along_columns(mine, 1)
     s3 = along_columns(mine, 3)
     s1, other = lax.optimization_barrier((s1, other))
+    s3, near = lax.optimization_barrier((s3, near))
     y1 = other_part(s1)
-    s3, near = lax.optimization_barrier((s3, near))
     y3 = other_part(s3)
+    s2, y1, y3 = lax.optimization_barrier((s2, y1, y3))
     y2 = other_part(s2)
 
     blocks = []
-    for block in (mine, other, s1, y1, s3, y3):
+    for block in (mine, other, s2, s1, s3, y2, y1, y3):
         blocks += [block, other_core(block)]
     f32 = functools.partial(jax.ShapeDtypeStruct, dtype=jnp.float32)
-    sent, kept = local_call(
-        early_kernel,
-        "early_scores",
-        [f32((share, total))] * 2,
-        [
-            pltpu.VMEM((layer_count, total, width), jnp.bfloat16),
-            pltpu.VMEM((layer_count, rows * layer_count, total), jnp.float32),
-        ],
-        4 * rows * layer_count * width * total,
-        6 * 2**20,
+    terms = [pltpu.VMEM((layer_count, share * layer_count, total), jnp.float32)]
+    sent, table = local_call(
+        sent_kernel,
+        "scores_sent",
+        [f32((share, total)), jax.ShapeDtypeStruct((layer_count, total, width), jnp.bfloat16)],
+        terms,
         near,
         *blocks,
     )
-    y2, sent = lax.optimization_barrier((y2, sent))
     received = lax.ppermute(sent, "layer", [(0, 1), (1, 0)])
-    late_sent, late_kept = local_call(
-        late_kernel,
-        "late_scores",
-        [f32((late, share))] * 2,
-        [
-            pltpu.VMEM((layer_count, late, width), jnp.bfloat16),
-            pltpu.VMEM((rows * layer_count, LANES), jnp.float32),
-        ],
-        4 * rows * layer_count * width * late,
-        5 * 2**20,
-        near,
-        s2,
-        other_core(s2),
-        y2,
-        other_core(y2),
-    )
-    late_received = lax.ppermute(late_sent, "layer", [(0, 1), (1, 0)])
-    return local_call(
-        sum_kernel,
-        "sum_scores",
-        f32((share, total)),
-        [pltpu.VMEM((total, share), jnp.float32)],
-        3 * share * total,
-        2**18,
-        kept,
-        received,
-        late_kept,
-        late_received,
-    )
+    kept = local_call(kept_kernel, "scores_kept", f32((share, total)), terms, near, table)
+    return kept + received
 
 
 def general(shape, train_grads, queries, left_factor, right_factor):

time: 34.1 us -> 32.6 us (0.956)
  Pallas kernels: 9.71 us -> 7.58 us
  other arithmetic: 0 us -> 0.64 us
    ppermute x1 -> x0, waiting for transfers between devices: 2.32 us -> none  [direct(): late_received = lax.ppermute(late_sent, 'layer', [(0, 1), (1, 0)])]
    pallas_call x3 -> x2, Pallas kernels: 3.97 us -> 1.84 us  [local_call(): pl.pallas_call(kernel, out_shape=out_shape, in_specs=[spec] * len(operand...]
    ppermute x1, waiting for transfers between devices: 0.08 us -> 1.93 us  [direct(): received = lax.ppermute(sent, 'layer', [(0, 1), (1, 0)])]
    ppermute x1 -> x0, starting transfers between devices: 1.37 us -> none  [direct(): late_received = lax.ppermute(late_sent, 'layer', [(0, 1), (1, 0)])]
    ppermute x8, waiting for transfers between devices: 0.02 us -> 1.33 us  [other_core(): lax.ppermute(value, 'train', [(k, k ^ 1) for k in range(COLUMNS * PAIR)])]
    ppermute x3, waiting for transfers between devices: 4.15 us -> 2.84 us  [along_columns(): return lax.ppermute(value, 'train', pairs)]
    ppermute x3, starting transfers between devices: 3.76 us -> 4.63 us  [other_part(): return lax.ppermute(value, 'parts', [(0, 1), (1, 0)])]
    add x0 -> x1, other arithmetic: none -> 0.64 us  [direct(): return kept + received]
  transfers between devices with their start and end apart: 16 -> 15, of which waited for: 5 -> 6; matrix products, arithmetic and copies ran while one was open for 0% -> 0% of each run, Pallas kernels for 21% -> 15%
where the time goes in v6:
time: 32.6 us; the launch traced here: 32.4 us
  starting transfers between devices  13.8 us (42%)
  waiting for transfers between devices  10.3 us (32%)
  Pallas kernels  7.58 us (23%)
  other arithmetic  0.64 us (2%)
    ppermute x3, starting transfers between devices, along_columns(): return lax.ppermute(value, 'train', pairs)  6.11 us
    ppermute x3, starting transfers between devices, other_part(): return lax.ppermute(value, 'parts', [(0, 1), (1, 0)])  4.63 us
    ppermute x3, waiting for transfers between devices, other_part(): return lax.ppermute(value, 'parts', [(0, 1), (1, 0)])  4.16 us
    pallas_call x2, Pallas kernels, condition_layer(): pl.pallas_call(functools.partial(condition_kernel, other), out_shape=jax....  3.55 us
    ppermute x3, waiting for transfers between devices, along_columns(): return lax.ppermute(value, 'train', pairs)  2.84 us
    pallas_call x1, Pallas kernels, copy_near(): pl.pallas_call(copy_kernel, out_shape=jax.ShapeDtypeStruct(value.shape, v...  2.2 us
    ppermute x1, waiting for transfers between devices, direct(): received = lax.ppermute(sent, 'layer', [(0, 1), (1, 0)])  1.93 us
    pallas_call x2, Pallas kernels, local_call(): pl.pallas_call(kernel, out_shape=out_shape, in_specs=[spec] * len(operand...  1.84 us
  transfers between devices with their start and end apart: 15, of which 6 were waited for; matrix products, arithmetic and copies ran while one was open for 0% of the time, Pallas kernels for 15%

profile of v6, /device:TPU:0, one launch (start us, length us, event | category | flops | bytes accessed | tf_op | source)
XLA Modules:
  0.0 32.4 jit_solution(2321197918556548073)
XLA Ops:
  0.0 1.8 %condition_mine.1.refs_0_ = bf16[16,4096]{1,0:T(8,128)(2,1)S(1)} custom-call(bf16[2,1,16,4096]{3,2,1,0:T(8,128)(2,1)} %queries.3, f32[2,64,64]{2,1,0:T(8,128)} %left.3, f32[2,64,64]{2,1,0:T(8,128)} %right.3), custom_call_target="tpu_custom_call" | custom-call | flops 134217728 | bytes 524288 | tf_op jit(solution)/shard_map/condition_mine/pallas_call | solution.py:107
  1.8 5.1 %collective-permute-start.2 = (bf16[16,4096]{1,0:T(8,128)(2,1)S(1)}, bf16[16,4096]{1,0:T(8,128)(2,1)S(1)}, u32[]{:S(2)}, u32[]{:S(2)}) collective-permute-start(bf16[16,4096]{1,0:T(8,128)(2,1)S(1)} %condition_mine.1.refs_0_), channel_id=1, source_target_pairs={{4,0},{6,2},{8,4},{10,6},{12,8},{14,10},{0,12},{2,14},{5,1},{7,3},... | collective-permute-start | bytes 393224 | tf_op jit(solution)/shard_map/ppermute | solution.py:133
  6.9 0.0 collective-permute-start
  6.9 1.0 %collective-permute-start.4 = (bf16[16,4096]{1,0:T(8,128)(2,1)S(1)}, bf16[16,4096]{1,0:T(8,128)(2,1)S(1)}, u32[]{:S(2)}, u32[]{:S(2)}) collective-permute-start(bf16[16,4096]{1,0:T(8,128)(2,1)S(1)} %condition_mine.1.refs_0_), channel_id=1, source_target_pairs={{8,0},{10,2},{12,4},{14,6},{0,8},{2,10},{4,12},{6,14},{9,1},{11,3}... | collective-permute-start | bytes 393224 | tf_op jit(solution)/shard_map/ppermute | solution.py:133
  7.9 2.2 %near.1.train = bf16[256,2,4096]{2,1,0:T(2,128)(2,1)S(1)} custom-call(bf16[256,2,4096]{2,1,0:T(2,128)(2,1)} %source.1), custom_call_target="tpu_custom_call" | custom-call | bytes 8388608 | tf_op jit(solution)/shard_map/near/pallas_call | solution.py:151
  10.1 1.8 %condition_other.1.refs_2_ = bf16[16,4096]{1,0:T(8,128)(2,1)S(1)} custom-call(bf16[2,1,16,4096]{3,2,1,0:T(8,128)(2,1)} %queries.3, f32[2,64,64]{2,1,0:T(8,128)} %left.3, f32[2,64,64]{2,1,0:T(8,128)} %right.3), custom_call_target="tpu_custom_call" | custom-call | flops 134217728 | bytes 524288 | tf_op jit(solution)/shard_map/condition_other/pallas_call | solution.py:107
  11.9 0.0 collective-permute-done.2.refs_6_
  11.9 1.6 %collective-permute-start.5 = (bf16[16,4096]{1,0:T(8,128)(2,1)S(1)}, bf16[16,4096]{1,0:T(8,128)(2,1)S(1)}, u32[]{:S(2)}, u32[]{:S(2)}) collective-permute-start(bf16[16,4096]{1,0:T(8,128)(2,1)S(1)} %collective-permute-done.2.refs_6_), channel_id=1, source_target_pairs={{0,16},{16,0},{1,17},{17,1},{2,18},{18,2},{3,19},{19,3},{4,20},{20... | collective-permute-start | bytes 393224 | tf_op jit(solution)/shard_map/ppermute | solution.py:141
  13.5 1.7 %collective-permute-done.refs_8_ = bf16[16,4096]{1,0:T(8,128)(2,1)S(1)} collective-permute-done((bf16[16,4096]{1,0:T(8,128)(2,1)S(1)}, bf16[16,4096]{1,0:T(8,128)(2,1)S(1)}, u32[]{:S(2)}, u32[]{:S(2)}) %collective-permute-start) | collective-permute-done | bytes 131104 | tf_op jit(solution)/shard_map/ppermute | solution.py:133
  15.1 1.5 %collective-permute-start.6 = (bf16[16,4096]{1,0:T(8,128)(2,1)S(1)}, bf16[16,4096]{1,0:T(8,128)(2,1)S(1)}, u32[]{:S(2)}, u32[]{:S(2)}) collective-permute-start(bf16[16,4096]{1,0:T(8,128)(2,1)S(1)} %collective-permute-done.refs_8_), channel_id=1, source_target_pairs={{0,16},{16,0},{1,17},{17,1},{2,18},{18,2},{3,19},{19,3},{4,20},{20... | collective-permute-start | bytes 393224 | tf_op jit(solution)/shard_map/ppermute | solution.py:141
  16.7 0.0 collective-permute-start.1
  16.7 0.5 %collective-permute-start.8 = (bf16[16,4096]{1,0:T(8,128)(2,1)S(1)}, bf16[16,4096]{1,0:T(8,128)(2,1)S(1)}, u32[]{:S(2)}, u32[]{:S(2)}) collective-permute-start(bf16[16,4096]{1,0:T(8,128)(2,1)S(1)} %collective-permute-done.2.refs_6_), channel_id=1, source_target_pairs={{0,2},{2,0},{4,6},{6,4},{8,10},{10,8},{12,14},{14,12},{1,3},{3,1},... | collective-permute-start | bytes 393224 | tf_op jit(solution)/shard_map/ppermute | solution.py:137
  17.2 1.2 %collective-permute-done.4.refs_4_ = bf16[16,4096]{1,0:T(8,128)(2,1)S(1)} collective-permute-done((bf16[16,4096]{1,0:T(8,128)(2,1)S(1)}, bf16[16,4096]{1,0:T(8,128)(2,1)S(1)}, u32[]{:S(2)}, u32[]{:S(2)}) %collective-permute-start.4) | collective-permute-done | bytes 131104 | tf_op jit(solution)/shard_map/ppermute | solution.py:133
  18.4 0.0 collective-permute-start.3
  18.4 0.0 collective-permute-done.5.refs_12_
  18.4 1.7 %collective-permute-done.6.refs_14_ = bf16[16,4096]{1,0:T(8,128)(2,1)S(1)} collective-permute-done((bf16[16,4096]{1,0:T(8,128)(2,1)S(1)}, bf16[16,4096]{1,0:T(8,128)(2,1)S(1)}, u32[]{:S(2)}, u32[]{:S(2)}) %collective-permute-start.6) | collective-permute-done | bytes 131104 | tf_op jit(solution)/shard_map/ppermute | solution.py:141
  20.1 1.5 %collective-permute-start.10 = (bf16[16,4096]{1,0:T(8,128)(2,1)S(1)}, bf16[16,4096]{1,0:T(8,128)(2,1)S(1)}, u32[]{:S(2)}, u32[]{:S(2)}) collective-permute-start(bf16[16,4096]{1,0:T(8,128)(2,1)S(1)} %collective-permute-done.4.refs_4_), channel_id=1, source_target_pairs={{0,16},{16,0},{1,17},{17,1},{2,18},{18,2},{3,19},{19,3},{4,20},{20... | collective-permute-start | bytes 393224 | tf_op jit(solution)/shard_map/ppermute | solution.py:141
  21.6 0.0 collective-permute-start.9
  21.6 0.0 collective-permute-done.1.refs_1_
  21.6 0.5 %collective-permute-start.7 = (bf16[16,4096]{1,0:T(8,128)(2,1)S(1)}, bf16[16,4096]{1,0:T(8,128)(2,1)S(1)}, u32[]{:S(2)}, u32[]{:S(2)}) collective-permute-start(bf16[16,4096]{1,0:T(8,128)(2,1)S(1)} %collective-permute-done.4.refs_4_), channel_id=1, source_target_pairs={{0,2},{2,0},{4,6},{6,4},{8,10},{10,8},{12,14},{14,12},{1,3},{3,1},... | collective-permute-start | bytes 393224 | tf_op jit(solution)/shard_map/ppermute | solution.py:137
  22.1 0.0 collective-permute-done.3.refs_3_
  22.1 0.1 collective-permute-start.12
  22.2 0.0 collective-permute-done.8.refs_7_
  22.2 0.4 %collective-permute-start.13 = (bf16[16,4096]{1,0:T(8,128)(2,1)S(1)}, bf16[16,4096]{1,0:T(8,128)(2,1)S(1)}, u32[]{:S(2)}, u32[]{:S(2)}) collective-permute-start(bf16[16,4096]{1,0:T(8,128)(2,1)S(1)} %collective-permute-done.6.refs_14_), channel_id=1, source_target_pairs={{0,2},{2,0},{4,6},{6,4},{8,10},{10,8},{12,14},{14,12},{1,3},{3,1},... | collective-permute-start | bytes 393224 | tf_op jit(solution)/shard_map/ppermute | solution.py:137
  22.7 2.4 %collective-permute-done.10.refs_10_ = bf16[16,4096]{1,0:T(8,128)(2,1)S(1)} collective-permute-done((bf16[16,4096]{1,0:T(8,128)(2,1)S(1)}, bf16[16,4096]{1,0:T(8,128)(2,1)S(1)}, u32[]{:S(2)}, u32[]{:S(2)}) %collective-permute-start.10) | collective-permute-done | bytes 131104 | tf_op jit(solution)/shard_map/ppermute | solution.py:141
  25.1 0.0 collective-permute-start.11
  25.1 0.0 collective-permute-done.9.refs_9_
  25.1 0.0 collective-permute-done.12.refs_13_
  25.1 0.0 collective-permute-done.13.refs_15_
  25.1 0.0 collective-permute-done.7.refs_5_
  25.1 1.3 %collective-permute-done.11.refs_11_ = bf16[16,4096]{1,0:T(8,128)(2,1)S(1)} collective-permute-done((bf16[16,4096]{1,0:T(8,128)(2,1)S(1)}, bf16[16,4096]{1,0:T(8,128)(2,1)S(1)}, u32[]{:S(2)}, u32[]{:S(2)}) %collective-permute-start.11) | collective-permute-done | bytes 131104 | tf_op jit(solution)/shard_map/ppermute | solution.py:137
  26.4 1.0 %scores_sent.1 = (f32[128,128]{1,0:T(8,128)S(1)}, bf16[2,128,4096]{2,1,0:T(8,128)(2,1)S(1)}) custom-call(bf16[256,2,4096]{2,1,0:T(2,128)(2,1)S(1)} %near.1.train, bf16[16,4096]{1,0:T(8,128)(2,1)S(1)} %condition_mine.1.refs_0_, bf16[16,4096]{1,0:T(8,128)(2,1)S(1)} %collective-permute-done.1.refs_1_, bf16[16,4096]{1,0:T(8,128)(2,1)S(1)} %condition_other.1.refs_2_, ...), custom_call_target="tpu_custom_call" | custom-call | flops 536870912 | bytes 4194304 | tf_op jit(solution)/shard_map/scores_sent/pallas_call | solution.py:208
  27.4 1.6 %collective-permute-start.14 = (f32[128,128]{1,0:T(8,128)S(1)}, f32[128,128]{1,0:T(8,128)S(1)}, u32[]{:S(2)}, u32[]{:S(2)}) collective-permute-start(f32[128,128]{1,0:T(8,128)S(1)} %get-tuple-element.22), channel_id=1, source_target_pairs={{0,1},{1,0},{2,3},{3,2},{4,5},{5,4},{6,7},{7,6},{8,9},{9,8},{10,11... | collective-permute-start | bytes 196616 | tf_op jit(solution)/shard_map/ppermute | solution.py:252
  29.0 0.8 %scores_kept.1 = f32[128,128]{1,0:T(8,128)S(1)} custom-call(bf16[256,2,4096]{2,1,0:T(2,128)(2,1)S(1)} %near.1.train, bf16[2,128,4096]{2,1,0:T(8,128)(2,1)S(1)} %get-tuple-element.21.table), custom_call_target="tpu_custom_call" | custom-call | flops 536870912 | bytes 4194304 | tf_op jit(solution)/shard_map/scores_kept/pallas_call | solution.py:208
  29.8 1.9 %collective-permute-done.14 = f32[128,128]{1,0:T(8,128)S(1)} collective-permute-done((f32[128,128]{1,0:T(8,128)S(1)}, f32[128,128]{1,0:T(8,128)S(1)}, u32[]{:S(2)}, u32[]{:S(2)}) %collective-permute-start.14) | collective-permute-done | bytes 65568 | tf_op jit(solution)/shard_map/ppermute | solution.py:252
  31.8 0.6 %add.3 = f32[128,128]{1,0:T(8,128)} add(f32[128,128]{1,0:T(8,128)S(1)} %scores_kept.1, f32[128,128]{1,0:T(8,128)S(1)} %collective-permute-done.14) | non-fusion elementwise | flops 16384 | bytes 196608 | tf_op jit(solution)/shard_map/add | solution.py:254
Async XLA Ops:
  1.8 10.1 %collective-permute-start.2 = (bf16[16,4096]{1,0:T(8,128)(2,1)S(1)}, bf16[16,4096]{1,0:T(8,128)(2,1)S(1)}, u32[]{:S(2)}, u32[]{:S(2)}) collective-permute-start(bf16[16,4096]{1,0:T(8,128)(2,1)S(1)} %condition_mine.1.refs_0_), channel_id=1, source_target_pairs={{4,0},{6,2},{8,4},{10,6},{12,8},{14,10},{0,12},{2,14},{5,1},{7,3},... | collective-permute-start | bytes 393224 | tf_op jit(solution)/shard_map/ppermute | solution.py:133
  6.9 8.3 %collective-permute-start = (bf16[16,4096]{1,0:T(8,128)(2,1)S(1)}, bf16[16,4096]{1,0:T(8,128)(2,1)S(1)}, u32[]{:S(2)}, u32[]{:S(2)}) collective-permute-start(bf16[16,4096]{1,0:T(8,128)(2,1)S(1)} %condition_mine.1.refs_0_), channel_id=1, source_target_pairs={{12,0},{14,2},{0,4},{2,6},{4,8},{6,10},{8,12},{10,14},{13,1},{15,3... | collective-permute-start | bytes 393224 | tf_op jit(solution)/shard_map/ppermute | solution.py:133
  6.9 11.5 %collective-permute-start.4 = (bf16[16,4096]{1,0:T(8,128)(2,1)S(1)}, bf16[16,4096]{1,0:T(8,128)(2,1)S(1)}, u32[]{:S(2)}, u32[]{:S(2)}) collective-permute-start(bf16[16,4096]{1,0:T(8,128)(2,1)S(1)} %condition_mine.1.refs_0_), channel_id=1, source_target_pairs={{8,0},{10,2},{12,4},{14,6},{0,8},{2,10},{4,12},{6,14},{9,1},{11,3}... | collective-permute-start | bytes 393224 | tf_op jit(solution)/shard_map/ppermute | solution.py:133
  11.9 6.5 %collective-permute-start.5 = (bf16[16,4096]{1,0:T(8,128)(2,1)S(1)}, bf16[16,4096]{1,0:T(8,128)(2,1)S(1)}, u32[]{:S(2)}, u32[]{:S(2)}) collective-permute-start(bf16[16,4096]{1,0:T(8,128)(2,1)S(1)} %collective-permute-done.2.refs_6_), channel_id=1, source_target_pairs={{0,16},{16,0},{1,17},{17,1},{2,18},{18,2},{3,19},{19,3},{4,20},{20... | collective-permute-start | bytes 393224 | tf_op jit(solution)/shard_map/ppermute | solution.py:141
  15.1 5.0 %collective-permute-start.6 = (bf16[16,4096]{1,0:T(8,128)(2,1)S(1)}, bf16[16,4096]{1,0:T(8,128)(2,1)S(1)}, u32[]{:S(2)}, u32[]{:S(2)}) collective-permute-start(bf16[16,4096]{1,0:T(8,128)(2,1)S(1)} %collective-permute-done.refs_8_), channel_id=1, source_target_pairs={{0,16},{16,0},{1,17},{17,1},{2,18},{18,2},{3,19},{19,3},{4,20},{20... | collective-permute-start | bytes 393224 | tf_op jit(solution)/shard_map/ppermute | solution.py:141
  16.7 5.0 %collective-permute-start.1 = (bf16[16,4096]{1,0:T(8,128)(2,1)S(1)}, bf16[16,4096]{1,0:T(8,128)(2,1)S(1)}, u32[]{:S(2)}, u32[]{:S(2)}) collective-permute-start(bf16[16,4096]{1,0:T(8,128)(2,1)S(1)} %condition_mine.1.refs_0_), channel_id=1, source_target_pairs={{0,2},{2,0},{4,6},{6,4},{8,10},{10,8},{12,14},{14,12},{1,3},{3,1},... | collective-permute-start | bytes 393224 | tf_op jit(solution)/shard_map/ppermute | solution.py:137
  16.7 5.6 %collective-permute-start.8 = (bf16[16,4096]{1,0:T(8,128)(2,1)S(1)}, bf16[16,4096]{1,0:T(8,128)(2,1)S(1)}, u32[]{:S(2)}, u32[]{:S(2)}) collective-permute-start(bf16[16,4096]{1,0:T(8,128)(2,1)S(1)} %collective-permute-done.2.refs_6_), channel_id=1, source_target_pairs={{0,2},{2,0},{4,6},{6,4},{8,10},{10,8},{12,14},{14,12},{1,3},{3,1},... | collective-permute-start | bytes 393224 | tf_op jit(solution)/shard_map/ppermute | solution.py:137
  18.4 3.8 %collective-permute-start.3 = (bf16[16,4096]{1,0:T(8,128)(2,1)S(1)}, bf16[16,4096]{1,0:T(8,128)(2,1)S(1)}, u32[]{:S(2)}, u32[]{:S(2)}) collective-permute-start(bf16[16,4096]{1,0:T(8,128)(2,1)S(1)} %condition_other.1.refs_2_), channel_id=1, source_target_pairs={{0,2},{2,0},{4,6},{6,4},{8,10},{10,8},{12,14},{14,12},{1,3},{3,1},... | collective-permute-start | bytes 393224 | tf_op jit(solution)/shard_map/ppermute | solution.py:137
  20.1 5.0 %collective-permute-start.10 = (bf16[16,4096]{1,0:T(8,128)(2,1)S(1)}, bf16[16,4096]{1,0:T(8,128)(2,1)S(1)}, u32[]{:S(2)}, u32[]{:S(2)}) collective-permute-start(bf16[16,4096]{1,0:T(8,128)(2,1)S(1)} %collective-permute-done.4.refs_4_), channel_id=1, source_target_pairs={{0,16},{16,0},{1,17},{17,1},{2,18},{18,2},{3,19},{19,3},{4,20},{20... | collective-permute-start | bytes 393224 | tf_op jit(solution)/shard_map/ppermute | solution.py:141
  21.6 3.5 %collective-permute-start.9 = (bf16[16,4096]{1,0:T(8,128)(2,1)S(1)}, bf16[16,4096]{1,0:T(8,128)(2,1)S(1)}, u32[]{:S(2)}, u32[]{:S(2)}) collective-permute-start(bf16[16,4096]{1,0:T(8,128)(2,1)S(1)} %collective-permute-done.refs_8_), channel_id=1, source_target_pairs={{0,2},{2,0},{4,6},{6,4},{8,10},{10,8},{12,14},{14,12},{1,3},{3,1},... | collective-permute-start | bytes 393224 | tf_op jit(solution)/shard_map/ppermute | solution.py:137
  21.6 3.5 %collective-permute-start.7 = (bf16[16,4096]{1,0:T(8,128)(2,1)S(1)}, bf16[16,4096]{1,0:T(8,128)(2,1)S(1)}, u32[]{:S(2)}, u32[]{:S(2)}) collective-permute-start(bf16[16,4096]{1,0:T(8,128)(2,1)S(1)} %collective-permute-done.4.refs_4_), channel_id=1, source_target_pairs={{0,2},{2,0},{4,6},{6,4},{8,10},{10,8},{12,14},{14,12},{1,3},{3,1},... | collective-permute-start | bytes 393224 | tf_op jit(solution)/shard_map/ppermute | solution.py:137
  22.1 2.9 %collective-permute-start.12 = (bf16[16,4096]{1,0:T(8,128)(2,1)S(1)}, bf16[16,4096]{1,0:T(8,128)(2,1)S(1)}, u32[]{:S(2)}, u32[]{:S(2)}) collective-permute-start(bf16[16,4096]{1,0:T(8,128)(2,1)S(1)} %collective-permute-done.5.refs_12_), channel_id=1, source_target_pairs={{0,2},{2,0},{4,6},{6,4},{8,10},{10,8},{12,14},{14,12},{1,3},{3,1},... | collective-permute-start | bytes 393224 | tf_op jit(solution)/shard_map/ppermute | solution.py:137
  22.2 2.9 %collective-permute-start.13 = (bf16[16,4096]{1,0:T(8,128)(2,1)S(1)}, bf16[16,4096]{1,0:T(8,128)(2,1)S(1)}, u32[]{:S(2)}, u32[]{:S(2)}) collective-permute-start(bf16[16,4096]{1,0:T(8,128)(2,1)S(1)} %collective-permute-done.6.refs_14_), channel_id=1, source_target_pairs={{0,2},{2,0},{4,6},{6,4},{8,10},{10,8},{12,14},{14,12},{1,3},{3,1},... | collective-permute-start | bytes 393224 | tf_op jit(solution)/shard_map/ppermute | solution.py:137
  25.1 1.3 %collective-permute-start.11 = (bf16[16,4096]{1,0:T(8,128)(2,1)S(1)}, bf16[16,4096]{1,0:T(8,128)(2,1)S(1)}, u32[]{:S(2)}, u32[]{:S(2)}) collective-permute-start(bf16[16,4096]{1,0:T(8,128)(2,1)S(1)} %collective-permute-done.10.refs_10_), channel_id=1, source_target_pairs={{0,2},{2,0},{4,6},{6,4},{8,10},{10,8},{12,14},{14,12},{1,3},{3,1},... | collective-permute-start | bytes 393224 | tf_op jit(solution)/shard_map/ppermute | solution.py:137
  27.4 4.3 %collective-permute-start.14 = (f32[128,128]{1,0:T(8,128)S(1)}, f32[128,128]{1,0:T(8,128)S(1)}, u32[]{:S(2)}, u32[]{:S(2)}) collective-permute-start(f32[128,128]{1,0:T(8,128)S(1)} %get-tuple-element.22), channel_id=1, source_target_pairs={{0,1},{1,0},{2,3},{3,2},{4,5},{5,4},{6,7},{7,6},{8,9},{9,8},{10,11... | collective-permute-start | bytes 196616 | tf_op jit(solution)/shard_map/ppermute | solution.py:252

commit v7 on v6

--- a/solution.py
+++ b/solution.py
@@ -226,15 +226,14 @@
     mine = condition_layer(False, queries, left_factor, right_factor)
     other = condition_layer(True, queries, left_factor, right_factor)
     near = copy_near(train_grads)
-    s2 = along_columns(mine, 2)
+    mine_late, other = lax.optimization_barrier((mine, other))
+    s2 = along_columns(mine_late, 2)
     s1 = along_columns(mine, 1)
     s3 = along_columns(mine, 3)
-    s1, other = lax.optimization_barrier((s1, other))
-    s3, near = lax.optimization_barrier((s3, near))
+    y2 = other_part(s2)
     y1 = other_part(s1)
     y3 = other_part(s3)
-    s2, y1, y3 = lax.optimization_barrier((s2, y1, y3))
-    y2 = other_part(s2)
+    y1, y3, near = lax.optimization_barrier((y1, y3, near))
 
     blocks = []
     for block in (mine, other, s2, s1, s3, y2, y1, y3):

time: 32.6 us -> 32 us (0.982)
  waiting for transfers between devices: 10.3 us -> 9.23 us
  starting transfers between devices: 13.8 us -> 14.3 us
    ppermute x3, waiting for transfers between devices: 4.16 us -> 0.59 us  [other_part(): return lax.ppermute(value, 'parts', [(0, 1), (1, 0)])]
    ppermute x3, waiting for transfers between devices: 2.84 us -> 5.62 us  [along_columns(): return lax.ppermute(value, 'train', pairs)]
    ppermute x8, starting transfers between devices: 1.54 us -> 2.11 us  [other_core(): lax.ppermute(value, 'train', [(k, k ^ 1) for k in range(COLUMNS * PAIR)])]
where the time goes in v7:
time: 32 us; the launch traced here: 31.8 us
  starting transfers between devices  14.3 us (45%)
  waiting for transfers between devices  9.23 us (29%)
  Pallas kernels  7.57 us (24%)
  other arithmetic  0.64 us (2%)
    ppermute x3, starting transfers between devices, along_columns(): return lax.ppermute(value, 'train', pairs)  6.18 us
    ppermute x3, waiting for transfers between devices, along_columns(): return lax.ppermute(value, 'train', pairs)  5.62 us
    ppermute x3, starting transfers between devices, other_part(): return lax.ppermute(value, 'parts', [(0, 1), (1, 0)])  4.45 us
    pallas_call x2, Pallas kernels, condition_layer(): pl.pallas_call(functools.partial(condition_kernel, other), out_shape=jax....  3.53 us
    pallas_call x1, Pallas kernels, copy_near(): pl.pallas_call(copy_kernel, out_shape=jax.ShapeDtypeStruct(value.shape, v...  2.2 us
    ppermute x8, starting transfers between devices, other_core(): lax.ppermute(value, 'train', [(k, k ^ 1) for k in range(COLUMNS * PAIR)])  2.11 us
    ppermute x1, waiting for transfers between devices, direct(): received = lax.ppermute(sent, 'layer', [(0, 1), (1, 0)])  1.99 us
    pallas_call x2, Pallas kernels, local_call(): pl.pallas_call(kernel, out_shape=out_shape, in_specs=[spec] * len(operand...  1.84 us
  transfers between devices with their start and end apart: 15, of which 6 were waited for; matrix products, arithmetic and copies ran while one was open for 0% of the time, Pallas kernels for 15%

profile of v7, /device:TPU:0, one launch (start us, length us, event | category | flops | bytes accessed | tf_op | source)
XLA Modules:
  0.0 31.8 jit_solution(6628891200197733806)
XLA Ops:
  0.0 1.8 %condition_mine.1.refs_0_ = bf16[16,4096]{1,0:T(8,128)(2,1)S(1)} custom-call(bf16[2,1,16,4096]{3,2,1,0:T(8,128)(2,1)} %queries.3, f32[2,64,64]{2,1,0:T(8,128)} %left.3, f32[2,64,64]{2,1,0:T(8,128)} %right.3), custom_call_target="tpu_custom_call" | custom-call | flops 134217728 | bytes 524288 | tf_op jit(solution)/shard_map/condition_mine/pallas_call | solution.py:107
  1.8 3.1 %collective-permute-start.2 = (bf16[16,4096]{1,0:T(8,128)(2,1)S(1)}, bf16[16,4096]{1,0:T(8,128)(2,1)S(1)}, u32[]{:S(2)}, u32[]{:S(2)}) collective-permute-start(bf16[16,4096]{1,0:T(8,128)(2,1)S(1)} %condition_mine.1.refs_0_), channel_id=1, source_target_pairs={{12,0},{14,2},{0,4},{2,6},{4,8},{6,10},{8,12},{10,14},{13,1},{15,3... | collective-permute-start | bytes 393224 | tf_op jit(solution)/shard_map/ppermute | solution.py:133
  4.9 2.1 %collective-permute-start = (bf16[16,4096]{1,0:T(8,128)(2,1)S(1)}, bf16[16,4096]{1,0:T(8,128)(2,1)S(1)}, u32[]{:S(2)}, u32[]{:S(2)}) collective-permute-start(bf16[16,4096]{1,0:T(8,128)(2,1)S(1)} %condition_mine.1.refs_0_), channel_id=1, source_target_pairs={{4,0},{6,2},{8,4},{10,6},{12,8},{14,10},{0,12},{2,14},{5,1},{7,3},... | collective-permute-start | bytes 393224 | tf_op jit(solution)/shard_map/ppermute | solution.py:133
  6.9 1.8 %condition_other.1.refs_2_ = bf16[16,4096]{1,0:T(8,128)(2,1)S(1)} custom-call(bf16[2,1,16,4096]{3,2,1,0:T(8,128)(2,1)} %queries.3, f32[2,64,64]{2,1,0:T(8,128)} %left.3, f32[2,64,64]{2,1,0:T(8,128)} %right.3), custom_call_target="tpu_custom_call" | custom-call | flops 134217728 | bytes 524288 | tf_op jit(solution)/shard_map/condition_other/pallas_call | solution.py:107
  8.7 1.0 %collective-permute-start.6 = (bf16[16,4096]{1,0:T(8,128)(2,1)S(1)}, bf16[16,4096]{1,0:T(8,128)(2,1)S(1)}, u32[]{:S(2)}, u32[]{:S(2)}) collective-permute-start(bf16[16,4096]{1,0:T(8,128)(2,1)S(1)} %condition_mine.1.refs_0_), channel_id=1, source_target_pairs={{8,0},{10,2},{12,4},{14,6},{0,8},{2,10},{4,12},{6,14},{9,1},{11,3}... | collective-permute-start | bytes 393224 | tf_op jit(solution)/shard_map/ppermute | solution.py:133
  9.7 1.5 %collective-permute-done.2.refs_8_ = bf16[16,4096]{1,0:T(8,128)(2,1)S(1)} collective-permute-done((bf16[16,4096]{1,0:T(8,128)(2,1)S(1)}, bf16[16,4096]{1,0:T(8,128)(2,1)S(1)}, u32[]{:S(2)}, u32[]{:S(2)}) %collective-permute-start.2) | collective-permute-done | bytes 131104 | tf_op jit(solution)/shard_map/ppermute | solution.py:133
  11.2 1.8 %collective-permute-start.3 = (bf16[16,4096]{1,0:T(8,128)(2,1)S(1)}, bf16[16,4096]{1,0:T(8,128)(2,1)S(1)}, u32[]{:S(2)}, u32[]{:S(2)}) collective-permute-start(bf16[16,4096]{1,0:T(8,128)(2,1)S(1)} %collective-permute-done.2.refs_8_), channel_id=1, source_target_pairs={{0,16},{16,0},{1,17},{17,1},{2,18},{18,2},{3,19},{19,3},{4,20},{20... | collective-permute-start | bytes 393224 | tf_op jit(solution)/shard_map/ppermute | solution.py:141
  13.0 0.0 collective-permute-done.refs_6_
  13.0 1.2 %collective-permute-start.1 = (bf16[16,4096]{1,0:T(8,128)(2,1)S(1)}, bf16[16,4096]{1,0:T(8,128)(2,1)S(1)}, u32[]{:S(2)}, u32[]{:S(2)}) collective-permute-start(bf16[16,4096]{1,0:T(8,128)(2,1)S(1)} %collective-permute-done.refs_6_), channel_id=1, source_target_pairs={{0,16},{16,0},{1,17},{17,1},{2,18},{18,2},{3,19},{19,3},{4,20},{20... | collective-permute-start | bytes 393224 | tf_op jit(solution)/shard_map/ppermute | solution.py:141
  14.1 0.0 collective-permute-start.5
  14.1 0.5 %collective-permute-start.4 = (bf16[16,4096]{1,0:T(8,128)(2,1)S(1)}, bf16[16,4096]{1,0:T(8,128)(2,1)S(1)}, u32[]{:S(2)}, u32[]{:S(2)}) collective-permute-start(bf16[16,4096]{1,0:T(8,128)(2,1)S(1)} %condition_mine.1.refs_0_), channel_id=1, source_target_pairs={{0,2},{2,0},{4,6},{6,4},{8,10},{10,8},{12,14},{14,12},{1,3},{3,1},... | collective-permute-start | bytes 393224 | tf_op jit(solution)/shard_map/ppermute | solution.py:137
  14.7 4.1 %collective-permute-done.6.refs_4_ = bf16[16,4096]{1,0:T(8,128)(2,1)S(1)} collective-permute-done((bf16[16,4096]{1,0:T(8,128)(2,1)S(1)}, bf16[16,4096]{1,0:T(8,128)(2,1)S(1)}, u32[]{:S(2)}, u32[]{:S(2)}) %collective-permute-start.6) | collective-permute-done | bytes 131104 | tf_op jit(solution)/shard_map/ppermute | solution.py:133
  18.8 1.5 %collective-permute-start.10 = (bf16[16,4096]{1,0:T(8,128)(2,1)S(1)}, bf16[16,4096]{1,0:T(8,128)(2,1)S(1)}, u32[]{:S(2)}, u32[]{:S(2)}) collective-permute-start(bf16[16,4096]{1,0:T(8,128)(2,1)S(1)} %collective-permute-done.6.refs_4_), channel_id=1, source_target_pairs={{0,16},{16,0},{1,17},{17,1},{2,18},{18,2},{3,19},{19,3},{4,20},{20... | collective-permute-start | bytes 393224 | tf_op jit(solution)/shard_map/ppermute | solution.py:141
  20.3 0.0 collective-permute-done.3.refs_14_
  20.3 0.0 collective-permute-start.7
  20.3 2.2 %near.1.train = bf16[256,2,4096]{2,1,0:T(2,128)(2,1)S(1)} custom-call(bf16[256,2,4096]{2,1,0:T(2,128)(2,1)} %source.1), custom_call_target="tpu_custom_call" | custom-call | bytes 8388608 | tf_op jit(solution)/shard_map/near/pallas_call | solution.py:151
  22.5 0.0 collective-permute-done.1.refs_12_
  22.5 0.6 %collective-permute-start.9 = (bf16[16,4096]{1,0:T(8,128)(2,1)S(1)}, bf16[16,4096]{1,0:T(8,128)(2,1)S(1)}, u32[]{:S(2)}, u32[]{:S(2)}) collective-permute-start(bf16[16,4096]{1,0:T(8,128)(2,1)S(1)} %collective-permute-done.2.refs_8_), channel_id=1, source_target_pairs={{0,2},{2,0},{4,6},{6,4},{8,10},{10,8},{12,14},{14,12},{1,3},{3,1},... | collective-permute-start | bytes 393224 | tf_op jit(solution)/shard_map/ppermute | solution.py:137
  23.1 0.0 collective-permute-done.5.refs_3_
  23.1 0.1 collective-permute-start.8
  23.2 0.0 collective-permute-done.4.refs_1_
  23.2 0.4 %collective-permute-start.12 = (bf16[16,4096]{1,0:T(8,128)(2,1)S(1)}, bf16[16,4096]{1,0:T(8,128)(2,1)S(1)}, u32[]{:S(2)}, u32[]{:S(2)}) collective-permute-start(bf16[16,4096]{1,0:T(8,128)(2,1)S(1)} %collective-permute-done.1.refs_12_), channel_id=1, source_target_pairs={{0,2},{2,0},{4,6},{6,4},{8,10},{10,8},{12,14},{14,12},{1,3},{3,1},... | collective-permute-start | bytes 393224 | tf_op jit(solution)/shard_map/ppermute | solution.py:137
  23.6 0.6 %collective-permute-done.10.refs_10_ = bf16[16,4096]{1,0:T(8,128)(2,1)S(1)} collective-permute-done((bf16[16,4096]{1,0:T(8,128)(2,1)S(1)}, bf16[16,4096]{1,0:T(8,128)(2,1)S(1)}, u32[]{:S(2)}, u32[]{:S(2)}) %collective-permute-start.10) | collective-permute-done | bytes 131104 | tf_op jit(solution)/shard_map/ppermute | solution.py:141
  24.2 0.0 collective-permute-start.11
  24.2 0.0 collective-permute-done.7.refs_5_
  24.2 0.5 %collective-permute-start.13 = (bf16[16,4096]{1,0:T(8,128)(2,1)S(1)}, bf16[16,4096]{1,0:T(8,128)(2,1)S(1)}, u32[]{:S(2)}, u32[]{:S(2)}) collective-permute-start(bf16[16,4096]{1,0:T(8,128)(2,1)S(1)} %collective-permute-done.3.refs_14_), channel_id=1, source_target_pairs={{0,2},{2,0},{4,6},{6,4},{8,10},{10,8},{12,14},{14,12},{1,3},{3,1},... | collective-permute-start | bytes 393224 | tf_op jit(solution)/shard_map/ppermute | solution.py:137
  24.7 0.0 collective-permute-done.9.refs_9_
  24.7 0.0 collective-permute-done.8.refs_7_
  24.7 0.8 %collective-permute-done.11.refs_11_ = bf16[16,4096]{1,0:T(8,128)(2,1)S(1)} collective-permute-done((bf16[16,4096]{1,0:T(8,128)(2,1)S(1)}, bf16[16,4096]{1,0:T(8,128)(2,1)S(1)}, u32[]{:S(2)}, u32[]{:S(2)}) %collective-permute-start.11) | collective-permute-done | bytes 131104 | tf_op jit(solution)/shard_map/ppermute | solution.py:137
  25.6 0.0 collective-permute-done.12.refs_13_
  25.6 0.2 collective-permute-done.13.refs_15_
  25.8 1.0 %scores_sent.1 = (f32[128,128]{1,0:T(8,128)S(1)}, bf16[2,128,4096]{2,1,0:T(8,128)(2,1)S(1)}) custom-call(bf16[256,2,4096]{2,1,0:T(2,128)(2,1)S(1)} %near.1.train, bf16[16,4096]{1,0:T(8,128)(2,1)S(1)} %condition_mine.1.refs_0_, bf16[16,4096]{1,0:T(8,128)(2,1)S(1)} %collective-permute-done.4.refs_1_, bf16[16,4096]{1,0:T(8,128)(2,1)S(1)} %condition_other.1.refs_2_, ...), custom_call_target="tpu_custom_call" | custom-call | flops 536870912 | bytes 4194304 | tf_op jit(solution)/shard_map/scores_sent/pallas_call | solution.py:208
  26.8 1.6 %collective-permute-start.14 = (f32[128,128]{1,0:T(8,128)S(1)}, f32[128,128]{1,0:T(8,128)S(1)}, u32[]{:S(2)}, u32[]{:S(2)}) collective-permute-start(f32[128,128]{1,0:T(8,128)S(1)} %get-tuple-element.18), channel_id=1, source_target_pairs={{0,1},{1,0},{2,3},{3,2},{4,5},{5,4},{6,7},{7,6},{8,9},{9,8},{10,11... | collective-permute-start | bytes 196616 | tf_op jit(solution)/shard_map/ppermute | solution.py:251
  28.3 0.8 %scores_kept.1 = f32[128,128]{1,0:T(8,128)S(1)} custom-call(bf16[256,2,4096]{2,1,0:T(2,128)(2,1)S(1)} %near.1.train, bf16[2,128,4096]{2,1,0:T(8,128)(2,1)S(1)} %get-tuple-element.17.table), custom_call_target="tpu_custom_call" | custom-call | flops 536870912 | bytes 4194304 | tf_op jit(solution)/shard_map/scores_kept/pallas_call | solution.py:208
  29.2 2.0 %collective-permute-done.14 = f32[128,128]{1,0:T(8,128)S(1)} collective-permute-done((f32[128,128]{1,0:T(8,128)S(1)}, f32[128,128]{1,0:T(8,128)S(1)}, u32[]{:S(2)}, u32[]{:S(2)}) %collective-permute-start.14) | collective-permute-done | bytes 65568 | tf_op jit(solution)/shard_map/ppermute | solution.py:251
  31.1 0.6 %add.3 = f32[128,128]{1,0:T(8,128)} add(f32[128,128]{1,0:T(8,128)S(1)} %scores_kept.1, f32[128,128]{1,0:T(8,128)S(1)} %collective-permute-done.14) | non-fusion elementwise | flops 16384 | bytes 196608 | tf_op jit(solution)/shard_map/add | solution.py:253
Async XLA Ops:
  1.8 9.4 %collective-permute-start.2 = (bf16[16,4096]{1,0:T(8,128)(2,1)S(1)}, bf16[16,4096]{1,0:T(8,128)(2,1)S(1)}, u32[]{:S(2)}, u32[]{:S(2)}) collective-permute-start(bf16[16,4096]{1,0:T(8,128)(2,1)S(1)} %condition_mine.1.refs_0_), channel_id=1, source_target_pairs={{12,0},{14,2},{0,4},{2,6},{4,8},{6,10},{8,12},{10,14},{13,1},{15,3... | collective-permute-start | bytes 393224 | tf_op jit(solution)/shard_map/ppermute | solution.py:133
  4.9 8.1 %collective-permute-start = (bf16[16,4096]{1,0:T(8,128)(2,1)S(1)}, bf16[16,4096]{1,0:T(8,128)(2,1)S(1)}, u32[]{:S(2)}, u32[]{:S(2)}) collective-permute-start(bf16[16,4096]{1,0:T(8,128)(2,1)S(1)} %condition_mine.1.refs_0_), channel_id=1, source_target_pairs={{4,0},{6,2},{8,4},{10,6},{12,8},{14,10},{0,12},{2,14},{5,1},{7,3},... | collective-permute-start | bytes 393224 | tf_op jit(solution)/shard_map/ppermute | solution.py:133
  8.7 10.1 %collective-permute-start.6 = (bf16[16,4096]{1,0:T(8,128)(2,1)S(1)}, bf16[16,4096]{1,0:T(8,128)(2,1)S(1)}, u32[]{:S(2)}, u32[]{:S(2)}) collective-permute-start(bf16[16,4096]{1,0:T(8,128)(2,1)S(1)} %condition_mine.1.refs_0_), channel_id=1, source_target_pairs={{8,0},{10,2},{12,4},{14,6},{0,8},{2,10},{4,12},{6,14},{9,1},{11,3}... | collective-permute-start | bytes 393224 | tf_op jit(solution)/shard_map/ppermute | solution.py:133
  11.2 9.1 %collective-permute-start.3 = (bf16[16,4096]{1,0:T(8,128)(2,1)S(1)}, bf16[16,4096]{1,0:T(8,128)(2,1)S(1)}, u32[]{:S(2)}, u32[]{:S(2)}) collective-permute-start(bf16[16,4096]{1,0:T(8,128)(2,1)S(1)} %collective-permute-done.2.refs_8_), channel_id=1, source_target_pairs={{0,16},{16,0},{1,17},{17,1},{2,18},{18,2},{3,19},{19,3},{4,20},{20... | collective-permute-start | bytes 393224 | tf_op jit(solution)/shard_map/ppermute | solution.py:141
  13.0 9.6 %collective-permute-start.1 = (bf16[16,4096]{1,0:T(8,128)(2,1)S(1)}, bf16[16,4096]{1,0:T(8,128)(2,1)S(1)}, u32[]{:S(2)}, u32[]{:S(2)}) collective-permute-start(bf16[16,4096]{1,0:T(8,128)(2,1)S(1)} %collective-permute-done.refs_6_), channel_id=1, source_target_pairs={{0,16},{16,0},{1,17},{17,1},{2,18},{18,2},{3,19},{19,3},{4,20},{20... | collective-permute-start | bytes 393224 | tf_op jit(solution)/shard_map/ppermute | solution.py:141
  14.1 9.0 %collective-permute-start.5 = (bf16[16,4096]{1,0:T(8,128)(2,1)S(1)}, bf16[16,4096]{1,0:T(8,128)(2,1)S(1)}, u32[]{:S(2)}, u32[]{:S(2)}) collective-permute-start(bf16[16,4096]{1,0:T(8,128)(2,1)S(1)} %condition_other.1.refs_2_), channel_id=1, source_target_pairs={{0,2},{2,0},{4,6},{6,4},{8,10},{10,8},{12,14},{14,12},{1,3},{3,1},... | collective-permute-start | bytes 393224 | tf_op jit(solution)/shard_map/ppermute | solution.py:137
  14.1 9.1 %collective-permute-start.4 = (bf16[16,4096]{1,0:T(8,128)(2,1)S(1)}, bf16[16,4096]{1,0:T(8,128)(2,1)S(1)}, u32[]{:S(2)}, u32[]{:S(2)}) collective-permute-start(bf16[16,4096]{1,0:T(8,128)(2,1)S(1)} %condition_mine.1.refs_0_), channel_id=1, source_target_pairs={{0,2},{2,0},{4,6},{6,4},{8,10},{10,8},{12,14},{14,12},{1,3},{3,1},... | collective-permute-start | bytes 393224 | tf_op jit(solution)/shard_map/ppermute | solution.py:137
  18.8 5.4 %collective-permute-start.10 = (bf16[16,4096]{1,0:T(8,128)(2,1)S(1)}, bf16[16,4096]{1,0:T(8,128)(2,1)S(1)}, u32[]{:S(2)}, u32[]{:S(2)}) collective-permute-start(bf16[16,4096]{1,0:T(8,128)(2,1)S(1)} %collective-permute-done.6.refs_4_), channel_id=1, source_target_pairs={{0,16},{16,0},{1,17},{17,1},{2,18},{18,2},{3,19},{19,3},{4,20},{20... | collective-permute-start | bytes 393224 | tf_op jit(solution)/shard_map/ppermute | solution.py:141
  20.3 3.9 %collective-permute-start.7 = (bf16[16,4096]{1,0:T(8,128)(2,1)S(1)}, bf16[16,4096]{1,0:T(8,128)(2,1)S(1)}, u32[]{:S(2)}, u32[]{:S(2)}) collective-permute-start(bf16[16,4096]{1,0:T(8,128)(2,1)S(1)} %collective-permute-done.6.refs_4_), channel_id=1, source_target_pairs={{0,2},{2,0},{4,6},{6,4},{8,10},{10,8},{12,14},{14,12},{1,3},{3,1},... | collective-permute-start | bytes 393224 | tf_op jit(solution)/shard_map/ppermute | solution.py:137
  22.5 2.2 %collective-permute-start.9 = (bf16[16,4096]{1,0:T(8,128)(2,1)S(1)}, bf16[16,4096]{1,0:T(8,128)(2,1)S(1)}, u32[]{:S(2)}, u32[]{:S(2)}) collective-permute-start(bf16[16,4096]{1,0:T(8,128)(2,1)S(1)} %collective-permute-done.2.refs_8_), channel_id=1, source_target_pairs={{0,2},{2,0},{4,6},{6,4},{8,10},{10,8},{12,14},{14,12},{1,3},{3,1},... | collective-permute-start | bytes 393224 | tf_op jit(solution)/shard_map/ppermute | solution.py:137
  23.1 1.6 %collective-permute-start.8 = (bf16[16,4096]{1,0:T(8,128)(2,1)S(1)}, bf16[16,4096]{1,0:T(8,128)(2,1)S(1)}, u32[]{:S(2)}, u32[]{:S(2)}) collective-permute-start(bf16[16,4096]{1,0:T(8,128)(2,1)S(1)} %collective-permute-done.refs_6_), channel_id=1, source_target_pairs={{0,2},{2,0},{4,6},{6,4},{8,10},{10,8},{12,14},{14,12},{1,3},{3,1},... | collective-permute-start | bytes 393224 | tf_op jit(solution)/shard_map/ppermute | solution.py:137
  23.2 2.4 %collective-permute-start.12 = (bf16[16,4096]{1,0:T(8,128)(2,1)S(1)}, bf16[16,4096]{1,0:T(8,128)(2,1)S(1)}, u32[]{:S(2)}, u32[]{:S(2)}) collective-permute-start(bf16[16,4096]{1,0:T(8,128)(2,1)S(1)} %collective-permute-done.1.refs_12_), channel_id=1, source_target_pairs={{0,2},{2,0},{4,6},{6,4},{8,10},{10,8},{12,14},{14,12},{1,3},{3,1},... | collective-permute-start | bytes 393224 | tf_op jit(solution)/shard_map/ppermute | solution.py:137
  24.2 1.3 %collective-permute-start.11 = (bf16[16,4096]{1,0:T(8,128)(2,1)S(1)}, bf16[16,4096]{1,0:T(8,128)(2,1)S(1)}, u32[]{:S(2)}, u32[]{:S(2)}) collective-permute-start(bf16[16,4096]{1,0:T(8,128)(2,1)S(1)} %collective-permute-done.10.refs_10_), channel_id=1, source_target_pairs={{0,2},{2,0},{4,6},{6,4},{8,10},{10,8},{12,14},{14,12},{1,3},{3,1},... | collective-permute-start | bytes 393224 | tf_op jit(solution)/shard_map/ppermute | solution.py:137
  24.2 1.5 %collective-permute-start.13 = (bf16[16,4096]{1,0:T(8,128)(2,1)S(1)}, bf16[16,4096]{1,0:T(8,128)(2,1)S(1)}, u32[]{:S(2)}, u32[]{:S(2)}) collective-permute-start(bf16[16,4096]{1,0:T(8,128)(2,1)S(1)} %collective-permute-done.3.refs_14_), channel_id=1, source_target_pairs={{0,2},{2,0},{4,6},{6,4},{8,10},{10,8},{12,14},{14,12},{1,3},{3,1},... | collective-permute-start | bytes 393224 | tf_op jit(solution)/shard_map/ppermute | solution.py:137
  26.8 4.4 %collective-permute-start.14 = (f32[128,128]{1,0:T(8,128)S(1)}, f32[128,128]{1,0:T(8,128)S(1)}, u32[]{:S(2)}, u32[]{:S(2)}) collective-permute-start(f32[128,128]{1,0:T(8,128)S(1)} %get-tuple-element.18), channel_id=1, source_target_pairs={{0,1},{1,0},{2,3},{3,2},{4,5},{5,4},{6,7},{7,6},{8,9},{9,8},{10,11... | collective-permute-start | bytes 196616 | tf_op jit(solution)/shard_map/ppermute | solution.py:251

commit v8 on v7

--- a/solution.py
+++ b/solution.py
@@ -80,7 +80,13 @@
         put(k, placed[k * count : (k + 1) * count, :].astype(jnp.bfloat16))
 
 
-def condition_kernel(other, queries, left, right, out, block_in, left_in, right_in, spread, stacked, placed, arrived):
+def condition_kernel(other, *refs):
+    if other:
+        queries, left, right, train, out, near, *scratch, near_arrived = refs
+        near_copy = pltpu.make_async_copy(train, near, near_arrived)
+    else:
+        queries, left, right, out, *scratch = refs
+    block_in, left_in, right_in, spread, stacked, placed, arrived = scratch
     part = lax.axis_index("parts")
     layer = 1 - part if other else part
     copies = [
@@ -91,6 +97,8 @@
     ]
     for copy in copies:
         copy.start()
+    if other:
+        near_copy.start()
     for copy in copies:
         copy.wait()
 
@@ -98,17 +106,19 @@
         out[:, k * LANES : (k + 1) * LANES] = tile
 
     condition_block(block_in[...], left_in[...], right_in[...], put, spread, stacked, placed)
-
-
-def condition_layer(other, queries, left_factor, right_factor):
+    if other:
+        near_copy.wait()
+
+
+def condition_layer(other, queries, left_factor, right_factor, *train):
     _, _, count, width = queries.shape
     pairs = width // LANES
     far = pl.BlockSpec(memory_space=pltpu.HBM)
     return pl.pallas_call(
         functools.partial(condition_kernel, other),
-        out_shape=jax.ShapeDtypeStruct((count, width), jnp.bfloat16),
-        in_specs=[far] * 3,
-        out_specs=pl.BlockSpec(memory_space=pltpu.VMEM),
+        out_shape=[jax.ShapeDtypeStruct(shape, jnp.bfloat16) for shape in ((count, width), *(x.shape for x in train))],
+        in_specs=[far] * (3 + len(train)),
+        out_specs=[pl.BlockSpec(memory_space=pltpu.VMEM)] * (1 + len(train)),
         scratch_shapes=[
             pltpu.VMEM((count, width), jnp.bfloat16),
             pltpu.VMEM(left_factor.shape[1:], jnp.float32),
@@ -117,11 +127,12 @@
             pltpu.VMEM((count // 2, 2 * pairs, LANES), jnp.float32),
             pltpu.VMEM((pairs * count, LANES), jnp.float32),
             pltpu.SemaphoreType.DMA((3,)),
+            *(pltpu.SemaphoreType.DMA for _ in train),
         ],
-        compiler_params=pltpu.CompilerParams(vmem_limit_bytes=8 * 2**20),
+        compiler_params=pltpu.CompilerParams(vmem_limit_bytes=12 * 2**20),
         cost_estimate=pl.CostEstimate(flops=2**27, bytes_accessed=2**19, transcendentals=0),
         name="condition_other" if other else "condition_mine",
-    )(*(pltpu.with_memory_space_constraint(x, pltpu.HBM) for x in (queries, left_factor, right_factor)))
+    )(*(pltpu.with_memory_space_constraint(x, pltpu.HBM) for x in (queries, left_factor, right_factor, *train)))
 
 
 def along_columns(value, step):
@@ -133,31 +144,19 @@
     return lax.ppermute(value, "train", pairs)
 
 
+def relay(value):
+    pairs = [
+        (a * PAIR + c, b * PAIR + c) for a, b in ((0, 2), (2, 3), (3, 1), (1, 0)) for c in range(PAIR)
+    ]
+    return lax.ppermute(value, "train", pairs)
+
+
 def other_core(value):
     return lax.ppermute(value, "train", [(k, k ^ 1) for k in range(COLUMNS * PAIR)])
 
 
 def other_part(value):
     return lax.ppermute(value, "parts", [(0, 1), (1, 0)])
-
-
-def copy_kernel(source, target, done):
-    copy = pltpu.make_async_copy(source, target, done)
-    copy.start()
-    copy.wait()
-
-
-def copy_near(value):
-    return pl.pallas_call(
-        copy_kernel,
-        out_shape=jax.ShapeDtypeStruct(value.shape, value.dtype),
-        in_specs=[pl.BlockSpec(memory_space=pltpu.HBM)],
-        out_specs=pl.BlockSpec(memory_space=pltpu.VMEM),
-        scratch_shapes=[pltpu.SemaphoreType.DMA],
-        compiler_params=pltpu.CompilerParams(vmem_limit_bytes=6 * 2**20),
-        cost_estimate=pl.CostEstimate(flops=0, bytes_accessed=2 * value.size * 2, transcendentals=0),
-        name="near",
-    )(pltpu.with_memory_space_constraint(value, pltpu.HBM))
 
 
 def place():
@@ -187,15 +186,27 @@
     column, core = place()
     count = blocks[0].shape[0]
 
-    def put(layer, step, twin, block):
+    def put(layer, step, twin, block, lane=0):
         member = lax.rem(column + step, COLUMNS) * PAIR + (1 - core if twin else core)
-        table[layer, pl.ds(pl.multiple_of(member * count, count), count), :] = block
-
+        table[layer, pl.ds(pl.multiple_of(member * count, count), count), lane : lane + block.shape[1]] = block
+
+    far = table.shape[2] // 2
     for twin in range(PAIR):
-        for k, (layer, step) in enumerate(
-            ((part, 0), (1 - part, 0), (part, 2), (part, 1), (part, 3), (1 - part, 2), (1 - part, 1), (1 - part, 3))
+        for k, (layer, step, lane) in enumerate(
+            (
+                (part, 0, 0),
+                (1 - part, 0, 0),
+                (part, 2, far),
+                (part, 2, 0),
+                (part, 1, 0),
+                (part, 3, 0),
+                (1 - part, 2, far),
+                (1 - part, 2, 0),
+                (1 - part, 1, 0),
+                (1 - part, 3, 0),
+            )
         ):
-            put(layer, step, twin, blocks[PAIR * k + twin][...])
+            put(layer, step, twin, blocks[PAIR * k + twin][...], lane)
     row_scores(train, table, 1 - lax.axis_index("layer"), terms, scores)
 
 
@@ -223,20 +234,24 @@
     total = count * COLUMNS * PAIR
     share = rows // 2
 
-    mine = condition_layer(False, queries, left_factor, right_factor)
-    other = condition_layer(True, queries, left_factor, right_factor)
-    near = copy_near(train_grads)
+    (mine,) = condition_layer(False, queries, left_factor, right_factor)
+    other, near = condition_layer(True, queries, left_factor, right_factor, train_grads)
+    half = width // 2
+    column, _ = place()
     mine_late, other = lax.optimization_barrier((mine, other))
-    s2 = along_columns(mine_late, 2)
+    s2a = along_columns(mine_late[:, :half], 2)
     s1 = along_columns(mine, 1)
     s3 = along_columns(mine, 3)
-    y2 = other_part(s2)
+    passed = jnp.where(column == 1, s1[:, half:], jnp.where(column == 2, s3[:, half:], mine[:, half:]))
+    s2b = relay(passed)
     y1 = other_part(s1)
     y3 = other_part(s3)
-    y1, y3, near = lax.optimization_barrier((y1, y3, near))
+    s2a, s2b = lax.optimization_barrier((s2a, s2b))
+    y2a = other_part(s2a)
+    y2b = other_part(s2b)
 
     blocks = []
-    for block in (mine, other, s2, s1, s3, y2, y1, y3):
+    for block in (mine, other, s2b, s2a, s1, s3, y2b, y2a, y1, y3):
         blocks += [block, other_core(block)]
     f32 = functools.partial(jax.ShapeDtypeStruct, dtype=jnp.float32)
     terms = [pltpu.VMEM((layer_count, share * layer_count, total), jnp.float32)]

time: 32 us -> 37.8 us (1.18)
  local copies, waits for them, and re-layouts: 0 us -> 4.12 us
  starting transfers between devices: 14.3 us -> 16.3 us
  Pallas kernels: 7.57 us -> 6.65 us
  waiting for transfers between devices: 9.23 us -> 9.94 us
    unnamed x0 -> x6, local copies, waits for them, and re-layouts: none -> 4.12 us
    ppermute x3 -> x4, waiting for transfers between devices: 0.59 us -> 3.83 us  [other_part(): return lax.ppermute(value, 'parts', [(0, 1), (1, 0)])]
    ppermute x3, waiting for transfers between devices: 5.62 us -> 2.91 us  [along_columns(): return lax.ppermute(value, 'train', pairs)]
    ppermute x0 -> x1, starting transfers between devices: none -> 2.03 us  [relay(): return lax.ppermute(value, 'train', pairs)]
    pallas_call x3 -> x2, Pallas kernels: 5.73 us -> 4.81 us  [condition_layer(): pl.pallas_call(functools.partial(condition_kernel, other), out_shape=[jax...]
    ppermute x3 -> x4, starting transfers between devices: 4.45 us -> 5.22 us  [other_part(): return lax.ppermute(value, 'parts', [(0, 1), (1, 0)])]
    ppermute x8 -> x10, starting transfers between devices: 2.11 us -> 1.33 us  [other_core(): lax.ppermute(value, 'train', [(k, k ^ 1) for k in range(COLUMNS * PAIR)])]
    ppermute x8 -> x10, waiting for transfers between devices: 1.03 us -> 1.27 us  [other_core(): lax.ppermute(value, 'train', [(k, k ^ 1) for k in range(COLUMNS * PAIR)])]
  transfers between devices with their start and end apart: 15 -> 19, of which waited for: 6 -> 8; matrix products, arithmetic and copies ran while one was open for 0% -> 0% of each run, Pallas kernels for 15% -> 10%
where the time goes in v8:
time: 37.8 us; the launch traced here: 37.7 us
  starting transfers between devices  16.3 us (43%)
  waiting for transfers between devices  9.94 us (26%)
  Pallas kernels  6.65 us (18%)
  local copies, waits for them, and re-layouts  4.12 us (11%)
  other arithmetic  0.65 us (2%)
    ppermute x3, starting transfers between devices, along_columns(): return lax.ppermute(value, 'train', pairs)  6.11 us
    ppermute x4, starting transfers between devices, other_part(): return lax.ppermute(value, 'parts', [(0, 1), (1, 0)])  5.22 us
    pallas_call x2, Pallas kernels, condition_layer(): pl.pallas_call(functools.partial(condition_kernel, other), out_shape=[jax...  4.81 us
    unnamed x6, local copies, waits for them, and re-layouts  4.12 us
    ppermute x4, waiting for transfers between devices, other_part(): return lax.ppermute(value, 'parts', [(0, 1), (1, 0)])  3.83 us
    ppermute x3, waiting for transfers between devices, along_columns(): return lax.ppermute(value, 'train', pairs)  2.91 us
    ppermute x1, starting transfers between devices, relay(): return lax.ppermute(value, 'train', pairs)  2.03 us
    ppermute x1, waiting for transfers between devices, direct(): received = lax.ppermute(sent, 'layer', [(0, 1), (1, 0)])  1.93 us
  transfers between devices with their start and end apart: 19, of which 8 were waited for; matrix products, arithmetic and copies ran while one was open for 0% of the time, Pallas kernels for 10%

profile of v8, /device:TPU:0, one launch (start us, length us, event | category | flops | bytes accessed | tf_op | source)
XLA Modules:
  0.0 37.7 jit_solution(8428824358636980309)
XLA Ops:
  0.0 1.8 %condition_mine.1.refs_0_ = bf16[16,4096]{1,0:T(8,128)(2,1)S(1)} custom-call(bf16[2,1,16,4096]{3,2,1,0:T(8,128)(2,1)} %refs_0_.3, f32[2,64,64]{2,1,0:T(8,128)} %refs_1_.3, f32[2,64,64]{2,1,0:T(8,128)} %refs_2_.3), custom_call_target="tpu_custom_call" | custom-call | flops 134217728 | bytes 524288 | tf_op jit(solution)/shard_map/condition_mine/pallas_call | solution.py:117
  1.8 3.1 %collective-permute-start.4 = (bf16[16,4096]{1,0:T(8,128)(2,1)S(1)}, bf16[16,4096]{1,0:T(8,128)(2,1)S(1)}, u32[]{:S(2)}, u32[]{:S(2)}) collective-permute-start(bf16[16,4096]{1,0:T(8,128)(2,1)S(1)} %condition_mine.1.refs_0_), channel_id=1, source_target_pairs={{12,0},{14,2},{0,4},{2,6},{4,8},{6,10},{8,12},{10,14},{13,1},{15,3... | collective-permute-start | bytes 393224 | tf_op jit(solution)/shard_map/ppermute | solution.py:144
  4.9 2.1 %collective-permute-start.3 = (bf16[16,4096]{1,0:T(8,128)(2,1)S(1)}, bf16[16,4096]{1,0:T(8,128)(2,1)S(1)}, u32[]{:S(2)}, u32[]{:S(2)}) collective-permute-start(bf16[16,4096]{1,0:T(8,128)(2,1)S(1)} %condition_mine.1.refs_0_), channel_id=1, source_target_pairs={{4,0},{6,2},{8,4},{10,6},{12,8},{14,10},{0,12},{2,14},{5,1},{7,3},... | collective-permute-start | bytes 393224 | tf_op jit(solution)/shard_map/ppermute | solution.py:144
  6.9 0.0 collective-permute-start
  6.9 3.0 %condition_other.1 = (bf16[16,4096]{1,0:T(8,128)(2,1)S(1)}, bf16[256,2,4096]{2,1,0:T(2,128)(2,1)S(1)}) custom-call(bf16[2,1,16,4096]{3,2,1,0:T(8,128)(2,1)} %refs_0_.3, f32[2,64,64]{2,1,0:T(8,128)} %refs_1_.3, f32[2,64,64]{2,1,0:T(8,128)} %refs_2_.3, bf16[256,2,4096]{2,1,0:T(2,128)(2,1)} %refs_3_.1), custom_call_target="tpu_custom_call" | custom-call | flops 134217728 | bytes 524288 | tf_op jit(solution)/shard_map/condition_other/pallas_call | solution.py:117
  10.0 0.0 copy-start
  10.0 1.9 %copy-done = bf16[256,2,4096]{2,1,0:T(2,128)(2,1)} copy-done((bf16[256,2,4096]{2,1,0:T(2,128)(2,1)}, bf16[256,2,4096]{2,1,0:T(2,128)(2,1)S(1)}, u32[]{:S(2)}) %copy-start) | copy-done | bytes 4194328
  11.9 0.9 %collective-permute-start.2 = (bf16[16,2048]{1,0:T(8,128)(2,1)S(1)}, bf16[16,2048]{1,0:T(8,128)(2,1)S(1)}, u32[]{:S(2)}, u32[]{:S(2)}) collective-permute-start(bf16[16,2048]{1,0:T(8,128)(2,1)S(1)} %slice.12), channel_id=1, source_target_pairs={{8,0},{10,2},{12,4},{14,6},{0,8},{2,10},{4,12},{6,14},{9,1},{11,3}... | collective-permute-start | bytes 196616 | tf_op jit(solution)/shard_map/ppermute | solution.py:144
  12.9 0.0 collective-permute-done.4.refs_10_
  12.9 0.0 collective-permute-done.3.refs_8_
  12.9 2.0 %collective-permute-start.5 = (bf16[16,2048]{1,0:T(8,128)(2,1)S(1)}, bf16[16,2048]{1,0:T(8,128)(2,1)S(1)}, u32[]{:S(2)}, u32[]{:S(2)}) collective-permute-start(bf16[16,2048]{1,0:T(8,128)(2,1)S(1)} %fusion), channel_id=1, source_target_pairs={{0,8},{2,10},{8,12},{10,14},{12,4},{14,6},{4,0},{6,2},{1,9},{3,11}... | collective-permute-start | bytes 196616 | tf_op jit(solution)/shard_map/ppermute | solution.py:151
  14.9 0.0 collective-permute-start.1
  14.9 1.7 %collective-permute-start.16 = (bf16[16,4096]{1,0:T(8,128)(2,1)S(1)}, bf16[16,4096]{1,0:T(8,128)(2,1)S(1)}, u32[]{:S(2)}, u32[]{:S(2)}) collective-permute-start(bf16[16,4096]{1,0:T(8,128)(2,1)S(1)} %collective-permute-done.4.refs_10_), channel_id=1, source_target_pairs={{0,16},{16,0},{1,17},{17,1},{2,18},{18,2},{3,19},{19,3},{4,20},{20... | collective-permute-start | bytes 393224 | tf_op jit(solution)/shard_map/ppermute | solution.py:159
  16.6 2.9 %collective-permute-done.2.refs_6_ = bf16[16,2048]{1,0:T(8,128)(2,1)S(1)} collective-permute-done((bf16[16,2048]{1,0:T(8,128)(2,1)S(1)}, bf16[16,2048]{1,0:T(8,128)(2,1)S(1)}, u32[]{:S(2)}, u32[]{:S(2)}) %collective-permute-start.2) | collective-permute-done | bytes 65568 | tf_op jit(solution)/shard_map/ppermute | solution.py:144
  19.5 0.1 collective-permute-start.9
  19.6 0.0 collective-permute-done.refs_1_
  19.6 1.5 %collective-permute-start.14 = (bf16[16,4096]{1,0:T(8,128)(2,1)S(1)}, bf16[16,4096]{1,0:T(8,128)(2,1)S(1)}, u32[]{:S(2)}, u32[]{:S(2)}) collective-permute-start(bf16[16,4096]{1,0:T(8,128)(2,1)S(1)} %collective-permute-done.3.refs_8_), channel_id=1, source_target_pairs={{0,16},{16,0},{1,17},{17,1},{2,18},{18,2},{3,19},{19,3},{4,20},{20... | collective-permute-start | bytes 393224 | tf_op jit(solution)/shard_map/ppermute | solution.py:159
  21.1 0.0 collective-permute-done.5.refs_4_
  21.1 0.2 collective-permute-start.8
  21.3 0.0 collective-permute-done.1.refs_3_
  21.3 0.5 %collective-permute-start.10 = (bf16[16,2048]{1,0:T(8,128)(2,1)S(1)}, bf16[16,2048]{1,0:T(8,128)(2,1)S(1)}, u32[]{:S(2)}, u32[]{:S(2)}) collective-permute-start(bf16[16,2048]{1,0:T(8,128)(2,1)S(1)} %collective-permute-done.5.refs_4_), channel_id=1, source_target_pairs={{0,16},{16,0},{1,17},{17,1},{2,18},{18,2},{3,19},{19,3},{4,20},{20... | collective-permute-start | bytes 196616 | tf_op jit(solution)/shard_map/ppermute | solution.py:159
  21.8 0.0 collective-permute-done.16.refs_18_
  21.8 0.1 collective-permute-start.6
  21.9 0.0 collective-permute-done.9.refs_11_
  21.9 1.5 %collective-permute-start.12 = (bf16[16,2048]{1,0:T(8,128)(2,1)S(1)}, bf16[16,2048]{1,0:T(8,128)(2,1)S(1)}, u32[]{:S(2)}, u32[]{:S(2)}) collective-permute-start(bf16[16,2048]{1,0:T(8,128)(2,1)S(1)} %collective-permute-done.2.refs_6_), channel_id=1, source_target_pairs={{0,16},{16,0},{1,17},{17,1},{2,18},{18,2},{3,19},{19,3},{4,20},{20... | collective-permute-start | bytes 196616 | tf_op jit(solution)/shard_map/ppermute | solution.py:159
  23.4 2.5 %collective-permute-done.14.refs_16_ = bf16[16,4096]{1,0:T(8,128)(2,1)S(1)} collective-permute-done((bf16[16,4096]{1,0:T(8,128)(2,1)S(1)}, bf16[16,4096]{1,0:T(8,128)(2,1)S(1)}, u32[]{:S(2)}, u32[]{:S(2)}) %collective-permute-start.14) | collective-permute-done | bytes 131104 | tf_op jit(solution)/shard_map/ppermute | solution.py:159
  25.9 0.0 collective-permute-start.17
  25.9 0.0 collective-permute-done.8.refs_9_
  25.9 0.5 %collective-permute-start.15 = (bf16[16,4096]{1,0:T(8,128)(2,1)S(1)}, bf16[16,4096]{1,0:T(8,128)(2,1)S(1)}, u32[]{:S(2)}, u32[]{:S(2)}) collective-permute-start(bf16[16,4096]{1,0:T(8,128)(2,1)S(1)} %collective-permute-done.14.refs_16_), channel_id=1, source_target_pairs={{0,2},{2,0},{4,6},{6,4},{8,10},{10,8},{12,14},{14,12},{1,3},{3,1},... | collective-permute-start | bytes 393224 | tf_op jit(solution)/shard_map/ppermute | solution.py:155
  26.4 0.9 %collective-permute-done.10.refs_12_ = bf16[16,2048]{1,0:T(8,128)(2,1)S(1)} collective-permute-done((bf16[16,2048]{1,0:T(8,128)(2,1)S(1)}, bf16[16,2048]{1,0:T(8,128)(2,1)S(1)}, u32[]{:S(2)}, u32[]{:S(2)}) %collective-permute-start.10) | collective-permute-done | bytes 65568 | tf_op jit(solution)/shard_map/ppermute | solution.py:159
  27.3 0.0 collective-permute-start.7
  27.3 0.0 collective-permute-done.6.refs_5_
  27.3 0.5 %collective-permute-start.11 = (bf16[16,2048]{1,0:T(8,128)(2,1)S(1)}, bf16[16,2048]{1,0:T(8,128)(2,1)S(1)}, u32[]{:S(2)}, u32[]{:S(2)}) collective-permute-start(bf16[16,2048]{1,0:T(8,128)(2,1)S(1)} %collective-permute-done.10.refs_12_), channel_id=1, source_target_pairs={{0,2},{2,0},{4,6},{6,4},{8,10},{10,8},{12,14},{14,12},{1,3},{3,1},... | collective-permute-start | bytes 196616 | tf_op jit(solution)/shard_map/ppermute | solution.py:155
  27.8 0.4 %collective-permute-done.12.refs_14_ = bf16[16,2048]{1,0:T(8,128)(2,1)S(1)} collective-permute-done((bf16[16,2048]{1,0:T(8,128)(2,1)S(1)}, bf16[16,2048]{1,0:T(8,128)(2,1)S(1)}, u32[]{:S(2)}, u32[]{:S(2)}) %collective-permute-start.12) | collective-permute-done | bytes 65568 | tf_op jit(solution)/shard_map/ppermute | solution.py:159
  28.2 0.0 collective-permute-start.13
  28.2 0.3 collective-permute-done.7.refs_7_
  28.6 0.2 collective-permute-done.11.refs_13_
  28.7 0.8 %collective-permute-done.13.refs_15_ = bf16[16,2048]{1,0:T(8,128)(2,1)S(1)} collective-permute-done((bf16[16,2048]{1,0:T(8,128)(2,1)S(1)}, bf16[16,2048]{1,0:T(8,128)(2,1)S(1)}, u32[]{:S(2)}, u32[]{:S(2)}) %collective-permute-start.13) | collective-permute-done | bytes 65568 | tf_op jit(solution)/shard_map/ppermute | solution.py:155
  29.5 0.0 collective-permute-done.17.refs_19_
  29.5 0.0 collective-permute-done.15.refs_17_
  29.5 0.0 copy-start.1
  29.5 2.2 %copy-done.1 = bf16[256,2,4096]{2,1,0:T(2,128)(2,1)S(1)} copy-done((bf16[256,2,4096]{2,1,0:T(2,128)(2,1)S(1)}, bf16[256,2,4096]{2,1,0:T(2,128)(2,1)}, u32[]{:S(2)}) %copy-start.1) | copy-done | bytes 4194328
  31.7 0.0 copy-start.2
  31.7 1.0 %scores_sent.1 = (f32[128,128]{1,0:T(8,128)S(1)}, bf16[2,128,4096]{2,1,0:T(8,128)(2,1)S(1)}) custom-call(bf16[256,2,4096]{2,1,0:T(2,128)(2,1)S(1)} %copy-done.1, bf16[16,4096]{1,0:T(8,128)(2,1)S(1)} %condition_mine.1.refs_0_, bf16[16,4096]{1,0:T(8,128)(2,1)S(1)} %collective-permute-done.refs_1_, bf16[16,4096]{1,0:T(8,128)(2,1)S(1)} %get-tuple-element.15.refs_2_, ...), custom_call_target="tpu_custom_call" | custom-call | flops 536870912 | bytes 4194304 | tf_op jit(solution)/shard_map/scores_sent/pallas_call | solution.py:219
  32.7 1.6 %collective-permute-start.18 = (f32[128,128]{1,0:T(8,128)S(1)}, f32[128,128]{1,0:T(8,128)S(1)}, u32[]{:S(2)}, u32[]{:S(2)}) collective-permute-start(f32[128,128]{1,0:T(8,128)S(1)} %get-tuple-element.20), channel_id=1, source_target_pairs={{0,1},{1,0},{2,3},{3,2},{4,5},{5,4},{6,7},{7,6},{8,9},{9,8},{10,11... | collective-permute-start | bytes 196616 | tf_op jit(solution)/shard_map/ppermute | solution.py:266
  34.3 0.0 copy-done.2
  34.3 0.8 %scores_kept.1 = f32[128,128]{1,0:T(8,128)S(1)} custom-call(bf16[256,2,4096]{2,1,0:T(2,128)(2,1)S(1)} %copy-done.2, bf16[2,128,4096]{2,1,0:T(8,128)(2,1)S(1)} %get-tuple-element.19.table), custom_call_target="tpu_custom_call" | custom-call | flops 536870912 | bytes 4194304 | tf_op jit(solution)/shard_map/scores_kept/pallas_call | solution.py:219
  35.1 1.9 %collective-permute-done.18 = f32[128,128]{1,0:T(8,128)S(1)} collective-permute-done((f32[128,128]{1,0:T(8,128)S(1)}, f32[128,128]{1,0:T(8,128)S(1)}, u32[]{:S(2)}, u32[]{:S(2)}) %collective-permute-start.18) | collective-permute-done | bytes 65568 | tf_op jit(solution)/shard_map/ppermute | solution.py:266
  37.0 0.6 %add.4 = f32[128,128]{1,0:T(8,128)} add(f32[128,128]{1,0:T(8,128)S(1)} %scores_kept.1, f32[128,128]{1,0:T(8,128)S(1)} %collective-permute-done.18) | non-fusion elementwise | flops 16384 | bytes 196608 | tf_op jit(solution)/shard_map/add | solution.py:268
  (2 shorter events, 0.0 us)
Async XLA Ops:
  1.8 11.1 %collective-permute-start.4 = (bf16[16,4096]{1,0:T(8,128)(2,1)S(1)}, bf16[16,4096]{1,0:T(8,128)(2,1)S(1)}, u32[]{:S(2)}, u32[]{:S(2)}) collective-permute-start(bf16[16,4096]{1,0:T(8,128)(2,1)S(1)} %condition_mine.1.refs_0_), channel_id=1, source_target_pairs={{12,0},{14,2},{0,4},{2,6},{4,8},{6,10},{8,12},{10,14},{13,1},{15,3... | collective-permute-start | bytes 393224 | tf_op jit(solution)/shard_map/ppermute | solution.py:144
  4.9 8.0 %collective-permute-start.3 = (bf16[16,4096]{1,0:T(8,128)(2,1)S(1)}, bf16[16,4096]{1,0:T(8,128)(2,1)S(1)}, u32[]{:S(2)}, u32[]{:S(2)}) collective-permute-start(bf16[16,4096]{1,0:T(8,128)(2,1)S(1)} %condition_mine.1.refs_0_), channel_id=1, source_target_pairs={{4,0},{6,2},{8,4},{10,6},{12,8},{14,10},{0,12},{2,14},{5,1},{7,3},... | collective-permute-start | bytes 393224 | tf_op jit(solution)/shard_map/ppermute | solution.py:144
  6.9 12.7 %collective-permute-start = (bf16[16,4096]{1,0:T(8,128)(2,1)S(1)}, bf16[16,4096]{1,0:T(8,128)(2,1)S(1)}, u32[]{:S(2)}, u32[]{:S(2)}) collective-permute-start(bf16[16,4096]{1,0:T(8,128)(2,1)S(1)} %condition_mine.1.refs_0_), channel_id=1, source_target_pairs={{0,2},{2,0},{4,6},{6,4},{8,10},{10,8},{12,14},{14,12},{1,3},{3,1},... | collective-permute-start | bytes 393224 | tf_op jit(solution)/shard_map/ppermute | solution.py:155
  10.0 1.9 %copy-start = (bf16[256,2,4096]{2,1,0:T(2,128)(2,1)}, bf16[256,2,4096]{2,1,0:T(2,128)(2,1)S(1)}, u32[]{:S(2)}) copy-start(bf16[256,2,4096]{2,1,0:T(2,128)(2,1)S(1)} %get-tuple-element.13.train) | copy-start | bytes 12582916
  11.9 7.6 %collective-permute-start.2 = (bf16[16,2048]{1,0:T(8,128)(2,1)S(1)}, bf16[16,2048]{1,0:T(8,128)(2,1)S(1)}, u32[]{:S(2)}, u32[]{:S(2)}) collective-permute-start(bf16[16,2048]{1,0:T(8,128)(2,1)S(1)} %slice.12), channel_id=1, source_target_pairs={{8,0},{10,2},{12,4},{14,6},{0,8},{2,10},{4,12},{6,14},{9,1},{11,3}... | collective-permute-start | bytes 196616 | tf_op jit(solution)/shard_map/ppermute | solution.py:144
  12.9 8.2 %collective-permute-start.5 = (bf16[16,2048]{1,0:T(8,128)(2,1)S(1)}, bf16[16,2048]{1,0:T(8,128)(2,1)S(1)}, u32[]{:S(2)}, u32[]{:S(2)}) collective-permute-start(bf16[16,2048]{1,0:T(8,128)(2,1)S(1)} %fusion), channel_id=1, source_target_pairs={{0,8},{2,10},{8,12},{10,14},{12,4},{14,6},{4,0},{6,2},{1,9},{3,11}... | collective-permute-start | bytes 196616 | tf_op jit(solution)/shard_map/ppermute | solution.py:151
  14.9 6.3 %collective-permute-start.1 = (bf16[16,4096]{1,0:T(8,128)(2,1)S(1)}, bf16[16,4096]{1,0:T(8,128)(2,1)S(1)}, u32[]{:S(2)}, u32[]{:S(2)}) collective-permute-start(bf16[16,4096]{1,0:T(8,128)(2,1)S(1)} %get-tuple-element.15.refs_2_), channel_id=1, source_target_pairs={{0,2},{2,0},{4,6},{6,4},{8,10},{10,8},{12,14},{14,12},{1,3},{3,1},... | collective-permute-start | bytes 393224 | tf_op jit(solution)/shard_map/ppermute | solution.py:155
  14.9 6.9 %collective-permute-start.16 = (bf16[16,4096]{1,0:T(8,128)(2,1)S(1)}, bf16[16,4096]{1,0:T(8,128)(2,1)S(1)}, u32[]{:S(2)}, u32[]{:S(2)}) collective-permute-start(bf16[16,4096]{1,0:T(8,128)(2,1)S(1)} %collective-permute-done.4.refs_10_), channel_id=1, source_target_pairs={{0,16},{16,0},{1,17},{17,1},{2,18},{18,2},{3,19},{19,3},{4,20},{20... | collective-permute-start | bytes 393224 | tf_op jit(solution)/shard_map/ppermute | solution.py:159
  19.5 2.3 %collective-permute-start.9 = (bf16[16,4096]{1,0:T(8,128)(2,1)S(1)}, bf16[16,4096]{1,0:T(8,128)(2,1)S(1)}, u32[]{:S(2)}, u32[]{:S(2)}) collective-permute-start(bf16[16,4096]{1,0:T(8,128)(2,1)S(1)} %collective-permute-done.4.refs_10_), channel_id=1, source_target_pairs={{0,2},{2,0},{4,6},{6,4},{8,10},{10,8},{12,14},{14,12},{1,3},{3,1},... | collective-permute-start | bytes 393224 | tf_op jit(solution)/shard_map/ppermute | solution.py:155
  19.6 6.3 %collective-permute-start.14 = (bf16[16,4096]{1,0:T(8,128)(2,1)S(1)}, bf16[16,4096]{1,0:T(8,128)(2,1)S(1)}, u32[]{:S(2)}, u32[]{:S(2)}) collective-permute-start(bf16[16,4096]{1,0:T(8,128)(2,1)S(1)} %collective-permute-done.3.refs_8_), channel_id=1, source_target_pairs={{0,16},{16,0},{1,17},{17,1},{2,18},{18,2},{3,19},{19,3},{4,20},{20... | collective-permute-start | bytes 393224 | tf_op jit(solution)/shard_map/ppermute | solution.py:159
  21.1 4.8 %collective-permute-start.8 = (bf16[16,4096]{1,0:T(8,128)(2,1)S(1)}, bf16[16,4096]{1,0:T(8,128)(2,1)S(1)}, u32[]{:S(2)}, u32[]{:S(2)}) collective-permute-start(bf16[16,4096]{1,0:T(8,128)(2,1)S(1)} %collective-permute-done.3.refs_8_), channel_id=1, source_target_pairs={{0,2},{2,0},{4,6},{6,4},{8,10},{10,8},{12,14},{14,12},{1,3},{3,1},... | collective-permute-start | bytes 393224 | tf_op jit(solution)/shard_map/ppermute | solution.py:155
  21.3 6.0 %collective-permute-start.10 = (bf16[16,2048]{1,0:T(8,128)(2,1)S(1)}, bf16[16,2048]{1,0:T(8,128)(2,1)S(1)}, u32[]{:S(2)}, u32[]{:S(2)}) collective-permute-start(bf16[16,2048]{1,0:T(8,128)(2,1)S(1)} %collective-permute-done.5.refs_4_), channel_id=1, source_target_pairs={{0,16},{16,0},{1,17},{17,1},{2,18},{18,2},{3,19},{19,3},{4,20},{20... | collective-permute-start | bytes 196616 | tf_op jit(solution)/shard_map/ppermute | solution.py:159
  21.8 5.5 %collective-permute-start.6 = (bf16[16,2048]{1,0:T(8,128)(2,1)S(1)}, bf16[16,2048]{1,0:T(8,128)(2,1)S(1)}, u32[]{:S(2)}, u32[]{:S(2)}) collective-permute-start(bf16[16,2048]{1,0:T(8,128)(2,1)S(1)} %collective-permute-done.5.refs_4_), channel_id=1, source_target_pairs={{0,2},{2,0},{4,6},{6,4},{8,10},{10,8},{12,14},{14,12},{1,3},{3,1},... | collective-permute-start | bytes 196616 | tf_op jit(solution)/shard_map/ppermute | solution.py:155
  21.9 6.4 %collective-permute-start.12 = (bf16[16,2048]{1,0:T(8,128)(2,1)S(1)}, bf16[16,2048]{1,0:T(8,128)(2,1)S(1)}, u32[]{:S(2)}, u32[]{:S(2)}) collective-permute-start(bf16[16,2048]{1,0:T(8,128)(2,1)S(1)} %collective-permute-done.2.refs_6_), channel_id=1, source_target_pairs={{0,16},{16,0},{1,17},{17,1},{2,18},{18,2},{3,19},{19,3},{4,20},{20... | collective-permute-start | bytes 196616 | tf_op jit(solution)/shard_map/ppermute | solution.py:159
  25.9 3.6 %collective-permute-start.17 = (bf16[16,4096]{1,0:T(8,128)(2,1)S(1)}, bf16[16,4096]{1,0:T(8,128)(2,1)S(1)}, u32[]{:S(2)}, u32[]{:S(2)}) collective-permute-start(bf16[16,4096]{1,0:T(8,128)(2,1)S(1)} %collective-permute-done.16.refs_18_), channel_id=1, source_target_pairs={{0,2},{2,0},{4,6},{6,4},{8,10},{10,8},{12,14},{14,12},{1,3},{3,1},... | collective-permute-start | bytes 393224 | tf_op jit(solution)/shard_map/ppermute | solution.py:155
  25.9 3.6 %collective-permute-start.15 = (bf16[16,4096]{1,0:T(8,128)(2,1)S(1)}, bf16[16,4096]{1,0:T(8,128)(2,1)S(1)}, u32[]{:S(2)}, u32[]{:S(2)}) collective-permute-start(bf16[16,4096]{1,0:T(8,128)(2,1)S(1)} %collective-permute-done.14.refs_16_), channel_id=1, source_target_pairs={{0,2},{2,0},{4,6},{6,4},{8,10},{10,8},{12,14},{14,12},{1,3},{3,1},... | collective-permute-start | bytes 393224 | tf_op jit(solution)/shard_map/ppermute | solution.py:155
  27.3 1.3 %collective-permute-start.7 = (bf16[16,2048]{1,0:T(8,128)(2,1)S(1)}, bf16[16,2048]{1,0:T(8,128)(2,1)S(1)}, u32[]{:S(2)}, u32[]{:S(2)}) collective-permute-start(bf16[16,2048]{1,0:T(8,128)(2,1)S(1)} %collective-permute-done.2.refs_6_), channel_id=1, source_target_pairs={{0,2},{2,0},{4,6},{6,4},{8,10},{10,8},{12,14},{14,12},{1,3},{3,1},... | collective-permute-start | bytes 196616 | tf_op jit(solution)/shard_map/ppermute | solution.py:155
  27.3 1.4 %collective-permute-start.11 = (bf16[16,2048]{1,0:T(8,128)(2,1)S(1)}, bf16[16,2048]{1,0:T(8,128)(2,1)S(1)}, u32[]{:S(2)}, u32[]{:S(2)}) collective-permute-start(bf16[16,2048]{1,0:T(8,128)(2,1)S(1)} %collective-permute-done.10.refs_12_), channel_id=1, source_target_pairs={{0,2},{2,0},{4,6},{6,4},{8,10},{10,8},{12,14},{14,12},{1,3},{3,1},... | collective-permute-start | bytes 196616 | tf_op jit(solution)/shard_map/ppermute | solution.py:155
  28.2 1.3 %collective-permute-start.13 = (bf16[16,2048]{1,0:T(8,128)(2,1)S(1)}, bf16[16,2048]{1,0:T(8,128)(2,1)S(1)}, u32[]{:S(2)}, u32[]{:S(2)}) collective-permute-start(bf16[16,2048]{1,0:T(8,128)(2,1)S(1)} %collective-permute-done.12.refs_14_), channel_id=1, source_target_pairs={{0,2},{2,0},{4,6},{6,4},{8,10},{10,8},{12,14},{14,12},{1,3},{3,1},... | collective-permute-start | bytes 196616 | tf_op jit(solution)/shard_map/ppermute | solution.py:155
  29.5 2.2 %copy-start.1 = (bf16[256,2,4096]{2,1,0:T(2,128)(2,1)S(1)}, bf16[256,2,4096]{2,1,0:T(2,128)(2,1)}, u32[]{:S(2)}) copy-start(bf16[256,2,4096]{2,1,0:T(2,128)(2,1)} %copy-done) | copy-start | bytes 12582916
  31.7 2.6 %copy-start.2 = (bf16[256,2,4096]{2,1,0:T(2,128)(2,1)S(1)}, bf16[256,2,4096]{2,1,0:T(2,128)(2,1)}, u32[]{:S(2)}) copy-start(bf16[256,2,4096]{2,1,0:T(2,128)(2,1)} %copy-done) | copy-start | bytes 12582916
  32.7 4.3 %collective-permute-start.18 = (f32[128,128]{1,0:T(8,128)S(1)}, f32[128,128]{1,0:T(8,128)S(1)}, u32[]{:S(2)}, u32[]{:S(2)}) collective-permute-start(f32[128,128]{1,0:T(8,128)S(1)} %get-tuple-element.20), channel_id=1, source_target_pairs={{0,1},{1,0},{2,3},{3,2},{4,5},{5,4},{6,7},{7,6},{8,9},{9,8},{10,11... | collective-permute-start | bytes 196616 | tf_op jit(solution)/shard_map/ppermute | solution.py:266

commit v9 on v7

--- a/solution.py
+++ b/solution.py
@@ -133,6 +133,13 @@
     return lax.ppermute(value, "train", pairs)
 
 
+def relay(value):
+    pairs = [
+        (a * PAIR + c, b * PAIR + c) for a, b in ((0, 2), (2, 3), (3, 1), (1, 0)) for c in range(PAIR)
+    ]
+    return lax.ppermute(value, "train", pairs)
+
+
 def other_core(value):
     return lax.ppermute(value, "train", [(k, k ^ 1) for k in range(COLUMNS * PAIR)])
 
@@ -226,13 +233,14 @@
     mine = condition_layer(False, queries, left_factor, right_factor)
     other = condition_layer(True, queries, left_factor, right_factor)
     near = copy_near(train_grads)
-    mine_late, other = lax.optimization_barrier((mine, other))
-    s2 = along_columns(mine_late, 2)
+    column, _ = place()
     s1 = along_columns(mine, 1)
     s3 = along_columns(mine, 3)
-    y2 = other_part(s2)
+    s3, other = lax.optimization_barrier((s3, other))
+    s2 = relay(jnp.where(column == 1, s1, jnp.where(column == 2, s3, mine)))
     y1 = other_part(s1)
     y3 = other_part(s3)
+    y2 = other_part(s2)
     y1, y3, near = lax.optimization_barrier((y1, y3, near))
 
     blocks = []

time: 32 us -> 30.9 us (0.966)
  waiting for transfers between devices: 9.23 us -> 7.89 us
    ppermute x3 -> x2, waiting for transfers between devices: 5.62 us -> 2.49 us  [along_columns(): return lax.ppermute(value, 'train', pairs)]
    ppermute x0 -> x1, starting transfers between devices: none -> 2.51 us  [relay(): return lax.ppermute(value, 'train', pairs)]
    ppermute x0 -> x1, waiting for transfers between devices: none -> 1.05 us  [relay(): return lax.ppermute(value, 'train', pairs)]
    ppermute x3, starting transfers between devices: 4.45 us -> 3.43 us  [other_part(): return lax.ppermute(value, 'parts', [(0, 1), (1, 0)])]
    ppermute x3 -> x2, starting transfers between devices: 6.18 us -> 5.17 us  [along_columns(): return lax.ppermute(value, 'train', pairs)]
    ppermute x3, waiting for transfers between devices: 0.59 us -> 1.3 us  [other_part(): return lax.ppermute(value, 'parts', [(0, 1), (1, 0)])]
    ppermute x8, starting transfers between devices: 2.11 us -> 1.6 us  [other_core(): lax.ppermute(value, 'train', [(k, k ^ 1) for k in range(COLUMNS * PAIR)])]
  transfers between devices with their start and end apart: 15 -> 15, of which waited for: 6 -> 7; matrix products, arithmetic and copies ran while one was open for 0% -> 0% of each run, Pallas kernels for 15% -> 16%
where the time goes in v9:
time: 30.9 us; the launch traced here: 30.7 us
  starting transfers between devices  14.5 us (47%)
  waiting for transfers between devices  7.89 us (26%)
  Pallas kernels  7.57 us (24%)
  other arithmetic  0.66 us (2%)
    ppermute x2, starting transfers between devices, along_columns(): return lax.ppermute(value, 'train', pairs)  5.17 us
    pallas_call x2, Pallas kernels, condition_layer(): pl.pallas_call(functools.partial(condition_kernel, other), out_shape=jax....  3.53 us
    ppermute x3, starting transfers between devices, other_part(): return lax.ppermute(value, 'parts', [(0, 1), (1, 0)])  3.43 us
    ppermute x1, starting transfers between devices, relay(): return lax.ppermute(value, 'train', pairs)  2.51 us
    ppermute x2, waiting for transfers between devices, along_columns(): return lax.ppermute(value, 'train', pairs)  2.49 us
    pallas_call x1, Pallas kernels, copy_near(): pl.pallas_call(copy_kernel, out_shape=jax.ShapeDtypeStruct(value.shape, v...  2.2 us
    pallas_call x2, Pallas kernels, local_call(): pl.pallas_call(kernel, out_shape=out_shape, in_specs=[spec] * len(operand...  1.84 us
    ppermute x1, starting transfers between devices, direct(): received = lax.ppermute(sent, 'layer', [(0, 1), (1, 0)])  1.78 us
  transfers between devices with their start and end apart: 15, of which 7 were waited for; matrix products, arithmetic and copies ran while one was open for 0% of the time, Pallas kernels for 16%

profile of v9, /device:TPU:0, one launch (start us, length us, event | category | flops | bytes accessed | tf_op | source)
XLA Modules:
  0.0 30.7 jit_solution(1411010366137766677)
XLA Ops:
  0.0 1.8 %condition_mine.1.refs_0_ = bf16[16,4096]{1,0:T(8,128)(2,1)S(1)} custom-call(bf16[2,1,16,4096]{3,2,1,0:T(8,128)(2,1)} %queries.3, f32[2,64,64]{2,1,0:T(8,128)} %left.3, f32[2,64,64]{2,1,0:T(8,128)} %right.3), custom_call_target="tpu_custom_call" | custom-call | flops 134217728 | bytes 524288 | tf_op jit(solution)/shard_map/condition_mine/pallas_call | solution.py:107
  1.8 3.1 %collective-permute-start.2 = (bf16[16,4096]{1,0:T(8,128)(2,1)S(1)}, bf16[16,4096]{1,0:T(8,128)(2,1)S(1)}, u32[]{:S(2)}, u32[]{:S(2)}) collective-permute-start(bf16[16,4096]{1,0:T(8,128)(2,1)S(1)} %condition_mine.1.refs_0_), channel_id=1, source_target_pairs={{12,0},{14,2},{0,4},{2,6},{4,8},{6,10},{8,12},{10,14},{13,1},{15,3... | collective-permute-start | bytes 393224 | tf_op jit(solution)/shard_map/ppermute | solution.py:133
  4.9 2.1 %collective-permute-start = (bf16[16,4096]{1,0:T(8,128)(2,1)S(1)}, bf16[16,4096]{1,0:T(8,128)(2,1)S(1)}, u32[]{:S(2)}, u32[]{:S(2)}) collective-permute-start(bf16[16,4096]{1,0:T(8,128)(2,1)S(1)} %condition_mine.1.refs_0_), channel_id=1, source_target_pairs={{4,0},{6,2},{8,4},{10,6},{12,8},{14,10},{0,12},{2,14},{5,1},{7,3},... | collective-permute-start | bytes 393224 | tf_op jit(solution)/shard_map/ppermute | solution.py:133
  6.9 1.8 %condition_other.1.refs_2_ = bf16[16,4096]{1,0:T(8,128)(2,1)S(1)} custom-call(bf16[2,1,16,4096]{3,2,1,0:T(8,128)(2,1)} %queries.3, f32[2,64,64]{2,1,0:T(8,128)} %left.3, f32[2,64,64]{2,1,0:T(8,128)} %right.3), custom_call_target="tpu_custom_call" | custom-call | flops 134217728 | bytes 524288 | tf_op jit(solution)/shard_map/condition_other/pallas_call | solution.py:107
  8.7 2.5 %collective-permute-done.2.refs_8_ = bf16[16,4096]{1,0:T(8,128)(2,1)S(1)} collective-permute-done((bf16[16,4096]{1,0:T(8,128)(2,1)S(1)}, bf16[16,4096]{1,0:T(8,128)(2,1)S(1)}, u32[]{:S(2)}, u32[]{:S(2)}) %collective-permute-start.2) | collective-permute-done | bytes 131104 | tf_op jit(solution)/shard_map/ppermute | solution.py:133
  11.2 1.8 %collective-permute-start.3 = (bf16[16,4096]{1,0:T(8,128)(2,1)S(1)}, bf16[16,4096]{1,0:T(8,128)(2,1)S(1)}, u32[]{:S(2)}, u32[]{:S(2)}) collective-permute-start(bf16[16,4096]{1,0:T(8,128)(2,1)S(1)} %collective-permute-done.2.refs_8_), channel_id=1, source_target_pairs={{0,16},{16,0},{1,17},{17,1},{2,18},{18,2},{3,19},{19,3},{4,20},{20... | collective-permute-start | bytes 393224 | tf_op jit(solution)/shard_map/ppermute | solution.py:148
  13.0 0.0 collective-permute-done.refs_6_
  13.0 2.5 %collective-permute-start.6 = (bf16[16,4096]{1,0:T(8,128)(2,1)S(1)}, bf16[16,4096]{1,0:T(8,128)(2,1)S(1)}, u32[]{:S(2)}, u32[]{:S(2)}) collective-permute-start(bf16[16,4096]{1,0:T(8,128)(2,1)S(1)} %select_select_fusion), channel_id=1, source_target_pairs={{0,8},{2,10},{8,12},{10,14},{12,4},{14,6},{4,0},{6,2},{1,9},{3,11}... | collective-permute-start | bytes 393224 | tf_op jit(solution)/shard_map/ppermute | solution.py:140
  15.5 0.5 %collective-permute-start.1 = (bf16[16,4096]{1,0:T(8,128)(2,1)S(1)}, bf16[16,4096]{1,0:T(8,128)(2,1)S(1)}, u32[]{:S(2)}, u32[]{:S(2)}) collective-permute-start(bf16[16,4096]{1,0:T(8,128)(2,1)S(1)} %collective-permute-done.refs_6_), channel_id=1, source_target_pairs={{0,16},{16,0},{1,17},{17,1},{2,18},{18,2},{3,19},{19,3},{4,20},{20... | collective-permute-start | bytes 393224 | tf_op jit(solution)/shard_map/ppermute | solution.py:148
  16.0 0.0 collective-permute-start.4
  16.0 0.5 %collective-permute-start.5 = (bf16[16,4096]{1,0:T(8,128)(2,1)S(1)}, bf16[16,4096]{1,0:T(8,128)(2,1)S(1)}, u32[]{:S(2)}, u32[]{:S(2)}) collective-permute-start(bf16[16,4096]{1,0:T(8,128)(2,1)S(1)} %condition_other.1.refs_2_), channel_id=1, source_target_pairs={{0,2},{2,0},{4,6},{6,4},{8,10},{10,8},{12,14},{14,12},{1,3},{3,1},... | collective-permute-start | bytes 393224 | tf_op jit(solution)/shard_map/ppermute | solution.py:144
  16.5 0.4 %collective-permute-done.3.refs_14_ = bf16[16,4096]{1,0:T(8,128)(2,1)S(1)} collective-permute-done((bf16[16,4096]{1,0:T(8,128)(2,1)S(1)}, bf16[16,4096]{1,0:T(8,128)(2,1)S(1)}, u32[]{:S(2)}, u32[]{:S(2)}) %collective-permute-start.3) | collective-permute-done | bytes 131104 | tf_op jit(solution)/shard_map/ppermute | solution.py:148
  17.0 0.0 collective-permute-start.9
  17.0 1.1 %collective-permute-done.6.refs_4_ = bf16[16,4096]{1,0:T(8,128)(2,1)S(1)} collective-permute-done((bf16[16,4096]{1,0:T(8,128)(2,1)S(1)}, bf16[16,4096]{1,0:T(8,128)(2,1)S(1)}, u32[]{:S(2)}, u32[]{:S(2)}) %collective-permute-start.6) | collective-permute-done | bytes 131104 | tf_op jit(solution)/shard_map/ppermute | solution.py:140
  18.0 1.2 %collective-permute-start.10 = (bf16[16,4096]{1,0:T(8,128)(2,1)S(1)}, bf16[16,4096]{1,0:T(8,128)(2,1)S(1)}, u32[]{:S(2)}, u32[]{:S(2)}) collective-permute-start(bf16[16,4096]{1,0:T(8,128)(2,1)S(1)} %collective-permute-done.6.refs_4_), channel_id=1, source_target_pairs={{0,16},{16,0},{1,17},{17,1},{2,18},{18,2},{3,19},{19,3},{4,20},{20... | collective-permute-start | bytes 393224 | tf_op jit(solution)/shard_map/ppermute | solution.py:148
  19.2 2.2 %near.1.train = bf16[256,2,4096]{2,1,0:T(2,128)(2,1)S(1)} custom-call(bf16[256,2,4096]{2,1,0:T(2,128)(2,1)} %source.1), custom_call_target="tpu_custom_call" | custom-call | bytes 8388608 | tf_op jit(solution)/shard_map/near/pallas_call | solution.py:158
  21.4 0.0 collective-permute-done.1.refs_12_
  21.4 0.3 collective-permute-start.8
  21.7 0.0 collective-permute-done.4.refs_1_
  21.7 0.3 collective-permute-start.12
  22.0 0.0 collective-permute-done.5.refs_3_
  22.0 0.2 collective-permute-start.7
  22.2 0.0 collective-permute-done.9.refs_9_
  22.2 0.3 collective-permute-start.13
  22.5 0.9 %collective-permute-done.10.refs_10_ = bf16[16,4096]{1,0:T(8,128)(2,1)S(1)} collective-permute-done((bf16[16,4096]{1,0:T(8,128)(2,1)S(1)}, bf16[16,4096]{1,0:T(8,128)(2,1)S(1)}, u32[]{:S(2)}, u32[]{:S(2)}) %collective-permute-start.10) | collective-permute-done | bytes 131104 | tf_op jit(solution)/shard_map/ppermute | solution.py:148
  23.4 0.0 collective-permute-start.11
  23.4 0.0 collective-permute-done.8.refs_7_
  23.4 0.0 collective-permute-done.7.refs_5_
  23.4 0.0 collective-permute-done.12.refs_13_
  23.4 0.2 collective-permute-done.13.refs_15_
  23.6 1.1 %collective-permute-done.11.refs_11_ = bf16[16,4096]{1,0:T(8,128)(2,1)S(1)} collective-permute-done((bf16[16,4096]{1,0:T(8,128)(2,1)S(1)}, bf16[16,4096]{1,0:T(8,128)(2,1)S(1)}, u32[]{:S(2)}, u32[]{:S(2)}) %collective-permute-start.11) | collective-permute-done | bytes 131104 | tf_op jit(solution)/shard_map/ppermute | solution.py:144
  24.7 1.0 %scores_sent.1 = (f32[128,128]{1,0:T(8,128)S(1)}, bf16[2,128,4096]{2,1,0:T(8,128)(2,1)S(1)}) custom-call(bf16[256,2,4096]{2,1,0:T(2,128)(2,1)S(1)} %near.1.train, bf16[16,4096]{1,0:T(8,128)(2,1)S(1)} %condition_mine.1.refs_0_, bf16[16,4096]{1,0:T(8,128)(2,1)S(1)} %collective-permute-done.4.refs_1_, bf16[16,4096]{1,0:T(8,128)(2,1)S(1)} %condition_other.1.refs_2_, ...), custom_call_target="tpu_custom_call" | custom-call | flops 536870912 | bytes 4194304 | tf_op jit(solution)/shard_map/scores_sent/pallas_call | solution.py:215
  25.7 1.8 %collective-permute-start.14 = (f32[128,128]{1,0:T(8,128)S(1)}, f32[128,128]{1,0:T(8,128)S(1)}, u32[]{:S(2)}, u32[]{:S(2)}) collective-permute-start(f32[128,128]{1,0:T(8,128)S(1)} %get-tuple-element.18), channel_id=1, source_target_pairs={{0,1},{1,0},{2,3},{3,2},{4,5},{5,4},{6,7},{7,6},{8,9},{9,8},{10,11... | collective-permute-start | bytes 196616 | tf_op jit(solution)/shard_map/ppermute | solution.py:259
  27.5 0.8 %scores_kept.1 = f32[128,128]{1,0:T(8,128)S(1)} custom-call(bf16[256,2,4096]{2,1,0:T(2,128)(2,1)S(1)} %near.1.train, bf16[2,128,4096]{2,1,0:T(8,128)(2,1)S(1)} %get-tuple-element.17.table), custom_call_target="tpu_custom_call" | custom-call | flops 536870912 | bytes 4194304 | tf_op jit(solution)/shard_map/scores_kept/pallas_call | solution.py:215
  28.3 1.7 %collective-permute-done.14 = f32[128,128]{1,0:T(8,128)S(1)} collective-permute-done((f32[128,128]{1,0:T(8,128)S(1)}, f32[128,128]{1,0:T(8,128)S(1)}, u32[]{:S(2)}, u32[]{:S(2)}) %collective-permute-start.14) | collective-permute-done | bytes 65568 | tf_op jit(solution)/shard_map/ppermute | solution.py:259
  30.0 0.6 %add.4 = f32[128,128]{1,0:T(8,128)} add(f32[128,128]{1,0:T(8,128)S(1)} %scores_kept.1, f32[128,128]{1,0:T(8,128)S(1)} %collective-permute-done.14) | non-fusion elementwise | flops 16384 | bytes 196608 | tf_op jit(solution)/shard_map/add | solution.py:261
  (1 shorter events, 0.0 us)
Async XLA Ops:
  1.8 9.4 %collective-permute-start.2 = (bf16[16,4096]{1,0:T(8,128)(2,1)S(1)}, bf16[16,4096]{1,0:T(8,128)(2,1)S(1)}, u32[]{:S(2)}, u32[]{:S(2)}) collective-permute-start(bf16[16,4096]{1,0:T(8,128)(2,1)S(1)} %condition_mine.1.refs_0_), channel_id=1, source_target_pairs={{12,0},{14,2},{0,4},{2,6},{4,8},{6,10},{8,12},{10,14},{13,1},{15,3... | collective-permute-start | bytes 393224 | tf_op jit(solution)/shard_map/ppermute | solution.py:133
  4.9 8.1 %collective-permute-start = (bf16[16,4096]{1,0:T(8,128)(2,1)S(1)}, bf16[16,4096]{1,0:T(8,128)(2,1)S(1)}, u32[]{:S(2)}, u32[]{:S(2)}) collective-permute-start(bf16[16,4096]{1,0:T(8,128)(2,1)S(1)} %condition_mine.1.refs_0_), channel_id=1, source_target_pairs={{4,0},{6,2},{8,4},{10,6},{12,8},{14,10},{0,12},{2,14},{5,1},{7,3},... | collective-permute-start | bytes 393224 | tf_op jit(solution)/shard_map/ppermute | solution.py:133
  11.2 5.8 %collective-permute-start.3 = (bf16[16,4096]{1,0:T(8,128)(2,1)S(1)}, bf16[16,4096]{1,0:T(8,128)(2,1)S(1)}, u32[]{:S(2)}, u32[]{:S(2)}) collective-permute-start(bf16[16,4096]{1,0:T(8,128)(2,1)S(1)} %collective-permute-done.2.refs_8_), channel_id=1, source_target_pairs={{0,16},{16,0},{1,17},{17,1},{2,18},{18,2},{3,19},{19,3},{4,20},{20... | collective-permute-start | bytes 393224 | tf_op jit(solution)/shard_map/ppermute | solution.py:148
  13.0 5.0 %collective-permute-start.6 = (bf16[16,4096]{1,0:T(8,128)(2,1)S(1)}, bf16[16,4096]{1,0:T(8,128)(2,1)S(1)}, u32[]{:S(2)}, u32[]{:S(2)}) collective-permute-start(bf16[16,4096]{1,0:T(8,128)(2,1)S(1)} %select_select_fusion), channel_id=1, source_target_pairs={{0,8},{2,10},{8,12},{10,14},{12,4},{14,6},{4,0},{6,2},{1,9},{3,11}... | collective-permute-start | bytes 393224 | tf_op jit(solution)/shard_map/ppermute | solution.py:140
  15.5 5.9 %collective-permute-start.1 = (bf16[16,4096]{1,0:T(8,128)(2,1)S(1)}, bf16[16,4096]{1,0:T(8,128)(2,1)S(1)}, u32[]{:S(2)}, u32[]{:S(2)}) collective-permute-start(bf16[16,4096]{1,0:T(8,128)(2,1)S(1)} %collective-permute-done.refs_6_), channel_id=1, source_target_pairs={{0,16},{16,0},{1,17},{17,1},{2,18},{18,2},{3,19},{19,3},{4,20},{20... | collective-permute-start | bytes 393224 | tf_op jit(solution)/shard_map/ppermute | solution.py:148
  16.0 5.7 %collective-permute-start.4 = (bf16[16,4096]{1,0:T(8,128)(2,1)S(1)}, bf16[16,4096]{1,0:T(8,128)(2,1)S(1)}, u32[]{:S(2)}, u32[]{:S(2)}) collective-permute-start(bf16[16,4096]{1,0:T(8,128)(2,1)S(1)} %condition_mine.1.refs_0_), channel_id=1, source_target_pairs={{0,2},{2,0},{4,6},{6,4},{8,10},{10,8},{12,14},{14,12},{1,3},{3,1},... | collective-permute-start | bytes 393224 | tf_op jit(solution)/shard_map/ppermute | solution.py:144
  16.0 6.0 %collective-permute-start.5 = (bf16[16,4096]{1,0:T(8,128)(2,1)S(1)}, bf16[16,4096]{1,0:T(8,128)(2,1)S(1)}, u32[]{:S(2)}, u32[]{:S(2)}) collective-permute-start(bf16[16,4096]{1,0:T(8,128)(2,1)S(1)} %condition_other.1.refs_2_), channel_id=1, source_target_pairs={{0,2},{2,0},{4,6},{6,4},{8,10},{10,8},{12,14},{14,12},{1,3},{3,1},... | collective-permute-start | bytes 393224 | tf_op jit(solution)/shard_map/ppermute | solution.py:144
  17.0 5.2 %collective-permute-start.9 = (bf16[16,4096]{1,0:T(8,128)(2,1)S(1)}, bf16[16,4096]{1,0:T(8,128)(2,1)S(1)}, u32[]{:S(2)}, u32[]{:S(2)}) collective-permute-start(bf16[16,4096]{1,0:T(8,128)(2,1)S(1)} %collective-permute-done.2.refs_8_), channel_id=1, source_target_pairs={{0,2},{2,0},{4,6},{6,4},{8,10},{10,8},{12,14},{14,12},{1,3},{3,1},... | collective-permute-start | bytes 393224 | tf_op jit(solution)/shard_map/ppermute | solution.py:144
  18.0 5.3 %collective-permute-start.10 = (bf16[16,4096]{1,0:T(8,128)(2,1)S(1)}, bf16[16,4096]{1,0:T(8,128)(2,1)S(1)}, u32[]{:S(2)}, u32[]{:S(2)}) collective-permute-start(bf16[16,4096]{1,0:T(8,128)(2,1)S(1)} %collective-permute-done.6.refs_4_), channel_id=1, source_target_pairs={{0,16},{16,0},{1,17},{17,1},{2,18},{18,2},{3,19},{19,3},{4,20},{20... | collective-permute-start | bytes 393224 | tf_op jit(solution)/shard_map/ppermute | solution.py:148
  21.4 2.0 %collective-permute-start.8 = (bf16[16,4096]{1,0:T(8,128)(2,1)S(1)}, bf16[16,4096]{1,0:T(8,128)(2,1)S(1)}, u32[]{:S(2)}, u32[]{:S(2)}) collective-permute-start(bf16[16,4096]{1,0:T(8,128)(2,1)S(1)} %collective-permute-done.refs_6_), channel_id=1, source_target_pairs={{0,2},{2,0},{4,6},{6,4},{8,10},{10,8},{12,14},{14,12},{1,3},{3,1},... | collective-permute-start | bytes 393224 | tf_op jit(solution)/shard_map/ppermute | solution.py:144
  21.7 1.7 %collective-permute-start.12 = (bf16[16,4096]{1,0:T(8,128)(2,1)S(1)}, bf16[16,4096]{1,0:T(8,128)(2,1)S(1)}, u32[]{:S(2)}, u32[]{:S(2)}) collective-permute-start(bf16[16,4096]{1,0:T(8,128)(2,1)S(1)} %collective-permute-done.1.refs_12_), channel_id=1, source_target_pairs={{0,2},{2,0},{4,6},{6,4},{8,10},{10,8},{12,14},{14,12},{1,3},{3,1},... | collective-permute-start | bytes 393224 | tf_op jit(solution)/shard_map/ppermute | solution.py:144
  22.0 1.4 %collective-permute-start.7 = (bf16[16,4096]{1,0:T(8,128)(2,1)S(1)}, bf16[16,4096]{1,0:T(8,128)(2,1)S(1)}, u32[]{:S(2)}, u32[]{:S(2)}) collective-permute-start(bf16[16,4096]{1,0:T(8,128)(2,1)S(1)} %collective-permute-done.6.refs_4_), channel_id=1, source_target_pairs={{0,2},{2,0},{4,6},{6,4},{8,10},{10,8},{12,14},{14,12},{1,3},{3,1},... | collective-permute-start | bytes 393224 | tf_op jit(solution)/shard_map/ppermute | solution.py:144
  22.2 1.3 %collective-permute-start.13 = (bf16[16,4096]{1,0:T(8,128)(2,1)S(1)}, bf16[16,4096]{1,0:T(8,128)(2,1)S(1)}, u32[]{:S(2)}, u32[]{:S(2)}) collective-permute-start(bf16[16,4096]{1,0:T(8,128)(2,1)S(1)} %collective-permute-done.3.refs_14_), channel_id=1, source_target_pairs={{0,2},{2,0},{4,6},{6,4},{8,10},{10,8},{12,14},{14,12},{1,3},{3,1},... | collective-permute-start | bytes 393224 | tf_op jit(solution)/shard_map/ppermute | solution.py:144
  23.4 1.3 %collective-permute-start.11 = (bf16[16,4096]{1,0:T(8,128)(2,1)S(1)}, bf16[16,4096]{1,0:T(8,128)(2,1)S(1)}, u32[]{:S(2)}, u32[]{:S(2)}) collective-permute-start(bf16[16,4096]{1,0:T(8,128)(2,1)S(1)} %collective-permute-done.10.refs_10_), channel_id=1, source_target_pairs={{0,2},{2,0},{4,6},{6,4},{8,10},{10,8},{12,14},{14,12},{1,3},{3,1},... | collective-permute-start | bytes 393224 | tf_op jit(solution)/shard_map/ppermute | solution.py:144
  25.7 4.3 %collective-permute-start.14 = (f32[128,128]{1,0:T(8,128)S(1)}, f32[128,128]{1,0:T(8,128)S(1)}, u32[]{:S(2)}, u32[]{:S(2)}) collective-permute-start(f32[128,128]{1,0:T(8,128)S(1)} %get-tuple-element.18), channel_id=1, source_target_pairs={{0,1},{1,0},{2,3},{3,2},{4,5},{5,4},{6,7},{7,6},{8,9},{9,8},{10,11... | collective-permute-start | bytes 196616 | tf_op jit(solution)/shard_map/ppermute | solution.py:259

commit v10 on v9

--- a/solution.py
+++ b/solution.py
@@ -231,20 +231,23 @@
     share = rows // 2
 
     mine = condition_layer(False, queries, left_factor, right_factor)
-    other = condition_layer(True, queries, left_factor, right_factor)
+    mine_c = other_core(mine)
+    left_late, mine_c = lax.optimization_barrier((left_factor, mine_c))
+    other = condition_layer(True, queries, left_late, right_factor)
     near = copy_near(train_grads)
     column, _ = place()
-    s1 = along_columns(mine, 1)
     s3 = along_columns(mine, 3)
-    s3, other = lax.optimization_barrier((s3, other))
+    mine_late, other = lax.optimization_barrier((mine, other))
+    s1 = along_columns(mine_late, 1)
     s2 = relay(jnp.where(column == 1, s1, jnp.where(column == 2, s3, mine)))
     y1 = other_part(s1)
     y3 = other_part(s3)
+    s2, y3 = lax.optimization_barrier((s2, y3))
     y2 = other_part(s2)
-    y1, y3, near = lax.optimization_barrier((y1, y3, near))
-
-    blocks = []
-    for block in (mine, other, s2, s1, s3, y2, y1, y3):
+    y1, near = lax.optimization_barrier((y1, near))
+
+    blocks = [mine, mine_c]
+    for block in (other, s2, s1, s3, y2, y1, y3):
         blocks += [block, other_core(block)]
     f32 = functools.partial(jax.ShapeDtypeStruct, dtype=jnp.float32)
     terms = [pltpu.VMEM((layer_count, share * layer_count, total), jnp.float32)]

time: 30.9 us -> 31.9 us (1.032)
  starting transfers between devices: 14.5 us -> 15.3 us
    ppermute x1, starting transfers between devices: 2.51 us -> 1.1 us  [relay(): return lax.ppermute(value, 'train', pairs)]
    ppermute x1, waiting for transfers between devices: 1.05 us -> 2.35 us  [relay(): return lax.ppermute(value, 'train', pairs)]
    ppermute x3, waiting for transfers between devices: 1.3 us -> 0.15 us  [other_part(): return lax.ppermute(value, 'parts', [(0, 1), (1, 0)])]
    ppermute x3, starting transfers between devices: 3.43 us -> 4.56 us  [other_part(): return lax.ppermute(value, 'parts', [(0, 1), (1, 0)])]
    ppermute x2, starting transfers between devices: 5.17 us -> 5.99 us  [along_columns(): return lax.ppermute(value, 'train', pairs)]
    ppermute x8, starting transfers between devices: 1.6 us -> 2.1 us  [other_core(): lax.ppermute(value, 'train', [(k, k ^ 1) for k in range(COLUMNS * PAIR)])]
  transfers between devices with their start and end apart: 15 -> 15, of which waited for: 7 -> 9; matrix products, arithmetic and copies ran while one was open for 0% -> 0% of each run, Pallas kernels for 16% -> 15%
where the time goes in v10:
time: 31.9 us; the launch traced here: 31.7 us
  starting transfers between devices  15.3 us (48%)
  waiting for transfers between devices  8.06 us (25%)
  Pallas kernels  7.57 us (24%)
  other arithmetic  0.66 us (2%)
    ppermute x2, starting transfers between devices, along_columns(): return lax.ppermute(value, 'train', pairs)  5.99 us
    ppermute x3, starting transfers between devices, other_part(): return lax.ppermute(value, 'parts', [(0, 1), (1, 0)])  4.56 us
    pallas_call x2, Pallas kernels, condition_layer(): pl.pallas_call(functools.partial(condition_kernel, other), out_shape=jax....  3.54 us
    ppermute x1, waiting for transfers between devices, relay(): return lax.ppermute(value, 'train', pairs)  2.35 us
    ppermute x2, waiting for transfers between devices, along_columns(): return lax.ppermute(value, 'train', pairs)  2.28 us
    pallas_call x1, Pallas kernels, copy_near(): pl.pallas_call(copy_kernel, out_shape=jax.ShapeDtypeStruct(value.shape, v...  2.2 us
    ppermute x8, starting transfers between devices, other_core(): lax.ppermute(value, 'train', [(k, k ^ 1) for k in range(COLUMNS * PAIR)])  2.1 us
    ppermute x1, waiting for transfers between devices, direct(): received = lax.ppermute(sent, 'layer', [(0, 1), (1, 0)])  1.92 us
  transfers between devices with their start and end apart: 15, of which 9 were waited for; matrix products, arithmetic and copies ran while one was open for 0% of the time, Pallas kernels for 15%

profile of v10, /device:TPU:0, one launch (start us, length us, event | category | flops | bytes accessed | tf_op | source)
XLA Modules:
  0.0 31.7 jit_solution(14491125137976977153)
XLA Ops:
  0.0 1.8 %condition_mine.1.refs_0_ = bf16[16,4096]{1,0:T(8,128)(2,1)S(1)} custom-call(bf16[2,1,16,4096]{3,2,1,0:T(8,128)(2,1)} %queries.3, f32[2,64,64]{2,1,0:T(8,128)} %left.2, f32[2,64,64]{2,1,0:T(8,128)} %right.3), custom_call_target="tpu_custom_call" | custom-call | flops 134217728 | bytes 524288 | tf_op jit(solution)/shard_map/condition_mine/pallas_call | solution.py:107
  1.8 0.5 %collective-permute-start = (bf16[16,4096]{1,0:T(8,128)(2,1)S(1)}, bf16[16,4096]{1,0:T(8,128)(2,1)S(1)}, u32[]{:S(2)}, u32[]{:S(2)}) collective-permute-start(bf16[16,4096]{1,0:T(8,128)(2,1)S(1)} %condition_mine.1.refs_0_), channel_id=1, source_target_pairs={{0,2},{2,0},{4,6},{6,4},{8,10},{10,8},{12,14},{14,12},{1,3},{3,1},... | collective-permute-start | bytes 393224 | tf_op jit(solution)/shard_map/ppermute | solution.py:144
  2.3 2.6 %collective-permute-start.4 = (bf16[16,4096]{1,0:T(8,128)(2,1)S(1)}, bf16[16,4096]{1,0:T(8,128)(2,1)S(1)}, u32[]{:S(2)}, u32[]{:S(2)}) collective-permute-start(bf16[16,4096]{1,0:T(8,128)(2,1)S(1)} %condition_mine.1.refs_0_), channel_id=1, source_target_pairs={{12,0},{14,2},{0,4},{2,6},{4,8},{6,10},{8,12},{10,14},{13,1},{15,3... | collective-permute-start | bytes 393224 | tf_op jit(solution)/shard_map/ppermute | solution.py:133
  4.9 0.0 collective-permute-done.refs_1_
  4.9 1.8 %condition_other.1.refs_2_ = bf16[16,4096]{1,0:T(8,128)(2,1)S(1)} custom-call(bf16[2,1,16,4096]{3,2,1,0:T(8,128)(2,1)} %queries.3, f32[2,64,64]{2,1,0:T(8,128)} %left.2, f32[2,64,64]{2,1,0:T(8,128)} %right.3), custom_call_target="tpu_custom_call" | custom-call | flops 134217728 | bytes 524288 | tf_op jit(solution)/shard_map/condition_other/pallas_call | solution.py:107
  6.7 3.4 %collective-permute-start.1 = (bf16[16,4096]{1,0:T(8,128)(2,1)S(1)}, bf16[16,4096]{1,0:T(8,128)(2,1)S(1)}, u32[]{:S(2)}, u32[]{:S(2)}) collective-permute-start(bf16[16,4096]{1,0:T(8,128)(2,1)S(1)} %condition_mine.1.refs_0_), channel_id=1, source_target_pairs={{4,0},{6,2},{8,4},{10,6},{12,8},{14,10},{0,12},{2,14},{5,1},{7,3},... | collective-permute-start | bytes 393224 | tf_op jit(solution)/shard_map/ppermute | solution.py:133
  10.1 1.1 %collective-permute-done.4.refs_8_ = bf16[16,4096]{1,0:T(8,128)(2,1)S(1)} collective-permute-done((bf16[16,4096]{1,0:T(8,128)(2,1)S(1)}, bf16[16,4096]{1,0:T(8,128)(2,1)S(1)}, u32[]{:S(2)}, u32[]{:S(2)}) %collective-permute-start.4) | collective-permute-done | bytes 131104 | tf_op jit(solution)/shard_map/ppermute | solution.py:133
  11.2 1.5 %collective-permute-start.6 = (bf16[16,4096]{1,0:T(8,128)(2,1)S(1)}, bf16[16,4096]{1,0:T(8,128)(2,1)S(1)}, u32[]{:S(2)}, u32[]{:S(2)}) collective-permute-start(bf16[16,4096]{1,0:T(8,128)(2,1)S(1)} %collective-permute-done.4.refs_8_), channel_id=1, source_target_pairs={{0,16},{16,0},{1,17},{17,1},{2,18},{18,2},{3,19},{19,3},{4,20},{20... | collective-permute-start | bytes 393224 | tf_op jit(solution)/shard_map/ppermute | solution.py:148
  12.7 1.2 %collective-permute-done.1.refs_6_ = bf16[16,4096]{1,0:T(8,128)(2,1)S(1)} collective-permute-done((bf16[16,4096]{1,0:T(8,128)(2,1)S(1)}, bf16[16,4096]{1,0:T(8,128)(2,1)S(1)}, u32[]{:S(2)}, u32[]{:S(2)}) %collective-permute-start.1) | collective-permute-done | bytes 131104 | tf_op jit(solution)/shard_map/ppermute | solution.py:133
  13.9 1.1 %collective-permute-start.5 = (bf16[16,4096]{1,0:T(8,128)(2,1)S(1)}, bf16[16,4096]{1,0:T(8,128)(2,1)S(1)}, u32[]{:S(2)}, u32[]{:S(2)}) collective-permute-start(bf16[16,4096]{1,0:T(8,128)(2,1)S(1)} %select_select_fusion), channel_id=1, source_target_pairs={{0,8},{2,10},{8,12},{10,14},{12,4},{14,6},{4,0},{6,2},{1,9},{3,11}... | collective-permute-start | bytes 393224 | tf_op jit(solution)/shard_map/ppermute | solution.py:140
  15.0 1.5 %collective-permute-start.2 = (bf16[16,4096]{1,0:T(8,128)(2,1)S(1)}, bf16[16,4096]{1,0:T(8,128)(2,1)S(1)}, u32[]{:S(2)}, u32[]{:S(2)}) collective-permute-start(bf16[16,4096]{1,0:T(8,128)(2,1)S(1)} %collective-permute-done.1.refs_6_), channel_id=1, source_target_pairs={{0,16},{16,0},{1,17},{17,1},{2,18},{18,2},{3,19},{19,3},{4,20},{20... | collective-permute-start | bytes 393224 | tf_op jit(solution)/shard_map/ppermute | solution.py:148
  16.5 0.0 collective-permute-start.3
  16.5 0.5 %collective-permute-start.9 = (bf16[16,4096]{1,0:T(8,128)(2,1)S(1)}, bf16[16,4096]{1,0:T(8,128)(2,1)S(1)}, u32[]{:S(2)}, u32[]{:S(2)}) collective-permute-start(bf16[16,4096]{1,0:T(8,128)(2,1)S(1)} %collective-permute-done.4.refs_8_), channel_id=1, source_target_pairs={{0,2},{2,0},{4,6},{6,4},{8,10},{10,8},{12,14},{14,12},{1,3},{3,1},... | collective-permute-start | bytes 393224 | tf_op jit(solution)/shard_map/ppermute | solution.py:144
  17.0 0.0 collective-permute-done.6.refs_14_
  17.0 2.4 %collective-permute-done.5.refs_4_ = bf16[16,4096]{1,0:T(8,128)(2,1)S(1)} collective-permute-done((bf16[16,4096]{1,0:T(8,128)(2,1)S(1)}, bf16[16,4096]{1,0:T(8,128)(2,1)S(1)}, u32[]{:S(2)}, u32[]{:S(2)}) %collective-permute-start.5) | collective-permute-done | bytes 131104 | tf_op jit(solution)/shard_map/ppermute | solution.py:140
  19.4 1.5 %collective-permute-start.10 = (bf16[16,4096]{1,0:T(8,128)(2,1)S(1)}, bf16[16,4096]{1,0:T(8,128)(2,1)S(1)}, u32[]{:S(2)}, u32[]{:S(2)}) collective-permute-start(bf16[16,4096]{1,0:T(8,128)(2,1)S(1)} %collective-permute-done.5.refs_4_), channel_id=1, source_target_pairs={{0,16},{16,0},{1,17},{17,1},{2,18},{18,2},{3,19},{19,3},{4,20},{20... | collective-permute-start | bytes 393224 | tf_op jit(solution)/shard_map/ppermute | solution.py:148
  20.9 2.2 %near.1.train = bf16[256,2,4096]{2,1,0:T(2,128)(2,1)S(1)} custom-call(bf16[256,2,4096]{2,1,0:T(2,128)(2,1)} %source.1), custom_call_target="tpu_custom_call" | custom-call | bytes 8388608 | tf_op jit(solution)/shard_map/near/pallas_call | solution.py:158
  23.1 0.1 collective-permute-start.8
  23.2 0.0 collective-permute-done.2.refs_12_
  23.2 0.5 %collective-permute-start.7 = (bf16[16,4096]{1,0:T(8,128)(2,1)S(1)}, bf16[16,4096]{1,0:T(8,128)(2,1)S(1)}, u32[]{:S(2)}, u32[]{:S(2)}) collective-permute-start(bf16[16,4096]{1,0:T(8,128)(2,1)S(1)} %collective-permute-done.5.refs_4_), channel_id=1, source_target_pairs={{0,2},{2,0},{4,6},{6,4},{8,10},{10,8},{12,14},{14,12},{1,3},{3,1},... | collective-permute-start | bytes 393224 | tf_op jit(solution)/shard_map/ppermute | solution.py:144
  23.7 0.0 collective-permute-done.9.refs_9_
  23.7 0.1 collective-permute-start.13
  23.8 0.0 collective-permute-done.3.refs_3_
  23.8 0.4 %collective-permute-start.12 = (bf16[16,4096]{1,0:T(8,128)(2,1)S(1)}, bf16[16,4096]{1,0:T(8,128)(2,1)S(1)}, u32[]{:S(2)}, u32[]{:S(2)}) collective-permute-start(bf16[16,4096]{1,0:T(8,128)(2,1)S(1)} %collective-permute-done.2.refs_12_), channel_id=1, source_target_pairs={{0,2},{2,0},{4,6},{6,4},{8,10},{10,8},{12,14},{14,12},{1,3},{3,1},... | collective-permute-start | bytes 393224 | tf_op jit(solution)/shard_map/ppermute | solution.py:144
  24.2 0.1 collective-permute-done.10.refs_10_
  24.4 0.0 collective-permute-start.11
  24.4 0.2 collective-permute-done.8.refs_7_
  24.5 0.5 %collective-permute-done.13.refs_15_ = bf16[16,4096]{1,0:T(8,128)(2,1)S(1)} collective-permute-done((bf16[16,4096]{1,0:T(8,128)(2,1)S(1)}, bf16[16,4096]{1,0:T(8,128)(2,1)S(1)}, u32[]{:S(2)}, u32[]{:S(2)}) %collective-permute-start.13) | collective-permute-done | bytes 131104 | tf_op jit(solution)/shard_map/ppermute | solution.py:144
  25.0 0.0 collective-permute-done.7.refs_5_
  25.0 0.2 collective-permute-done.12.refs_13_
  25.2 0.5 %collective-permute-done.11.refs_11_ = bf16[16,4096]{1,0:T(8,128)(2,1)S(1)} collective-permute-done((bf16[16,4096]{1,0:T(8,128)(2,1)S(1)}, bf16[16,4096]{1,0:T(8,128)(2,1)S(1)}, u32[]{:S(2)}, u32[]{:S(2)}) %collective-permute-start.11) | collective-permute-done | bytes 131104 | tf_op jit(solution)/shard_map/ppermute | solution.py:144
  25.7 1.0 %scores_sent.1 = (f32[128,128]{1,0:T(8,128)S(1)}, bf16[2,128,4096]{2,1,0:T(8,128)(2,1)S(1)}) custom-call(bf16[256,2,4096]{2,1,0:T(2,128)(2,1)S(1)} %near.1.train, bf16[16,4096]{1,0:T(8,128)(2,1)S(1)} %condition_mine.1.refs_0_, bf16[16,4096]{1,0:T(8,128)(2,1)S(1)} %collective-permute-done.refs_1_, bf16[16,4096]{1,0:T(8,128)(2,1)S(1)} %condition_other.1.refs_2_, ...), custom_call_target="tpu_custom_call" | custom-call | flops 536870912 | bytes 4194304 | tf_op jit(solution)/shard_map/scores_sent/pallas_call | solution.py:215
  26.7 1.6 %collective-permute-start.14 = (f32[128,128]{1,0:T(8,128)S(1)}, f32[128,128]{1,0:T(8,128)S(1)}, u32[]{:S(2)}, u32[]{:S(2)}) collective-permute-start(f32[128,128]{1,0:T(8,128)S(1)} %get-tuple-element.24), channel_id=1, source_target_pairs={{0,1},{1,0},{2,3},{3,2},{4,5},{5,4},{6,7},{7,6},{8,9},{9,8},{10,11... | collective-permute-start | bytes 196616 | tf_op jit(solution)/shard_map/ppermute | solution.py:262
  28.3 0.8 %scores_kept.1 = f32[128,128]{1,0:T(8,128)S(1)} custom-call(bf16[256,2,4096]{2,1,0:T(2,128)(2,1)S(1)} %near.1.train, bf16[2,128,4096]{2,1,0:T(8,128)(2,1)S(1)} %get-tuple-element.23.table), custom_call_target="tpu_custom_call" | custom-call | flops 536870912 | bytes 4194304 | tf_op jit(solution)/shard_map/scores_kept/pallas_call | solution.py:215
  29.1 1.9 %collective-permute-done.14 = f32[128,128]{1,0:T(8,128)S(1)} collective-permute-done((f32[128,128]{1,0:T(8,128)S(1)}, f32[128,128]{1,0:T(8,128)S(1)}, u32[]{:S(2)}, u32[]{:S(2)}) %collective-permute-start.14) | collective-permute-done | bytes 65568 | tf_op jit(solution)/shard_map/ppermute | solution.py:262
  31.0 0.6 %add.4 = f32[128,128]{1,0:T(8,128)} add(f32[128,128]{1,0:T(8,128)S(1)} %scores_kept.1, f32[128,128]{1,0:T(8,128)S(1)} %collective-permute-done.14) | non-fusion elementwise | flops 16384 | bytes 196608 | tf_op jit(solution)/shard_map/add | solution.py:264
  (1 shorter events, 0.0 us)
Async XLA Ops:
  1.8 3.2 %collective-permute-start = (bf16[16,4096]{1,0:T(8,128)(2,1)S(1)}, bf16[16,4096]{1,0:T(8,128)(2,1)S(1)}, u32[]{:S(2)}, u32[]{:S(2)}) collective-permute-start(bf16[16,4096]{1,0:T(8,128)(2,1)S(1)} %condition_mine.1.refs_0_), channel_id=1, source_target_pairs={{0,2},{2,0},{4,6},{6,4},{8,10},{10,8},{12,14},{14,12},{1,3},{3,1},... | collective-permute-start | bytes 393224 | tf_op jit(solution)/shard_map/ppermute | solution.py:144
  2.3 8.9 %collective-permute-start.4 = (bf16[16,4096]{1,0:T(8,128)(2,1)S(1)}, bf16[16,4096]{1,0:T(8,128)(2,1)S(1)}, u32[]{:S(2)}, u32[]{:S(2)}) collective-permute-start(bf16[16,4096]{1,0:T(8,128)(2,1)S(1)} %condition_mine.1.refs_0_), channel_id=1, source_target_pairs={{12,0},{14,2},{0,4},{2,6},{4,8},{6,10},{8,12},{10,14},{13,1},{15,3... | collective-permute-start | bytes 393224 | tf_op jit(solution)/shard_map/ppermute | solution.py:133
  6.7 7.2 %collective-permute-start.1 = (bf16[16,4096]{1,0:T(8,128)(2,1)S(1)}, bf16[16,4096]{1,0:T(8,128)(2,1)S(1)}, u32[]{:S(2)}, u32[]{:S(2)}) collective-permute-start(bf16[16,4096]{1,0:T(8,128)(2,1)S(1)} %condition_mine.1.refs_0_), channel_id=1, source_target_pairs={{4,0},{6,2},{8,4},{10,6},{12,8},{14,10},{0,12},{2,14},{5,1},{7,3},... | collective-permute-start | bytes 393224 | tf_op jit(solution)/shard_map/ppermute | solution.py:133
  11.2 5.9 %collective-permute-start.6 = (bf16[16,4096]{1,0:T(8,128)(2,1)S(1)}, bf16[16,4096]{1,0:T(8,128)(2,1)S(1)}, u32[]{:S(2)}, u32[]{:S(2)}) collective-permute-start(bf16[16,4096]{1,0:T(8,128)(2,1)S(1)} %collective-permute-done.4.refs_8_), channel_id=1, source_target_pairs={{0,16},{16,0},{1,17},{17,1},{2,18},{18,2},{3,19},{19,3},{4,20},{20... | collective-permute-start | bytes 393224 | tf_op jit(solution)/shard_map/ppermute | solution.py:148
  13.9 5.5 %collective-permute-start.5 = (bf16[16,4096]{1,0:T(8,128)(2,1)S(1)}, bf16[16,4096]{1,0:T(8,128)(2,1)S(1)}, u32[]{:S(2)}, u32[]{:S(2)}) collective-permute-start(bf16[16,4096]{1,0:T(8,128)(2,1)S(1)} %select_select_fusion), channel_id=1, source_target_pairs={{0,8},{2,10},{8,12},{10,14},{12,4},{14,6},{4,0},{6,2},{1,9},{3,11}... | collective-permute-start | bytes 393224 | tf_op jit(solution)/shard_map/ppermute | solution.py:140
  15.0 8.2 %collective-permute-start.2 = (bf16[16,4096]{1,0:T(8,128)(2,1)S(1)}, bf16[16,4096]{1,0:T(8,128)(2,1)S(1)}, u32[]{:S(2)}, u32[]{:S(2)}) collective-permute-start(bf16[16,4096]{1,0:T(8,128)(2,1)S(1)} %collective-permute-done.1.refs_6_), channel_id=1, source_target_pairs={{0,16},{16,0},{1,17},{17,1},{2,18},{18,2},{3,19},{19,3},{4,20},{20... | collective-permute-start | bytes 393224 | tf_op jit(solution)/shard_map/ppermute | solution.py:148
  16.5 7.3 %collective-permute-start.3 = (bf16[16,4096]{1,0:T(8,128)(2,1)S(1)}, bf16[16,4096]{1,0:T(8,128)(2,1)S(1)}, u32[]{:S(2)}, u32[]{:S(2)}) collective-permute-start(bf16[16,4096]{1,0:T(8,128)(2,1)S(1)} %condition_other.1.refs_2_), channel_id=1, source_target_pairs={{0,2},{2,0},{4,6},{6,4},{8,10},{10,8},{12,14},{14,12},{1,3},{3,1},... | collective-permute-start | bytes 393224 | tf_op jit(solution)/shard_map/ppermute | solution.py:144
  16.5 7.2 %collective-permute-start.9 = (bf16[16,4096]{1,0:T(8,128)(2,1)S(1)}, bf16[16,4096]{1,0:T(8,128)(2,1)S(1)}, u32[]{:S(2)}, u32[]{:S(2)}) collective-permute-start(bf16[16,4096]{1,0:T(8,128)(2,1)S(1)} %collective-permute-done.4.refs_8_), channel_id=1, source_target_pairs={{0,2},{2,0},{4,6},{6,4},{8,10},{10,8},{12,14},{14,12},{1,3},{3,1},... | collective-permute-start | bytes 393224 | tf_op jit(solution)/shard_map/ppermute | solution.py:144
  19.4 5.0 %collective-permute-start.10 = (bf16[16,4096]{1,0:T(8,128)(2,1)S(1)}, bf16[16,4096]{1,0:T(8,128)(2,1)S(1)}, u32[]{:S(2)}, u32[]{:S(2)}) collective-permute-start(bf16[16,4096]{1,0:T(8,128)(2,1)S(1)} %collective-permute-done.5.refs_4_), channel_id=1, source_target_pairs={{0,16},{16,0},{1,17},{17,1},{2,18},{18,2},{3,19},{19,3},{4,20},{20... | collective-permute-start | bytes 393224 | tf_op jit(solution)/shard_map/ppermute | solution.py:148
  23.1 1.4 %collective-permute-start.8 = (bf16[16,4096]{1,0:T(8,128)(2,1)S(1)}, bf16[16,4096]{1,0:T(8,128)(2,1)S(1)}, u32[]{:S(2)}, u32[]{:S(2)}) collective-permute-start(bf16[16,4096]{1,0:T(8,128)(2,1)S(1)} %collective-permute-done.1.refs_6_), channel_id=1, source_target_pairs={{0,2},{2,0},{4,6},{6,4},{8,10},{10,8},{12,14},{14,12},{1,3},{3,1},... | collective-permute-start | bytes 393224 | tf_op jit(solution)/shard_map/ppermute | solution.py:144
  23.2 1.8 %collective-permute-start.7 = (bf16[16,4096]{1,0:T(8,128)(2,1)S(1)}, bf16[16,4096]{1,0:T(8,128)(2,1)S(1)}, u32[]{:S(2)}, u32[]{:S(2)}) collective-permute-start(bf16[16,4096]{1,0:T(8,128)(2,1)S(1)} %collective-permute-done.5.refs_4_), channel_id=1, source_target_pairs={{0,2},{2,0},{4,6},{6,4},{8,10},{10,8},{12,14},{14,12},{1,3},{3,1},... | collective-permute-start | bytes 393224 | tf_op jit(solution)/shard_map/ppermute | solution.py:144
  23.7 1.3 %collective-permute-start.13 = (bf16[16,4096]{1,0:T(8,128)(2,1)S(1)}, bf16[16,4096]{1,0:T(8,128)(2,1)S(1)}, u32[]{:S(2)}, u32[]{:S(2)}) collective-permute-start(bf16[16,4096]{1,0:T(8,128)(2,1)S(1)} %collective-permute-done.6.refs_14_), channel_id=1, source_target_pairs={{0,2},{2,0},{4,6},{6,4},{8,10},{10,8},{12,14},{14,12},{1,3},{3,1},... | collective-permute-start | bytes 393224 | tf_op jit(solution)/shard_map/ppermute | solution.py:144
  23.8 1.4 %collective-permute-start.12 = (bf16[16,4096]{1,0:T(8,128)(2,1)S(1)}, bf16[16,4096]{1,0:T(8,128)(2,1)S(1)}, u32[]{:S(2)}, u32[]{:S(2)}) collective-permute-start(bf16[16,4096]{1,0:T(8,128)(2,1)S(1)} %collective-permute-done.2.refs_12_), channel_id=1, source_target_pairs={{0,2},{2,0},{4,6},{6,4},{8,10},{10,8},{12,14},{14,12},{1,3},{3,1},... | collective-permute-start | bytes 393224 | tf_op jit(solution)/shard_map/ppermute | solution.py:144
  24.4 1.3 %collective-permute-start.11 = (bf16[16,4096]{1,0:T(8,128)(2,1)S(1)}, bf16[16,4096]{1,0:T(8,128)(2,1)S(1)}, u32[]{:S(2)}, u32[]{:S(2)}) collective-permute-start(bf16[16,4096]{1,0:T(8,128)(2,1)S(1)} %collective-permute-done.10.refs_10_), channel_id=1, source_target_pairs={{0,2},{2,0},{4,6},{6,4},{8,10},{10,8},{12,14},{14,12},{1,3},{3,1},... | collective-permute-start | bytes 393224 | tf_op jit(solution)/shard_map/ppermute | solution.py:144
  26.7 4.3 %collective-permute-start.14 = (f32[128,128]{1,0:T(8,128)S(1)}, f32[128,128]{1,0:T(8,128)S(1)}, u32[]{:S(2)}, u32[]{:S(2)}) collective-permute-start(f32[128,128]{1,0:T(8,128)S(1)} %get-tuple-element.24), channel_id=1, source_target_pairs={{0,1},{1,0},{2,3},{3,2},{4,5},{5,4},{6,7},{7,6},{8,9},{9,8},{10,11... | collective-permute-start | bytes 196616 | tf_op jit(solution)/shard_map/ppermute | solution.py:262

commit v11 on v9

--- a/solution.py
+++ b/solution.py
@@ -236,12 +236,13 @@
     column, _ = place()
     s1 = along_columns(mine, 1)
     s3 = along_columns(mine, 3)
-    s3, other = lax.optimization_barrier((s3, other))
+    s1, s3, other = lax.optimization_barrier((s1, s3, other))
     s2 = relay(jnp.where(column == 1, s1, jnp.where(column == 2, s3, mine)))
     y1 = other_part(s1)
     y3 = other_part(s3)
     y2 = other_part(s2)
-    y1, y3, near = lax.optimization_barrier((y1, y3, near))
+    y1, y3, _ = lax.optimization_barrier((y1, y3, s2))
+    y2, near = lax.optimization_barrier((y2, near))
 
     blocks = []
     for block in (mine, other, s2, s1, s3, y2, y1, y3):

time: 30.9 us -> 32.1 us (1.039)
  waiting for transfers between devices: 7.89 us -> 10.2 us
  starting transfers between devices: 14.5 us -> 13.5 us
    ppermute x2, waiting for transfers between devices: 2.49 us -> 3.9 us  [along_columns(): return lax.ppermute(value, 'train', pairs)]
    ppermute x1, starting transfers between devices: 2.51 us -> 1.35 us  [relay(): return lax.ppermute(value, 'train', pairs)]
    ppermute x1, waiting for transfers between devices: 1.05 us -> 1.64 us  [relay(): return lax.ppermute(value, 'train', pairs)]
    ppermute x1, waiting for transfers between devices: 1.7 us -> 2.24 us  [direct(): received = lax.ppermute(sent, 'layer', [(0, 1), (1, 0)])]
    ppermute x8, starting transfers between devices: 1.6 us -> 2.11 us  [other_core(): lax.ppermute(value, 'train', [(k, k ^ 1) for k in range(COLUMNS * PAIR)])]
    ppermute x1, starting transfers between devices: 1.78 us -> 1.3 us  [direct(): received = lax.ppermute(sent, 'layer', [(0, 1), (1, 0)])]
  transfers between devices with their start and end apart: 15 -> 15, of which waited for: 7 -> 8; matrix products, arithmetic and copies ran while one was open for 0% -> 0% of each run, Pallas kernels for 16% -> 15%
where the time goes in v11:
time: 32.1 us; the launch traced here: 31.9 us
  starting transfers between devices  13.5 us (42%)
  waiting for transfers between devices  10.2 us (32%)
  Pallas kernels  7.57 us (24%)
  other arithmetic  0.66 us (2%)
    ppermute x2, starting transfers between devices, along_columns(): return lax.ppermute(value, 'train', pairs)  5.17 us
    ppermute x2, waiting for transfers between devices, along_columns(): return lax.ppermute(value, 'train', pairs)  3.9 us
    ppermute x3, starting transfers between devices, other_part(): return lax.ppermute(value, 'parts', [(0, 1), (1, 0)])  3.55 us
    pallas_call x2, Pallas kernels, condition_layer(): pl.pallas_call(functools.partial(condition_kernel, other), out_shape=jax....  3.53 us
    ppermute x1, waiting for transfers between devices, direct(): received = lax.ppermute(sent, 'layer', [(0, 1), (1, 0)])  2.24 us
    pallas_call x1, Pallas kernels, copy_near(): pl.pallas_call(copy_kernel, out_shape=jax.ShapeDtypeStruct(value.shape, v...  2.2 us
    ppermute x8, starting transfers between devices, other_core(): lax.ppermute(value, 'train', [(k, k ^ 1) for k in range(COLUMNS * PAIR)])  2.11 us
    pallas_call x2, Pallas kernels, local_call(): pl.pallas_call(kernel, out_shape=out_shape, in_specs=[spec] * len(operand...  1.84 us
  transfers between devices with their start and end apart: 15, of which 8 were waited for; matrix products, arithmetic and copies ran while one was open for 0% of the time, Pallas kernels for 15%

profile of v11, /device:TPU:0, one launch (start us, length us, event | category | flops | bytes accessed | tf_op | source)
XLA Modules:
  0.0 31.9 jit_solution(5145457253465461020)
XLA Ops:
  0.0 1.8 %condition_mine.1.refs_0_ = bf16[16,4096]{1,0:T(8,128)(2,1)S(1)} custom-call(bf16[2,1,16,4096]{3,2,1,0:T(8,128)(2,1)} %queries.3, f32[2,64,64]{2,1,0:T(8,128)} %left.3, f32[2,64,64]{2,1,0:T(8,128)} %right.3), custom_call_target="tpu_custom_call" | custom-call | flops 134217728 | bytes 524288 | tf_op jit(solution)/shard_map/condition_mine/pallas_call | solution.py:107
  1.8 3.1 %collective-permute-start.1 = (bf16[16,4096]{1,0:T(8,128)(2,1)S(1)}, bf16[16,4096]{1,0:T(8,128)(2,1)S(1)}, u32[]{:S(2)}, u32[]{:S(2)}) collective-permute-start(bf16[16,4096]{1,0:T(8,128)(2,1)S(1)} %condition_mine.1.refs_0_), channel_id=1, source_target_pairs={{12,0},{14,2},{0,4},{2,6},{4,8},{6,10},{8,12},{10,14},{13,1},{15,3... | collective-permute-start | bytes 393224 | tf_op jit(solution)/shard_map/ppermute | solution.py:133
  4.9 2.1 %collective-permute-start = (bf16[16,4096]{1,0:T(8,128)(2,1)S(1)}, bf16[16,4096]{1,0:T(8,128)(2,1)S(1)}, u32[]{:S(2)}, u32[]{:S(2)}) collective-permute-start(bf16[16,4096]{1,0:T(8,128)(2,1)S(1)} %condition_mine.1.refs_0_), channel_id=1, source_target_pairs={{4,0},{6,2},{8,4},{10,6},{12,8},{14,10},{0,12},{2,14},{5,1},{7,3},... | collective-permute-start | bytes 393224 | tf_op jit(solution)/shard_map/ppermute | solution.py:133
  6.9 1.8 %condition_other.1.refs_2_ = bf16[16,4096]{1,0:T(8,128)(2,1)S(1)} custom-call(bf16[2,1,16,4096]{3,2,1,0:T(8,128)(2,1)} %queries.3, f32[2,64,64]{2,1,0:T(8,128)} %left.3, f32[2,64,64]{2,1,0:T(8,128)} %right.3), custom_call_target="tpu_custom_call" | custom-call | flops 134217728 | bytes 524288 | tf_op jit(solution)/shard_map/condition_other/pallas_call | solution.py:107
  8.7 2.5 %collective-permute-done.1.refs_8_ = bf16[16,4096]{1,0:T(8,128)(2,1)S(1)} collective-permute-done((bf16[16,4096]{1,0:T(8,128)(2,1)S(1)}, bf16[16,4096]{1,0:T(8,128)(2,1)S(1)}, u32[]{:S(2)}, u32[]{:S(2)}) %collective-permute-start.1) | collective-permute-done | bytes 131104 | tf_op jit(solution)/shard_map/ppermute | solution.py:133
  11.2 1.4 %collective-permute-done.refs_6_ = bf16[16,4096]{1,0:T(8,128)(2,1)S(1)} collective-permute-done((bf16[16,4096]{1,0:T(8,128)(2,1)S(1)}, bf16[16,4096]{1,0:T(8,128)(2,1)S(1)}, u32[]{:S(2)}, u32[]{:S(2)}) %collective-permute-start) | collective-permute-done | bytes 131104 | tf_op jit(solution)/shard_map/ppermute | solution.py:133
  12.6 1.3 %collective-permute-start.2 = (bf16[16,4096]{1,0:T(8,128)(2,1)S(1)}, bf16[16,4096]{1,0:T(8,128)(2,1)S(1)}, u32[]{:S(2)}, u32[]{:S(2)}) collective-permute-start(bf16[16,4096]{1,0:T(8,128)(2,1)S(1)} %select_select_fusion), channel_id=1, source_target_pairs={{0,8},{2,10},{8,12},{10,14},{12,4},{14,6},{4,0},{6,2},{1,9},{3,11}... | collective-permute-start | bytes 393224 | tf_op jit(solution)/shard_map/ppermute | solution.py:140
  14.0 1.5 %collective-permute-start.10 = (bf16[16,4096]{1,0:T(8,128)(2,1)S(1)}, bf16[16,4096]{1,0:T(8,128)(2,1)S(1)}, u32[]{:S(2)}, u32[]{:S(2)}) collective-permute-start(bf16[16,4096]{1,0:T(8,128)(2,1)S(1)} %collective-permute-done.refs_6_), channel_id=1, source_target_pairs={{0,16},{16,0},{1,17},{17,1},{2,18},{18,2},{3,19},{19,3},{4,20},{20... | collective-permute-start | bytes 393224 | tf_op jit(solution)/shard_map/ppermute | solution.py:148
  15.5 0.5 %collective-permute-start.11 = (bf16[16,4096]{1,0:T(8,128)(2,1)S(1)}, bf16[16,4096]{1,0:T(8,128)(2,1)S(1)}, u32[]{:S(2)}, u32[]{:S(2)}) collective-permute-start(bf16[16,4096]{1,0:T(8,128)(2,1)S(1)} %collective-permute-done.1.refs_8_), channel_id=1, source_target_pairs={{0,16},{16,0},{1,17},{17,1},{2,18},{18,2},{3,19},{19,3},{4,20},{20... | collective-permute-start | bytes 393224 | tf_op jit(solution)/shard_map/ppermute | solution.py:148
  16.0 1.6 %collective-permute-done.2.refs_4_ = bf16[16,4096]{1,0:T(8,128)(2,1)S(1)} collective-permute-done((bf16[16,4096]{1,0:T(8,128)(2,1)S(1)}, bf16[16,4096]{1,0:T(8,128)(2,1)S(1)}, u32[]{:S(2)}, u32[]{:S(2)}) %collective-permute-start.2) | collective-permute-done | bytes 131104 | tf_op jit(solution)/shard_map/ppermute | solution.py:140
  17.7 1.5 %collective-permute-start.3 = (bf16[16,4096]{1,0:T(8,128)(2,1)S(1)}, bf16[16,4096]{1,0:T(8,128)(2,1)S(1)}, u32[]{:S(2)}, u32[]{:S(2)}) collective-permute-start(bf16[16,4096]{1,0:T(8,128)(2,1)S(1)} %collective-permute-done.2.refs_4_), channel_id=1, source_target_pairs={{0,16},{16,0},{1,17},{17,1},{2,18},{18,2},{3,19},{19,3},{4,20},{20... | collective-permute-start | bytes 393224 | tf_op jit(solution)/shard_map/ppermute | solution.py:148
  19.2 0.0 collective-permute-start.4
  19.2 0.5 %collective-permute-start.5 = (bf16[16,4096]{1,0:T(8,128)(2,1)S(1)}, bf16[16,4096]{1,0:T(8,128)(2,1)S(1)}, u32[]{:S(2)}, u32[]{:S(2)}) collective-permute-start(bf16[16,4096]{1,0:T(8,128)(2,1)S(1)} %condition_other.1.refs_2_), channel_id=1, source_target_pairs={{0,2},{2,0},{4,6},{6,4},{8,10},{10,8},{12,14},{14,12},{1,3},{3,1},... | collective-permute-start | bytes 393224 | tf_op jit(solution)/shard_map/ppermute | solution.py:144
  19.7 0.7 %collective-permute-done.10.refs_12_ = bf16[16,4096]{1,0:T(8,128)(2,1)S(1)} collective-permute-done((bf16[16,4096]{1,0:T(8,128)(2,1)S(1)}, bf16[16,4096]{1,0:T(8,128)(2,1)S(1)}, u32[]{:S(2)}, u32[]{:S(2)}) %collective-permute-start.10) | collective-permute-done | bytes 131104 | tf_op jit(solution)/shard_map/ppermute | solution.py:148
  20.4 0.0 collective-permute-start.7
  20.4 2.2 %near.1.train = bf16[256,2,4096]{2,1,0:T(2,128)(2,1)S(1)} custom-call(bf16[256,2,4096]{2,1,0:T(2,128)(2,1)} %source.1), custom_call_target="tpu_custom_call" | custom-call | bytes 8388608 | tf_op jit(solution)/shard_map/near/pallas_call | solution.py:158
  22.6 0.0 collective-permute-done.11.refs_14_
  22.6 0.6 %collective-permute-start.8 = (bf16[16,4096]{1,0:T(8,128)(2,1)S(1)}, bf16[16,4096]{1,0:T(8,128)(2,1)S(1)}, u32[]{:S(2)}, u32[]{:S(2)}) collective-permute-start(bf16[16,4096]{1,0:T(8,128)(2,1)S(1)} %collective-permute-done.1.refs_8_), channel_id=1, source_target_pairs={{0,2},{2,0},{4,6},{6,4},{8,10},{10,8},{12,14},{14,12},{1,3},{3,1},... | collective-permute-start | bytes 393224 | tf_op jit(solution)/shard_map/ppermute | solution.py:144
  23.2 0.6 %collective-permute-done.3.refs_10_ = bf16[16,4096]{1,0:T(8,128)(2,1)S(1)} collective-permute-done((bf16[16,4096]{1,0:T(8,128)(2,1)S(1)}, bf16[16,4096]{1,0:T(8,128)(2,1)S(1)}, u32[]{:S(2)}, u32[]{:S(2)}) %collective-permute-start.3) | collective-permute-done | bytes 131104 | tf_op jit(solution)/shard_map/ppermute | solution.py:148
  23.9 0.0 collective-permute-start.12
  23.9 0.0 collective-permute-done.4.refs_1_
  23.9 0.5 %collective-permute-start.13 = (bf16[16,4096]{1,0:T(8,128)(2,1)S(1)}, bf16[16,4096]{1,0:T(8,128)(2,1)S(1)}, u32[]{:S(2)}, u32[]{:S(2)}) collective-permute-start(bf16[16,4096]{1,0:T(8,128)(2,1)S(1)} %collective-permute-done.11.refs_14_), channel_id=1, source_target_pairs={{0,2},{2,0},{4,6},{6,4},{8,10},{10,8},{12,14},{14,12},{1,3},{3,1},... | collective-permute-start | bytes 393224 | tf_op jit(solution)/shard_map/ppermute | solution.py:144
  24.4 0.0 collective-permute-done.5.refs_3_
  24.4 0.1 collective-permute-start.6
  24.4 0.0 collective-permute-done.7.refs_7_
  24.4 0.4 %collective-permute-start.9 = (bf16[16,4096]{1,0:T(8,128)(2,1)S(1)}, bf16[16,4096]{1,0:T(8,128)(2,1)S(1)}, u32[]{:S(2)}, u32[]{:S(2)}) collective-permute-start(bf16[16,4096]{1,0:T(8,128)(2,1)S(1)} %collective-permute-done.3.refs_10_), channel_id=1, source_target_pairs={{0,2},{2,0},{4,6},{6,4},{8,10},{10,8},{12,14},{14,12},{1,3},{3,1},... | collective-permute-start | bytes 393224 | tf_op jit(solution)/shard_map/ppermute | solution.py:144
  24.9 0.0 collective-permute-done.8.refs_9_
  24.9 0.8 %collective-permute-done.6.refs_5_ = bf16[16,4096]{1,0:T(8,128)(2,1)S(1)} collective-permute-done((bf16[16,4096]{1,0:T(8,128)(2,1)S(1)}, bf16[16,4096]{1,0:T(8,128)(2,1)S(1)}, u32[]{:S(2)}, u32[]{:S(2)}) %collective-permute-start.6) | collective-permute-done | bytes 131104 | tf_op jit(solution)/shard_map/ppermute | solution.py:144
  25.7 0.0 collective-permute-done.12.refs_13_
  25.7 0.0 collective-permute-done.13.refs_15_
  25.7 0.2 collective-permute-done.9.refs_11_
  25.9 1.0 %scores_sent.1 = (f32[128,128]{1,0:T(8,128)S(1)}, bf16[2,128,4096]{2,1,0:T(8,128)(2,1)S(1)}) custom-call(bf16[256,2,4096]{2,1,0:T(2,128)(2,1)S(1)} %near.1.train, bf16[16,4096]{1,0:T(8,128)(2,1)S(1)} %condition_mine.1.refs_0_, bf16[16,4096]{1,0:T(8,128)(2,1)S(1)} %collective-permute-done.4.refs_1_, bf16[16,4096]{1,0:T(8,128)(2,1)S(1)} %condition_other.1.refs_2_, ...), custom_call_target="tpu_custom_call" | custom-call | flops 536870912 | bytes 4194304 | tf_op jit(solution)/shard_map/scores_sent/pallas_call | solution.py:215
  26.9 1.3 %collective-permute-start.14 = (f32[128,128]{1,0:T(8,128)S(1)}, f32[128,128]{1,0:T(8,128)S(1)}, u32[]{:S(2)}, u32[]{:S(2)}) collective-permute-start(f32[128,128]{1,0:T(8,128)S(1)} %get-tuple-element.22), channel_id=1, source_target_pairs={{0,1},{1,0},{2,3},{3,2},{4,5},{5,4},{6,7},{7,6},{8,9},{9,8},{10,11... | collective-permute-start | bytes 196616 | tf_op jit(solution)/shard_map/ppermute | solution.py:260
  28.2 0.8 %scores_kept.1 = f32[128,128]{1,0:T(8,128)S(1)} custom-call(bf16[256,2,4096]{2,1,0:T(2,128)(2,1)S(1)} %near.1.train, bf16[2,128,4096]{2,1,0:T(8,128)(2,1)S(1)} %get-tuple-element.21.table), custom_call_target="tpu_custom_call" | custom-call | flops 536870912 | bytes 4194304 | tf_op jit(solution)/shard_map/scores_kept/pallas_call | solution.py:215
  29.1 2.2 %collective-permute-done.14 = f32[128,128]{1,0:T(8,128)S(1)} collective-permute-done((f32[128,128]{1,0:T(8,128)S(1)}, f32[128,128]{1,0:T(8,128)S(1)}, u32[]{:S(2)}, u32[]{:S(2)}) %collective-permute-start.14) | collective-permute-done | bytes 65568 | tf_op jit(solution)/shard_map/ppermute | solution.py:260
  31.3 0.6 %add.4 = f32[128,128]{1,0:T(8,128)} add(f32[128,128]{1,0:T(8,128)S(1)} %scores_kept.1, f32[128,128]{1,0:T(8,128)S(1)} %collective-permute-done.14) | non-fusion elementwise | flops 16384 | bytes 196608 | tf_op jit(solution)/shard_map/add | solution.py:262
  (1 shorter events, 0.0 us)
Async XLA Ops:
  1.8 9.4 %collective-permute-start.1 = (bf16[16,4096]{1,0:T(8,128)(2,1)S(1)}, bf16[16,4096]{1,0:T(8,128)(2,1)S(1)}, u32[]{:S(2)}, u32[]{:S(2)}) collective-permute-start(bf16[16,4096]{1,0:T(8,128)(2,1)S(1)} %condition_mine.1.refs_0_), channel_id=1, source_target_pairs={{12,0},{14,2},{0,4},{2,6},{4,8},{6,10},{8,12},{10,14},{13,1},{15,3... | collective-permute-start | bytes 393224 | tf_op jit(solution)/shard_map/ppermute | solution.py:133
  4.9 7.8 %collective-permute-start = (bf16[16,4096]{1,0:T(8,128)(2,1)S(1)}, bf16[16,4096]{1,0:T(8,128)(2,1)S(1)}, u32[]{:S(2)}, u32[]{:S(2)}) collective-permute-start(bf16[16,4096]{1,0:T(8,128)(2,1)S(1)} %condition_mine.1.refs_0_), channel_id=1, source_target_pairs={{4,0},{6,2},{8,4},{10,6},{12,8},{14,10},{0,12},{2,14},{5,1},{7,3},... | collective-permute-start | bytes 393224 | tf_op jit(solution)/shard_map/ppermute | solution.py:133
  12.6 5.0 %collective-permute-start.2 = (bf16[16,4096]{1,0:T(8,128)(2,1)S(1)}, bf16[16,4096]{1,0:T(8,128)(2,1)S(1)}, u32[]{:S(2)}, u32[]{:S(2)}) collective-permute-start(bf16[16,4096]{1,0:T(8,128)(2,1)S(1)} %select_select_fusion), channel_id=1, source_target_pairs={{0,8},{2,10},{8,12},{10,14},{12,4},{14,6},{4,0},{6,2},{1,9},{3,11}... | collective-permute-start | bytes 393224 | tf_op jit(solution)/shard_map/ppermute | solution.py:140
  14.0 6.4 %collective-permute-start.10 = (bf16[16,4096]{1,0:T(8,128)(2,1)S(1)}, bf16[16,4096]{1,0:T(8,128)(2,1)S(1)}, u32[]{:S(2)}, u32[]{:S(2)}) collective-permute-start(bf16[16,4096]{1,0:T(8,128)(2,1)S(1)} %collective-permute-done.refs_6_), channel_id=1, source_target_pairs={{0,16},{16,0},{1,17},{17,1},{2,18},{18,2},{3,19},{19,3},{4,20},{20... | collective-permute-start | bytes 393224 | tf_op jit(solution)/shard_map/ppermute | solution.py:148
  15.5 7.1 %collective-permute-start.11 = (bf16[16,4096]{1,0:T(8,128)(2,1)S(1)}, bf16[16,4096]{1,0:T(8,128)(2,1)S(1)}, u32[]{:S(2)}, u32[]{:S(2)}) collective-permute-start(bf16[16,4096]{1,0:T(8,128)(2,1)S(1)} %collective-permute-done.1.refs_8_), channel_id=1, source_target_pairs={{0,16},{16,0},{1,17},{17,1},{2,18},{18,2},{3,19},{19,3},{4,20},{20... | collective-permute-start | bytes 393224 | tf_op jit(solution)/shard_map/ppermute | solution.py:148
  17.7 6.2 %collective-permute-start.3 = (bf16[16,4096]{1,0:T(8,128)(2,1)S(1)}, bf16[16,4096]{1,0:T(8,128)(2,1)S(1)}, u32[]{:S(2)}, u32[]{:S(2)}) collective-permute-start(bf16[16,4096]{1,0:T(8,128)(2,1)S(1)} %collective-permute-done.2.refs_4_), channel_id=1, source_target_pairs={{0,16},{16,0},{1,17},{17,1},{2,18},{18,2},{3,19},{19,3},{4,20},{20... | collective-permute-start | bytes 393224 | tf_op jit(solution)/shard_map/ppermute | solution.py:148
  19.2 4.7 %collective-permute-start.4 = (bf16[16,4096]{1,0:T(8,128)(2,1)S(1)}, bf16[16,4096]{1,0:T(8,128)(2,1)S(1)}, u32[]{:S(2)}, u32[]{:S(2)}) collective-permute-start(bf16[16,4096]{1,0:T(8,128)(2,1)S(1)} %condition_mine.1.refs_0_), channel_id=1, source_target_pairs={{0,2},{2,0},{4,6},{6,4},{8,10},{10,8},{12,14},{14,12},{1,3},{3,1},... | collective-permute-start | bytes 393224 | tf_op jit(solution)/shard_map/ppermute | solution.py:144
  19.2 5.2 %collective-permute-start.5 = (bf16[16,4096]{1,0:T(8,128)(2,1)S(1)}, bf16[16,4096]{1,0:T(8,128)(2,1)S(1)}, u32[]{:S(2)}, u32[]{:S(2)}) collective-permute-start(bf16[16,4096]{1,0:T(8,128)(2,1)S(1)} %condition_other.1.refs_2_), channel_id=1, source_target_pairs={{0,2},{2,0},{4,6},{6,4},{8,10},{10,8},{12,14},{14,12},{1,3},{3,1},... | collective-permute-start | bytes 393224 | tf_op jit(solution)/shard_map/ppermute | solution.py:144
  20.4 4.0 %collective-permute-start.7 = (bf16[16,4096]{1,0:T(8,128)(2,1)S(1)}, bf16[16,4096]{1,0:T(8,128)(2,1)S(1)}, u32[]{:S(2)}, u32[]{:S(2)}) collective-permute-start(bf16[16,4096]{1,0:T(8,128)(2,1)S(1)} %collective-permute-done.refs_6_), channel_id=1, source_target_pairs={{0,2},{2,0},{4,6},{6,4},{8,10},{10,8},{12,14},{14,12},{1,3},{3,1},... | collective-permute-start | bytes 393224 | tf_op jit(solution)/shard_map/ppermute | solution.py:144
  22.6 2.2 %collective-permute-start.8 = (bf16[16,4096]{1,0:T(8,128)(2,1)S(1)}, bf16[16,4096]{1,0:T(8,128)(2,1)S(1)}, u32[]{:S(2)}, u32[]{:S(2)}) collective-permute-start(bf16[16,4096]{1,0:T(8,128)(2,1)S(1)} %collective-permute-done.1.refs_8_), channel_id=1, source_target_pairs={{0,2},{2,0},{4,6},{6,4},{8,10},{10,8},{12,14},{14,12},{1,3},{3,1},... | collective-permute-start | bytes 393224 | tf_op jit(solution)/shard_map/ppermute | solution.py:144
  23.9 1.9 %collective-permute-start.12 = (bf16[16,4096]{1,0:T(8,128)(2,1)S(1)}, bf16[16,4096]{1,0:T(8,128)(2,1)S(1)}, u32[]{:S(2)}, u32[]{:S(2)}) collective-permute-start(bf16[16,4096]{1,0:T(8,128)(2,1)S(1)} %collective-permute-done.10.refs_12_), channel_id=1, source_target_pairs={{0,2},{2,0},{4,6},{6,4},{8,10},{10,8},{12,14},{14,12},{1,3},{3,1},... | collective-permute-start | bytes 393224 | tf_op jit(solution)/shard_map/ppermute | solution.py:144
  23.9 1.9 %collective-permute-start.13 = (bf16[16,4096]{1,0:T(8,128)(2,1)S(1)}, bf16[16,4096]{1,0:T(8,128)(2,1)S(1)}, u32[]{:S(2)}, u32[]{:S(2)}) collective-permute-start(bf16[16,4096]{1,0:T(8,128)(2,1)S(1)} %collective-permute-done.11.refs_14_), channel_id=1, source_target_pairs={{0,2},{2,0},{4,6},{6,4},{8,10},{10,8},{12,14},{14,12},{1,3},{3,1},... | collective-permute-start | bytes 393224 | tf_op jit(solution)/shard_map/ppermute | solution.py:144
  24.4 1.3 %collective-permute-start.6 = (bf16[16,4096]{1,0:T(8,128)(2,1)S(1)}, bf16[16,4096]{1,0:T(8,128)(2,1)S(1)}, u32[]{:S(2)}, u32[]{:S(2)}) collective-permute-start(bf16[16,4096]{1,0:T(8,128)(2,1)S(1)} %collective-permute-done.2.refs_4_), channel_id=1, source_target_pairs={{0,2},{2,0},{4,6},{6,4},{8,10},{10,8},{12,14},{14,12},{1,3},{3,1},... | collective-permute-start | bytes 393224 | tf_op jit(solution)/shard_map/ppermute | solution.py:144
  24.4 1.5 %collective-permute-start.9 = (bf16[16,4096]{1,0:T(8,128)(2,1)S(1)}, bf16[16,4096]{1,0:T(8,128)(2,1)S(1)}, u32[]{:S(2)}, u32[]{:S(2)}) collective-permute-start(bf16[16,4096]{1,0:T(8,128)(2,1)S(1)} %collective-permute-done.3.refs_10_), channel_id=1, source_target_pairs={{0,2},{2,0},{4,6},{6,4},{8,10},{10,8},{12,14},{14,12},{1,3},{3,1},... | collective-permute-start | bytes 393224 | tf_op jit(solution)/shard_map/ppermute | solution.py:144
  26.9 4.4 %collective-permute-start.14 = (f32[128,128]{1,0:T(8,128)S(1)}, f32[128,128]{1,0:T(8,128)S(1)}, u32[]{:S(2)}, u32[]{:S(2)}) collective-permute-start(f32[128,128]{1,0:T(8,128)S(1)} %get-tuple-element.22), channel_id=1, source_target_pairs={{0,1},{1,0},{2,3},{3,2},{4,5},{5,4},{6,7},{7,6},{8,9},{9,8},{10,11... | collective-permute-start | bytes 196616 | tf_op jit(solution)/shard_map/ppermute | solution.py:260

commit v12 on v6

--- a/solution.py
+++ b/solution.py
@@ -80,56 +80,67 @@
         put(k, placed[k * count : (k + 1) * count, :].astype(jnp.bfloat16))
 
 
-def condition_kernel(other, queries, left, right, out, block_in, left_in, right_in, spread, stacked, placed, arrived):
-    part = lax.axis_index("parts")
-    layer = 1 - part if other else part
-    copies = [
-        pltpu.make_async_copy(source, target, arrived.at[k])
-        for k, (source, target) in enumerate(
-            ((queries.at[layer, 0], block_in), (right.at[layer], right_in), (left.at[layer], left_in))
-        )
+def condition_scratch(layers, count, width):
+    pairs = width // LANES
+    return [
+        pltpu.VMEM((layers, 2, pairs * count, LANES), jnp.float32),
+        pltpu.VMEM((layers, count // 2, 2 * pairs, LANES), jnp.float32),
+        pltpu.VMEM((layers, pairs * count, LANES), jnp.float32),
     ]
-    for copy in copies:
-        copy.start()
+
+
+def condition_kernel(queries, left, right, own, mine, block_in, left_in, right_in, spread, stacked, placed, arrived):
+    layers = queries.shape[0]
+    copies = []
+    for k, (source, target) in enumerate(((left, left_in), (right, right_in), (queries.at[:, 0], block_in))):
+        copies.append(pltpu.make_async_copy(source, target, arrived.at[k]))
+        copies[-1].start()
     for copy in copies:
         copy.wait()
-
-    def put(k, tile):
-        out[:, k * LANES : (k + 1) * LANES] = tile
-
-    condition_block(block_in[...], left_in[...], right_in[...], put, spread, stacked, placed)
-
-
-def condition_layer(other, queries, left_factor, right_factor):
-    _, _, count, width = queries.shape
-    pairs = width // LANES
+    for layer in range(layers):
+
+        def put(k, tile):
+            own[layer, :, k * LANES : (k + 1) * LANES] = tile
+
+        condition_block(
+            block_in[layer],
+            left_in[layer],
+            right_in[layer],
+            put,
+            spread.at[layer],
+            stacked.at[layer],
+            placed.at[layer],
+        )
+    mine[...] = own[lax.axis_index("parts")]
+
+
+def condition_near(queries, left_factor, right_factor):
+    layers, _, count, width = queries.shape
+    spec = pl.BlockSpec(memory_space=pltpu.VMEM)
     far = pl.BlockSpec(memory_space=pltpu.HBM)
     return pl.pallas_call(
-        functools.partial(condition_kernel, other),
-        out_shape=jax.ShapeDtypeStruct((count, width), jnp.bfloat16),
+        condition_kernel,
+        out_shape=[
+            jax.ShapeDtypeStruct((layers, count, width), jnp.bfloat16),
+            jax.ShapeDtypeStruct((count, width), jnp.bfloat16),
+        ],
         in_specs=[far] * 3,
-        out_specs=pl.BlockSpec(memory_space=pltpu.VMEM),
+        out_specs=[spec] * 2,
         scratch_shapes=[
-            pltpu.VMEM((count, width), jnp.bfloat16),
-            pltpu.VMEM(left_factor.shape[1:], jnp.float32),
-            pltpu.VMEM(right_factor.shape[1:], jnp.float32),
-            pltpu.VMEM((2, pairs * count, LANES), jnp.float32),
-            pltpu.VMEM((count // 2, 2 * pairs, LANES), jnp.float32),
-            pltpu.VMEM((pairs * count, LANES), jnp.float32),
+            pltpu.VMEM((layers, count, width), jnp.bfloat16),
+            pltpu.VMEM(left_factor.shape, jnp.float32),
+            pltpu.VMEM(right_factor.shape, jnp.float32),
+            *condition_scratch(layers, count, width),
             pltpu.SemaphoreType.DMA((3,)),
         ],
         compiler_params=pltpu.CompilerParams(vmem_limit_bytes=8 * 2**20),
-        cost_estimate=pl.CostEstimate(flops=2**27, bytes_accessed=2**19, transcendentals=0),
-        name="condition_other" if other else "condition_mine",
+        cost_estimate=pl.CostEstimate(flops=2**28, bytes_accessed=2**20, transcendentals=0),
+        name="condition",
     )(*(pltpu.with_memory_space_constraint(x, pltpu.HBM) for x in (queries, left_factor, right_factor)))
 
 
-def along_columns(value, step):
-    pairs = [
-        (((k + step) % COLUMNS) * PAIR + c, k * PAIR + c)
-        for k in range(COLUMNS)
-        for c in range(PAIR)
-    ]
+def along_columns(value, *steps):
+    pairs = [(a * PAIR + c, b * PAIR + c) for a, b in steps for c in range(PAIR)]
     return lax.ppermute(value, "train", pairs)
 
 
@@ -155,7 +166,7 @@
         out_specs=pl.BlockSpec(memory_space=pltpu.VMEM),
         scratch_shapes=[pltpu.SemaphoreType.DMA],
         compiler_params=pltpu.CompilerParams(vmem_limit_bytes=6 * 2**20),
-        cost_estimate=pl.CostEstimate(flops=0, bytes_accessed=2 * value.size * 2, transcendentals=0),
+        cost_estimate=pl.CostEstimate(flops=0, bytes_accessed=2**23, transcendentals=0),
         name="near",
     )(pltpu.with_memory_space_constraint(value, pltpu.HBM))
 
@@ -185,15 +196,17 @@
     blocks, (scores, table, terms) = refs[:-3], refs[-3:]
     part = lax.axis_index("parts")
     column, core = place()
-    count = blocks[0].shape[0]
+    count = blocks[0].shape[1]
 
     def put(layer, step, twin, block):
         member = lax.rem(column + step, COLUMNS) * PAIR + (1 - core if twin else core)
         table[layer, pl.ds(pl.multiple_of(member * count, count), count), :] = block
 
     for twin in range(PAIR):
+        for layer in range(table.shape[0]):
+            put(layer, 0, twin, blocks[twin][layer])
         for k, (layer, step) in enumerate(
-            ((part, 0), (1 - part, 0), (part, 2), (part, 1), (part, 3), (1 - part, 2), (1 - part, 1), (1 - part, 3))
+            ((part, 2), (part, 1), (part, 3), (1 - part, 2), (1 - part, 1), (1 - part, 3)), 1
         ):
             put(layer, step, twin, blocks[PAIR * k + twin][...])
     row_scores(train, table, 1 - lax.axis_index("layer"), terms, scores)
@@ -223,21 +236,23 @@
     total = count * COLUMNS * PAIR
     share = rows // 2
 
-    mine = condition_layer(False, queries, left_factor, right_factor)
-    other = condition_layer(True, queries, left_factor, right_factor)
+    own, mine = condition_near(queries, left_factor, right_factor)
     near = copy_near(train_grads)
-    s2 = along_columns(mine, 2)
-    s1 = along_columns(mine, 1)
-    s3 = along_columns(mine, 3)
-    s1, other = lax.optimization_barrier((s1, other))
-    s3, near = lax.optimization_barrier((s3, near))
+    column, _ = place()
+    before = along_columns(mine, (0, 1), (1, 2), (2, 3))
+    after = along_columns(mine, (3, 2), (2, 1), (1, 0))
+    ends = along_columns(mine, (0, 3), (3, 0))
+    passed = jnp.where(column == 1, after, jnp.where(column == 2, before, mine))
+    s2 = along_columns(passed, (0, 2), (2, 3), (3, 1), (1, 0))
+    before, after, ends, near = lax.optimization_barrier((before, after, ends, near))
+    s1 = jnp.where(column == 3, ends, after)
+    s3 = jnp.where(column == 0, ends, before)
     y1 = other_part(s1)
     y3 = other_part(s3)
-    s2, y1, y3 = lax.optimization_barrier((s2, y1, y3))
     y2 = other_part(s2)
 
     blocks = []
-    for block in (mine, other, s2, s1, s3, y2, y1, y3):
+    for block in (own, s2, s1, s3, y2, y1, y3):
         blocks += [block, other_core(block)]
     f32 = functools.partial(jax.ShapeDtypeStruct, dtype=jnp.float32)
     terms = [pltpu.VMEM((layer_count, share * layer_count, total), jnp.float32)]

time: 32.6 us -> 36.5 us (1.12)
  starting transfers between devices: 13.8 us -> 17.2 us
  waiting for transfers between devices: 10.3 us -> 11.6 us
  Pallas kernels: 7.58 us -> 6.62 us
    ppermute x3 -> x4, starting transfers between devices: 6.11 us -> 11 us  [along_columns(): return lax.ppermute(value, 'train', pairs)]
    ppermute x3, waiting for transfers between devices: 4.16 us -> 5.34 us  [other_part(): return lax.ppermute(value, 'parts', [(0, 1), (1, 0)])]
    pallas_call x2 -> x1, Pallas kernels: 3.55 us -> 2.58 us  [condition_near(): pl.pallas_call(condition_kernel, out_shape=[jax.ShapeDtypeStruct((layers,...]
    ppermute x8 -> x7, starting transfers between devices: 1.54 us -> 0.59 us  [other_core(): lax.ppermute(value, 'train', [(k, k ^ 1) for k in range(COLUMNS * PAIR)])]
    ppermute x3, starting transfers between devices: 4.63 us -> 3.72 us  [other_part(): return lax.ppermute(value, 'parts', [(0, 1), (1, 0)])]
    ppermute x3 -> x4, waiting for transfers between devices: 2.84 us -> 3.36 us  [along_columns(): return lax.ppermute(value, 'train', pairs)]
    ppermute x8 -> x7, waiting for transfers between devices: 1.33 us -> 1.33 us  [other_core(): lax.ppermute(value, 'train', [(k, k ^ 1) for k in range(COLUMNS * PAIR)])]
  transfers between devices with their start and end apart: 15 -> 15, of which waited for: 6 -> 7; matrix products, arithmetic and copies ran while one was open for 0% -> 0% of each run, Pallas kernels for 15% -> 8%
where the time goes in v12:
time: 36.5 us; the launch traced here: 36.2 us
  starting transfers between devices  17.2 us (47%)
  waiting for transfers between devices  11.6 us (32%)
  Pallas kernels  6.62 us (18%)
  other arithmetic  0.68 us (2%)
    ppermute x4, starting transfers between devices, along_columns(): return lax.ppermute(value, 'train', pairs)  11 us
    ppermute x3, waiting for transfers between devices, other_part(): return lax.ppermute(value, 'parts', [(0, 1), (1, 0)])  5.34 us
    ppermute x3, starting transfers between devices, other_part(): return lax.ppermute(value, 'parts', [(0, 1), (1, 0)])  3.72 us
    ppermute x4, waiting for transfers between devices, along_columns(): return lax.ppermute(value, 'train', pairs)  3.36 us
    pallas_call x1, Pallas kernels, condition_near(): pl.pallas_call(condition_kernel, out_shape=[jax.ShapeDtypeStruct((layers,...  2.58 us
    pallas_call x1, Pallas kernels, copy_near(): pl.pallas_call(copy_kernel, out_shape=jax.ShapeDtypeStruct(value.shape, v...  2.2 us
    ppermute x1, starting transfers between devices, direct(): received = lax.ppermute(sent, 'layer', [(0, 1), (1, 0)])  1.88 us
    pallas_call x2, Pallas kernels, local_call(): pl.pallas_call(kernel, out_shape=out_shape, in_specs=[spec] * len(operand...  1.84 us
  transfers between devices with their start and end apart: 15, of which 7 were waited for; matrix products, arithmetic and copies ran while one was open for 0% of the time, Pallas kernels for 8%

profile of v12, /device:TPU:0, one launch (start us, length us, event | category | flops | bytes accessed | tf_op | source)
XLA Modules:
  0.0 36.2 jit_solution(8592022005745183998)
XLA Ops:
  0.0 2.6 %condition.1 = (bf16[2,16,4096]{2,1,0:T(8,128)(2,1)S(1)}, bf16[16,4096]{1,0:T(8,128)(2,1)S(1)}) custom-call(bf16[2,1,16,4096]{3,2,1,0:T(8,128)(2,1)} %queries.1, f32[2,64,64]{2,1,0:T(8,128)} %left.1, f32[2,64,64]{2,1,0:T(8,128)} %right.1), custom_call_target="tpu_custom_call" | custom-call | flops 268435456 | bytes 1048576 | tf_op jit(solution)/shard_map/condition/pallas_call | solution.py:121
  2.6 1.3 %collective-permute-start.1 = (bf16[16,4096]{1,0:T(8,128)(2,1)S(1)}, bf16[16,4096]{1,0:T(8,128)(2,1)S(1)}, u32[]{:S(2)}, u32[]{:S(2)}) collective-permute-start(bf16[16,4096]{1,0:T(8,128)(2,1)S(1)} %get-tuple-element.13), channel_id=1, source_target_pairs={{12,8},{14,10},{8,4},{10,6},{4,0},{6,2},{13,9},{15,11},{9,5},{11,7... | collective-permute-start | bytes 393224 | tf_op jit(solution)/shard_map/ppermute | solution.py:144
  3.9 5.6 %collective-permute-start = (bf16[16,4096]{1,0:T(8,128)(2,1)S(1)}, bf16[16,4096]{1,0:T(8,128)(2,1)S(1)}, u32[]{:S(2)}, u32[]{:S(2)}) collective-permute-start(bf16[16,4096]{1,0:T(8,128)(2,1)S(1)} %get-tuple-element.13), channel_id=1, source_target_pairs={{0,4},{2,6},{4,8},{6,10},{8,12},{10,14},{1,5},{3,7},{5,9},{7,11},{... | collective-permute-start | bytes 393224 | tf_op jit(solution)/shard_map/ppermute | solution.py:144
  9.5 3.8 %collective-permute-start.2 = (bf16[16,4096]{1,0:T(8,128)(2,1)S(1)}, bf16[16,4096]{1,0:T(8,128)(2,1)S(1)}, u32[]{:S(2)}, u32[]{:S(2)}) collective-permute-start(bf16[16,4096]{1,0:T(8,128)(2,1)S(1)} %get-tuple-element.13), channel_id=1, source_target_pairs={{0,12},{2,14},{12,0},{14,2},{1,13},{3,15},{13,1},{15,3},{16,28},{1... | collective-permute-start | bytes 393224 | tf_op jit(solution)/shard_map/ppermute | solution.py:144
  13.2 0.1 collective-permute-start.3
  13.3 2.2 %near.1.train = bf16[256,2,4096]{2,1,0:T(2,128)(2,1)S(1)} custom-call(bf16[256,2,4096]{2,1,0:T(2,128)(2,1)} %source.1), custom_call_target="tpu_custom_call" | custom-call | bytes 8388608 | tf_op jit(solution)/shard_map/near/pallas_call | solution.py:162
  15.5 0.0 collective-permute-done.1
  15.5 0.0 collective-permute-done
  15.6 0.3 collective-permute-start.4
  15.9 2.2 %collective-permute-done.2 = bf16[16,4096]{1,0:T(8,128)(2,1)S(1)} collective-permute-done((bf16[16,4096]{1,0:T(8,128)(2,1)S(1)}, bf16[16,4096]{1,0:T(8,128)(2,1)S(1)}, u32[]{:S(2)}, u32[]{:S(2)}) %collective-permute-start.2) | collective-permute-done | bytes 131104 | tf_op jit(solution)/shard_map/ppermute | solution.py:144
  18.1 2.0 %collective-permute-start.12 = (bf16[16,4096]{1,0:T(8,128)(2,1)S(1)}, bf16[16,4096]{1,0:T(8,128)(2,1)S(1)}, u32[]{:S(2)}, u32[]{:S(2)}) collective-permute-start(bf16[16,4096]{1,0:T(8,128)(2,1)S(1)} %get-tuple-element.21.refs_6_), channel_id=1, source_target_pairs={{0,16},{16,0},{1,17},{17,1},{2,18},{18,2},{3,19},{19,3},{4,20},{20... | collective-permute-start | bytes 393224 | tf_op jit(solution)/shard_map/ppermute | solution.py:152
  20.2 0.0 collective-permute-start.7
  20.2 0.2 collective-permute-start.10
  20.3 1.2 %collective-permute-done.4.refs_2_ = bf16[16,4096]{1,0:T(8,128)(2,1)S(1)} collective-permute-done((bf16[16,4096]{1,0:T(8,128)(2,1)S(1)}, bf16[16,4096]{1,0:T(8,128)(2,1)S(1)}, u32[]{:S(2)}, u32[]{:S(2)}) %collective-permute-start.4) | collective-permute-done | bytes 131104 | tf_op jit(solution)/shard_map/ppermute | solution.py:144
  21.5 1.5 %collective-permute-start.8 = (bf16[16,4096]{1,0:T(8,128)(2,1)S(1)}, bf16[16,4096]{1,0:T(8,128)(2,1)S(1)}, u32[]{:S(2)}, u32[]{:S(2)}) collective-permute-start(bf16[16,4096]{1,0:T(8,128)(2,1)S(1)} %collective-permute-done.4.refs_2_), channel_id=1, source_target_pairs={{0,16},{16,0},{1,17},{17,1},{2,18},{18,2},{3,19},{19,3},{4,20},{20... | collective-permute-start | bytes 393224 | tf_op jit(solution)/shard_map/ppermute | solution.py:152
  23.0 0.0 collective-permute-done.3.refs_1_
  23.0 0.0 collective-permute-start.6
  23.0 1.0 %collective-permute-done.12.refs_12_ = bf16[16,4096]{1,0:T(8,128)(2,1)S(1)} collective-permute-done((bf16[16,4096]{1,0:T(8,128)(2,1)S(1)}, bf16[16,4096]{1,0:T(8,128)(2,1)S(1)}, u32[]{:S(2)}, u32[]{:S(2)}) %collective-permute-start.12) | collective-permute-done | bytes 131104 | tf_op jit(solution)/shard_map/ppermute | solution.py:152
  24.1 0.0 collective-permute-start.5
  24.1 0.0 collective-permute-done.7.refs_7_
  24.1 0.5 %collective-permute-start.13 = (bf16[16,4096]{1,0:T(8,128)(2,1)S(1)}, bf16[16,4096]{1,0:T(8,128)(2,1)S(1)}, u32[]{:S(2)}, u32[]{:S(2)}) collective-permute-start(bf16[16,4096]{1,0:T(8,128)(2,1)S(1)} %collective-permute-done.12.refs_12_), channel_id=1, source_target_pairs={{0,2},{2,0},{4,6},{6,4},{8,10},{10,8},{12,14},{14,12},{1,3},{3,1},... | collective-permute-start | bytes 393224 | tf_op jit(solution)/shard_map/ppermute | solution.py:148
  24.6 2.1 %collective-permute-done.10.refs_10_ = bf16[16,4096]{1,0:T(8,128)(2,1)S(1)} collective-permute-done((bf16[16,4096]{1,0:T(8,128)(2,1)S(1)}, bf16[16,4096]{1,0:T(8,128)(2,1)S(1)}, u32[]{:S(2)}, u32[]{:S(2)}) %collective-permute-start.10) | collective-permute-done | bytes 131104 | tf_op jit(solution)/shard_map/ppermute | solution.py:152
  26.7 0.0 collective-permute-start.11
  26.7 2.2 %collective-permute-done.8.refs_8_ = bf16[16,4096]{1,0:T(8,128)(2,1)S(1)} collective-permute-done((bf16[16,4096]{1,0:T(8,128)(2,1)S(1)}, bf16[16,4096]{1,0:T(8,128)(2,1)S(1)}, u32[]{:S(2)}, u32[]{:S(2)}) %collective-permute-start.8) | collective-permute-done | bytes 131104 | tf_op jit(solution)/shard_map/ppermute | solution.py:152
  28.9 0.0 collective-permute-start.9
  28.9 0.0 collective-permute-done.6.refs_5_
  28.9 0.0 collective-permute-done.5.refs_3_
  28.9 0.0 collective-permute-done.13.refs_13_
  28.9 0.0 collective-permute-done.11.refs_11_
  28.9 1.3 %collective-permute-done.9.refs_9_ = bf16[16,4096]{1,0:T(8,128)(2,1)S(1)} collective-permute-done((bf16[16,4096]{1,0:T(8,128)(2,1)S(1)}, bf16[16,4096]{1,0:T(8,128)(2,1)S(1)}, u32[]{:S(2)}, u32[]{:S(2)}) %collective-permute-start.9) | collective-permute-done | bytes 131104 | tf_op jit(solution)/shard_map/ppermute | solution.py:148
  30.3 1.0 %scores_sent.1 = (f32[128,128]{1,0:T(8,128)S(1)}, bf16[2,128,4096]{2,1,0:T(8,128)(2,1)S(1)}) custom-call(bf16[256,2,4096]{2,1,0:T(2,128)(2,1)S(1)} %near.1.train, bf16[2,16,4096]{2,1,0:T(8,128)(2,1)S(1)} %get-tuple-element.15.refs_0_, bf16[2,16,4096]{2,1,0:T(8,128)(2,1)S(1)} %collective-permute-done.3.refs_1_, ...), custom_call_target="tpu_custom_call" | custom-call | flops 536870912 | bytes 4194304 | tf_op jit(solution)/shard_map/scores_sent/pallas_call | solution.py:221
  31.3 1.9 %collective-permute-start.14 = (f32[128,128]{1,0:T(8,128)S(1)}, f32[128,128]{1,0:T(8,128)S(1)}, u32[]{:S(2)}, u32[]{:S(2)}) collective-permute-start(f32[128,128]{1,0:T(8,128)S(1)} %get-tuple-element.20), channel_id=1, source_target_pairs={{0,1},{1,0},{2,3},{3,2},{4,5},{5,4},{6,7},{7,6},{8,9},{9,8},{10,11... | collective-permute-start | bytes 196616 | tf_op jit(solution)/shard_map/ppermute | solution.py:267
  33.1 0.8 %scores_kept.1 = f32[128,128]{1,0:T(8,128)S(1)} custom-call(bf16[256,2,4096]{2,1,0:T(2,128)(2,1)S(1)} %near.1.train, bf16[2,128,4096]{2,1,0:T(8,128)(2,1)S(1)} %get-tuple-element.19.table), custom_call_target="tpu_custom_call" | custom-call | flops 536870912 | bytes 4194304 | tf_op jit(solution)/shard_map/scores_kept/pallas_call | solution.py:221
  34.0 1.6 %collective-permute-done.14 = f32[128,128]{1,0:T(8,128)S(1)} collective-permute-done((f32[128,128]{1,0:T(8,128)S(1)}, f32[128,128]{1,0:T(8,128)S(1)}, u32[]{:S(2)}, u32[]{:S(2)}) %collective-permute-start.14) | collective-permute-done | bytes 65568 | tf_op jit(solution)/shard_map/ppermute | solution.py:267
  35.6 0.6 %add.4 = f32[128,128]{1,0:T(8,128)} add(f32[128,128]{1,0:T(8,128)S(1)} %scores_kept.1, f32[128,128]{1,0:T(8,128)S(1)} %collective-permute-done.14) | non-fusion elementwise | flops 16384 | bytes 196608 | tf_op jit(solution)/shard_map/add | solution.py:269
  (2 shorter events, 0.0 us)
Async XLA Ops:
  2.6 12.9 %collective-permute-start.1 = (bf16[16,4096]{1,0:T(8,128)(2,1)S(1)}, bf16[16,4096]{1,0:T(8,128)(2,1)S(1)}, u32[]{:S(2)}, u32[]{:S(2)}) collective-permute-start(bf16[16,4096]{1,0:T(8,128)(2,1)S(1)} %get-tuple-element.13), channel_id=1, source_target_pairs={{12,8},{14,10},{8,4},{10,6},{4,0},{6,2},{13,9},{15,11},{9,5},{11,7... | collective-permute-start | bytes 393224 | tf_op jit(solution)/shard_map/ppermute | solution.py:144
  3.9 11.7 %collective-permute-start = (bf16[16,4096]{1,0:T(8,128)(2,1)S(1)}, bf16[16,4096]{1,0:T(8,128)(2,1)S(1)}, u32[]{:S(2)}, u32[]{:S(2)}) collective-permute-start(bf16[16,4096]{1,0:T(8,128)(2,1)S(1)} %get-tuple-element.13), channel_id=1, source_target_pairs={{0,4},{2,6},{4,8},{6,10},{8,12},{10,14},{1,5},{3,7},{5,9},{7,11},{... | collective-permute-start | bytes 393224 | tf_op jit(solution)/shard_map/ppermute | solution.py:144
  9.5 8.7 %collective-permute-start.2 = (bf16[16,4096]{1,0:T(8,128)(2,1)S(1)}, bf16[16,4096]{1,0:T(8,128)(2,1)S(1)}, u32[]{:S(2)}, u32[]{:S(2)}) collective-permute-start(bf16[16,4096]{1,0:T(8,128)(2,1)S(1)} %get-tuple-element.13), channel_id=1, source_target_pairs={{0,12},{2,14},{12,0},{14,2},{1,13},{3,15},{13,1},{15,3},{16,28},{1... | collective-permute-start | bytes 393224 | tf_op jit(solution)/shard_map/ppermute | solution.py:144
  13.2 9.8 %collective-permute-start.3 = (bf16[2,16,4096]{2,1,0:T(8,128)(2,1)S(1)}, bf16[2,16,4096]{2,1,0:T(8,128)(2,1)S(1)}, u32[]{:S(2)}, u32[]{:S(2)}) collective-permute-start(bf16[2,16,4096]{2,1,0:T(8,128)(2,1)S(1)} %get-tuple-element.15.refs_0_), channel_id=1, source_target_pairs={{0,2},{2,0},{4,6},{6,4},{8,10},{10,8},{12,14},{14,12},{1,3},{3,1},... | collective-permute-start | bytes 786440 | tf_op jit(solution)/shard_map/ppermute | solution.py:148
  15.6 5.9 %collective-permute-start.4 = (bf16[16,4096]{1,0:T(8,128)(2,1)S(1)}, bf16[16,4096]{1,0:T(8,128)(2,1)S(1)}, u32[]{:S(2)}, u32[]{:S(2)}) collective-permute-start(bf16[16,4096]{1,0:T(8,128)(2,1)S(1)} %select_select_fusion), channel_id=1, source_target_pairs={{0,8},{2,10},{8,12},{10,14},{12,4},{14,6},{4,0},{6,2},{1,9},{3,11}... | collective-permute-start | bytes 393224 | tf_op jit(solution)/shard_map/ppermute | solution.py:144
  18.1 5.9 %collective-permute-start.12 = (bf16[16,4096]{1,0:T(8,128)(2,1)S(1)}, bf16[16,4096]{1,0:T(8,128)(2,1)S(1)}, u32[]{:S(2)}, u32[]{:S(2)}) collective-permute-start(bf16[16,4096]{1,0:T(8,128)(2,1)S(1)} %get-tuple-element.21.refs_6_), channel_id=1, source_target_pairs={{0,16},{16,0},{1,17},{17,1},{2,18},{18,2},{3,19},{19,3},{4,20},{20... | collective-permute-start | bytes 393224 | tf_op jit(solution)/shard_map/ppermute | solution.py:152
  20.2 3.9 %collective-permute-start.7 = (bf16[16,4096]{1,0:T(8,128)(2,1)S(1)}, bf16[16,4096]{1,0:T(8,128)(2,1)S(1)}, u32[]{:S(2)}, u32[]{:S(2)}) collective-permute-start(bf16[16,4096]{1,0:T(8,128)(2,1)S(1)} %get-tuple-element.21.refs_6_), channel_id=1, source_target_pairs={{0,2},{2,0},{4,6},{6,4},{8,10},{10,8},{12,14},{14,12},{1,3},{3,1},... | collective-permute-start | bytes 393224 | tf_op jit(solution)/shard_map/ppermute | solution.py:148
  20.2 6.5 %collective-permute-start.10 = (bf16[16,4096]{1,0:T(8,128)(2,1)S(1)}, bf16[16,4096]{1,0:T(8,128)(2,1)S(1)}, u32[]{:S(2)}, u32[]{:S(2)}) collective-permute-start(bf16[16,4096]{1,0:T(8,128)(2,1)S(1)} %get-tuple-element.22.refs_4_), channel_id=1, source_target_pairs={{0,16},{16,0},{1,17},{17,1},{2,18},{18,2},{3,19},{19,3},{4,20},{20... | collective-permute-start | bytes 393224 | tf_op jit(solution)/shard_map/ppermute | solution.py:152
  21.5 7.4 %collective-permute-start.8 = (bf16[16,4096]{1,0:T(8,128)(2,1)S(1)}, bf16[16,4096]{1,0:T(8,128)(2,1)S(1)}, u32[]{:S(2)}, u32[]{:S(2)}) collective-permute-start(bf16[16,4096]{1,0:T(8,128)(2,1)S(1)} %collective-permute-done.4.refs_2_), channel_id=1, source_target_pairs={{0,16},{16,0},{1,17},{17,1},{2,18},{18,2},{3,19},{19,3},{4,20},{20... | collective-permute-start | bytes 393224 | tf_op jit(solution)/shard_map/ppermute | solution.py:152
  23.0 5.9 %collective-permute-start.6 = (bf16[16,4096]{1,0:T(8,128)(2,1)S(1)}, bf16[16,4096]{1,0:T(8,128)(2,1)S(1)}, u32[]{:S(2)}, u32[]{:S(2)}) collective-permute-start(bf16[16,4096]{1,0:T(8,128)(2,1)S(1)} %get-tuple-element.22.refs_4_), channel_id=1, source_target_pairs={{0,2},{2,0},{4,6},{6,4},{8,10},{10,8},{12,14},{14,12},{1,3},{3,1},... | collective-permute-start | bytes 393224 | tf_op jit(solution)/shard_map/ppermute | solution.py:148
  24.1 4.8 %collective-permute-start.5 = (bf16[16,4096]{1,0:T(8,128)(2,1)S(1)}, bf16[16,4096]{1,0:T(8,128)(2,1)S(1)}, u32[]{:S(2)}, u32[]{:S(2)}) collective-permute-start(bf16[16,4096]{1,0:T(8,128)(2,1)S(1)} %collective-permute-done.4.refs_2_), channel_id=1, source_target_pairs={{0,2},{2,0},{4,6},{6,4},{8,10},{10,8},{12,14},{14,12},{1,3},{3,1},... | collective-permute-start | bytes 393224 | tf_op jit(solution)/shard_map/ppermute | solution.py:148
  24.1 4.8 %collective-permute-start.13 = (bf16[16,4096]{1,0:T(8,128)(2,1)S(1)}, bf16[16,4096]{1,0:T(8,128)(2,1)S(1)}, u32[]{:S(2)}, u32[]{:S(2)}) collective-permute-start(bf16[16,4096]{1,0:T(8,128)(2,1)S(1)} %collective-permute-done.12.refs_12_), channel_id=1, source_target_pairs={{0,2},{2,0},{4,6},{6,4},{8,10},{10,8},{12,14},{14,12},{1,3},{3,1},... | collective-permute-start | bytes 393224 | tf_op jit(solution)/shard_map/ppermute | solution.py:148
  26.7 2.2 %collective-permute-start.11 = (bf16[16,4096]{1,0:T(8,128)(2,1)S(1)}, bf16[16,4096]{1,0:T(8,128)(2,1)S(1)}, u32[]{:S(2)}, u32[]{:S(2)}) collective-permute-start(bf16[16,4096]{1,0:T(8,128)(2,1)S(1)} %collective-permute-done.10.refs_10_), channel_id=1, source_target_pairs={{0,2},{2,0},{4,6},{6,4},{8,10},{10,8},{12,14},{14,12},{1,3},{3,1},... | collective-permute-start | bytes 393224 | tf_op jit(solution)/shard_map/ppermute | solution.py:148
  28.9 1.3 %collective-permute-start.9 = (bf16[16,4096]{1,0:T(8,128)(2,1)S(1)}, bf16[16,4096]{1,0:T(8,128)(2,1)S(1)}, u32[]{:S(2)}, u32[]{:S(2)}) collective-permute-start(bf16[16,4096]{1,0:T(8,128)(2,1)S(1)} %collective-permute-done.8.refs_8_), channel_id=1, source_target_pairs={{0,2},{2,0},{4,6},{6,4},{8,10},{10,8},{12,14},{14,12},{1,3},{3,1},... | collective-permute-start | bytes 393224 | tf_op jit(solution)/shard_map/ppermute | solution.py:148
  31.3 4.3 %collective-permute-start.14 = (f32[128,128]{1,0:T(8,128)S(1)}, f32[128,128]{1,0:T(8,128)S(1)}, u32[]{:S(2)}, u32[]{:S(2)}) collective-permute-start(f32[128,128]{1,0:T(8,128)S(1)} %get-tuple-element.20), channel_id=1, source_target_pairs={{0,1},{1,0},{2,3},{3,2},{4,5},{5,4},{6,7},{7,6},{8,9},{9,8},{10,11... | collective-permute-start | bytes 196616 | tf_op jit(solution)/shard_map/ppermute | solution.py:267

commit v13 on v7

--- a/solution.py
+++ b/solution.py
@@ -124,21 +124,18 @@
     )(*(pltpu.with_memory_space_constraint(x, pltpu.HBM) for x in (queries, left_factor, right_factor)))
 
 
-def along_columns(value, step):
-    pairs = [
-        (((k + step) % COLUMNS) * PAIR + c, k * PAIR + c)
-        for k in range(COLUMNS)
-        for c in range(PAIR)
-    ]
-    return lax.ppermute(value, "train", pairs)
+def along_columns(value, flip):
+    return lax.ppermute(value, "train", [(k, k ^ (flip * PAIR)) for k in range(COLUMNS * PAIR)])
 
 
 def other_core(value):
     return lax.ppermute(value, "train", [(k, k ^ 1) for k in range(COLUMNS * PAIR)])
 
 
-def other_part(value):
-    return lax.ppermute(value, "parts", [(0, 1), (1, 0)])
+def other_part(value, cross=False):
+    train = COLUMNS * PAIR
+    pairs = [(part * train + k, (1 - part) * train + (k ^ cross)) for part in range(2) for k in range(train)]
+    return lax.ppermute(value, ("parts", "train"), pairs)
 
 
 def copy_kernel(source, target, done):
@@ -187,15 +184,24 @@
     column, core = place()
     count = blocks[0].shape[0]
 
-    def put(layer, step, twin, block):
-        member = lax.rem(column + step, COLUMNS) * PAIR + (1 - core if twin else core)
+    def put(layer, flip, other, block):
+        member = (column ^ flip) * PAIR + (core ^ other)
         table[layer, pl.ds(pl.multiple_of(member * count, count), count), :] = block
 
     for twin in range(PAIR):
-        for k, (layer, step) in enumerate(
-            ((part, 0), (1 - part, 0), (part, 2), (part, 1), (part, 3), (1 - part, 2), (1 - part, 1), (1 - part, 3))
+        for k, (layer, flip, cross) in enumerate(
+            (
+                (part, 0, 0),
+                (1 - part, 0, 0),
+                (part, 2, 0),
+                (part, 1, 0),
+                (part, 3, 0),
+                (1 - part, 2, 0),
+                (1 - part, 1, 1),
+                (1 - part, 3, 0),
+            )
         ):
-            put(layer, step, twin, blocks[PAIR * k + twin][...])
+            put(layer, flip, twin ^ cross, blocks[PAIR * k + twin][...])
     row_scores(train, table, 1 - lax.axis_index("layer"), terms, scores)
 
 
@@ -230,9 +236,9 @@
     s2 = along_columns(mine_late, 2)
     s1 = along_columns(mine, 1)
     s3 = along_columns(mine, 3)
+    y1 = other_part(s1, cross=True)
+    y3 = other_part(s3)
     y2 = other_part(s2)
-    y1 = other_part(s1)
-    y3 = other_part(s3)
     y1, y3, near = lax.optimization_barrier((y1, y3, near))
 
     blocks = []

time: 32 us -> 30.7 us (0.959)
  waiting for transfers between devices: 9.23 us -> 8.38 us
  starting transfers between devices: 14.3 us -> 13.9 us
    ppermute x6, waiting for transfers between devices: 6.22 us -> 5.36 us  [the longest x3 5.22 us: along_columns(): lax.ppermute(value, 'train', [(k, k ^ flip * PAIR) for k in range(COLUMNS...]
    ppermute x6, starting transfers between devices: 10.6 us -> 9.78 us  [the longest x3 5.82 us: along_columns(): lax.ppermute(value, 'train', [(k, k ^ flip * PAIR) for k in range(COLUMNS...]
    ppermute x8, starting transfers between devices: 2.11 us -> 2.52 us  [other_core(): lax.ppermute(value, 'train', [(k, k ^ 1) for k in range(COLUMNS * PAIR)])]
  transfers between devices with their start and end apart: 15 -> 15, of which waited for: 6 -> 8; matrix products, arithmetic and copies ran while one was open for 0% -> 0% of each run, Pallas kernels for 15% -> 16%
where the time goes in v13:
time: 30.7 us; the launch traced here: 30.5 us
  starting transfers between devices  13.9 us (45%)
  waiting for transfers between devices  8.38 us (27%)
  Pallas kernels  7.57 us (25%)
  other arithmetic  0.64 us (2%)
    ppermute x3, starting transfers between devices, along_columns(): lax.ppermute(value, 'train', [(k, k ^ flip * PAIR) for k in range(COLUMNS...  5.82 us
    ppermute x3, waiting for transfers between devices, along_columns(): lax.ppermute(value, 'train', [(k, k ^ flip * PAIR) for k in range(COLUMNS...  5.22 us
    ppermute x3, starting transfers between devices, other_part(): return lax.ppermute(value, ('parts', 'train'), pairs)  3.96 us
    pallas_call x2, Pallas kernels, condition_layer(): pl.pallas_call(functools.partial(condition_kernel, other), out_shape=jax....  3.53 us
    ppermute x8, starting transfers between devices, other_core(): lax.ppermute(value, 'train', [(k, k ^ 1) for k in range(COLUMNS * PAIR)])  2.52 us
    pallas_call x1, Pallas kernels, copy_near(): pl.pallas_call(copy_kernel, out_shape=jax.ShapeDtypeStruct(value.shape, v...  2.2 us
    ppermute x1, waiting for transfers between devices, direct(): received = lax.ppermute(sent, 'layer', [(0, 1), (1, 0)])  1.99 us
    pallas_call x2, Pallas kernels, local_call(): pl.pallas_call(kernel, out_shape=out_shape, in_specs=[spec] * len(operand...  1.84 us
  transfers between devices with their start and end apart: 15, of which 8 were waited for; matrix products, arithmetic and copies ran while one was open for 0% of the time, Pallas kernels for 16%

profile of v13, /device:TPU:0, one launch (start us, length us, event | category | flops | bytes accessed | tf_op | source)
XLA Modules:
  0.0 30.5 jit_solution(9682218490406508773)
XLA Ops:
  0.0 1.8 %condition_mine.1.refs_0_ = bf16[16,4096]{1,0:T(8,128)(2,1)S(1)} custom-call(bf16[2,1,16,4096]{3,2,1,0:T(8,128)(2,1)} %queries.3, f32[2,64,64]{2,1,0:T(8,128)} %left.3, f32[2,64,64]{2,1,0:T(8,128)} %right.3), custom_call_target="tpu_custom_call" | custom-call | flops 134217728 | bytes 524288 | tf_op jit(solution)/shard_map/condition_mine/pallas_call | solution.py:107
  1.8 5.1 %collective-permute-start.2 = (bf16[16,4096]{1,0:T(8,128)(2,1)S(1)}, bf16[16,4096]{1,0:T(8,128)(2,1)S(1)}, u32[]{:S(2)}, u32[]{:S(2)}) collective-permute-start(bf16[16,4096]{1,0:T(8,128)(2,1)S(1)} %condition_mine.1.refs_0_), channel_id=1, source_target_pairs={{0,12},{2,14},{4,8},{6,10},{8,4},{10,6},{12,0},{14,2},{1,13},{3,15... | collective-permute-start | bytes 393224 | tf_op jit(solution)/shard_map/ppermute | solution.py:128
  6.9 0.0 collective-permute-start
  6.9 1.8 %condition_other.1.refs_2_ = bf16[16,4096]{1,0:T(8,128)(2,1)S(1)} custom-call(bf16[2,1,16,4096]{3,2,1,0:T(8,128)(2,1)} %queries.3, f32[2,64,64]{2,1,0:T(8,128)} %left.3, f32[2,64,64]{2,1,0:T(8,128)} %right.3), custom_call_target="tpu_custom_call" | custom-call | flops 134217728 | bytes 524288 | tf_op jit(solution)/shard_map/condition_other/pallas_call | solution.py:107
  8.7 0.7 %collective-permute-start.6 = (bf16[16,4096]{1,0:T(8,128)(2,1)S(1)}, bf16[16,4096]{1,0:T(8,128)(2,1)S(1)}, u32[]{:S(2)}, u32[]{:S(2)}) collective-permute-start(bf16[16,4096]{1,0:T(8,128)(2,1)S(1)} %condition_mine.1.refs_0_), channel_id=1, source_target_pairs={{0,8},{2,10},{4,12},{6,14},{8,0},{10,2},{12,4},{14,6},{1,9},{3,11}... | collective-permute-start | bytes 393224 | tf_op jit(solution)/shard_map/ppermute | solution.py:128
  9.4 1.9 %collective-permute-done.2.refs_8_ = bf16[16,4096]{1,0:T(8,128)(2,1)S(1)} collective-permute-done((bf16[16,4096]{1,0:T(8,128)(2,1)S(1)}, bf16[16,4096]{1,0:T(8,128)(2,1)S(1)}, u32[]{:S(2)}, u32[]{:S(2)}) %collective-permute-start.2) | collective-permute-done | bytes 131104 | tf_op jit(solution)/shard_map/ppermute | solution.py:128
  11.3 1.7 %collective-permute-start.3 = (bf16[16,4096]{1,0:T(8,128)(2,1)S(1)}, bf16[16,4096]{1,0:T(8,128)(2,1)S(1)}, u32[]{:S(2)}, u32[]{:S(2)}) collective-permute-start(bf16[16,4096]{1,0:T(8,128)(2,1)S(1)} %collective-permute-done.2.refs_8_), channel_id=1, source_target_pairs={{0,16},{2,18},{4,20},{6,22},{8,24},{10,26},{12,28},{14,30},{16,0},... | collective-permute-start | bytes 393224 | tf_op jit(solution)/shard_map/ppermute | solution.py:138
  13.0 1.3 %collective-permute-done.refs_6_ = bf16[16,4096]{1,0:T(8,128)(2,1)S(1)} collective-permute-done((bf16[16,4096]{1,0:T(8,128)(2,1)S(1)}, bf16[16,4096]{1,0:T(8,128)(2,1)S(1)}, u32[]{:S(2)}, u32[]{:S(2)}) %collective-permute-start) | collective-permute-done | bytes 131104 | tf_op jit(solution)/shard_map/ppermute | solution.py:128
  14.3 0.7 %collective-permute-start.1 = (bf16[16,4096]{1,0:T(8,128)(2,1)S(1)}, bf16[16,4096]{1,0:T(8,128)(2,1)S(1)}, u32[]{:S(2)}, u32[]{:S(2)}) collective-permute-start(bf16[16,4096]{1,0:T(8,128)(2,1)S(1)} %collective-permute-done.refs_6_), channel_id=1, source_target_pairs={{0,18},{2,16},{4,22},{6,20},{8,26},{10,24},{12,30},{14,28},{16,2},... | collective-permute-start | bytes 393224 | tf_op jit(solution)/shard_map/ppermute | solution.py:138
  15.0 0.9 %collective-permute-start.5 = (bf16[16,4096]{1,0:T(8,128)(2,1)S(1)}, bf16[16,4096]{1,0:T(8,128)(2,1)S(1)}, u32[]{:S(2)}, u32[]{:S(2)}) collective-permute-start(bf16[16,4096]{1,0:T(8,128)(2,1)S(1)} %condition_other.1.refs_2_), channel_id=1, source_target_pairs={{0,2},{2,0},{4,6},{6,4},{8,10},{10,8},{12,14},{14,12},{1,3},{3,1},... | collective-permute-start | bytes 393224 | tf_op jit(solution)/shard_map/ppermute | solution.py:132
  15.9 0.0 collective-permute-start.4
  15.9 2.0 %collective-permute-done.6.refs_4_ = bf16[16,4096]{1,0:T(8,128)(2,1)S(1)} collective-permute-done((bf16[16,4096]{1,0:T(8,128)(2,1)S(1)}, bf16[16,4096]{1,0:T(8,128)(2,1)S(1)}, u32[]{:S(2)}, u32[]{:S(2)}) %collective-permute-start.6) | collective-permute-done | bytes 131104 | tf_op jit(solution)/shard_map/ppermute | solution.py:128
  18.0 1.5 %collective-permute-start.10 = (bf16[16,4096]{1,0:T(8,128)(2,1)S(1)}, bf16[16,4096]{1,0:T(8,128)(2,1)S(1)}, u32[]{:S(2)}, u32[]{:S(2)}) collective-permute-start(bf16[16,4096]{1,0:T(8,128)(2,1)S(1)} %collective-permute-done.6.refs_4_), channel_id=1, source_target_pairs={{0,16},{2,18},{4,20},{6,22},{8,24},{10,26},{12,28},{14,30},{16,0},... | collective-permute-start | bytes 393224 | tf_op jit(solution)/shard_map/ppermute | solution.py:138
  19.5 0.0 collective-permute-done.3.refs_14_
  19.5 0.0 collective-permute-start.7
  19.5 2.2 %near.1.train = bf16[256,2,4096]{2,1,0:T(2,128)(2,1)S(1)} custom-call(bf16[256,2,4096]{2,1,0:T(2,128)(2,1)} %source.1), custom_call_target="tpu_custom_call" | custom-call | bytes 8388608 | tf_op jit(solution)/shard_map/near/pallas_call | solution.py:148
  21.7 0.0 collective-permute-done.1.refs_12_
  21.7 0.6 %collective-permute-start.9 = (bf16[16,4096]{1,0:T(8,128)(2,1)S(1)}, bf16[16,4096]{1,0:T(8,128)(2,1)S(1)}, u32[]{:S(2)}, u32[]{:S(2)}) collective-permute-start(bf16[16,4096]{1,0:T(8,128)(2,1)S(1)} %collective-permute-done.2.refs_8_), channel_id=1, source_target_pairs={{0,2},{2,0},{4,6},{6,4},{8,10},{10,8},{12,14},{14,12},{1,3},{3,1},... | collective-permute-start | bytes 393224 | tf_op jit(solution)/shard_map/ppermute | solution.py:132
  22.3 0.0 collective-permute-done.5.refs_3_
  22.3 0.1 collective-permute-start.8
  22.4 0.0 collective-permute-done.4.refs_1_
  22.4 0.4 %collective-permute-start.12 = (bf16[16,4096]{1,0:T(8,128)(2,1)S(1)}, bf16[16,4096]{1,0:T(8,128)(2,1)S(1)}, u32[]{:S(2)}, u32[]{:S(2)}) collective-permute-start(bf16[16,4096]{1,0:T(8,128)(2,1)S(1)} %collective-permute-done.1.refs_12_), channel_id=1, source_target_pairs={{0,2},{2,0},{4,6},{6,4},{8,10},{10,8},{12,14},{14,12},{1,3},{3,1},... | collective-permute-start | bytes 393224 | tf_op jit(solution)/shard_map/ppermute | solution.py:132
  22.8 0.1 collective-permute-done.10.refs_10_
  22.9 0.0 collective-permute-start.11
  22.9 0.0 collective-permute-done.7.refs_5_
  22.9 0.5 %collective-permute-start.13 = (bf16[16,4096]{1,0:T(8,128)(2,1)S(1)}, bf16[16,4096]{1,0:T(8,128)(2,1)S(1)}, u32[]{:S(2)}, u32[]{:S(2)}) collective-permute-start(bf16[16,4096]{1,0:T(8,128)(2,1)S(1)} %collective-permute-done.3.refs_14_), channel_id=1, source_target_pairs={{0,2},{2,0},{4,6},{6,4},{8,10},{10,8},{12,14},{14,12},{1,3},{3,1},... | collective-permute-start | bytes 393224 | tf_op jit(solution)/shard_map/ppermute | solution.py:132
  23.4 0.0 collective-permute-done.9.refs_9_
  23.5 0.2 collective-permute-done.8.refs_7_
  23.6 0.6 %collective-permute-done.11.refs_11_ = bf16[16,4096]{1,0:T(8,128)(2,1)S(1)} collective-permute-done((bf16[16,4096]{1,0:T(8,128)(2,1)S(1)}, bf16[16,4096]{1,0:T(8,128)(2,1)S(1)}, u32[]{:S(2)}, u32[]{:S(2)}) %collective-permute-start.11) | collective-permute-done | bytes 131104 | tf_op jit(solution)/shard_map/ppermute | solution.py:132
  24.3 0.0 collective-permute-done.12.refs_13_
  24.3 0.2 collective-permute-done.13.refs_15_
  24.5 1.0 %scores_sent.1 = (f32[128,128]{1,0:T(8,128)S(1)}, bf16[2,128,4096]{2,1,0:T(8,128)(2,1)S(1)}) custom-call(bf16[256,2,4096]{2,1,0:T(2,128)(2,1)S(1)} %near.1.train, bf16[16,4096]{1,0:T(8,128)(2,1)S(1)} %condition_mine.1.refs_0_, bf16[16,4096]{1,0:T(8,128)(2,1)S(1)} %collective-permute-done.4.refs_1_, bf16[16,4096]{1,0:T(8,128)(2,1)S(1)} %condition_other.1.refs_2_, ...), custom_call_target="tpu_custom_call" | custom-call | flops 536870912 | bytes 4194304 | tf_op jit(solution)/shard_map/scores_sent/pallas_call | solution.py:214
  25.5 1.6 %collective-permute-start.14 = (f32[128,128]{1,0:T(8,128)S(1)}, f32[128,128]{1,0:T(8,128)S(1)}, u32[]{:S(2)}, u32[]{:S(2)}) collective-permute-start(f32[128,128]{1,0:T(8,128)S(1)} %get-tuple-element.18), channel_id=1, source_target_pairs={{0,1},{1,0},{2,3},{3,2},{4,5},{5,4},{6,7},{7,6},{8,9},{9,8},{10,11... | collective-permute-start | bytes 196616 | tf_op jit(solution)/shard_map/ppermute | solution.py:257
  27.0 0.8 %scores_kept.1 = f32[128,128]{1,0:T(8,128)S(1)} custom-call(bf16[256,2,4096]{2,1,0:T(2,128)(2,1)S(1)} %near.1.train, bf16[2,128,4096]{2,1,0:T(8,128)(2,1)S(1)} %get-tuple-element.17.table), custom_call_target="tpu_custom_call" | custom-call | flops 536870912 | bytes 4194304 | tf_op jit(solution)/shard_map/scores_kept/pallas_call | solution.py:214
  27.9 2.0 %collective-permute-done.14 = f32[128,128]{1,0:T(8,128)S(1)} collective-permute-done((f32[128,128]{1,0:T(8,128)S(1)}, f32[128,128]{1,0:T(8,128)S(1)}, u32[]{:S(2)}, u32[]{:S(2)}) %collective-permute-start.14) | collective-permute-done | bytes 65568 | tf_op jit(solution)/shard_map/ppermute | solution.py:257
  29.9 0.6 %add.3 = f32[128,128]{1,0:T(8,128)} add(f32[128,128]{1,0:T(8,128)S(1)} %scores_kept.1, f32[128,128]{1,0:T(8,128)S(1)} %collective-permute-done.14) | non-fusion elementwise | flops 16384 | bytes 196608 | tf_op jit(solution)/shard_map/add | solution.py:259
Async XLA Ops:
  1.8 9.5 %collective-permute-start.2 = (bf16[16,4096]{1,0:T(8,128)(2,1)S(1)}, bf16[16,4096]{1,0:T(8,128)(2,1)S(1)}, u32[]{:S(2)}, u32[]{:S(2)}) collective-permute-start(bf16[16,4096]{1,0:T(8,128)(2,1)S(1)} %condition_mine.1.refs_0_), channel_id=1, source_target_pairs={{0,12},{2,14},{4,8},{6,10},{8,4},{10,6},{12,0},{14,2},{1,13},{3,15... | collective-permute-start | bytes 393224 | tf_op jit(solution)/shard_map/ppermute | solution.py:128
  6.9 7.4 %collective-permute-start = (bf16[16,4096]{1,0:T(8,128)(2,1)S(1)}, bf16[16,4096]{1,0:T(8,128)(2,1)S(1)}, u32[]{:S(2)}, u32[]{:S(2)}) collective-permute-start(bf16[16,4096]{1,0:T(8,128)(2,1)S(1)} %condition_mine.1.refs_0_), channel_id=1, source_target_pairs={{0,4},{2,6},{4,0},{6,2},{8,12},{10,14},{12,8},{14,10},{1,5},{3,7},... | collective-permute-start | bytes 393224 | tf_op jit(solution)/shard_map/ppermute | solution.py:128
  8.7 9.3 %collective-permute-start.6 = (bf16[16,4096]{1,0:T(8,128)(2,1)S(1)}, bf16[16,4096]{1,0:T(8,128)(2,1)S(1)}, u32[]{:S(2)}, u32[]{:S(2)}) collective-permute-start(bf16[16,4096]{1,0:T(8,128)(2,1)S(1)} %condition_mine.1.refs_0_), channel_id=1, source_target_pairs={{0,8},{2,10},{4,12},{6,14},{8,0},{10,2},{12,4},{14,6},{1,9},{3,11}... | collective-permute-start | bytes 393224 | tf_op jit(solution)/shard_map/ppermute | solution.py:128
  11.3 8.2 %collective-permute-start.3 = (bf16[16,4096]{1,0:T(8,128)(2,1)S(1)}, bf16[16,4096]{1,0:T(8,128)(2,1)S(1)}, u32[]{:S(2)}, u32[]{:S(2)}) collective-permute-start(bf16[16,4096]{1,0:T(8,128)(2,1)S(1)} %collective-permute-done.2.refs_8_), channel_id=1, source_target_pairs={{0,16},{2,18},{4,20},{6,22},{8,24},{10,26},{12,28},{14,30},{16,0},... | collective-permute-start | bytes 393224 | tf_op jit(solution)/shard_map/ppermute | solution.py:138
  14.3 7.4 %collective-permute-start.1 = (bf16[16,4096]{1,0:T(8,128)(2,1)S(1)}, bf16[16,4096]{1,0:T(8,128)(2,1)S(1)}, u32[]{:S(2)}, u32[]{:S(2)}) collective-permute-start(bf16[16,4096]{1,0:T(8,128)(2,1)S(1)} %collective-permute-done.refs_6_), channel_id=1, source_target_pairs={{0,18},{2,16},{4,22},{6,20},{8,26},{10,24},{12,30},{14,28},{16,2},... | collective-permute-start | bytes 393224 | tf_op jit(solution)/shard_map/ppermute | solution.py:138
  15.0 7.3 %collective-permute-start.5 = (bf16[16,4096]{1,0:T(8,128)(2,1)S(1)}, bf16[16,4096]{1,0:T(8,128)(2,1)S(1)}, u32[]{:S(2)}, u32[]{:S(2)}) collective-permute-start(bf16[16,4096]{1,0:T(8,128)(2,1)S(1)} %condition_other.1.refs_2_), channel_id=1, source_target_pairs={{0,2},{2,0},{4,6},{6,4},{8,10},{10,8},{12,14},{14,12},{1,3},{3,1},... | collective-permute-start | bytes 393224 | tf_op jit(solution)/shard_map/ppermute | solution.py:132
  15.9 6.4 %collective-permute-start.4 = (bf16[16,4096]{1,0:T(8,128)(2,1)S(1)}, bf16[16,4096]{1,0:T(8,128)(2,1)S(1)}, u32[]{:S(2)}, u32[]{:S(2)}) collective-permute-start(bf16[16,4096]{1,0:T(8,128)(2,1)S(1)} %condition_mine.1.refs_0_), channel_id=1, source_target_pairs={{0,2},{2,0},{4,6},{6,4},{8,10},{10,8},{12,14},{14,12},{1,3},{3,1},... | collective-permute-start | bytes 393224 | tf_op jit(solution)/shard_map/ppermute | solution.py:132
  18.0 5.0 %collective-permute-start.10 = (bf16[16,4096]{1,0:T(8,128)(2,1)S(1)}, bf16[16,4096]{1,0:T(8,128)(2,1)S(1)}, u32[]{:S(2)}, u32[]{:S(2)}) collective-permute-start(bf16[16,4096]{1,0:T(8,128)(2,1)S(1)} %collective-permute-done.6.refs_4_), channel_id=1, source_target_pairs={{0,16},{2,18},{4,20},{6,22},{8,24},{10,26},{12,28},{14,30},{16,0},... | collective-permute-start | bytes 393224 | tf_op jit(solution)/shard_map/ppermute | solution.py:138
  19.5 3.4 %collective-permute-start.7 = (bf16[16,4096]{1,0:T(8,128)(2,1)S(1)}, bf16[16,4096]{1,0:T(8,128)(2,1)S(1)}, u32[]{:S(2)}, u32[]{:S(2)}) collective-permute-start(bf16[16,4096]{1,0:T(8,128)(2,1)S(1)} %collective-permute-done.6.refs_4_), channel_id=1, source_target_pairs={{0,2},{2,0},{4,6},{6,4},{8,10},{10,8},{12,14},{14,12},{1,3},{3,1},... | collective-permute-start | bytes 393224 | tf_op jit(solution)/shard_map/ppermute | solution.py:132
  21.7 1.7 %collective-permute-start.9 = (bf16[16,4096]{1,0:T(8,128)(2,1)S(1)}, bf16[16,4096]{1,0:T(8,128)(2,1)S(1)}, u32[]{:S(2)}, u32[]{:S(2)}) collective-permute-start(bf16[16,4096]{1,0:T(8,128)(2,1)S(1)} %collective-permute-done.2.refs_8_), channel_id=1, source_target_pairs={{0,2},{2,0},{4,6},{6,4},{8,10},{10,8},{12,14},{14,12},{1,3},{3,1},... | collective-permute-start | bytes 393224 | tf_op jit(solution)/shard_map/ppermute | solution.py:132
  22.3 1.3 %collective-permute-start.8 = (bf16[16,4096]{1,0:T(8,128)(2,1)S(1)}, bf16[16,4096]{1,0:T(8,128)(2,1)S(1)}, u32[]{:S(2)}, u32[]{:S(2)}) collective-permute-start(bf16[16,4096]{1,0:T(8,128)(2,1)S(1)} %collective-permute-done.refs_6_), channel_id=1, source_target_pairs={{0,2},{2,0},{4,6},{6,4},{8,10},{10,8},{12,14},{14,12},{1,3},{3,1},... | collective-permute-start | bytes 393224 | tf_op jit(solution)/shard_map/ppermute | solution.py:132
  22.4 1.9 %collective-permute-start.12 = (bf16[16,4096]{1,0:T(8,128)(2,1)S(1)}, bf16[16,4096]{1,0:T(8,128)(2,1)S(1)}, u32[]{:S(2)}, u32[]{:S(2)}) collective-permute-start(bf16[16,4096]{1,0:T(8,128)(2,1)S(1)} %collective-permute-done.1.refs_12_), channel_id=1, source_target_pairs={{0,2},{2,0},{4,6},{6,4},{8,10},{10,8},{12,14},{14,12},{1,3},{3,1},... | collective-permute-start | bytes 393224 | tf_op jit(solution)/shard_map/ppermute | solution.py:132
  22.9 1.3 %collective-permute-start.11 = (bf16[16,4096]{1,0:T(8,128)(2,1)S(1)}, bf16[16,4096]{1,0:T(8,128)(2,1)S(1)}, u32[]{:S(2)}, u32[]{:S(2)}) collective-permute-start(bf16[16,4096]{1,0:T(8,128)(2,1)S(1)} %collective-permute-done.10.refs_10_), channel_id=1, source_target_pairs={{0,2},{2,0},{4,6},{6,4},{8,10},{10,8},{12,14},{14,12},{1,3},{3,1},... | collective-permute-start | bytes 393224 | tf_op jit(solution)/shard_map/ppermute | solution.py:132
  22.9 1.5 %collective-permute-start.13 = (bf16[16,4096]{1,0:T(8,128)(2,1)S(1)}, bf16[16,4096]{1,0:T(8,128)(2,1)S(1)}, u32[]{:S(2)}, u32[]{:S(2)}) collective-permute-start(bf16[16,4096]{1,0:T(8,128)(2,1)S(1)} %collective-permute-done.3.refs_14_), channel_id=1, source_target_pairs={{0,2},{2,0},{4,6},{6,4},{8,10},{10,8},{12,14},{14,12},{1,3},{3,1},... | collective-permute-start | bytes 393224 | tf_op jit(solution)/shard_map/ppermute | solution.py:132
  25.5 4.4 %collective-permute-start.14 = (f32[128,128]{1,0:T(8,128)S(1)}, f32[128,128]{1,0:T(8,128)S(1)}, u32[]{:S(2)}, u32[]{:S(2)}) collective-permute-start(f32[128,128]{1,0:T(8,128)S(1)} %get-tuple-element.18), channel_id=1, source_target_pairs={{0,1},{1,0},{2,3},{3,2},{4,5},{5,4},{6,7},{7,6},{8,9},{9,8},{10,11... | collective-permute-start | bytes 196616 | tf_op jit(solution)/shard_map/ppermute | solution.py:257

commit v14 on v13

--- a/solution.py
+++ b/solution.py
@@ -232,14 +232,14 @@
     mine = condition_layer(False, queries, left_factor, right_factor)
     other = condition_layer(True, queries, left_factor, right_factor)
     near = copy_near(train_grads)
-    mine_late, other = lax.optimization_barrier((mine, other))
-    s2 = along_columns(mine_late, 2)
+    s2 = along_columns(mine, 2)
     s1 = along_columns(mine, 1)
     s3 = along_columns(mine, 3)
+    s1, other = lax.optimization_barrier((s1, other))
     y1 = other_part(s1, cross=True)
     y3 = other_part(s3)
     y2 = other_part(s2)
-    y1, y3, near = lax.optimization_barrier((y1, y3, near))
+    y1, near = lax.optimization_barrier((y1, near))
 
     blocks = []
     for block in (mine, other, s2, s1, s3, y2, y1, y3):

time: 30.7 us -> 31.8 us (1.036)
  waiting for transfers between devices: 8.38 us -> 9.78 us
    ppermute x3, waiting for transfers between devices: 5.22 us -> 6.62 us  [along_columns(): lax.ppermute(value, 'train', [(k, k ^ flip * PAIR) for k in range(COLUMNS...]
    ppermute x3, starting transfers between devices: 3.96 us -> 3.51 us  [other_part(): return lax.ppermute(value, ('parts', 'train'), pairs)]
  transfers between devices with their start and end apart: 15 -> 15, of which waited for: 8 -> 8; matrix products, arithmetic and copies ran while one was open for 0% -> 0% of each run, Pallas kernels for 16% -> 15%
where the time goes in v14:
time: 31.8 us; the launch traced here: 31.6 us
  starting transfers between devices  13.6 us (43%)
  waiting for transfers between devices  9.78 us (31%)
  Pallas kernels  7.57 us (24%)
  other arithmetic  0.64 us (2%)
    ppermute x3, waiting for transfers between devices, along_columns(): lax.ppermute(value, 'train', [(k, k ^ flip * PAIR) for k in range(COLUMNS...  6.62 us
    ppermute x3, starting transfers between devices, along_columns(): lax.ppermute(value, 'train', [(k, k ^ flip * PAIR) for k in range(COLUMNS...  5.68 us
    pallas_call x2, Pallas kernels, condition_layer(): pl.pallas_call(functools.partial(condition_kernel, other), out_shape=jax....  3.53 us
    ppermute x3, starting transfers between devices, other_part(): return lax.ppermute(value, ('parts', 'train'), pairs)  3.51 us
    ppermute x8, starting transfers between devices, other_core(): lax.ppermute(value, 'train', [(k, k ^ 1) for k in range(COLUMNS * PAIR)])  2.83 us
    pallas_call x1, Pallas kernels, copy_near(): pl.pallas_call(copy_kernel, out_shape=jax.ShapeDtypeStruct(value.shape, v...  2.2 us
    ppermute x1, waiting for transfers between devices, direct(): received = lax.ppermute(sent, 'layer', [(0, 1), (1, 0)])  1.99 us
    pallas_call x2, Pallas kernels, local_call(): pl.pallas_call(kernel, out_shape=out_shape, in_specs=[spec] * len(operand...  1.84 us
  transfers between devices with their start and end apart: 15, of which 8 were waited for; matrix products, arithmetic and copies ran while one was open for 0% of the time, Pallas kernels for 15%

profile of v14, /device:TPU:0, one launch (start us, length us, event | category | flops | bytes accessed | tf_op | source)
XLA Modules:
  0.0 31.6 jit_solution(5752928475982183736)
XLA Ops:
  0.0 1.8 %condition_mine.1.refs_0_ = bf16[16,4096]{1,0:T(8,128)(2,1)S(1)} custom-call(bf16[2,1,16,4096]{3,2,1,0:T(8,128)(2,1)} %queries.3, f32[2,64,64]{2,1,0:T(8,128)} %left.3, f32[2,64,64]{2,1,0:T(8,128)} %right.3), custom_call_target="tpu_custom_call" | custom-call | flops 134217728 | bytes 524288 | tf_op jit(solution)/shard_map/condition_mine/pallas_call | solution.py:107
  1.8 3.1 %collective-permute-start = (bf16[16,4096]{1,0:T(8,128)(2,1)S(1)}, bf16[16,4096]{1,0:T(8,128)(2,1)S(1)}, u32[]{:S(2)}, u32[]{:S(2)}) collective-permute-start(bf16[16,4096]{1,0:T(8,128)(2,1)S(1)} %condition_mine.1.refs_0_), channel_id=1, source_target_pairs={{0,4},{2,6},{4,0},{6,2},{8,12},{10,14},{12,8},{14,10},{1,5},{3,7},... | collective-permute-start | bytes 393224 | tf_op jit(solution)/shard_map/ppermute | solution.py:128
  4.9 2.5 %collective-permute-start.7 = (bf16[16,4096]{1,0:T(8,128)(2,1)S(1)}, bf16[16,4096]{1,0:T(8,128)(2,1)S(1)}, u32[]{:S(2)}, u32[]{:S(2)}) collective-permute-start(bf16[16,4096]{1,0:T(8,128)(2,1)S(1)} %condition_mine.1.refs_0_), channel_id=1, source_target_pairs={{0,12},{2,14},{4,8},{6,10},{8,4},{10,6},{12,0},{14,2},{1,13},{3,15... | collective-permute-start | bytes 393224 | tf_op jit(solution)/shard_map/ppermute | solution.py:128
  7.3 0.1 collective-permute-start.4
  7.5 1.8 %condition_other.1.refs_2_ = bf16[16,4096]{1,0:T(8,128)(2,1)S(1)} custom-call(bf16[2,1,16,4096]{3,2,1,0:T(8,128)(2,1)} %queries.3, f32[2,64,64]{2,1,0:T(8,128)} %left.3, f32[2,64,64]{2,1,0:T(8,128)} %right.3), custom_call_target="tpu_custom_call" | custom-call | flops 134217728 | bytes 524288 | tf_op jit(solution)/shard_map/condition_other/pallas_call | solution.py:107
  9.2 0.0 collective-permute-done.refs_6_
  9.2 0.5 %collective-permute-start.1 = (bf16[16,4096]{1,0:T(8,128)(2,1)S(1)}, bf16[16,4096]{1,0:T(8,128)(2,1)S(1)}, u32[]{:S(2)}, u32[]{:S(2)}) collective-permute-start(bf16[16,4096]{1,0:T(8,128)(2,1)S(1)} %collective-permute-done.refs_6_), channel_id=1, source_target_pairs={{0,18},{2,16},{4,22},{6,20},{8,26},{10,24},{12,30},{14,28},{16,2},... | collective-permute-start | bytes 393224 | tf_op jit(solution)/shard_map/ppermute | solution.py:138
  9.7 1.2 %collective-permute-start.2 = (bf16[16,4096]{1,0:T(8,128)(2,1)S(1)}, bf16[16,4096]{1,0:T(8,128)(2,1)S(1)}, u32[]{:S(2)}, u32[]{:S(2)}) collective-permute-start(bf16[16,4096]{1,0:T(8,128)(2,1)S(1)} %condition_mine.1.refs_0_), channel_id=1, source_target_pairs={{0,2},{2,0},{4,6},{6,4},{8,10},{10,8},{12,14},{14,12},{1,3},{3,1},... | collective-permute-start | bytes 393224 | tf_op jit(solution)/shard_map/ppermute | solution.py:132
  10.9 3.7 %collective-permute-done.7.refs_8_ = bf16[16,4096]{1,0:T(8,128)(2,1)S(1)} collective-permute-done((bf16[16,4096]{1,0:T(8,128)(2,1)S(1)}, bf16[16,4096]{1,0:T(8,128)(2,1)S(1)}, u32[]{:S(2)}, u32[]{:S(2)}) %collective-permute-start.7) | collective-permute-done | bytes 131104 | tf_op jit(solution)/shard_map/ppermute | solution.py:128
  14.6 1.5 %collective-permute-start.12 = (bf16[16,4096]{1,0:T(8,128)(2,1)S(1)}, bf16[16,4096]{1,0:T(8,128)(2,1)S(1)}, u32[]{:S(2)}, u32[]{:S(2)}) collective-permute-start(bf16[16,4096]{1,0:T(8,128)(2,1)S(1)} %collective-permute-done.7.refs_8_), channel_id=1, source_target_pairs={{0,16},{2,18},{4,20},{6,22},{8,24},{10,26},{12,28},{14,30},{16,0},... | collective-permute-start | bytes 393224 | tf_op jit(solution)/shard_map/ppermute | solution.py:138
  16.1 0.0 collective-permute-start.8
  16.1 3.0 %collective-permute-done.4.refs_4_ = bf16[16,4096]{1,0:T(8,128)(2,1)S(1)} collective-permute-done((bf16[16,4096]{1,0:T(8,128)(2,1)S(1)}, bf16[16,4096]{1,0:T(8,128)(2,1)S(1)}, u32[]{:S(2)}, u32[]{:S(2)}) %collective-permute-start.4) | collective-permute-done | bytes 131104 | tf_op jit(solution)/shard_map/ppermute | solution.py:128
  19.1 1.5 %collective-permute-start.9 = (bf16[16,4096]{1,0:T(8,128)(2,1)S(1)}, bf16[16,4096]{1,0:T(8,128)(2,1)S(1)}, u32[]{:S(2)}, u32[]{:S(2)}) collective-permute-start(bf16[16,4096]{1,0:T(8,128)(2,1)S(1)} %collective-permute-done.4.refs_4_), channel_id=1, source_target_pairs={{0,16},{2,18},{4,20},{6,22},{8,24},{10,26},{12,28},{14,30},{16,0},... | collective-permute-start | bytes 393224 | tf_op jit(solution)/shard_map/ppermute | solution.py:138
  20.6 0.0 collective-permute-done.1.refs_12_
  20.6 0.0 collective-permute-start.5
  20.6 2.2 %near.1.train = bf16[256,2,4096]{2,1,0:T(2,128)(2,1)S(1)} custom-call(bf16[256,2,4096]{2,1,0:T(2,128)(2,1)} %source.1), custom_call_target="tpu_custom_call" | custom-call | bytes 8388608 | tf_op jit(solution)/shard_map/near/pallas_call | solution.py:148
  22.8 0.0 collective-permute-done.2.refs_1_
  22.8 0.6 %collective-permute-start.6 = (bf16[16,4096]{1,0:T(8,128)(2,1)S(1)}, bf16[16,4096]{1,0:T(8,128)(2,1)S(1)}, u32[]{:S(2)}, u32[]{:S(2)}) collective-permute-start(bf16[16,4096]{1,0:T(8,128)(2,1)S(1)} %collective-permute-done.refs_6_), channel_id=1, source_target_pairs={{0,2},{2,0},{4,6},{6,4},{8,10},{10,8},{12,14},{14,12},{1,3},{3,1},... | collective-permute-start | bytes 393224 | tf_op jit(solution)/shard_map/ppermute | solution.py:132
  23.4 0.0 collective-permute-done.12.refs_14_
  23.4 0.1 collective-permute-start.3
  23.5 0.0 collective-permute-done.8.refs_9_
  23.5 0.4 %collective-permute-start.13 = (bf16[16,4096]{1,0:T(8,128)(2,1)S(1)}, bf16[16,4096]{1,0:T(8,128)(2,1)S(1)}, u32[]{:S(2)}, u32[]{:S(2)}) collective-permute-start(bf16[16,4096]{1,0:T(8,128)(2,1)S(1)} %collective-permute-done.12.refs_14_), channel_id=1, source_target_pairs={{0,2},{2,0},{4,6},{6,4},{8,10},{10,8},{12,14},{14,12},{1,3},{3,1},... | collective-permute-start | bytes 393224 | tf_op jit(solution)/shard_map/ppermute | solution.py:132
  23.9 0.1 collective-permute-done.9.refs_10_
  24.1 0.0 collective-permute-start.10
  24.1 0.0 collective-permute-done.5.refs_5_
  24.1 0.5 %collective-permute-start.11 = (bf16[16,4096]{1,0:T(8,128)(2,1)S(1)}, bf16[16,4096]{1,0:T(8,128)(2,1)S(1)}, u32[]{:S(2)}, u32[]{:S(2)}) collective-permute-start(bf16[16,4096]{1,0:T(8,128)(2,1)S(1)} %collective-permute-done.1.refs_12_), channel_id=1, source_target_pairs={{0,2},{2,0},{4,6},{6,4},{8,10},{10,8},{12,14},{14,12},{1,3},{3,1},... | collective-permute-start | bytes 393224 | tf_op jit(solution)/shard_map/ppermute | solution.py:132
  24.6 0.2 collective-permute-done.3.refs_3_
  24.8 0.0 collective-permute-done.6.refs_7_
  24.8 0.2 collective-permute-done.13.refs_15_
  24.9 0.5 %collective-permute-done.10.refs_11_ = bf16[16,4096]{1,0:T(8,128)(2,1)S(1)} collective-permute-done((bf16[16,4096]{1,0:T(8,128)(2,1)S(1)}, bf16[16,4096]{1,0:T(8,128)(2,1)S(1)}, u32[]{:S(2)}, u32[]{:S(2)}) %collective-permute-start.10) | collective-permute-done | bytes 131104 | tf_op jit(solution)/shard_map/ppermute | solution.py:132
  25.4 0.2 collective-permute-done.11.refs_13_
  25.6 1.0 %scores_sent.1 = (f32[128,128]{1,0:T(8,128)S(1)}, bf16[2,128,4096]{2,1,0:T(8,128)(2,1)S(1)}) custom-call(bf16[256,2,4096]{2,1,0:T(2,128)(2,1)S(1)} %near.1.train, bf16[16,4096]{1,0:T(8,128)(2,1)S(1)} %condition_mine.1.refs_0_, bf16[16,4096]{1,0:T(8,128)(2,1)S(1)} %collective-permute-done.2.refs_1_, bf16[16,4096]{1,0:T(8,128)(2,1)S(1)} %condition_other.1.refs_2_, ...), custom_call_target="tpu_custom_call" | custom-call | flops 536870912 | bytes 4194304 | tf_op jit(solution)/shard_map/scores_sent/pallas_call | solution.py:214
  26.6 1.6 %collective-permute-start.14 = (f32[128,128]{1,0:T(8,128)S(1)}, f32[128,128]{1,0:T(8,128)S(1)}, u32[]{:S(2)}, u32[]{:S(2)}) collective-permute-start(f32[128,128]{1,0:T(8,128)S(1)} %get-tuple-element.16), channel_id=1, source_target_pairs={{0,1},{1,0},{2,3},{3,2},{4,5},{5,4},{6,7},{7,6},{8,9},{9,8},{10,11... | collective-permute-start | bytes 196616 | tf_op jit(solution)/shard_map/ppermute | solution.py:257
  28.2 0.8 %scores_kept.1 = f32[128,128]{1,0:T(8,128)S(1)} custom-call(bf16[256,2,4096]{2,1,0:T(2,128)(2,1)S(1)} %near.1.train, bf16[2,128,4096]{2,1,0:T(8,128)(2,1)S(1)} %get-tuple-element.15.table), custom_call_target="tpu_custom_call" | custom-call | flops 536870912 | bytes 4194304 | tf_op jit(solution)/shard_map/scores_kept/pallas_call | solution.py:214
  29.0 2.0 %collective-permute-done.14 = f32[128,128]{1,0:T(8,128)S(1)} collective-permute-done((f32[128,128]{1,0:T(8,128)S(1)}, f32[128,128]{1,0:T(8,128)S(1)}, u32[]{:S(2)}, u32[]{:S(2)}) %collective-permute-start.14) | collective-permute-done | bytes 65568 | tf_op jit(solution)/shard_map/ppermute | solution.py:257
  31.0 0.6 %add.3 = f32[128,128]{1,0:T(8,128)} add(f32[128,128]{1,0:T(8,128)S(1)} %scores_kept.1, f32[128,128]{1,0:T(8,128)S(1)} %collective-permute-done.14) | non-fusion elementwise | flops 16384 | bytes 196608 | tf_op jit(solution)/shard_map/add | solution.py:259
Async XLA Ops:
  1.8 7.5 %collective-permute-start = (bf16[16,4096]{1,0:T(8,128)(2,1)S(1)}, bf16[16,4096]{1,0:T(8,128)(2,1)S(1)}, u32[]{:S(2)}, u32[]{:S(2)}) collective-permute-start(bf16[16,4096]{1,0:T(8,128)(2,1)S(1)} %condition_mine.1.refs_0_), channel_id=1, source_target_pairs={{0,4},{2,6},{4,0},{6,2},{8,12},{10,14},{12,8},{14,10},{1,5},{3,7},... | collective-permute-start | bytes 393224 | tf_op jit(solution)/shard_map/ppermute | solution.py:128
  4.9 9.7 %collective-permute-start.7 = (bf16[16,4096]{1,0:T(8,128)(2,1)S(1)}, bf16[16,4096]{1,0:T(8,128)(2,1)S(1)}, u32[]{:S(2)}, u32[]{:S(2)}) collective-permute-start(bf16[16,4096]{1,0:T(8,128)(2,1)S(1)} %condition_mine.1.refs_0_), channel_id=1, source_target_pairs={{0,12},{2,14},{4,8},{6,10},{8,4},{10,6},{12,0},{14,2},{1,13},{3,15... | collective-permute-start | bytes 393224 | tf_op jit(solution)/shard_map/ppermute | solution.py:128
  7.3 11.8 %collective-permute-start.4 = (bf16[16,4096]{1,0:T(8,128)(2,1)S(1)}, bf16[16,4096]{1,0:T(8,128)(2,1)S(1)}, u32[]{:S(2)}, u32[]{:S(2)}) collective-permute-start(bf16[16,4096]{1,0:T(8,128)(2,1)S(1)} %condition_mine.1.refs_0_), channel_id=1, source_target_pairs={{0,8},{2,10},{4,12},{6,14},{8,0},{10,2},{12,4},{14,6},{1,9},{3,11}... | collective-permute-start | bytes 393224 | tf_op jit(solution)/shard_map/ppermute | solution.py:128
  9.2 11.4 %collective-permute-start.1 = (bf16[16,4096]{1,0:T(8,128)(2,1)S(1)}, bf16[16,4096]{1,0:T(8,128)(2,1)S(1)}, u32[]{:S(2)}, u32[]{:S(2)}) collective-permute-start(bf16[16,4096]{1,0:T(8,128)(2,1)S(1)} %collective-permute-done.refs_6_), channel_id=1, source_target_pairs={{0,18},{2,16},{4,22},{6,20},{8,26},{10,24},{12,30},{14,28},{16,2},... | collective-permute-start | bytes 393224 | tf_op jit(solution)/shard_map/ppermute | solution.py:138
  9.7 13.1 %collective-permute-start.2 = (bf16[16,4096]{1,0:T(8,128)(2,1)S(1)}, bf16[16,4096]{1,0:T(8,128)(2,1)S(1)}, u32[]{:S(2)}, u32[]{:S(2)}) collective-permute-start(bf16[16,4096]{1,0:T(8,128)(2,1)S(1)} %condition_mine.1.refs_0_), channel_id=1, source_target_pairs={{0,2},{2,0},{4,6},{6,4},{8,10},{10,8},{12,14},{14,12},{1,3},{3,1},... | collective-permute-start | bytes 393224 | tf_op jit(solution)/shard_map/ppermute | solution.py:132
  14.6 8.8 %collective-permute-start.12 = (bf16[16,4096]{1,0:T(8,128)(2,1)S(1)}, bf16[16,4096]{1,0:T(8,128)(2,1)S(1)}, u32[]{:S(2)}, u32[]{:S(2)}) collective-permute-start(bf16[16,4096]{1,0:T(8,128)(2,1)S(1)} %collective-permute-done.7.refs_8_), channel_id=1, source_target_pairs={{0,16},{2,18},{4,20},{6,22},{8,24},{10,26},{12,28},{14,30},{16,0},... | collective-permute-start | bytes 393224 | tf_op jit(solution)/shard_map/ppermute | solution.py:138
  16.1 7.4 %collective-permute-start.8 = (bf16[16,4096]{1,0:T(8,128)(2,1)S(1)}, bf16[16,4096]{1,0:T(8,128)(2,1)S(1)}, u32[]{:S(2)}, u32[]{:S(2)}) collective-permute-start(bf16[16,4096]{1,0:T(8,128)(2,1)S(1)} %collective-permute-done.7.refs_8_), channel_id=1, source_target_pairs={{0,2},{2,0},{4,6},{6,4},{8,10},{10,8},{12,14},{14,12},{1,3},{3,1},... | collective-permute-start | bytes 393224 | tf_op jit(solution)/shard_map/ppermute | solution.py:132
  19.1 5.0 %collective-permute-start.9 = (bf16[16,4096]{1,0:T(8,128)(2,1)S(1)}, bf16[16,4096]{1,0:T(8,128)(2,1)S(1)}, u32[]{:S(2)}, u32[]{:S(2)}) collective-permute-start(bf16[16,4096]{1,0:T(8,128)(2,1)S(1)} %collective-permute-done.4.refs_4_), channel_id=1, source_target_pairs={{0,16},{2,18},{4,20},{6,22},{8,24},{10,26},{12,28},{14,30},{16,0},... | collective-permute-start | bytes 393224 | tf_op jit(solution)/shard_map/ppermute | solution.py:138
  20.6 3.5 %collective-permute-start.5 = (bf16[16,4096]{1,0:T(8,128)(2,1)S(1)}, bf16[16,4096]{1,0:T(8,128)(2,1)S(1)}, u32[]{:S(2)}, u32[]{:S(2)}) collective-permute-start(bf16[16,4096]{1,0:T(8,128)(2,1)S(1)} %collective-permute-done.4.refs_4_), channel_id=1, source_target_pairs={{0,2},{2,0},{4,6},{6,4},{8,10},{10,8},{12,14},{14,12},{1,3},{3,1},... | collective-permute-start | bytes 393224 | tf_op jit(solution)/shard_map/ppermute | solution.py:132
  22.8 1.9 %collective-permute-start.6 = (bf16[16,4096]{1,0:T(8,128)(2,1)S(1)}, bf16[16,4096]{1,0:T(8,128)(2,1)S(1)}, u32[]{:S(2)}, u32[]{:S(2)}) collective-permute-start(bf16[16,4096]{1,0:T(8,128)(2,1)S(1)} %collective-permute-done.refs_6_), channel_id=1, source_target_pairs={{0,2},{2,0},{4,6},{6,4},{8,10},{10,8},{12,14},{14,12},{1,3},{3,1},... | collective-permute-start | bytes 393224 | tf_op jit(solution)/shard_map/ppermute | solution.py:132
  23.4 1.3 %collective-permute-start.3 = (bf16[16,4096]{1,0:T(8,128)(2,1)S(1)}, bf16[16,4096]{1,0:T(8,128)(2,1)S(1)}, u32[]{:S(2)}, u32[]{:S(2)}) collective-permute-start(bf16[16,4096]{1,0:T(8,128)(2,1)S(1)} %condition_other.1.refs_2_), channel_id=1, source_target_pairs={{0,2},{2,0},{4,6},{6,4},{8,10},{10,8},{12,14},{14,12},{1,3},{3,1},... | collective-permute-start | bytes 393224 | tf_op jit(solution)/shard_map/ppermute | solution.py:132
  23.5 1.4 %collective-permute-start.13 = (bf16[16,4096]{1,0:T(8,128)(2,1)S(1)}, bf16[16,4096]{1,0:T(8,128)(2,1)S(1)}, u32[]{:S(2)}, u32[]{:S(2)}) collective-permute-start(bf16[16,4096]{1,0:T(8,128)(2,1)S(1)} %collective-permute-done.12.refs_14_), channel_id=1, source_target_pairs={{0,2},{2,0},{4,6},{6,4},{8,10},{10,8},{12,14},{14,12},{1,3},{3,1},... | collective-permute-start | bytes 393224 | tf_op jit(solution)/shard_map/ppermute | solution.py:132
  24.1 1.3 %collective-permute-start.10 = (bf16[16,4096]{1,0:T(8,128)(2,1)S(1)}, bf16[16,4096]{1,0:T(8,128)(2,1)S(1)}, u32[]{:S(2)}, u32[]{:S(2)}) collective-permute-start(bf16[16,4096]{1,0:T(8,128)(2,1)S(1)} %collective-permute-done.9.refs_10_), channel_id=1, source_target_pairs={{0,2},{2,0},{4,6},{6,4},{8,10},{10,8},{12,14},{14,12},{1,3},{3,1},... | collective-permute-start | bytes 393224 | tf_op jit(solution)/shard_map/ppermute | solution.py:132
  24.1 1.5 %collective-permute-start.11 = (bf16[16,4096]{1,0:T(8,128)(2,1)S(1)}, bf16[16,4096]{1,0:T(8,128)(2,1)S(1)}, u32[]{:S(2)}, u32[]{:S(2)}) collective-permute-start(bf16[16,4096]{1,0:T(8,128)(2,1)S(1)} %collective-permute-done.1.refs_12_), channel_id=1, source_target_pairs={{0,2},{2,0},{4,6},{6,4},{8,10},{10,8},{12,14},{14,12},{1,3},{3,1},... | collective-permute-start | bytes 393224 | tf_op jit(solution)/shard_map/ppermute | solution.py:132
  26.6 4.4 %collective-permute-start.14 = (f32[128,128]{1,0:T(8,128)S(1)}, f32[128,128]{1,0:T(8,128)S(1)}, u32[]{:S(2)}, u32[]{:S(2)}) collective-permute-start(f32[128,128]{1,0:T(8,128)S(1)} %get-tuple-element.16), channel_id=1, source_target_pairs={{0,1},{1,0},{2,3},{3,2},{4,5},{5,4},{6,7},{7,6},{8,9},{9,8},{10,11... | collective-permute-start | bytes 196616 | tf_op jit(solution)/shard_map/ppermute | solution.py:257

commit v15 on v13

--- a/solution.py
+++ b/solution.py
@@ -232,10 +232,10 @@
     mine = condition_layer(False, queries, left_factor, right_factor)
     other = condition_layer(True, queries, left_factor, right_factor)
     near = copy_near(train_grads)
-    mine_late, other = lax.optimization_barrier((mine, other))
-    s2 = along_columns(mine_late, 2)
     s1 = along_columns(mine, 1)
     s3 = along_columns(mine, 3)
+    s3, other = lax.optimization_barrier((s3, other))
+    s2 = along_columns(s3, 1)
     y1 = other_part(s1, cross=True)
     y3 = other_part(s3)
     y2 = other_part(s2)

time: 30.7 us -> 31.4 us (1.023)
  waiting for transfers between devices: 8.38 us -> 8.79 us
    ppermute x3, waiting for transfers between devices: 0.14 us -> 2.11 us  [other_part(): return lax.ppermute(value, ('parts', 'train'), pairs)]
    ppermute x3, waiting for transfers between devices: 5.22 us -> 3.48 us  [along_columns(): lax.ppermute(value, 'train', [(k, k ^ flip * PAIR) for k in range(COLUMNS...]
    ppermute x3, starting transfers between devices: 5.82 us -> 6.77 us  [along_columns(): lax.ppermute(value, 'train', [(k, k ^ flip * PAIR) for k in range(COLUMNS...]
    ppermute x8, starting transfers between devices: 2.52 us -> 2.06 us  [other_core(): lax.ppermute(value, 'train', [(k, k ^ 1) for k in range(COLUMNS * PAIR)])]
  transfers between devices with their start and end apart: 15 -> 15, of which waited for: 8 -> 8; matrix products, arithmetic and copies ran while one was open for 0% -> 0% of each run, Pallas kernels for 16% -> 15%
where the time goes in v15:
time: 31.4 us; the launch traced here: 31.2 us
  starting transfers between devices  14.2 us (45%)
  waiting for transfers between devices  8.79 us (28%)
  Pallas kernels  7.57 us (24%)
  other arithmetic  0.64 us (2%)
    ppermute x3, starting transfers between devices, along_columns(): lax.ppermute(value, 'train', [(k, k ^ flip * PAIR) for k in range(COLUMNS...  6.77 us
    ppermute x3, starting transfers between devices, other_part(): return lax.ppermute(value, ('parts', 'train'), pairs)  3.78 us
    pallas_call x2, Pallas kernels, condition_layer(): pl.pallas_call(functools.partial(condition_kernel, other), out_shape=jax....  3.53 us
    ppermute x3, waiting for transfers between devices, along_columns(): lax.ppermute(value, 'train', [(k, k ^ flip * PAIR) for k in range(COLUMNS...  3.48 us
    pallas_call x1, Pallas kernels, copy_near(): pl.pallas_call(copy_kernel, out_shape=jax.ShapeDtypeStruct(value.shape, v...  2.2 us
    ppermute x3, waiting for transfers between devices, other_part(): return lax.ppermute(value, ('parts', 'train'), pairs)  2.11 us
    ppermute x8, starting transfers between devices, other_core(): lax.ppermute(value, 'train', [(k, k ^ 1) for k in range(COLUMNS * PAIR)])  2.06 us
    ppermute x1, waiting for transfers between devices, direct(): received = lax.ppermute(sent, 'layer', [(0, 1), (1, 0)])  1.93 us
  transfers between devices with their start and end apart: 15, of which 8 were waited for; matrix products, arithmetic and copies ran while one was open for 0% of the time, Pallas kernels for 15%

profile of v15, /device:TPU:0, one launch (start us, length us, event | category | flops | bytes accessed | tf_op | source)
XLA Modules:
  0.0 31.2 jit_solution(890978713081793996)
XLA Ops:
  0.0 1.8 %condition_mine.1.refs_0_ = bf16[16,4096]{1,0:T(8,128)(2,1)S(1)} custom-call(bf16[2,1,16,4096]{3,2,1,0:T(8,128)(2,1)} %queries.3, f32[2,64,64]{2,1,0:T(8,128)} %left.3, f32[2,64,64]{2,1,0:T(8,128)} %right.3), custom_call_target="tpu_custom_call" | custom-call | flops 134217728 | bytes 524288 | tf_op jit(solution)/shard_map/condition_mine/pallas_call | solution.py:107
  1.8 5.1 %collective-permute-start.2 = (bf16[16,4096]{1,0:T(8,128)(2,1)S(1)}, bf16[16,4096]{1,0:T(8,128)(2,1)S(1)}, u32[]{:S(2)}, u32[]{:S(2)}) collective-permute-start(bf16[16,4096]{1,0:T(8,128)(2,1)S(1)} %condition_mine.1.refs_0_), channel_id=1, source_target_pairs={{0,12},{2,14},{4,8},{6,10},{8,4},{10,6},{12,0},{14,2},{1,13},{3,15... | collective-permute-start | bytes 393224 | tf_op jit(solution)/shard_map/ppermute | solution.py:128
  6.9 0.0 collective-permute-start
  6.9 1.8 %condition_other.1.refs_2_ = bf16[16,4096]{1,0:T(8,128)(2,1)S(1)} custom-call(bf16[2,1,16,4096]{3,2,1,0:T(8,128)(2,1)} %queries.3, f32[2,64,64]{2,1,0:T(8,128)} %left.3, f32[2,64,64]{2,1,0:T(8,128)} %right.3), custom_call_target="tpu_custom_call" | custom-call | flops 134217728 | bytes 524288 | tf_op jit(solution)/shard_map/condition_other/pallas_call | solution.py:107
  8.7 2.6 %collective-permute-done.2.refs_8_ = bf16[16,4096]{1,0:T(8,128)(2,1)S(1)} collective-permute-done((bf16[16,4096]{1,0:T(8,128)(2,1)S(1)}, bf16[16,4096]{1,0:T(8,128)(2,1)S(1)}, u32[]{:S(2)}, u32[]{:S(2)}) %collective-permute-start.2) | collective-permute-done | bytes 131104 | tf_op jit(solution)/shard_map/ppermute | solution.py:128
  11.3 1.6 %collective-permute-start.6 = (bf16[16,4096]{1,0:T(8,128)(2,1)S(1)}, bf16[16,4096]{1,0:T(8,128)(2,1)S(1)}, u32[]{:S(2)}, u32[]{:S(2)}) collective-permute-start(bf16[16,4096]{1,0:T(8,128)(2,1)S(1)} %collective-permute-done.2.refs_8_), channel_id=1, source_target_pairs={{0,4},{2,6},{4,0},{6,2},{8,12},{10,14},{12,8},{14,10},{1,5},{3,7},... | collective-permute-start | bytes 393224 | tf_op jit(solution)/shard_map/ppermute | solution.py:128
  12.9 1.5 %collective-permute-start.3 = (bf16[16,4096]{1,0:T(8,128)(2,1)S(1)}, bf16[16,4096]{1,0:T(8,128)(2,1)S(1)}, u32[]{:S(2)}, u32[]{:S(2)}) collective-permute-start(bf16[16,4096]{1,0:T(8,128)(2,1)S(1)} %collective-permute-done.2.refs_8_), channel_id=1, source_target_pairs={{0,16},{2,18},{4,20},{6,22},{8,24},{10,26},{12,28},{14,30},{16,0},... | collective-permute-start | bytes 393224 | tf_op jit(solution)/shard_map/ppermute | solution.py:138
  14.4 0.0 collective-permute-done.refs_6_
  14.4 0.0 collective-permute-start.1
  14.4 0.9 %collective-permute-start.4 = (bf16[16,4096]{1,0:T(8,128)(2,1)S(1)}, bf16[16,4096]{1,0:T(8,128)(2,1)S(1)}, u32[]{:S(2)}, u32[]{:S(2)}) collective-permute-start(bf16[16,4096]{1,0:T(8,128)(2,1)S(1)} %condition_mine.1.refs_0_), channel_id=1, source_target_pairs={{0,2},{2,0},{4,6},{6,4},{8,10},{10,8},{12,14},{14,12},{1,3},{3,1},... | collective-permute-start | bytes 393224 | tf_op jit(solution)/shard_map/ppermute | solution.py:132
  15.3 0.0 collective-permute-start.5
  15.3 0.9 %collective-permute-done.6.refs_4_ = bf16[16,4096]{1,0:T(8,128)(2,1)S(1)} collective-permute-done((bf16[16,4096]{1,0:T(8,128)(2,1)S(1)}, bf16[16,4096]{1,0:T(8,128)(2,1)S(1)}, u32[]{:S(2)}, u32[]{:S(2)}) %collective-permute-start.6) | collective-permute-done | bytes 131104 | tf_op jit(solution)/shard_map/ppermute | solution.py:128
  16.2 0.0 collective-permute-start.9
  16.2 2.1 %collective-permute-done.3.refs_14_ = bf16[16,4096]{1,0:T(8,128)(2,1)S(1)} collective-permute-done((bf16[16,4096]{1,0:T(8,128)(2,1)S(1)}, bf16[16,4096]{1,0:T(8,128)(2,1)S(1)}, u32[]{:S(2)}, u32[]{:S(2)}) %collective-permute-start.3) | collective-permute-done | bytes 131104 | tf_op jit(solution)/shard_map/ppermute | solution.py:138
  18.3 2.3 %collective-permute-start.10 = (bf16[16,4096]{1,0:T(8,128)(2,1)S(1)}, bf16[16,4096]{1,0:T(8,128)(2,1)S(1)}, u32[]{:S(2)}, u32[]{:S(2)}) collective-permute-start(bf16[16,4096]{1,0:T(8,128)(2,1)S(1)} %collective-permute-done.6.refs_4_), channel_id=1, source_target_pairs={{0,16},{2,18},{4,20},{6,22},{8,24},{10,26},{12,28},{14,30},{16,0},... | collective-permute-start | bytes 393224 | tf_op jit(solution)/shard_map/ppermute | solution.py:138
  20.6 2.2 %near.1.train = bf16[256,2,4096]{2,1,0:T(2,128)(2,1)S(1)} custom-call(bf16[256,2,4096]{2,1,0:T(2,128)(2,1)} %source.1), custom_call_target="tpu_custom_call" | custom-call | bytes 8388608 | tf_op jit(solution)/shard_map/near/pallas_call | solution.py:148
  22.8 0.0 collective-permute-done.1.refs_12_
  22.8 0.1 collective-permute-start.8
  22.9 0.0 collective-permute-done.4.refs_1_
  22.9 0.5 %collective-permute-start.12 = (bf16[16,4096]{1,0:T(8,128)(2,1)S(1)}, bf16[16,4096]{1,0:T(8,128)(2,1)S(1)}, u32[]{:S(2)}, u32[]{:S(2)}) collective-permute-start(bf16[16,4096]{1,0:T(8,128)(2,1)S(1)} %collective-permute-done.1.refs_12_), channel_id=1, source_target_pairs={{0,2},{2,0},{4,6},{6,4},{8,10},{10,8},{12,14},{14,12},{1,3},{3,1},... | collective-permute-start | bytes 393224 | tf_op jit(solution)/shard_map/ppermute | solution.py:132
  23.4 0.0 collective-permute-done.5.refs_3_
  23.4 0.1 collective-permute-start.7
  23.5 0.0 collective-permute-done.9.refs_9_
  23.5 0.4 %collective-permute-start.13 = (bf16[16,4096]{1,0:T(8,128)(2,1)S(1)}, bf16[16,4096]{1,0:T(8,128)(2,1)S(1)}, u32[]{:S(2)}, u32[]{:S(2)}) collective-permute-start(bf16[16,4096]{1,0:T(8,128)(2,1)S(1)} %collective-permute-done.3.refs_14_), channel_id=1, source_target_pairs={{0,2},{2,0},{4,6},{6,4},{8,10},{10,8},{12,14},{14,12},{1,3},{3,1},... | collective-permute-start | bytes 393224 | tf_op jit(solution)/shard_map/ppermute | solution.py:132
  23.9 0.0 collective-permute-done.10.refs_10_
  23.9 0.1 collective-permute-start.11
  24.0 0.2 collective-permute-done.8.refs_7_
  24.2 0.5 %collective-permute-done.7.refs_5_ = bf16[16,4096]{1,0:T(8,128)(2,1)S(1)} collective-permute-done((bf16[16,4096]{1,0:T(8,128)(2,1)S(1)}, bf16[16,4096]{1,0:T(8,128)(2,1)S(1)}, u32[]{:S(2)}, u32[]{:S(2)}) %collective-permute-start.7) | collective-permute-done | bytes 131104 | tf_op jit(solution)/shard_map/ppermute | solution.py:132
  24.7 0.0 collective-permute-done.12.refs_13_
  24.7 0.2 collective-permute-done.13.refs_15_
  24.9 0.3 %collective-permute-done.11.refs_11_ = bf16[16,4096]{1,0:T(8,128)(2,1)S(1)} collective-permute-done((bf16[16,4096]{1,0:T(8,128)(2,1)S(1)}, bf16[16,4096]{1,0:T(8,128)(2,1)S(1)}, u32[]{:S(2)}, u32[]{:S(2)}) %collective-permute-start.11) | collective-permute-done | bytes 131104 | tf_op jit(solution)/shard_map/ppermute | solution.py:132
  25.3 1.0 %scores_sent.1 = (f32[128,128]{1,0:T(8,128)S(1)}, bf16[2,128,4096]{2,1,0:T(8,128)(2,1)S(1)}) custom-call(bf16[256,2,4096]{2,1,0:T(2,128)(2,1)S(1)} %near.1.train, bf16[16,4096]{1,0:T(8,128)(2,1)S(1)} %condition_mine.1.refs_0_, bf16[16,4096]{1,0:T(8,128)(2,1)S(1)} %collective-permute-done.4.refs_1_, bf16[16,4096]{1,0:T(8,128)(2,1)S(1)} %condition_other.1.refs_2_, ...), custom_call_target="tpu_custom_call" | custom-call | flops 536870912 | bytes 4194304 | tf_op jit(solution)/shard_map/scores_sent/pallas_call | solution.py:214
  26.3 1.6 %collective-permute-start.14 = (f32[128,128]{1,0:T(8,128)S(1)}, f32[128,128]{1,0:T(8,128)S(1)}, u32[]{:S(2)}, u32[]{:S(2)}) collective-permute-start(f32[128,128]{1,0:T(8,128)S(1)} %get-tuple-element.18), channel_id=1, source_target_pairs={{0,1},{1,0},{2,3},{3,2},{4,5},{5,4},{6,7},{7,6},{8,9},{9,8},{10,11... | collective-permute-start | bytes 196616 | tf_op jit(solution)/shard_map/ppermute | solution.py:257
  27.8 0.8 %scores_kept.1 = f32[128,128]{1,0:T(8,128)S(1)} custom-call(bf16[256,2,4096]{2,1,0:T(2,128)(2,1)S(1)} %near.1.train, bf16[2,128,4096]{2,1,0:T(8,128)(2,1)S(1)} %get-tuple-element.17.table), custom_call_target="tpu_custom_call" | custom-call | flops 536870912 | bytes 4194304 | tf_op jit(solution)/shard_map/scores_kept/pallas_call | solution.py:214
  28.7 1.9 %collective-permute-done.14 = f32[128,128]{1,0:T(8,128)S(1)} collective-permute-done((f32[128,128]{1,0:T(8,128)S(1)}, f32[128,128]{1,0:T(8,128)S(1)}, u32[]{:S(2)}, u32[]{:S(2)}) %collective-permute-start.14) | collective-permute-done | bytes 65568 | tf_op jit(solution)/shard_map/ppermute | solution.py:257
  30.6 0.6 %add.3 = f32[128,128]{1,0:T(8,128)} add(f32[128,128]{1,0:T(8,128)S(1)} %scores_kept.1, f32[128,128]{1,0:T(8,128)S(1)} %collective-permute-done.14) | non-fusion elementwise | flops 16384 | bytes 196608 | tf_op jit(solution)/shard_map/add | solution.py:259
Async XLA Ops:
  1.8 9.5 %collective-permute-start.2 = (bf16[16,4096]{1,0:T(8,128)(2,1)S(1)}, bf16[16,4096]{1,0:T(8,128)(2,1)S(1)}, u32[]{:S(2)}, u32[]{:S(2)}) collective-permute-start(bf16[16,4096]{1,0:T(8,128)(2,1)S(1)} %condition_mine.1.refs_0_), channel_id=1, source_target_pairs={{0,12},{2,14},{4,8},{6,10},{8,4},{10,6},{12,0},{14,2},{1,13},{3,15... | collective-permute-start | bytes 393224 | tf_op jit(solution)/shard_map/ppermute | solution.py:128
  6.9 7.5 %collective-permute-start = (bf16[16,4096]{1,0:T(8,128)(2,1)S(1)}, bf16[16,4096]{1,0:T(8,128)(2,1)S(1)}, u32[]{:S(2)}, u32[]{:S(2)}) collective-permute-start(bf16[16,4096]{1,0:T(8,128)(2,1)S(1)} %condition_mine.1.refs_0_), channel_id=1, source_target_pairs={{0,4},{2,6},{4,0},{6,2},{8,12},{10,14},{12,8},{14,10},{1,5},{3,7},... | collective-permute-start | bytes 393224 | tf_op jit(solution)/shard_map/ppermute | solution.py:128
  11.3 5.0 %collective-permute-start.6 = (bf16[16,4096]{1,0:T(8,128)(2,1)S(1)}, bf16[16,4096]{1,0:T(8,128)(2,1)S(1)}, u32[]{:S(2)}, u32[]{:S(2)}) collective-permute-start(bf16[16,4096]{1,0:T(8,128)(2,1)S(1)} %collective-permute-done.2.refs_8_), channel_id=1, source_target_pairs={{0,4},{2,6},{4,0},{6,2},{8,12},{10,14},{12,8},{14,10},{1,5},{3,7},... | collective-permute-start | bytes 393224 | tf_op jit(solution)/shard_map/ppermute | solution.py:128
  12.9 5.4 %collective-permute-start.3 = (bf16[16,4096]{1,0:T(8,128)(2,1)S(1)}, bf16[16,4096]{1,0:T(8,128)(2,1)S(1)}, u32[]{:S(2)}, u32[]{:S(2)}) collective-permute-start(bf16[16,4096]{1,0:T(8,128)(2,1)S(1)} %collective-permute-done.2.refs_8_), channel_id=1, source_target_pairs={{0,16},{2,18},{4,20},{6,22},{8,24},{10,26},{12,28},{14,30},{16,0},... | collective-permute-start | bytes 393224 | tf_op jit(solution)/shard_map/ppermute | solution.py:138
  14.4 8.4 %collective-permute-start.1 = (bf16[16,4096]{1,0:T(8,128)(2,1)S(1)}, bf16[16,4096]{1,0:T(8,128)(2,1)S(1)}, u32[]{:S(2)}, u32[]{:S(2)}) collective-permute-start(bf16[16,4096]{1,0:T(8,128)(2,1)S(1)} %collective-permute-done.refs_6_), channel_id=1, source_target_pairs={{0,18},{2,16},{4,22},{6,20},{8,26},{10,24},{12,30},{14,28},{16,2},... | collective-permute-start | bytes 393224 | tf_op jit(solution)/shard_map/ppermute | solution.py:138
  14.4 8.4 %collective-permute-start.4 = (bf16[16,4096]{1,0:T(8,128)(2,1)S(1)}, bf16[16,4096]{1,0:T(8,128)(2,1)S(1)}, u32[]{:S(2)}, u32[]{:S(2)}) collective-permute-start(bf16[16,4096]{1,0:T(8,128)(2,1)S(1)} %condition_mine.1.refs_0_), channel_id=1, source_target_pairs={{0,2},{2,0},{4,6},{6,4},{8,10},{10,8},{12,14},{14,12},{1,3},{3,1},... | collective-permute-start | bytes 393224 | tf_op jit(solution)/shard_map/ppermute | solution.py:132
  15.3 8.1 %collective-permute-start.5 = (bf16[16,4096]{1,0:T(8,128)(2,1)S(1)}, bf16[16,4096]{1,0:T(8,128)(2,1)S(1)}, u32[]{:S(2)}, u32[]{:S(2)}) collective-permute-start(bf16[16,4096]{1,0:T(8,128)(2,1)S(1)} %condition_other.1.refs_2_), channel_id=1, source_target_pairs={{0,2},{2,0},{4,6},{6,4},{8,10},{10,8},{12,14},{14,12},{1,3},{3,1},... | collective-permute-start | bytes 393224 | tf_op jit(solution)/shard_map/ppermute | solution.py:132
  16.2 7.2 %collective-permute-start.9 = (bf16[16,4096]{1,0:T(8,128)(2,1)S(1)}, bf16[16,4096]{1,0:T(8,128)(2,1)S(1)}, u32[]{:S(2)}, u32[]{:S(2)}) collective-permute-start(bf16[16,4096]{1,0:T(8,128)(2,1)S(1)} %collective-permute-done.2.refs_8_), channel_id=1, source_target_pairs={{0,2},{2,0},{4,6},{6,4},{8,10},{10,8},{12,14},{14,12},{1,3},{3,1},... | collective-permute-start | bytes 393224 | tf_op jit(solution)/shard_map/ppermute | solution.py:132
  18.3 5.6 %collective-permute-start.10 = (bf16[16,4096]{1,0:T(8,128)(2,1)S(1)}, bf16[16,4096]{1,0:T(8,128)(2,1)S(1)}, u32[]{:S(2)}, u32[]{:S(2)}) collective-permute-start(bf16[16,4096]{1,0:T(8,128)(2,1)S(1)} %collective-permute-done.6.refs_4_), channel_id=1, source_target_pairs={{0,16},{2,18},{4,20},{6,22},{8,24},{10,26},{12,28},{14,30},{16,0},... | collective-permute-start | bytes 393224 | tf_op jit(solution)/shard_map/ppermute | solution.py:138
  22.8 1.4 %collective-permute-start.8 = (bf16[16,4096]{1,0:T(8,128)(2,1)S(1)}, bf16[16,4096]{1,0:T(8,128)(2,1)S(1)}, u32[]{:S(2)}, u32[]{:S(2)}) collective-permute-start(bf16[16,4096]{1,0:T(8,128)(2,1)S(1)} %collective-permute-done.refs_6_), channel_id=1, source_target_pairs={{0,2},{2,0},{4,6},{6,4},{8,10},{10,8},{12,14},{14,12},{1,3},{3,1},... | collective-permute-start | bytes 393224 | tf_op jit(solution)/shard_map/ppermute | solution.py:132
  22.9 1.8 %collective-permute-start.12 = (bf16[16,4096]{1,0:T(8,128)(2,1)S(1)}, bf16[16,4096]{1,0:T(8,128)(2,1)S(1)}, u32[]{:S(2)}, u32[]{:S(2)}) collective-permute-start(bf16[16,4096]{1,0:T(8,128)(2,1)S(1)} %collective-permute-done.1.refs_12_), channel_id=1, source_target_pairs={{0,2},{2,0},{4,6},{6,4},{8,10},{10,8},{12,14},{14,12},{1,3},{3,1},... | collective-permute-start | bytes 393224 | tf_op jit(solution)/shard_map/ppermute | solution.py:132
  23.4 1.3 %collective-permute-start.7 = (bf16[16,4096]{1,0:T(8,128)(2,1)S(1)}, bf16[16,4096]{1,0:T(8,128)(2,1)S(1)}, u32[]{:S(2)}, u32[]{:S(2)}) collective-permute-start(bf16[16,4096]{1,0:T(8,128)(2,1)S(1)} %collective-permute-done.6.refs_4_), channel_id=1, source_target_pairs={{0,2},{2,0},{4,6},{6,4},{8,10},{10,8},{12,14},{14,12},{1,3},{3,1},... | collective-permute-start | bytes 393224 | tf_op jit(solution)/shard_map/ppermute | solution.py:132
  23.5 1.4 %collective-permute-start.13 = (bf16[16,4096]{1,0:T(8,128)(2,1)S(1)}, bf16[16,4096]{1,0:T(8,128)(2,1)S(1)}, u32[]{:S(2)}, u32[]{:S(2)}) collective-permute-start(bf16[16,4096]{1,0:T(8,128)(2,1)S(1)} %collective-permute-done.3.refs_14_), channel_id=1, source_target_pairs={{0,2},{2,0},{4,6},{6,4},{8,10},{10,8},{12,14},{14,12},{1,3},{3,1},... | collective-permute-start | bytes 393224 | tf_op jit(solution)/shard_map/ppermute | solution.py:132
  23.9 1.3 %collective-permute-start.11 = (bf16[16,4096]{1,0:T(8,128)(2,1)S(1)}, bf16[16,4096]{1,0:T(8,128)(2,1)S(1)}, u32[]{:S(2)}, u32[]{:S(2)}) collective-permute-start(bf16[16,4096]{1,0:T(8,128)(2,1)S(1)} %collective-permute-done.10.refs_10_), channel_id=1, source_target_pairs={{0,2},{2,0},{4,6},{6,4},{8,10},{10,8},{12,14},{14,12},{1,3},{3,1},... | collective-permute-start | bytes 393224 | tf_op jit(solution)/shard_map/ppermute | solution.py:132
  26.3 4.3 %collective-permute-start.14 = (f32[128,128]{1,0:T(8,128)S(1)}, f32[128,128]{1,0:T(8,128)S(1)}, u32[]{:S(2)}, u32[]{:S(2)}) collective-permute-start(f32[128,128]{1,0:T(8,128)S(1)} %get-tuple-element.18), channel_id=1, source_target_pairs={{0,1},{1,0},{2,3},{3,2},{4,5},{5,4},{6,7},{7,6},{8,9},{9,8},{10,11... | collective-permute-start | bytes 196616 | tf_op jit(solution)/shard_map/ppermute | solution.py:257

commit v16 on v14

--- a/solution.py
+++ b/solution.py
@@ -197,8 +197,8 @@
                 (part, 1, 0),
                 (part, 3, 0),
                 (1 - part, 2, 0),
-                (1 - part, 1, 1),
-                (1 - part, 3, 0),
+                (1 - part, 1, 0),
+                (1 - part, 3, 1),
             )
         ):
             put(layer, flip, twin ^ cross, blocks[PAIR * k + twin][...])
@@ -235,14 +235,13 @@
     s2 = along_columns(mine, 2)
     s1 = along_columns(mine, 1)
     s3 = along_columns(mine, 3)
-    s1, other = lax.optimization_barrier((s1, other))
-    y1 = other_part(s1, cross=True)
-    y3 = other_part(s3)
+    t1 = along_columns(other, 1)
     y2 = other_part(s2)
-    y1, near = lax.optimization_barrier((y1, near))
+    y3 = other_part(s3, cross=True)
+    y3, near = lax.optimization_barrier((y3, near))
 
     blocks = []
-    for block in (mine, other, s2, s1, s3, y2, y1, y3):
+    for block in (mine, other, s2, s1, s3, y2, t1, y3):
         blocks += [block, other_core(block)]
     f32 = functools.partial(jax.ShapeDtypeStruct, dtype=jnp.float32)
     terms = [pltpu.VMEM((layer_count, share * layer_count, total), jnp.float32)]

time: 31.8 us -> 30.8 us (0.969)
  waiting for transfers between devices: 9.78 us -> 7.98 us
  starting transfers between devices: 13.6 us -> 14.4 us
    ppermute x3 -> x4, starting transfers between devices: 5.68 us -> 8 us  [along_columns(): lax.ppermute(value, 'train', [(k, k ^ flip * PAIR) for k in range(COLUMNS...]
    ppermute x3 -> x2, starting transfers between devices: 3.51 us -> 1.53 us  [other_part(): return lax.ppermute(value, ('parts', 'train'), pairs)]
    ppermute x3 -> x4, waiting for transfers between devices: 6.62 us -> 4.84 us  [along_columns(): lax.ppermute(value, 'train', [(k, k ^ flip * PAIR) for k in range(COLUMNS...]
    ppermute x8, starting transfers between devices: 2.83 us -> 3.27 us  [other_core(): lax.ppermute(value, 'train', [(k, k ^ 1) for k in range(COLUMNS * PAIR)])]
  transfers between devices with their start and end apart: 15 -> 15, of which waited for: 8 -> 7; matrix products, arithmetic and copies ran while one was open for 0% -> 0% of each run, Pallas kernels for 15% -> 16%
where the time goes in v16:
time: 30.8 us; the launch traced here: 30.6 us
  starting transfers between devices  14.4 us (47%)
  waiting for transfers between devices  7.98 us (26%)
  Pallas kernels  7.56 us (25%)
  other arithmetic  0.64 us (2%)
    ppermute x4, starting transfers between devices, along_columns(): lax.ppermute(value, 'train', [(k, k ^ flip * PAIR) for k in range(COLUMNS...  8 us
    ppermute x4, waiting for transfers between devices, along_columns(): lax.ppermute(value, 'train', [(k, k ^ flip * PAIR) for k in range(COLUMNS...  4.84 us
    pallas_call x2, Pallas kernels, condition_layer(): pl.pallas_call(functools.partial(condition_kernel, other), out_shape=jax....  3.54 us
    ppermute x8, starting transfers between devices, other_core(): lax.ppermute(value, 'train', [(k, k ^ 1) for k in range(COLUMNS * PAIR)])  3.27 us
    pallas_call x1, Pallas kernels, copy_near(): pl.pallas_call(copy_kernel, out_shape=jax.ShapeDtypeStruct(value.shape, v...  2.2 us
    ppermute x1, waiting for transfers between devices, direct(): received = lax.ppermute(sent, 'layer', [(0, 1), (1, 0)])  1.98 us
    pallas_call x2, Pallas kernels, local_call(): pl.pallas_call(kernel, out_shape=out_shape, in_specs=[spec] * len(operand...  1.83 us
    ppermute x1, starting transfers between devices, direct(): received = lax.ppermute(sent, 'layer', [(0, 1), (1, 0)])  1.56 us
  transfers between devices with their start and end apart: 15, of which 7 were waited for; matrix products, arithmetic and copies ran while one was open for 0% of the time, Pallas kernels for 16%

profile of v16, /device:TPU:0, one launch (start us, length us, event | category | flops | bytes accessed | tf_op | source)
XLA Modules:
  0.0 30.6 jit_solution(15119430211197799829)
XLA Ops:
  0.0 1.8 %condition_mine.1.refs_0_ = bf16[16,4096]{1,0:T(8,128)(2,1)S(1)} custom-call(bf16[2,1,16,4096]{3,2,1,0:T(8,128)(2,1)} %queries.3, f32[2,64,64]{2,1,0:T(8,128)} %left.3, f32[2,64,64]{2,1,0:T(8,128)} %right.3), custom_call_target="tpu_custom_call" | custom-call | flops 134217728 | bytes 524288 | tf_op jit(solution)/shard_map/condition_mine/pallas_call | solution.py:107
  1.8 5.1 %collective-permute-start = (bf16[16,4096]{1,0:T(8,128)(2,1)S(1)}, bf16[16,4096]{1,0:T(8,128)(2,1)S(1)}, u32[]{:S(2)}, u32[]{:S(2)}) collective-permute-start(bf16[16,4096]{1,0:T(8,128)(2,1)S(1)} %condition_mine.1.refs_0_), channel_id=1, source_target_pairs={{0,12},{2,14},{4,8},{6,10},{8,4},{10,6},{12,0},{14,2},{1,13},{3,15... | collective-permute-start | bytes 393224 | tf_op jit(solution)/shard_map/ppermute | solution.py:128
  6.9 1.8 %condition_other.1.refs_2_ = bf16[16,4096]{1,0:T(8,128)(2,1)S(1)} custom-call(bf16[2,1,16,4096]{3,2,1,0:T(8,128)(2,1)} %queries.3, f32[2,64,64]{2,1,0:T(8,128)} %left.3, f32[2,64,64]{2,1,0:T(8,128)} %right.3), custom_call_target="tpu_custom_call" | custom-call | flops 134217728 | bytes 524288 | tf_op jit(solution)/shard_map/condition_other/pallas_call | solution.py:107
  8.7 0.1 collective-permute-start.11
  8.7 0.6 %collective-permute-start.4 = (bf16[16,4096]{1,0:T(8,128)(2,1)S(1)}, bf16[16,4096]{1,0:T(8,128)(2,1)S(1)}, u32[]{:S(2)}, u32[]{:S(2)}) collective-permute-start(bf16[16,4096]{1,0:T(8,128)(2,1)S(1)} %condition_mine.1.refs_0_), channel_id=1, source_target_pairs={{0,8},{2,10},{4,12},{6,14},{8,0},{10,2},{12,4},{14,6},{1,9},{3,11}... | collective-permute-start | bytes 393224 | tf_op jit(solution)/shard_map/ppermute | solution.py:128
  9.3 1.7 %collective-permute-done.refs_8_ = bf16[16,4096]{1,0:T(8,128)(2,1)S(1)} collective-permute-done((bf16[16,4096]{1,0:T(8,128)(2,1)S(1)}, bf16[16,4096]{1,0:T(8,128)(2,1)S(1)}, u32[]{:S(2)}, u32[]{:S(2)}) %collective-permute-start) | collective-permute-done | bytes 131104 | tf_op jit(solution)/shard_map/ppermute | solution.py:128
  11.1 0.0 collective-permute-start.1
  11.1 1.7 %collective-permute-start.3 = (bf16[16,4096]{1,0:T(8,128)(2,1)S(1)}, bf16[16,4096]{1,0:T(8,128)(2,1)S(1)}, u32[]{:S(2)}, u32[]{:S(2)}) collective-permute-start(bf16[16,4096]{1,0:T(8,128)(2,1)S(1)} %condition_other.1.refs_2_), channel_id=1, source_target_pairs={{0,2},{2,0},{4,6},{6,4},{8,10},{10,8},{12,14},{14,12},{1,3},{3,1},... | collective-permute-start | bytes 393224 | tf_op jit(solution)/shard_map/ppermute | solution.py:132
  12.7 2.2 %collective-permute-start.6 = (bf16[16,4096]{1,0:T(8,128)(2,1)S(1)}, bf16[16,4096]{1,0:T(8,128)(2,1)S(1)}, u32[]{:S(2)}, u32[]{:S(2)}) collective-permute-start(bf16[16,4096]{1,0:T(8,128)(2,1)S(1)} %condition_mine.1.refs_0_), channel_id=1, source_target_pairs={{0,4},{2,6},{4,0},{6,2},{8,12},{10,14},{12,8},{14,10},{1,5},{3,7},... | collective-permute-start | bytes 393224 | tf_op jit(solution)/shard_map/ppermute | solution.py:128
  15.0 0.0 collective-permute-done.11.refs_12_
  15.0 0.0 collective-permute-start.2
  15.0 3.1 %collective-permute-done.4.refs_4_ = bf16[16,4096]{1,0:T(8,128)(2,1)S(1)} collective-permute-done((bf16[16,4096]{1,0:T(8,128)(2,1)S(1)}, bf16[16,4096]{1,0:T(8,128)(2,1)S(1)}, u32[]{:S(2)}, u32[]{:S(2)}) %collective-permute-start.4) | collective-permute-done | bytes 131104 | tf_op jit(solution)/shard_map/ppermute | solution.py:128
  18.1 1.5 %collective-permute-start.9 = (bf16[16,4096]{1,0:T(8,128)(2,1)S(1)}, bf16[16,4096]{1,0:T(8,128)(2,1)S(1)}, u32[]{:S(2)}, u32[]{:S(2)}) collective-permute-start(bf16[16,4096]{1,0:T(8,128)(2,1)S(1)} %collective-permute-done.4.refs_4_), channel_id=1, source_target_pairs={{0,16},{2,18},{4,20},{6,22},{8,24},{10,26},{12,28},{14,30},{16,0},... | collective-permute-start | bytes 393224 | tf_op jit(solution)/shard_map/ppermute | solution.py:138
  19.6 0.0 collective-permute-done.1.refs_14_
  19.6 0.0 collective-permute-start.12
  19.6 2.2 %near.1.train = bf16[256,2,4096]{2,1,0:T(2,128)(2,1)S(1)} custom-call(bf16[256,2,4096]{2,1,0:T(2,128)(2,1)} %source.1), custom_call_target="tpu_custom_call" | custom-call | bytes 8388608 | tf_op jit(solution)/shard_map/near/pallas_call | solution.py:148
  21.8 0.0 collective-permute-done.3.refs_3_
  21.8 0.6 %collective-permute-start.5 = (bf16[16,4096]{1,0:T(8,128)(2,1)S(1)}, bf16[16,4096]{1,0:T(8,128)(2,1)S(1)}, u32[]{:S(2)}, u32[]{:S(2)}) collective-permute-start(bf16[16,4096]{1,0:T(8,128)(2,1)S(1)} %collective-permute-done.4.refs_4_), channel_id=1, source_target_pairs={{0,2},{2,0},{4,6},{6,4},{8,10},{10,8},{12,14},{14,12},{1,3},{3,1},... | collective-permute-start | bytes 393224 | tf_op jit(solution)/shard_map/ppermute | solution.py:132
  22.4 0.0 collective-permute-done.6.refs_6_
  22.4 0.1 collective-permute-start.8
  22.5 0.0 collective-permute-done.2.refs_1_
  22.5 0.4 %collective-permute-start.7 = (bf16[16,4096]{1,0:T(8,128)(2,1)S(1)}, bf16[16,4096]{1,0:T(8,128)(2,1)S(1)}, u32[]{:S(2)}, u32[]{:S(2)}) collective-permute-start(bf16[16,4096]{1,0:T(8,128)(2,1)S(1)} %collective-permute-done.6.refs_6_), channel_id=1, source_target_pairs={{0,2},{2,0},{4,6},{6,4},{8,10},{10,8},{12,14},{14,12},{1,3},{3,1},... | collective-permute-start | bytes 393224 | tf_op jit(solution)/shard_map/ppermute | solution.py:132
  22.9 0.1 collective-permute-done.9.refs_10_
  23.0 0.0 collective-permute-start.10
  23.0 0.0 collective-permute-done.12.refs_13_
  23.0 0.5 %collective-permute-start.13 = (bf16[16,4096]{1,0:T(8,128)(2,1)S(1)}, bf16[16,4096]{1,0:T(8,128)(2,1)S(1)}, u32[]{:S(2)}, u32[]{:S(2)}) collective-permute-start(bf16[16,4096]{1,0:T(8,128)(2,1)S(1)} %collective-permute-done.1.refs_14_), channel_id=1, source_target_pairs={{0,2},{2,0},{4,6},{6,4},{8,10},{10,8},{12,14},{14,12},{1,3},{3,1},... | collective-permute-start | bytes 393224 | tf_op jit(solution)/shard_map/ppermute | solution.py:132
  23.6 0.4 %collective-permute-done.7.refs_7_ = bf16[16,4096]{1,0:T(8,128)(2,1)S(1)} collective-permute-done((bf16[16,4096]{1,0:T(8,128)(2,1)S(1)}, bf16[16,4096]{1,0:T(8,128)(2,1)S(1)}, u32[]{:S(2)}, u32[]{:S(2)}) %collective-permute-start.7) | collective-permute-done | bytes 131104 | tf_op jit(solution)/shard_map/ppermute | solution.py:132
  23.9 0.0 collective-permute-done.5.refs_5_
  23.9 0.0 collective-permute-done.8.refs_9_
  23.9 0.5 %collective-permute-done.10.refs_11_ = bf16[16,4096]{1,0:T(8,128)(2,1)S(1)} collective-permute-done((bf16[16,4096]{1,0:T(8,128)(2,1)S(1)}, bf16[16,4096]{1,0:T(8,128)(2,1)S(1)}, u32[]{:S(2)}, u32[]{:S(2)}) %collective-permute-start.10) | collective-permute-done | bytes 131104 | tf_op jit(solution)/shard_map/ppermute | solution.py:132
  24.4 0.2 collective-permute-done.13.refs_15_
  24.6 1.0 %scores_sent.1 = (f32[128,128]{1,0:T(8,128)S(1)}, bf16[2,128,4096]{2,1,0:T(8,128)(2,1)S(1)}) custom-call(bf16[256,2,4096]{2,1,0:T(2,128)(2,1)S(1)} %near.1.train, bf16[16,4096]{1,0:T(8,128)(2,1)S(1)} %condition_mine.1.refs_0_, bf16[16,4096]{1,0:T(8,128)(2,1)S(1)} %collective-permute-done.2.refs_1_, bf16[16,4096]{1,0:T(8,128)(2,1)S(1)} %condition_other.1.refs_2_, ...), custom_call_target="tpu_custom_call" | custom-call | flops 536870912 | bytes 4194304 | tf_op jit(solution)/shard_map/scores_sent/pallas_call | solution.py:214
  25.6 1.6 %collective-permute-start.14 = (f32[128,128]{1,0:T(8,128)S(1)}, f32[128,128]{1,0:T(8,128)S(1)}, u32[]{:S(2)}, u32[]{:S(2)}) collective-permute-start(f32[128,128]{1,0:T(8,128)S(1)} %get-tuple-element.12), channel_id=1, source_target_pairs={{0,1},{1,0},{2,3},{3,2},{4,5},{5,4},{6,7},{7,6},{8,9},{9,8},{10,11... | collective-permute-start | bytes 196616 | tf_op jit(solution)/shard_map/ppermute | solution.py:256
  27.1 0.8 %scores_kept.1 = f32[128,128]{1,0:T(8,128)S(1)} custom-call(bf16[256,2,4096]{2,1,0:T(2,128)(2,1)S(1)} %near.1.train, bf16[2,128,4096]{2,1,0:T(8,128)(2,1)S(1)} %get-tuple-element.11.table), custom_call_target="tpu_custom_call" | custom-call | flops 536870912 | bytes 4194304 | tf_op jit(solution)/shard_map/scores_kept/pallas_call | solution.py:214
  28.0 2.0 %collective-permute-done.14 = f32[128,128]{1,0:T(8,128)S(1)} collective-permute-done((f32[128,128]{1,0:T(8,128)S(1)}, f32[128,128]{1,0:T(8,128)S(1)}, u32[]{:S(2)}, u32[]{:S(2)}) %collective-permute-start.14) | collective-permute-done | bytes 65568 | tf_op jit(solution)/shard_map/ppermute | solution.py:256
  30.0 0.6 %add.3 = f32[128,128]{1,0:T(8,128)} add(f32[128,128]{1,0:T(8,128)S(1)} %scores_kept.1, f32[128,128]{1,0:T(8,128)S(1)} %collective-permute-done.14) | non-fusion elementwise | flops 16384 | bytes 196608 | tf_op jit(solution)/shard_map/add | solution.py:258
Async XLA Ops:
  1.8 9.3 %collective-permute-start = (bf16[16,4096]{1,0:T(8,128)(2,1)S(1)}, bf16[16,4096]{1,0:T(8,128)(2,1)S(1)}, u32[]{:S(2)}, u32[]{:S(2)}) collective-permute-start(bf16[16,4096]{1,0:T(8,128)(2,1)S(1)} %condition_mine.1.refs_0_), channel_id=1, source_target_pairs={{0,12},{2,14},{4,8},{6,10},{8,4},{10,6},{12,0},{14,2},{1,13},{3,15... | collective-permute-start | bytes 393224 | tf_op jit(solution)/shard_map/ppermute | solution.py:128
  8.7 6.3 %collective-permute-start.11 = (bf16[16,4096]{1,0:T(8,128)(2,1)S(1)}, bf16[16,4096]{1,0:T(8,128)(2,1)S(1)}, u32[]{:S(2)}, u32[]{:S(2)}) collective-permute-start(bf16[16,4096]{1,0:T(8,128)(2,1)S(1)} %condition_other.1.refs_2_), channel_id=1, source_target_pairs={{0,4},{2,6},{4,0},{6,2},{8,12},{10,14},{12,8},{14,10},{1,5},{3,7},... | collective-permute-start | bytes 393224 | tf_op jit(solution)/shard_map/ppermute | solution.py:128
  8.7 9.3 %collective-permute-start.4 = (bf16[16,4096]{1,0:T(8,128)(2,1)S(1)}, bf16[16,4096]{1,0:T(8,128)(2,1)S(1)}, u32[]{:S(2)}, u32[]{:S(2)}) collective-permute-start(bf16[16,4096]{1,0:T(8,128)(2,1)S(1)} %condition_mine.1.refs_0_), channel_id=1, source_target_pairs={{0,8},{2,10},{4,12},{6,14},{8,0},{10,2},{12,4},{14,6},{1,9},{3,11}... | collective-permute-start | bytes 393224 | tf_op jit(solution)/shard_map/ppermute | solution.py:128
  11.1 8.5 %collective-permute-start.1 = (bf16[16,4096]{1,0:T(8,128)(2,1)S(1)}, bf16[16,4096]{1,0:T(8,128)(2,1)S(1)}, u32[]{:S(2)}, u32[]{:S(2)}) collective-permute-start(bf16[16,4096]{1,0:T(8,128)(2,1)S(1)} %collective-permute-done.refs_8_), channel_id=1, source_target_pairs={{0,18},{2,16},{4,22},{6,20},{8,26},{10,24},{12,30},{14,28},{16,2},... | collective-permute-start | bytes 393224 | tf_op jit(solution)/shard_map/ppermute | solution.py:138
  11.1 10.7 %collective-permute-start.3 = (bf16[16,4096]{1,0:T(8,128)(2,1)S(1)}, bf16[16,4096]{1,0:T(8,128)(2,1)S(1)}, u32[]{:S(2)}, u32[]{:S(2)}) collective-permute-start(bf16[16,4096]{1,0:T(8,128)(2,1)S(1)} %condition_other.1.refs_2_), channel_id=1, source_target_pairs={{0,2},{2,0},{4,6},{6,4},{8,10},{10,8},{12,14},{14,12},{1,3},{3,1},... | collective-permute-start | bytes 393224 | tf_op jit(solution)/shard_map/ppermute | solution.py:132
  12.7 9.7 %collective-permute-start.6 = (bf16[16,4096]{1,0:T(8,128)(2,1)S(1)}, bf16[16,4096]{1,0:T(8,128)(2,1)S(1)}, u32[]{:S(2)}, u32[]{:S(2)}) collective-permute-start(bf16[16,4096]{1,0:T(8,128)(2,1)S(1)} %condition_mine.1.refs_0_), channel_id=1, source_target_pairs={{0,4},{2,6},{4,0},{6,2},{8,12},{10,14},{12,8},{14,10},{1,5},{3,7},... | collective-permute-start | bytes 393224 | tf_op jit(solution)/shard_map/ppermute | solution.py:128
  15.0 7.5 %collective-permute-start.2 = (bf16[16,4096]{1,0:T(8,128)(2,1)S(1)}, bf16[16,4096]{1,0:T(8,128)(2,1)S(1)}, u32[]{:S(2)}, u32[]{:S(2)}) collective-permute-start(bf16[16,4096]{1,0:T(8,128)(2,1)S(1)} %condition_mine.1.refs_0_), channel_id=1, source_target_pairs={{0,2},{2,0},{4,6},{6,4},{8,10},{10,8},{12,14},{14,12},{1,3},{3,1},... | collective-permute-start | bytes 393224 | tf_op jit(solution)/shard_map/ppermute | solution.py:132
  18.1 5.0 %collective-permute-start.9 = (bf16[16,4096]{1,0:T(8,128)(2,1)S(1)}, bf16[16,4096]{1,0:T(8,128)(2,1)S(1)}, u32[]{:S(2)}, u32[]{:S(2)}) collective-permute-start(bf16[16,4096]{1,0:T(8,128)(2,1)S(1)} %collective-permute-done.4.refs_4_), channel_id=1, source_target_pairs={{0,16},{2,18},{4,20},{6,22},{8,24},{10,26},{12,28},{14,30},{16,0},... | collective-permute-start | bytes 393224 | tf_op jit(solution)/shard_map/ppermute | solution.py:138
  19.6 3.4 %collective-permute-start.12 = (bf16[16,4096]{1,0:T(8,128)(2,1)S(1)}, bf16[16,4096]{1,0:T(8,128)(2,1)S(1)}, u32[]{:S(2)}, u32[]{:S(2)}) collective-permute-start(bf16[16,4096]{1,0:T(8,128)(2,1)S(1)} %collective-permute-done.11.refs_12_), channel_id=1, source_target_pairs={{0,2},{2,0},{4,6},{6,4},{8,10},{10,8},{12,14},{14,12},{1,3},{3,1},... | collective-permute-start | bytes 393224 | tf_op jit(solution)/shard_map/ppermute | solution.py:132
  21.8 2.1 %collective-permute-start.5 = (bf16[16,4096]{1,0:T(8,128)(2,1)S(1)}, bf16[16,4096]{1,0:T(8,128)(2,1)S(1)}, u32[]{:S(2)}, u32[]{:S(2)}) collective-permute-start(bf16[16,4096]{1,0:T(8,128)(2,1)S(1)} %collective-permute-done.4.refs_4_), channel_id=1, source_target_pairs={{0,2},{2,0},{4,6},{6,4},{8,10},{10,8},{12,14},{14,12},{1,3},{3,1},... | collective-permute-start | bytes 393224 | tf_op jit(solution)/shard_map/ppermute | solution.py:132
  22.4 1.5 %collective-permute-start.8 = (bf16[16,4096]{1,0:T(8,128)(2,1)S(1)}, bf16[16,4096]{1,0:T(8,128)(2,1)S(1)}, u32[]{:S(2)}, u32[]{:S(2)}) collective-permute-start(bf16[16,4096]{1,0:T(8,128)(2,1)S(1)} %collective-permute-done.refs_8_), channel_id=1, source_target_pairs={{0,2},{2,0},{4,6},{6,4},{8,10},{10,8},{12,14},{14,12},{1,3},{3,1},... | collective-permute-start | bytes 393224 | tf_op jit(solution)/shard_map/ppermute | solution.py:132
  22.5 1.4 %collective-permute-start.7 = (bf16[16,4096]{1,0:T(8,128)(2,1)S(1)}, bf16[16,4096]{1,0:T(8,128)(2,1)S(1)}, u32[]{:S(2)}, u32[]{:S(2)}) collective-permute-start(bf16[16,4096]{1,0:T(8,128)(2,1)S(1)} %collective-permute-done.6.refs_6_), channel_id=1, source_target_pairs={{0,2},{2,0},{4,6},{6,4},{8,10},{10,8},{12,14},{14,12},{1,3},{3,1},... | collective-permute-start | bytes 393224 | tf_op jit(solution)/shard_map/ppermute | solution.py:132
  23.0 1.3 %collective-permute-start.10 = (bf16[16,4096]{1,0:T(8,128)(2,1)S(1)}, bf16[16,4096]{1,0:T(8,128)(2,1)S(1)}, u32[]{:S(2)}, u32[]{:S(2)}) collective-permute-start(bf16[16,4096]{1,0:T(8,128)(2,1)S(1)} %collective-permute-done.9.refs_10_), channel_id=1, source_target_pairs={{0,2},{2,0},{4,6},{6,4},{8,10},{10,8},{12,14},{14,12},{1,3},{3,1},... | collective-permute-start | bytes 393224 | tf_op jit(solution)/shard_map/ppermute | solution.py:132
  23.0 1.5 %collective-permute-start.13 = (bf16[16,4096]{1,0:T(8,128)(2,1)S(1)}, bf16[16,4096]{1,0:T(8,128)(2,1)S(1)}, u32[]{:S(2)}, u32[]{:S(2)}) collective-permute-start(bf16[16,4096]{1,0:T(8,128)(2,1)S(1)} %collective-permute-done.1.refs_14_), channel_id=1, source_target_pairs={{0,2},{2,0},{4,6},{6,4},{8,10},{10,8},{12,14},{14,12},{1,3},{3,1},... | collective-permute-start | bytes 393224 | tf_op jit(solution)/shard_map/ppermute | solution.py:132
  25.6 4.4 %collective-permute-start.14 = (f32[128,128]{1,0:T(8,128)S(1)}, f32[128,128]{1,0:T(8,128)S(1)}, u32[]{:S(2)}, u32[]{:S(2)}) collective-permute-start(f32[128,128]{1,0:T(8,128)S(1)} %get-tuple-element.12), channel_id=1, source_target_pairs={{0,1},{1,0},{2,3},{3,2},{4,5},{5,4},{6,7},{7,6},{8,9},{9,8},{10,11... | collective-permute-start | bytes 196616 | tf_op jit(solution)/shard_map/ppermute | solution.py:256

commit v17 on v15

--- a/solution.py
+++ b/solution.py
@@ -234,15 +234,15 @@
     near = copy_near(train_grads)
     s1 = along_columns(mine, 1)
     s3 = along_columns(mine, 3)
-    s3, other = lax.optimization_barrier((s3, other))
     s2 = along_columns(s3, 1)
+    t2 = along_columns(other, 2)
     y1 = other_part(s1, cross=True)
     y3 = other_part(s3)
-    y2 = other_part(s2)
-    y1, y3, near = lax.optimization_barrier((y1, y3, near))
+    s2, y1, y3, t2 = lax.optimization_barrier((s2, y1, y3, t2))
+    other, near = lax.optimization_barrier((other, near))
 
     blocks = []
-    for block in (mine, other, s2, s1, s3, y2, y1, y3):
+    for block in (mine, other, s2, s1, s3, t2, y1, y3):
         blocks += [block, other_core(block)]
     f32 = functools.partial(jax.ShapeDtypeStruct, dtype=jnp.float32)
     terms = [pltpu.VMEM((layer_count, share * layer_count, total), jnp.float32)]

time: 31.4 us -> 30.4 us (0.968)
  waiting for transfers between devices: 8.79 us -> 8.01 us
    ppermute x3 -> x2, waiting for transfers between devices: 2.11 us -> 0.01 us  [other_part(): return lax.ppermute(value, ('parts', 'train'), pairs)]
    ppermute x3 -> x2, starting transfers between devices: 3.78 us -> 1.92 us  [other_part(): return lax.ppermute(value, ('parts', 'train'), pairs)]
    ppermute x3 -> x4, starting transfers between devices: 6.77 us -> 8.4 us  [along_columns(): lax.ppermute(value, 'train', [(k, k ^ flip * PAIR) for k in range(COLUMNS...]
    ppermute x3 -> x4, waiting for transfers between devices: 3.48 us -> 4.91 us  [along_columns(): lax.ppermute(value, 'train', [(k, k ^ flip * PAIR) for k in range(COLUMNS...]
  transfers between devices with their start and end apart: 15 -> 15, of which waited for: 8 -> 6; matrix products, arithmetic and copies ran while one was open for 0% -> 0% of each run, Pallas kernels for 15% -> 16%
where the time goes in v17:
time: 30.4 us; the launch traced here: 30.2 us
  starting transfers between devices  14 us (46%)
  waiting for transfers between devices  8.01 us (26%)
  Pallas kernels  7.57 us (25%)
  other arithmetic  0.64 us (2%)
    ppermute x4, starting transfers between devices, along_columns(): lax.ppermute(value, 'train', [(k, k ^ flip * PAIR) for k in range(COLUMNS...  8.4 us
    ppermute x4, waiting for transfers between devices, along_columns(): lax.ppermute(value, 'train', [(k, k ^ flip * PAIR) for k in range(COLUMNS...  4.91 us
    pallas_call x2, Pallas kernels, condition_layer(): pl.pallas_call(functools.partial(condition_kernel, other), out_shape=jax....  3.53 us
    pallas_call x1, Pallas kernels, copy_near(): pl.pallas_call(copy_kernel, out_shape=jax.ShapeDtypeStruct(value.shape, v...  2.2 us
    ppermute x8, starting transfers between devices, other_core(): lax.ppermute(value, 'train', [(k, k ^ 1) for k in range(COLUMNS * PAIR)])  2.11 us
    ppermute x1, waiting for transfers between devices, direct(): received = lax.ppermute(sent, 'layer', [(0, 1), (1, 0)])  1.93 us
    ppermute x2, starting transfers between devices, other_part(): return lax.ppermute(value, ('parts', 'train'), pairs)  1.92 us
    pallas_call x2, Pallas kernels, local_call(): pl.pallas_call(kernel, out_shape=out_shape, in_specs=[spec] * len(operand...  1.84 us
  transfers between devices with their start and end apart: 15, of which 6 were waited for; matrix products, arithmetic and copies ran while one was open for 0% of the time, Pallas kernels for 16%

profile of v17, /device:TPU:0, one launch (start us, length us, event | category | flops | bytes accessed | tf_op | source)
XLA Modules:
  0.0 30.2 jit_solution(1797139467517413648)
XLA Ops:
  0.0 1.8 %condition_mine.1.refs_0_ = bf16[16,4096]{1,0:T(8,128)(2,1)S(1)} custom-call(bf16[2,1,16,4096]{3,2,1,0:T(8,128)(2,1)} %queries.3, f32[2,64,64]{2,1,0:T(8,128)} %left.3, f32[2,64,64]{2,1,0:T(8,128)} %right.3), custom_call_target="tpu_custom_call" | custom-call | flops 134217728 | bytes 524288 | tf_op jit(solution)/shard_map/condition_mine/pallas_call | solution.py:107
  1.8 3.1 %collective-permute-start.4 = (bf16[16,4096]{1,0:T(8,128)(2,1)S(1)}, bf16[16,4096]{1,0:T(8,128)(2,1)S(1)}, u32[]{:S(2)}, u32[]{:S(2)}) collective-permute-start(bf16[16,4096]{1,0:T(8,128)(2,1)S(1)} %condition_mine.1.refs_0_), channel_id=1, source_target_pairs={{0,4},{2,6},{4,0},{6,2},{8,12},{10,14},{12,8},{14,10},{1,5},{3,7},... | collective-permute-start | bytes 393224 | tf_op jit(solution)/shard_map/ppermute | solution.py:128
  4.9 2.5 %collective-permute-start.2 = (bf16[16,4096]{1,0:T(8,128)(2,1)S(1)}, bf16[16,4096]{1,0:T(8,128)(2,1)S(1)}, u32[]{:S(2)}, u32[]{:S(2)}) collective-permute-start(bf16[16,4096]{1,0:T(8,128)(2,1)S(1)} %condition_mine.1.refs_0_), channel_id=1, source_target_pairs={{0,12},{2,14},{4,8},{6,10},{8,4},{10,6},{12,0},{14,2},{1,13},{3,15... | collective-permute-start | bytes 393224 | tf_op jit(solution)/shard_map/ppermute | solution.py:128
  7.3 1.8 %condition_other.1.refs_2_ = bf16[16,4096]{1,0:T(8,128)(2,1)S(1)} custom-call(bf16[2,1,16,4096]{3,2,1,0:T(8,128)(2,1)} %queries.3, f32[2,64,64]{2,1,0:T(8,128)} %left.3, f32[2,64,64]{2,1,0:T(8,128)} %right.3), custom_call_target="tpu_custom_call" | custom-call | flops 134217728 | bytes 524288 | tf_op jit(solution)/shard_map/condition_other/pallas_call | solution.py:107
  9.1 0.2 collective-permute-start.7
  9.3 0.0 collective-permute-done.4.refs_6_
  9.3 0.4 %collective-permute-start.5 = (bf16[16,4096]{1,0:T(8,128)(2,1)S(1)}, bf16[16,4096]{1,0:T(8,128)(2,1)S(1)}, u32[]{:S(2)}, u32[]{:S(2)}) collective-permute-start(bf16[16,4096]{1,0:T(8,128)(2,1)S(1)} %collective-permute-done.4.refs_6_), channel_id=1, source_target_pairs={{0,18},{2,16},{4,22},{6,20},{8,26},{10,24},{12,30},{14,28},{16,2},... | collective-permute-start | bytes 393224 | tf_op jit(solution)/shard_map/ppermute | solution.py:138
  9.7 4.9 %collective-permute-done.2.refs_8_ = bf16[16,4096]{1,0:T(8,128)(2,1)S(1)} collective-permute-done((bf16[16,4096]{1,0:T(8,128)(2,1)S(1)}, bf16[16,4096]{1,0:T(8,128)(2,1)S(1)}, u32[]{:S(2)}, u32[]{:S(2)}) %collective-permute-start.2) | collective-permute-done | bytes 131104 | tf_op jit(solution)/shard_map/ppermute | solution.py:128
  14.6 1.5 %collective-permute-start.6 = (bf16[16,4096]{1,0:T(8,128)(2,1)S(1)}, bf16[16,4096]{1,0:T(8,128)(2,1)S(1)}, u32[]{:S(2)}, u32[]{:S(2)}) collective-permute-start(bf16[16,4096]{1,0:T(8,128)(2,1)S(1)} %collective-permute-done.2.refs_8_), channel_id=1, source_target_pairs={{0,16},{2,18},{4,20},{6,22},{8,24},{10,26},{12,28},{14,30},{16,0},... | collective-permute-start | bytes 393224 | tf_op jit(solution)/shard_map/ppermute | solution.py:138
  16.1 2.7 %collective-permute-start.3 = (bf16[16,4096]{1,0:T(8,128)(2,1)S(1)}, bf16[16,4096]{1,0:T(8,128)(2,1)S(1)}, u32[]{:S(2)}, u32[]{:S(2)}) collective-permute-start(bf16[16,4096]{1,0:T(8,128)(2,1)S(1)} %collective-permute-done.2.refs_8_), channel_id=1, source_target_pairs={{0,4},{2,6},{4,0},{6,2},{8,12},{10,14},{12,8},{14,10},{1,5},{3,7},... | collective-permute-start | bytes 393224 | tf_op jit(solution)/shard_map/ppermute | solution.py:128
  18.8 0.0 collective-permute-start
  18.8 2.2 %near.1.train = bf16[256,2,4096]{2,1,0:T(2,128)(2,1)S(1)} custom-call(bf16[256,2,4096]{2,1,0:T(2,128)(2,1)} %source.1), custom_call_target="tpu_custom_call" | custom-call | bytes 8388608 | tf_op jit(solution)/shard_map/near/pallas_call | solution.py:148
  21.0 0.0 collective-permute-done.7.refs_10_
  21.0 0.6 %collective-permute-start.1 = (bf16[16,4096]{1,0:T(8,128)(2,1)S(1)}, bf16[16,4096]{1,0:T(8,128)(2,1)S(1)}, u32[]{:S(2)}, u32[]{:S(2)}) collective-permute-start(bf16[16,4096]{1,0:T(8,128)(2,1)S(1)} %condition_other.1.refs_2_), channel_id=1, source_target_pairs={{0,2},{2,0},{4,6},{6,4},{8,10},{10,8},{12,14},{14,12},{1,3},{3,1},... | collective-permute-start | bytes 393224 | tf_op jit(solution)/shard_map/ppermute | solution.py:132
  21.6 0.0 collective-permute-done.5.refs_12_
  21.6 0.1 collective-permute-start.9
  21.7 0.0 collective-permute-done.6.refs_14_
  21.7 0.4 %collective-permute-start.10 = (bf16[16,4096]{1,0:T(8,128)(2,1)S(1)}, bf16[16,4096]{1,0:T(8,128)(2,1)S(1)}, u32[]{:S(2)}, u32[]{:S(2)}) collective-permute-start(bf16[16,4096]{1,0:T(8,128)(2,1)S(1)} %collective-permute-done.2.refs_8_), channel_id=1, source_target_pairs={{0,2},{2,0},{4,6},{6,4},{8,10},{10,8},{12,14},{14,12},{1,3},{3,1},... | collective-permute-start | bytes 393224 | tf_op jit(solution)/shard_map/ppermute | solution.py:132
  22.1 0.0 collective-permute-done.3.refs_4_
  22.1 0.1 collective-permute-start.8
  22.2 0.0 collective-permute-done.refs_1_
  22.2 0.4 %collective-permute-start.11 = (bf16[16,4096]{1,0:T(8,128)(2,1)S(1)}, bf16[16,4096]{1,0:T(8,128)(2,1)S(1)}, u32[]{:S(2)}, u32[]{:S(2)}) collective-permute-start(bf16[16,4096]{1,0:T(8,128)(2,1)S(1)} %collective-permute-done.7.refs_10_), channel_id=1, source_target_pairs={{0,2},{2,0},{4,6},{6,4},{8,10},{10,8},{12,14},{14,12},{1,3},{3,1},... | collective-permute-start | bytes 393224 | tf_op jit(solution)/shard_map/ppermute | solution.py:132
  22.6 0.0 collective-permute-done.1.refs_3_
  22.6 0.3 %collective-permute-start.12 = (bf16[16,4096]{1,0:T(8,128)(2,1)S(1)}, bf16[16,4096]{1,0:T(8,128)(2,1)S(1)}, u32[]{:S(2)}, u32[]{:S(2)}) collective-permute-start(bf16[16,4096]{1,0:T(8,128)(2,1)S(1)} %collective-permute-done.5.refs_12_), channel_id=1, source_target_pairs={{0,2},{2,0},{4,6},{6,4},{8,10},{10,8},{12,14},{14,12},{1,3},{3,1},... | collective-permute-start | bytes 393224 | tf_op jit(solution)/shard_map/ppermute | solution.py:132
  22.9 0.0 collective-permute-done.9.refs_7_
  22.9 0.2 collective-permute-start.13
  23.1 0.0 collective-permute-done.10.refs_9_
  23.1 0.3 %collective-permute-done.8.refs_5_ = bf16[16,4096]{1,0:T(8,128)(2,1)S(1)} collective-permute-done((bf16[16,4096]{1,0:T(8,128)(2,1)S(1)}, bf16[16,4096]{1,0:T(8,128)(2,1)S(1)}, u32[]{:S(2)}, u32[]{:S(2)}) %collective-permute-start.8) | collective-permute-done | bytes 131104 | tf_op jit(solution)/shard_map/ppermute | solution.py:132
  23.4 0.2 collective-permute-done.11.refs_11_
  23.6 0.3 %collective-permute-done.12.refs_13_ = bf16[16,4096]{1,0:T(8,128)(2,1)S(1)} collective-permute-done((bf16[16,4096]{1,0:T(8,128)(2,1)S(1)}, bf16[16,4096]{1,0:T(8,128)(2,1)S(1)}, u32[]{:S(2)}, u32[]{:S(2)}) %collective-permute-start.12) | collective-permute-done | bytes 131104 | tf_op jit(solution)/shard_map/ppermute | solution.py:132
  24.0 0.3 %collective-permute-done.13.refs_15_ = bf16[16,4096]{1,0:T(8,128)(2,1)S(1)} collective-permute-done((bf16[16,4096]{1,0:T(8,128)(2,1)S(1)}, bf16[16,4096]{1,0:T(8,128)(2,1)S(1)}, u32[]{:S(2)}, u32[]{:S(2)}) %collective-permute-start.13) | collective-permute-done | bytes 131104 | tf_op jit(solution)/shard_map/ppermute | solution.py:132
  24.3 1.0 %scores_sent.1 = (f32[128,128]{1,0:T(8,128)S(1)}, bf16[2,128,4096]{2,1,0:T(8,128)(2,1)S(1)}) custom-call(bf16[256,2,4096]{2,1,0:T(2,128)(2,1)S(1)} %near.1.train, bf16[16,4096]{1,0:T(8,128)(2,1)S(1)} %condition_mine.1.refs_0_, bf16[16,4096]{1,0:T(8,128)(2,1)S(1)} %collective-permute-done.refs_1_, bf16[16,4096]{1,0:T(8,128)(2,1)S(1)} %condition_other.1.refs_2_, ...), custom_call_target="tpu_custom_call" | custom-call | flops 536870912 | bytes 4194304 | tf_op jit(solution)/shard_map/scores_sent/pallas_call | solution.py:214
  25.3 1.6 %collective-permute-start.14 = (f32[128,128]{1,0:T(8,128)S(1)}, f32[128,128]{1,0:T(8,128)S(1)}, u32[]{:S(2)}, u32[]{:S(2)}) collective-permute-start(f32[128,128]{1,0:T(8,128)S(1)} %get-tuple-element.20), channel_id=1, source_target_pairs={{0,1},{1,0},{2,3},{3,2},{4,5},{5,4},{6,7},{7,6},{8,9},{9,8},{10,11... | collective-permute-start | bytes 196616 | tf_op jit(solution)/shard_map/ppermute | solution.py:257
  26.8 0.8 %scores_kept.1 = f32[128,128]{1,0:T(8,128)S(1)} custom-call(bf16[256,2,4096]{2,1,0:T(2,128)(2,1)S(1)} %near.1.train, bf16[2,128,4096]{2,1,0:T(8,128)(2,1)S(1)} %get-tuple-element.19.table), custom_call_target="tpu_custom_call" | custom-call | flops 536870912 | bytes 4194304 | tf_op jit(solution)/shard_map/scores_kept/pallas_call | solution.py:214
  27.7 1.9 %collective-permute-done.14 = f32[128,128]{1,0:T(8,128)S(1)} collective-permute-done((f32[128,128]{1,0:T(8,128)S(1)}, f32[128,128]{1,0:T(8,128)S(1)}, u32[]{:S(2)}, u32[]{:S(2)}) %collective-permute-start.14) | collective-permute-done | bytes 65568 | tf_op jit(solution)/shard_map/ppermute | solution.py:257
  29.6 0.6 %add.3 = f32[128,128]{1,0:T(8,128)} add(f32[128,128]{1,0:T(8,128)S(1)} %scores_kept.1, f32[128,128]{1,0:T(8,128)S(1)} %collective-permute-done.14) | non-fusion elementwise | flops 16384 | bytes 196608 | tf_op jit(solution)/shard_map/add | solution.py:259
Async XLA Ops:
  1.8 7.5 %collective-permute-start.4 = (bf16[16,4096]{1,0:T(8,128)(2,1)S(1)}, bf16[16,4096]{1,0:T(8,128)(2,1)S(1)}, u32[]{:S(2)}, u32[]{:S(2)}) collective-permute-start(bf16[16,4096]{1,0:T(8,128)(2,1)S(1)} %condition_mine.1.refs_0_), channel_id=1, source_target_pairs={{0,4},{2,6},{4,0},{6,2},{8,12},{10,14},{12,8},{14,10},{1,5},{3,7},... | collective-permute-start | bytes 393224 | tf_op jit(solution)/shard_map/ppermute | solution.py:128
  4.9 9.7 %collective-permute-start.2 = (bf16[16,4096]{1,0:T(8,128)(2,1)S(1)}, bf16[16,4096]{1,0:T(8,128)(2,1)S(1)}, u32[]{:S(2)}, u32[]{:S(2)}) collective-permute-start(bf16[16,4096]{1,0:T(8,128)(2,1)S(1)} %condition_mine.1.refs_0_), channel_id=1, source_target_pairs={{0,12},{2,14},{4,8},{6,10},{8,4},{10,6},{12,0},{14,2},{1,13},{3,15... | collective-permute-start | bytes 393224 | tf_op jit(solution)/shard_map/ppermute | solution.py:128
  9.1 11.9 %collective-permute-start.7 = (bf16[16,4096]{1,0:T(8,128)(2,1)S(1)}, bf16[16,4096]{1,0:T(8,128)(2,1)S(1)}, u32[]{:S(2)}, u32[]{:S(2)}) collective-permute-start(bf16[16,4096]{1,0:T(8,128)(2,1)S(1)} %condition_other.1.refs_2_), channel_id=1, source_target_pairs={{0,8},{2,10},{4,12},{6,14},{8,0},{10,2},{12,4},{14,6},{1,9},{3,11}... | collective-permute-start | bytes 393224 | tf_op jit(solution)/shard_map/ppermute | solution.py:128
  9.3 12.3 %collective-permute-start.5 = (bf16[16,4096]{1,0:T(8,128)(2,1)S(1)}, bf16[16,4096]{1,0:T(8,128)(2,1)S(1)}, u32[]{:S(2)}, u32[]{:S(2)}) collective-permute-start(bf16[16,4096]{1,0:T(8,128)(2,1)S(1)} %collective-permute-done.4.refs_6_), channel_id=1, source_target_pairs={{0,18},{2,16},{4,22},{6,20},{8,26},{10,24},{12,30},{14,28},{16,2},... | collective-permute-start | bytes 393224 | tf_op jit(solution)/shard_map/ppermute | solution.py:138
  14.6 7.1 %collective-permute-start.6 = (bf16[16,4096]{1,0:T(8,128)(2,1)S(1)}, bf16[16,4096]{1,0:T(8,128)(2,1)S(1)}, u32[]{:S(2)}, u32[]{:S(2)}) collective-permute-start(bf16[16,4096]{1,0:T(8,128)(2,1)S(1)} %collective-permute-done.2.refs_8_), channel_id=1, source_target_pairs={{0,16},{2,18},{4,20},{6,22},{8,24},{10,26},{12,28},{14,30},{16,0},... | collective-permute-start | bytes 393224 | tf_op jit(solution)/shard_map/ppermute | solution.py:138
  16.1 6.0 %collective-permute-start.3 = (bf16[16,4096]{1,0:T(8,128)(2,1)S(1)}, bf16[16,4096]{1,0:T(8,128)(2,1)S(1)}, u32[]{:S(2)}, u32[]{:S(2)}) collective-permute-start(bf16[16,4096]{1,0:T(8,128)(2,1)S(1)} %collective-permute-done.2.refs_8_), channel_id=1, source_target_pairs={{0,4},{2,6},{4,0},{6,2},{8,12},{10,14},{12,8},{14,10},{1,5},{3,7},... | collective-permute-start | bytes 393224 | tf_op jit(solution)/shard_map/ppermute | solution.py:128
  18.8 3.4 %collective-permute-start = (bf16[16,4096]{1,0:T(8,128)(2,1)S(1)}, bf16[16,4096]{1,0:T(8,128)(2,1)S(1)}, u32[]{:S(2)}, u32[]{:S(2)}) collective-permute-start(bf16[16,4096]{1,0:T(8,128)(2,1)S(1)} %condition_mine.1.refs_0_), channel_id=1, source_target_pairs={{0,2},{2,0},{4,6},{6,4},{8,10},{10,8},{12,14},{14,12},{1,3},{3,1},... | collective-permute-start | bytes 393224 | tf_op jit(solution)/shard_map/ppermute | solution.py:132
  21.0 1.6 %collective-permute-start.1 = (bf16[16,4096]{1,0:T(8,128)(2,1)S(1)}, bf16[16,4096]{1,0:T(8,128)(2,1)S(1)}, u32[]{:S(2)}, u32[]{:S(2)}) collective-permute-start(bf16[16,4096]{1,0:T(8,128)(2,1)S(1)} %condition_other.1.refs_2_), channel_id=1, source_target_pairs={{0,2},{2,0},{4,6},{6,4},{8,10},{10,8},{12,14},{14,12},{1,3},{3,1},... | collective-permute-start | bytes 393224 | tf_op jit(solution)/shard_map/ppermute | solution.py:132
  21.6 1.3 %collective-permute-start.9 = (bf16[16,4096]{1,0:T(8,128)(2,1)S(1)}, bf16[16,4096]{1,0:T(8,128)(2,1)S(1)}, u32[]{:S(2)}, u32[]{:S(2)}) collective-permute-start(bf16[16,4096]{1,0:T(8,128)(2,1)S(1)} %collective-permute-done.4.refs_6_), channel_id=1, source_target_pairs={{0,2},{2,0},{4,6},{6,4},{8,10},{10,8},{12,14},{14,12},{1,3},{3,1},... | collective-permute-start | bytes 393224 | tf_op jit(solution)/shard_map/ppermute | solution.py:132
  21.7 1.5 %collective-permute-start.10 = (bf16[16,4096]{1,0:T(8,128)(2,1)S(1)}, bf16[16,4096]{1,0:T(8,128)(2,1)S(1)}, u32[]{:S(2)}, u32[]{:S(2)}) collective-permute-start(bf16[16,4096]{1,0:T(8,128)(2,1)S(1)} %collective-permute-done.2.refs_8_), channel_id=1, source_target_pairs={{0,2},{2,0},{4,6},{6,4},{8,10},{10,8},{12,14},{14,12},{1,3},{3,1},... | collective-permute-start | bytes 393224 | tf_op jit(solution)/shard_map/ppermute | solution.py:132
  22.1 1.3 %collective-permute-start.8 = (bf16[16,4096]{1,0:T(8,128)(2,1)S(1)}, bf16[16,4096]{1,0:T(8,128)(2,1)S(1)}, u32[]{:S(2)}, u32[]{:S(2)}) collective-permute-start(bf16[16,4096]{1,0:T(8,128)(2,1)S(1)} %collective-permute-done.3.refs_4_), channel_id=1, source_target_pairs={{0,2},{2,0},{4,6},{6,4},{8,10},{10,8},{12,14},{14,12},{1,3},{3,1},... | collective-permute-start | bytes 393224 | tf_op jit(solution)/shard_map/ppermute | solution.py:132
  22.2 1.4 %collective-permute-start.11 = (bf16[16,4096]{1,0:T(8,128)(2,1)S(1)}, bf16[16,4096]{1,0:T(8,128)(2,1)S(1)}, u32[]{:S(2)}, u32[]{:S(2)}) collective-permute-start(bf16[16,4096]{1,0:T(8,128)(2,1)S(1)} %collective-permute-done.7.refs_10_), channel_id=1, source_target_pairs={{0,2},{2,0},{4,6},{6,4},{8,10},{10,8},{12,14},{14,12},{1,3},{3,1},... | collective-permute-start | bytes 393224 | tf_op jit(solution)/shard_map/ppermute | solution.py:132
  22.6 1.3 %collective-permute-start.12 = (bf16[16,4096]{1,0:T(8,128)(2,1)S(1)}, bf16[16,4096]{1,0:T(8,128)(2,1)S(1)}, u32[]{:S(2)}, u32[]{:S(2)}) collective-permute-start(bf16[16,4096]{1,0:T(8,128)(2,1)S(1)} %collective-permute-done.5.refs_12_), channel_id=1, source_target_pairs={{0,2},{2,0},{4,6},{6,4},{8,10},{10,8},{12,14},{14,12},{1,3},{3,1},... | collective-permute-start | bytes 393224 | tf_op jit(solution)/shard_map/ppermute | solution.py:132
  22.9 1.3 %collective-permute-start.13 = (bf16[16,4096]{1,0:T(8,128)(2,1)S(1)}, bf16[16,4096]{1,0:T(8,128)(2,1)S(1)}, u32[]{:S(2)}, u32[]{:S(2)}) collective-permute-start(bf16[16,4096]{1,0:T(8,128)(2,1)S(1)} %collective-permute-done.6.refs_14_), channel_id=1, source_target_pairs={{0,2},{2,0},{4,6},{6,4},{8,10},{10,8},{12,14},{14,12},{1,3},{3,1},... | collective-permute-start | bytes 393224 | tf_op jit(solution)/shard_map/ppermute | solution.py:132
  25.3 4.3 %collective-permute-start.14 = (f32[128,128]{1,0:T(8,128)S(1)}, f32[128,128]{1,0:T(8,128)S(1)}, u32[]{:S(2)}, u32[]{:S(2)}) collective-permute-start(f32[128,128]{1,0:T(8,128)S(1)} %get-tuple-element.20), channel_id=1, source_target_pairs={{0,1},{1,0},{2,3},{3,2},{4,5},{5,4},{6,7},{7,6},{8,9},{9,8},{10,11... | collective-permute-start | bytes 196616 | tf_op jit(solution)/shard_map/ppermute | solution.py:257

commit v18 on v17

--- a/solution.py
+++ b/solution.py
@@ -234,12 +234,12 @@
     near = copy_near(train_grads)
     s1 = along_columns(mine, 1)
     s3 = along_columns(mine, 3)
+    s3, near = lax.optimization_barrier((s3, near))
     s2 = along_columns(s3, 1)
     t2 = along_columns(other, 2)
     y1 = other_part(s1, cross=True)
     y3 = other_part(s3)
     s2, y1, y3, t2 = lax.optimization_barrier((s2, y1, y3, t2))
-    other, near = lax.optimization_barrier((other, near))
 
     blocks = []
     for block in (mine, other, s2, s1, s3, t2, y1, y3):

time: 30.4 us -> 30 us (0.987)
  starting transfers between devices: 14 us -> 13.6 us
    ppermute x8, starting transfers between devices: 2.11 us -> 1.69 us  [other_core(): lax.ppermute(value, 'train', [(k, k ^ 1) for k in range(COLUMNS * PAIR)])]
  transfers between devices with their start and end apart: 15 -> 15, of which waited for: 6 -> 8; matrix products, arithmetic and copies ran while one was open for 0% -> 0% of each run, Pallas kernels for 16% -> 16%
where the time goes in v18:
time: 30 us; the launch traced here: 29.8 us
  starting transfers between devices  13.6 us (45%)
  waiting for transfers between devices  8.03 us (27%)
  Pallas kernels  7.56 us (25%)
  other arithmetic  0.64 us (2%)
    ppermute x4, starting transfers between devices, along_columns(): lax.ppermute(value, 'train', [(k, k ^ flip * PAIR) for k in range(COLUMNS...  8.4 us
    ppermute x4, waiting for transfers between devices, along_columns(): lax.ppermute(value, 'train', [(k, k ^ flip * PAIR) for k in range(COLUMNS...  5.02 us
    pallas_call x2, Pallas kernels, condition_layer(): pl.pallas_call(functools.partial(condition_kernel, other), out_shape=jax....  3.53 us
    pallas_call x1, Pallas kernels, copy_near(): pl.pallas_call(copy_kernel, out_shape=jax.ShapeDtypeStruct(value.shape, v...  2.2 us
    ppermute x1, waiting for transfers between devices, direct(): received = lax.ppermute(sent, 'layer', [(0, 1), (1, 0)])  1.98 us
    ppermute x2, starting transfers between devices, other_part(): return lax.ppermute(value, ('parts', 'train'), pairs)  1.92 us
    pallas_call x2, Pallas kernels, local_call(): pl.pallas_call(kernel, out_shape=out_shape, in_specs=[spec] * len(operand...  1.83 us
    ppermute x8, starting transfers between devices, other_core(): lax.ppermute(value, 'train', [(k, k ^ 1) for k in range(COLUMNS * PAIR)])  1.69 us
  transfers between devices with their start and end apart: 15, of which 8 were waited for; matrix products, arithmetic and copies ran while one was open for 0% of the time, Pallas kernels for 16%

profile of v18, /device:TPU:0, one launch (start us, length us, event | category | flops | bytes accessed | tf_op | source)
XLA Modules:
  0.0 29.8 jit_solution(3133723648332876079)
XLA Ops:
  0.0 1.8 %condition_mine.1.refs_0_ = bf16[16,4096]{1,0:T(8,128)(2,1)S(1)} custom-call(bf16[2,1,16,4096]{3,2,1,0:T(8,128)(2,1)} %queries.3, f32[2,64,64]{2,1,0:T(8,128)} %left.3, f32[2,64,64]{2,1,0:T(8,128)} %right.3), custom_call_target="tpu_custom_call" | custom-call | flops 134217728 | bytes 524288 | tf_op jit(solution)/shard_map/condition_mine/pallas_call | solution.py:107
  1.8 3.1 %collective-permute-start.4 = (bf16[16,4096]{1,0:T(8,128)(2,1)S(1)}, bf16[16,4096]{1,0:T(8,128)(2,1)S(1)}, u32[]{:S(2)}, u32[]{:S(2)}) collective-permute-start(bf16[16,4096]{1,0:T(8,128)(2,1)S(1)} %condition_mine.1.refs_0_), channel_id=1, source_target_pairs={{0,4},{2,6},{4,0},{6,2},{8,12},{10,14},{12,8},{14,10},{1,5},{3,7},... | collective-permute-start | bytes 393224 | tf_op jit(solution)/shard_map/ppermute | solution.py:128
  4.9 2.5 %collective-permute-start = (bf16[16,4096]{1,0:T(8,128)(2,1)S(1)}, bf16[16,4096]{1,0:T(8,128)(2,1)S(1)}, u32[]{:S(2)}, u32[]{:S(2)}) collective-permute-start(bf16[16,4096]{1,0:T(8,128)(2,1)S(1)} %condition_mine.1.refs_0_), channel_id=1, source_target_pairs={{0,12},{2,14},{4,8},{6,10},{8,4},{10,6},{12,0},{14,2},{1,13},{3,15... | collective-permute-start | bytes 393224 | tf_op jit(solution)/shard_map/ppermute | solution.py:128
  7.3 1.8 %condition_other.1.refs_2_ = bf16[16,4096]{1,0:T(8,128)(2,1)S(1)} custom-call(bf16[2,1,16,4096]{3,2,1,0:T(8,128)(2,1)} %queries.3, f32[2,64,64]{2,1,0:T(8,128)} %left.3, f32[2,64,64]{2,1,0:T(8,128)} %right.3), custom_call_target="tpu_custom_call" | custom-call | flops 134217728 | bytes 524288 | tf_op jit(solution)/shard_map/condition_other/pallas_call | solution.py:107
  9.1 0.2 collective-permute-start.7
  9.3 0.0 collective-permute-done.4.refs_6_
  9.3 0.4 %collective-permute-start.5 = (bf16[16,4096]{1,0:T(8,128)(2,1)S(1)}, bf16[16,4096]{1,0:T(8,128)(2,1)S(1)}, u32[]{:S(2)}, u32[]{:S(2)}) collective-permute-start(bf16[16,4096]{1,0:T(8,128)(2,1)S(1)} %collective-permute-done.4.refs_6_), channel_id=1, source_target_pairs={{0,18},{2,16},{4,22},{6,20},{8,26},{10,24},{12,30},{14,28},{16,2},... | collective-permute-start | bytes 393224 | tf_op jit(solution)/shard_map/ppermute | solution.py:138
  9.7 2.2 %near.1.train = bf16[256,2,4096]{2,1,0:T(2,128)(2,1)S(1)} custom-call(bf16[256,2,4096]{2,1,0:T(2,128)(2,1)} %source.1), custom_call_target="tpu_custom_call" | custom-call | bytes 8388608 | tf_op jit(solution)/shard_map/near/pallas_call | solution.py:148
  11.9 2.7 %collective-permute-done.refs_8_ = bf16[16,4096]{1,0:T(8,128)(2,1)S(1)} collective-permute-done((bf16[16,4096]{1,0:T(8,128)(2,1)S(1)}, bf16[16,4096]{1,0:T(8,128)(2,1)S(1)}, u32[]{:S(2)}, u32[]{:S(2)}) %collective-permute-start) | collective-permute-done | bytes 131104 | tf_op jit(solution)/shard_map/ppermute | solution.py:128
  14.6 1.5 %collective-permute-start.6 = (bf16[16,4096]{1,0:T(8,128)(2,1)S(1)}, bf16[16,4096]{1,0:T(8,128)(2,1)S(1)}, u32[]{:S(2)}, u32[]{:S(2)}) collective-permute-start(bf16[16,4096]{1,0:T(8,128)(2,1)S(1)} %collective-permute-done.refs_8_), channel_id=1, source_target_pairs={{0,16},{2,18},{4,20},{6,22},{8,24},{10,26},{12,28},{14,30},{16,0},... | collective-permute-start | bytes 393224 | tf_op jit(solution)/shard_map/ppermute | solution.py:138
  16.1 2.7 %collective-permute-start.3 = (bf16[16,4096]{1,0:T(8,128)(2,1)S(1)}, bf16[16,4096]{1,0:T(8,128)(2,1)S(1)}, u32[]{:S(2)}, u32[]{:S(2)}) collective-permute-start(bf16[16,4096]{1,0:T(8,128)(2,1)S(1)} %collective-permute-done.refs_8_), channel_id=1, source_target_pairs={{0,4},{2,6},{4,0},{6,2},{8,12},{10,14},{12,8},{14,10},{1,5},{3,7},... | collective-permute-start | bytes 393224 | tf_op jit(solution)/shard_map/ppermute | solution.py:128
  18.8 0.0 collective-permute-start.2
  18.8 0.4 %collective-permute-done.7.refs_10_ = bf16[16,4096]{1,0:T(8,128)(2,1)S(1)} collective-permute-done((bf16[16,4096]{1,0:T(8,128)(2,1)S(1)}, bf16[16,4096]{1,0:T(8,128)(2,1)S(1)}, u32[]{:S(2)}, u32[]{:S(2)}) %collective-permute-start.7) | collective-permute-done | bytes 131104 | tf_op jit(solution)/shard_map/ppermute | solution.py:128
  19.1 0.2 collective-permute-start.1
  19.3 0.0 collective-permute-done.5.refs_12_
  19.3 0.4 %collective-permute-start.9 = (bf16[16,4096]{1,0:T(8,128)(2,1)S(1)}, bf16[16,4096]{1,0:T(8,128)(2,1)S(1)}, u32[]{:S(2)}, u32[]{:S(2)}) collective-permute-start(bf16[16,4096]{1,0:T(8,128)(2,1)S(1)} %collective-permute-done.4.refs_6_), channel_id=1, source_target_pairs={{0,2},{2,0},{4,6},{6,4},{8,10},{10,8},{12,14},{14,12},{1,3},{3,1},... | collective-permute-start | bytes 393224 | tf_op jit(solution)/shard_map/ppermute | solution.py:132
  19.7 0.0 collective-permute-done.6.refs_14_
  19.7 0.2 collective-permute-start.10
  19.8 2.0 %collective-permute-done.3.refs_4_ = bf16[16,4096]{1,0:T(8,128)(2,1)S(1)} collective-permute-done((bf16[16,4096]{1,0:T(8,128)(2,1)S(1)}, bf16[16,4096]{1,0:T(8,128)(2,1)S(1)}, u32[]{:S(2)}, u32[]{:S(2)}) %collective-permute-start.3) | collective-permute-done | bytes 131104 | tf_op jit(solution)/shard_map/ppermute | solution.py:128
  21.8 0.0 collective-permute-start.8
  21.8 0.0 collective-permute-done.2.refs_3_
  21.8 0.5 %collective-permute-start.11 = (bf16[16,4096]{1,0:T(8,128)(2,1)S(1)}, bf16[16,4096]{1,0:T(8,128)(2,1)S(1)}, u32[]{:S(2)}, u32[]{:S(2)}) collective-permute-start(bf16[16,4096]{1,0:T(8,128)(2,1)S(1)} %collective-permute-done.7.refs_10_), channel_id=1, source_target_pairs={{0,2},{2,0},{4,6},{6,4},{8,10},{10,8},{12,14},{14,12},{1,3},{3,1},... | collective-permute-start | bytes 393224 | tf_op jit(solution)/shard_map/ppermute | solution.py:132
  22.3 0.0 collective-permute-done.1.refs_1_
  22.3 0.1 collective-permute-start.12
  22.4 0.0 collective-permute-done.9.refs_7_
  22.4 0.4 %collective-permute-start.13 = (bf16[16,4096]{1,0:T(8,128)(2,1)S(1)}, bf16[16,4096]{1,0:T(8,128)(2,1)S(1)}, u32[]{:S(2)}, u32[]{:S(2)}) collective-permute-start(bf16[16,4096]{1,0:T(8,128)(2,1)S(1)} %collective-permute-done.6.refs_14_), channel_id=1, source_target_pairs={{0,2},{2,0},{4,6},{6,4},{8,10},{10,8},{12,14},{14,12},{1,3},{3,1},... | collective-permute-start | bytes 393224 | tf_op jit(solution)/shard_map/ppermute | solution.py:132
  22.8 0.0 collective-permute-done.10.refs_9_
  22.8 0.3 %collective-permute-done.8.refs_5_ = bf16[16,4096]{1,0:T(8,128)(2,1)S(1)} collective-permute-done((bf16[16,4096]{1,0:T(8,128)(2,1)S(1)}, bf16[16,4096]{1,0:T(8,128)(2,1)S(1)}, u32[]{:S(2)}, u32[]{:S(2)}) %collective-permute-start.8) | collective-permute-done | bytes 131104 | tf_op jit(solution)/shard_map/ppermute | solution.py:132
  23.1 0.2 collective-permute-done.11.refs_11_
  23.3 0.3 %collective-permute-done.12.refs_13_ = bf16[16,4096]{1,0:T(8,128)(2,1)S(1)} collective-permute-done((bf16[16,4096]{1,0:T(8,128)(2,1)S(1)}, bf16[16,4096]{1,0:T(8,128)(2,1)S(1)}, u32[]{:S(2)}, u32[]{:S(2)}) %collective-permute-start.12) | collective-permute-done | bytes 131104 | tf_op jit(solution)/shard_map/ppermute | solution.py:132
  23.6 0.2 collective-permute-done.13.refs_15_
  23.8 1.0 %scores_sent.1 = (f32[128,128]{1,0:T(8,128)S(1)}, bf16[2,128,4096]{2,1,0:T(8,128)(2,1)S(1)}) custom-call(bf16[256,2,4096]{2,1,0:T(2,128)(2,1)S(1)} %near.1.train, bf16[16,4096]{1,0:T(8,128)(2,1)S(1)} %condition_mine.1.refs_0_, bf16[16,4096]{1,0:T(8,128)(2,1)S(1)} %collective-permute-done.1.refs_1_, bf16[16,4096]{1,0:T(8,128)(2,1)S(1)} %condition_other.1.refs_2_, ...), custom_call_target="tpu_custom_call" | custom-call | flops 536870912 | bytes 4194304 | tf_op jit(solution)/shard_map/scores_sent/pallas_call | solution.py:214
  24.8 1.6 %collective-permute-start.14 = (f32[128,128]{1,0:T(8,128)S(1)}, f32[128,128]{1,0:T(8,128)S(1)}, u32[]{:S(2)}, u32[]{:S(2)}) collective-permute-start(f32[128,128]{1,0:T(8,128)S(1)} %get-tuple-element.20), channel_id=1, source_target_pairs={{0,1},{1,0},{2,3},{3,2},{4,5},{5,4},{6,7},{7,6},{8,9},{9,8},{10,11... | collective-permute-start | bytes 196616 | tf_op jit(solution)/shard_map/ppermute | solution.py:257
  26.4 0.8 %scores_kept.1 = f32[128,128]{1,0:T(8,128)S(1)} custom-call(bf16[256,2,4096]{2,1,0:T(2,128)(2,1)S(1)} %near.1.train, bf16[2,128,4096]{2,1,0:T(8,128)(2,1)S(1)} %get-tuple-element.19.table), custom_call_target="tpu_custom_call" | custom-call | flops 536870912 | bytes 4194304 | tf_op jit(solution)/shard_map/scores_kept/pallas_call | solution.py:214
  27.2 2.0 %collective-permute-done.14 = f32[128,128]{1,0:T(8,128)S(1)} collective-permute-done((f32[128,128]{1,0:T(8,128)S(1)}, f32[128,128]{1,0:T(8,128)S(1)}, u32[]{:S(2)}, u32[]{:S(2)}) %collective-permute-start.14) | collective-permute-done | bytes 65568 | tf_op jit(solution)/shard_map/ppermute | solution.py:257
  29.2 0.6 %add.3 = f32[128,128]{1,0:T(8,128)} add(f32[128,128]{1,0:T(8,128)S(1)} %scores_kept.1, f32[128,128]{1,0:T(8,128)S(1)} %collective-permute-done.14) | non-fusion elementwise | flops 16384 | bytes 196608 | tf_op jit(solution)/shard_map/add | solution.py:259
Async XLA Ops:
  1.8 7.5 %collective-permute-start.4 = (bf16[16,4096]{1,0:T(8,128)(2,1)S(1)}, bf16[16,4096]{1,0:T(8,128)(2,1)S(1)}, u32[]{:S(2)}, u32[]{:S(2)}) collective-permute-start(bf16[16,4096]{1,0:T(8,128)(2,1)S(1)} %condition_mine.1.refs_0_), channel_id=1, source_target_pairs={{0,4},{2,6},{4,0},{6,2},{8,12},{10,14},{12,8},{14,10},{1,5},{3,7},... | collective-permute-start | bytes 393224 | tf_op jit(solution)/shard_map/ppermute | solution.py:128
  4.9 9.7 %collective-permute-start = (bf16[16,4096]{1,0:T(8,128)(2,1)S(1)}, bf16[16,4096]{1,0:T(8,128)(2,1)S(1)}, u32[]{:S(2)}, u32[]{:S(2)}) collective-permute-start(bf16[16,4096]{1,0:T(8,128)(2,1)S(1)} %condition_mine.1.refs_0_), channel_id=1, source_target_pairs={{0,12},{2,14},{4,8},{6,10},{8,4},{10,6},{12,0},{14,2},{1,13},{3,15... | collective-permute-start | bytes 393224 | tf_op jit(solution)/shard_map/ppermute | solution.py:128
  9.1 10.0 %collective-permute-start.7 = (bf16[16,4096]{1,0:T(8,128)(2,1)S(1)}, bf16[16,4096]{1,0:T(8,128)(2,1)S(1)}, u32[]{:S(2)}, u32[]{:S(2)}) collective-permute-start(bf16[16,4096]{1,0:T(8,128)(2,1)S(1)} %condition_other.1.refs_2_), channel_id=1, source_target_pairs={{0,8},{2,10},{4,12},{6,14},{8,0},{10,2},{12,4},{14,6},{1,9},{3,11}... | collective-permute-start | bytes 393224 | tf_op jit(solution)/shard_map/ppermute | solution.py:128
  9.3 10.0 %collective-permute-start.5 = (bf16[16,4096]{1,0:T(8,128)(2,1)S(1)}, bf16[16,4096]{1,0:T(8,128)(2,1)S(1)}, u32[]{:S(2)}, u32[]{:S(2)}) collective-permute-start(bf16[16,4096]{1,0:T(8,128)(2,1)S(1)} %collective-permute-done.4.refs_6_), channel_id=1, source_target_pairs={{0,18},{2,16},{4,22},{6,20},{8,26},{10,24},{12,30},{14,28},{16,2},... | collective-permute-start | bytes 393224 | tf_op jit(solution)/shard_map/ppermute | solution.py:138
  14.6 5.1 %collective-permute-start.6 = (bf16[16,4096]{1,0:T(8,128)(2,1)S(1)}, bf16[16,4096]{1,0:T(8,128)(2,1)S(1)}, u32[]{:S(2)}, u32[]{:S(2)}) collective-permute-start(bf16[16,4096]{1,0:T(8,128)(2,1)S(1)} %collective-permute-done.refs_8_), channel_id=1, source_target_pairs={{0,16},{2,18},{4,20},{6,22},{8,24},{10,26},{12,28},{14,30},{16,0},... | collective-permute-start | bytes 393224 | tf_op jit(solution)/shard_map/ppermute | solution.py:138
  16.1 5.6 %collective-permute-start.3 = (bf16[16,4096]{1,0:T(8,128)(2,1)S(1)}, bf16[16,4096]{1,0:T(8,128)(2,1)S(1)}, u32[]{:S(2)}, u32[]{:S(2)}) collective-permute-start(bf16[16,4096]{1,0:T(8,128)(2,1)S(1)} %collective-permute-done.refs_8_), channel_id=1, source_target_pairs={{0,4},{2,6},{4,0},{6,2},{8,12},{10,14},{12,8},{14,10},{1,5},{3,7},... | collective-permute-start | bytes 393224 | tf_op jit(solution)/shard_map/ppermute | solution.py:128
  18.8 3.0 %collective-permute-start.2 = (bf16[16,4096]{1,0:T(8,128)(2,1)S(1)}, bf16[16,4096]{1,0:T(8,128)(2,1)S(1)}, u32[]{:S(2)}, u32[]{:S(2)}) collective-permute-start(bf16[16,4096]{1,0:T(8,128)(2,1)S(1)} %condition_other.1.refs_2_), channel_id=1, source_target_pairs={{0,2},{2,0},{4,6},{6,4},{8,10},{10,8},{12,14},{14,12},{1,3},{3,1},... | collective-permute-start | bytes 393224 | tf_op jit(solution)/shard_map/ppermute | solution.py:132
  19.1 3.1 %collective-permute-start.1 = (bf16[16,4096]{1,0:T(8,128)(2,1)S(1)}, bf16[16,4096]{1,0:T(8,128)(2,1)S(1)}, u32[]{:S(2)}, u32[]{:S(2)}) collective-permute-start(bf16[16,4096]{1,0:T(8,128)(2,1)S(1)} %condition_mine.1.refs_0_), channel_id=1, source_target_pairs={{0,2},{2,0},{4,6},{6,4},{8,10},{10,8},{12,14},{14,12},{1,3},{3,1},... | collective-permute-start | bytes 393224 | tf_op jit(solution)/shard_map/ppermute | solution.py:132
  19.3 3.1 %collective-permute-start.9 = (bf16[16,4096]{1,0:T(8,128)(2,1)S(1)}, bf16[16,4096]{1,0:T(8,128)(2,1)S(1)}, u32[]{:S(2)}, u32[]{:S(2)}) collective-permute-start(bf16[16,4096]{1,0:T(8,128)(2,1)S(1)} %collective-permute-done.4.refs_6_), channel_id=1, source_target_pairs={{0,2},{2,0},{4,6},{6,4},{8,10},{10,8},{12,14},{14,12},{1,3},{3,1},... | collective-permute-start | bytes 393224 | tf_op jit(solution)/shard_map/ppermute | solution.py:132
  19.7 3.1 %collective-permute-start.10 = (bf16[16,4096]{1,0:T(8,128)(2,1)S(1)}, bf16[16,4096]{1,0:T(8,128)(2,1)S(1)}, u32[]{:S(2)}, u32[]{:S(2)}) collective-permute-start(bf16[16,4096]{1,0:T(8,128)(2,1)S(1)} %collective-permute-done.refs_8_), channel_id=1, source_target_pairs={{0,2},{2,0},{4,6},{6,4},{8,10},{10,8},{12,14},{14,12},{1,3},{3,1},... | collective-permute-start | bytes 393224 | tf_op jit(solution)/shard_map/ppermute | solution.py:132
  21.8 1.3 %collective-permute-start.8 = (bf16[16,4096]{1,0:T(8,128)(2,1)S(1)}, bf16[16,4096]{1,0:T(8,128)(2,1)S(1)}, u32[]{:S(2)}, u32[]{:S(2)}) collective-permute-start(bf16[16,4096]{1,0:T(8,128)(2,1)S(1)} %collective-permute-done.3.refs_4_), channel_id=1, source_target_pairs={{0,2},{2,0},{4,6},{6,4},{8,10},{10,8},{12,14},{14,12},{1,3},{3,1},... | collective-permute-start | bytes 393224 | tf_op jit(solution)/shard_map/ppermute | solution.py:132
  21.8 1.5 %collective-permute-start.11 = (bf16[16,4096]{1,0:T(8,128)(2,1)S(1)}, bf16[16,4096]{1,0:T(8,128)(2,1)S(1)}, u32[]{:S(2)}, u32[]{:S(2)}) collective-permute-start(bf16[16,4096]{1,0:T(8,128)(2,1)S(1)} %collective-permute-done.7.refs_10_), channel_id=1, source_target_pairs={{0,2},{2,0},{4,6},{6,4},{8,10},{10,8},{12,14},{14,12},{1,3},{3,1},... | collective-permute-start | bytes 393224 | tf_op jit(solution)/shard_map/ppermute | solution.py:132
  22.3 1.3 %collective-permute-start.12 = (bf16[16,4096]{1,0:T(8,128)(2,1)S(1)}, bf16[16,4096]{1,0:T(8,128)(2,1)S(1)}, u32[]{:S(2)}, u32[]{:S(2)}) collective-permute-start(bf16[16,4096]{1,0:T(8,128)(2,1)S(1)} %collective-permute-done.5.refs_12_), channel_id=1, source_target_pairs={{0,2},{2,0},{4,6},{6,4},{8,10},{10,8},{12,14},{14,12},{1,3},{3,1},... | collective-permute-start | bytes 393224 | tf_op jit(solution)/shard_map/ppermute | solution.py:132
  22.4 1.5 %collective-permute-start.13 = (bf16[16,4096]{1,0:T(8,128)(2,1)S(1)}, bf16[16,4096]{1,0:T(8,128)(2,1)S(1)}, u32[]{:S(2)}, u32[]{:S(2)}) collective-permute-start(bf16[16,4096]{1,0:T(8,128)(2,1)S(1)} %collective-permute-done.6.refs_14_), channel_id=1, source_target_pairs={{0,2},{2,0},{4,6},{6,4},{8,10},{10,8},{12,14},{14,12},{1,3},{3,1},... | collective-permute-start | bytes 393224 | tf_op jit(solution)/shard_map/ppermute | solution.py:132
  24.8 4.4 %collective-permute-start.14 = (f32[128,128]{1,0:T(8,128)S(1)}, f32[128,128]{1,0:T(8,128)S(1)}, u32[]{:S(2)}, u32[]{:S(2)}) collective-permute-start(f32[128,128]{1,0:T(8,128)S(1)} %get-tuple-element.20), channel_id=1, source_target_pairs={{0,1},{1,0},{2,3},{3,2},{4,5},{5,4},{6,7},{7,6},{8,9},{9,8},{10,11... | collective-permute-start | bytes 196616 | tf_op jit(solution)/shard_map/ppermute | solution.py:257

commit v19 on v18

--- a/solution.py
+++ b/solution.py
@@ -191,14 +191,14 @@
     for twin in range(PAIR):
         for k, (layer, flip, cross) in enumerate(
             (
+                (1 - part, 1, 1),
+                (1 - part, 3, 0),
                 (part, 0, 0),
                 (1 - part, 0, 0),
-                (part, 2, 0),
                 (part, 1, 0),
                 (part, 3, 0),
+                (part, 2, 0),
                 (1 - part, 2, 0),
-                (1 - part, 1, 1),
-                (1 - part, 3, 0),
             )
         ):
             put(layer, flip, twin ^ cross, blocks[PAIR * k + twin][...])
@@ -234,15 +234,16 @@
     near = copy_near(train_grads)
     s1 = along_columns(mine, 1)
     s3 = along_columns(mine, 3)
-    s3, near = lax.optimization_barrier((s3, near))
+    s1, s3, other, near = lax.optimization_barrier((s1, s3, other, near))
     s2 = along_columns(s3, 1)
     t2 = along_columns(other, 2)
     y1 = other_part(s1, cross=True)
     y3 = other_part(s3)
-    s2, y1, y3, t2 = lax.optimization_barrier((s2, y1, y3, t2))
+    s2, t2 = lax.optimization_barrier((s2, t2))
+    y1, y3 = lax.optimization_barrier((y1, y3))
 
     blocks = []
-    for block in (mine, other, s2, s1, s3, t2, y1, y3):
+    for block in (y1, y3, mine, other, s1, s3, s2, t2):
         blocks += [block, other_core(block)]
     f32 = functools.partial(jax.ShapeDtypeStruct, dtype=jnp.float32)
     terms = [pltpu.VMEM((layer_count, share * layer_count, total), jnp.float32)]

time: 30 us -> 32.5 us (1.083)
  waiting for transfers between devices: 8.03 us -> 11.6 us
  starting transfers between devices: 13.6 us -> 12.5 us
    ppermute x4, waiting for transfers between devices: 5.02 us -> 7 us  [along_columns(): lax.ppermute(value, 'train', [(k, k ^ flip * PAIR) for k in range(COLUMNS...]
    ppermute x2, waiting for transfers between devices: 0.01 us -> 1.57 us  [other_part(): return lax.ppermute(value, ('parts', 'train'), pairs)]
    ppermute x4, starting transfers between devices: 8.4 us -> 7.46 us  [along_columns(): lax.ppermute(value, 'train', [(k, k ^ flip * PAIR) for k in range(COLUMNS...]
    ppermute x2, starting transfers between devices: 1.92 us -> 1.55 us  [other_part(): return lax.ppermute(value, ('parts', 'train'), pairs)]
  transfers between devices with their start and end apart: 15 -> 15, of which waited for: 8 -> 9; matrix products, arithmetic and copies ran while one was open for 0% -> 0% of each run, Pallas kernels for 16% -> 15%
where the time goes in v19:
time: 32.5 us; the launch traced here: 32.3 us
  starting transfers between devices  12.5 us (38%)
  waiting for transfers between devices  11.6 us (36%)
  Pallas kernels  7.58 us (23%)
  other arithmetic  0.64 us (2%)
    ppermute x4, starting transfers between devices, along_columns(): lax.ppermute(value, 'train', [(k, k ^ flip * PAIR) for k in range(COLUMNS...  7.46 us
    ppermute x4, waiting for transfers between devices, along_columns(): lax.ppermute(value, 'train', [(k, k ^ flip * PAIR) for k in range(COLUMNS...  7 us
    pallas_call x2, Pallas kernels, condition_layer(): pl.pallas_call(functools.partial(condition_kernel, other), out_shape=jax....  3.55 us
    pallas_call x1, Pallas kernels, copy_near(): pl.pallas_call(copy_kernel, out_shape=jax.ShapeDtypeStruct(value.shape, v...  2.2 us
    ppermute x1, waiting for transfers between devices, direct(): received = lax.ppermute(sent, 'layer', [(0, 1), (1, 0)])  1.99 us
    ppermute x8, starting transfers between devices, other_core(): lax.ppermute(value, 'train', [(k, k ^ 1) for k in range(COLUMNS * PAIR)])  1.91 us
    pallas_call x2, Pallas kernels, local_call(): pl.pallas_call(kernel, out_shape=out_shape, in_specs=[spec] * len(operand...  1.83 us
    ppermute x2, waiting for transfers between devices, other_part(): return lax.ppermute(value, ('parts', 'train'), pairs)  1.57 us
  transfers between devices with their start and end apart: 15, of which 9 were waited for; matrix products, arithmetic and copies ran while one was open for 0% of the time, Pallas kernels for 15%

profile of v19, /device:TPU:0, one launch (start us, length us, event | category | flops | bytes accessed | tf_op | source)
XLA Modules:
  0.0 32.3 jit_solution(5761859217274866098)
XLA Ops:
  0.0 1.8 %condition_mine.1.refs_4_ = bf16[16,4096]{1,0:T(8,128)(2,1)S(1)} custom-call(bf16[2,1,16,4096]{3,2,1,0:T(8,128)(2,1)} %queries.3, f32[2,64,64]{2,1,0:T(8,128)} %left.3, f32[2,64,64]{2,1,0:T(8,128)} %right.3), custom_call_target="tpu_custom_call" | custom-call | flops 134217728 | bytes 524288 | tf_op jit(solution)/shard_map/condition_mine/pallas_call | solution.py:107
  1.8 5.1 %collective-permute-start.1 = (bf16[16,4096]{1,0:T(8,128)(2,1)S(1)}, bf16[16,4096]{1,0:T(8,128)(2,1)S(1)}, u32[]{:S(2)}, u32[]{:S(2)}) collective-permute-start(bf16[16,4096]{1,0:T(8,128)(2,1)S(1)} %condition_mine.1.refs_4_), channel_id=1, source_target_pairs={{0,12},{2,14},{4,8},{6,10},{8,4},{10,6},{12,0},{14,2},{1,13},{3,15... | collective-permute-start | bytes 393224 | tf_op jit(solution)/shard_map/ppermute | solution.py:128
  6.9 0.0 collective-permute-start
  6.9 2.2 %near.1.train = bf16[256,2,4096]{2,1,0:T(2,128)(2,1)S(1)} custom-call(bf16[256,2,4096]{2,1,0:T(2,128)(2,1)} %source.1), custom_call_target="tpu_custom_call" | custom-call | bytes 8388608 | tf_op jit(solution)/shard_map/near/pallas_call | solution.py:148
  9.1 1.8 %condition_other.1.refs_6_ = bf16[16,4096]{1,0:T(8,128)(2,1)S(1)} custom-call(bf16[2,1,16,4096]{3,2,1,0:T(8,128)(2,1)} %queries.3, f32[2,64,64]{2,1,0:T(8,128)} %left.3, f32[2,64,64]{2,1,0:T(8,128)} %right.3), custom_call_target="tpu_custom_call" | custom-call | flops 134217728 | bytes 524288 | tf_op jit(solution)/shard_map/condition_other/pallas_call | solution.py:107
  10.9 0.4 %collective-permute-done.1.refs_10_ = bf16[16,4096]{1,0:T(8,128)(2,1)S(1)} collective-permute-done((bf16[16,4096]{1,0:T(8,128)(2,1)S(1)}, bf16[16,4096]{1,0:T(8,128)(2,1)S(1)}, u32[]{:S(2)}, u32[]{:S(2)}) %collective-permute-start.1) | collective-permute-done | bytes 131104 | tf_op jit(solution)/shard_map/ppermute | solution.py:128
  11.3 2.0 %collective-permute-done.refs_8_ = bf16[16,4096]{1,0:T(8,128)(2,1)S(1)} collective-permute-done((bf16[16,4096]{1,0:T(8,128)(2,1)S(1)}, bf16[16,4096]{1,0:T(8,128)(2,1)S(1)}, u32[]{:S(2)}, u32[]{:S(2)}) %collective-permute-start) | collective-permute-done | bytes 131104 | tf_op jit(solution)/shard_map/ppermute | solution.py:128
  13.3 0.5 %collective-permute-start.11 = (bf16[16,4096]{1,0:T(8,128)(2,1)S(1)}, bf16[16,4096]{1,0:T(8,128)(2,1)S(1)}, u32[]{:S(2)}, u32[]{:S(2)}) collective-permute-start(bf16[16,4096]{1,0:T(8,128)(2,1)S(1)} %condition_other.1.refs_6_), channel_id=1, source_target_pairs={{0,8},{2,10},{4,12},{6,14},{8,0},{10,2},{12,4},{14,6},{1,9},{3,11}... | collective-permute-start | bytes 393224 | tf_op jit(solution)/shard_map/ppermute | solution.py:128
  13.8 1.8 %collective-permute-start.10 = (bf16[16,4096]{1,0:T(8,128)(2,1)S(1)}, bf16[16,4096]{1,0:T(8,128)(2,1)S(1)}, u32[]{:S(2)}, u32[]{:S(2)}) collective-permute-start(bf16[16,4096]{1,0:T(8,128)(2,1)S(1)} %collective-permute-done.1.refs_10_), channel_id=1, source_target_pairs={{0,4},{2,6},{4,0},{6,2},{8,12},{10,14},{12,8},{14,10},{1,5},{3,7},... | collective-permute-start | bytes 393224 | tf_op jit(solution)/shard_map/ppermute | solution.py:128
  15.6 0.0 collective-permute-start.2
  15.6 1.6 %collective-permute-start.3 = (bf16[16,4096]{1,0:T(8,128)(2,1)S(1)}, bf16[16,4096]{1,0:T(8,128)(2,1)S(1)}, u32[]{:S(2)}, u32[]{:S(2)}) collective-permute-start(bf16[16,4096]{1,0:T(8,128)(2,1)S(1)} %collective-permute-done.1.refs_10_), channel_id=1, source_target_pairs={{0,16},{2,18},{4,20},{6,22},{8,24},{10,26},{12,28},{14,30},{16,0},... | collective-permute-start | bytes 393224 | tf_op jit(solution)/shard_map/ppermute | solution.py:138
  17.2 0.3 collective-permute-start.6
  17.5 4.6 %collective-permute-done.11.refs_14_ = bf16[16,4096]{1,0:T(8,128)(2,1)S(1)} collective-permute-done((bf16[16,4096]{1,0:T(8,128)(2,1)S(1)}, bf16[16,4096]{1,0:T(8,128)(2,1)S(1)}, u32[]{:S(2)}, u32[]{:S(2)}) %collective-permute-start.11) | collective-permute-done | bytes 131104 | tf_op jit(solution)/shard_map/ppermute | solution.py:128
  22.1 0.0 collective-permute-start.8
  22.1 0.0 collective-permute-done.10.refs_12_
  22.1 0.5 %collective-permute-start.7 = (bf16[16,4096]{1,0:T(8,128)(2,1)S(1)}, bf16[16,4096]{1,0:T(8,128)(2,1)S(1)}, u32[]{:S(2)}, u32[]{:S(2)}) collective-permute-start(bf16[16,4096]{1,0:T(8,128)(2,1)S(1)} %condition_other.1.refs_6_), channel_id=1, source_target_pairs={{0,2},{2,0},{4,6},{6,4},{8,10},{10,8},{12,14},{14,12},{1,3},{3,1},... | collective-permute-start | bytes 393224 | tf_op jit(solution)/shard_map/ppermute | solution.py:132
  22.6 0.0 collective-permute-done.2.refs_0_
  22.6 0.1 collective-permute-start.9
  22.7 1.6 %collective-permute-done.3.refs_2_ = bf16[16,4096]{1,0:T(8,128)(2,1)S(1)} collective-permute-done((bf16[16,4096]{1,0:T(8,128)(2,1)S(1)}, bf16[16,4096]{1,0:T(8,128)(2,1)S(1)}, u32[]{:S(2)}, u32[]{:S(2)}) %collective-permute-start.3) | collective-permute-done | bytes 131104 | tf_op jit(solution)/shard_map/ppermute | solution.py:138
  24.2 0.0 collective-permute-start.12
  24.3 0.0 collective-permute-done.6.refs_5_
  24.3 0.5 %collective-permute-start.13 = (bf16[16,4096]{1,0:T(8,128)(2,1)S(1)}, bf16[16,4096]{1,0:T(8,128)(2,1)S(1)}, u32[]{:S(2)}, u32[]{:S(2)}) collective-permute-start(bf16[16,4096]{1,0:T(8,128)(2,1)S(1)} %collective-permute-done.11.refs_14_), channel_id=1, source_target_pairs={{0,2},{2,0},{4,6},{6,4},{8,10},{10,8},{12,14},{14,12},{1,3},{3,1},... | collective-permute-start | bytes 393224 | tf_op jit(solution)/shard_map/ppermute | solution.py:132
  24.8 0.0 collective-permute-done.8.refs_9_
  24.8 0.1 collective-permute-start.4
  24.8 0.0 collective-permute-done.7.refs_7_
  24.8 0.4 %collective-permute-start.5 = (bf16[16,4096]{1,0:T(8,128)(2,1)S(1)}, bf16[16,4096]{1,0:T(8,128)(2,1)S(1)}, u32[]{:S(2)}, u32[]{:S(2)}) collective-permute-start(bf16[16,4096]{1,0:T(8,128)(2,1)S(1)} %collective-permute-done.3.refs_2_), channel_id=1, source_target_pairs={{0,2},{2,0},{4,6},{6,4},{8,10},{10,8},{12,14},{14,12},{1,3},{3,1},... | collective-permute-start | bytes 393224 | tf_op jit(solution)/shard_map/ppermute | solution.py:132
  25.3 0.0 collective-permute-done.9.refs_11_
  25.3 0.3 collective-permute-done.12.refs_13_
  25.6 0.2 collective-permute-done.13.refs_15_
  25.8 0.3 %collective-permute-done.4.refs_1_ = bf16[16,4096]{1,0:T(8,128)(2,1)S(1)} collective-permute-done((bf16[16,4096]{1,0:T(8,128)(2,1)S(1)}, bf16[16,4096]{1,0:T(8,128)(2,1)S(1)}, u32[]{:S(2)}, u32[]{:S(2)}) %collective-permute-start.4) | collective-permute-done | bytes 131104 | tf_op jit(solution)/shard_map/ppermute | solution.py:132
  26.1 0.2 collective-permute-done.5.refs_3_
  26.3 1.0 %scores_sent.1 = (f32[128,128]{1,0:T(8,128)S(1)}, bf16[2,128,4096]{2,1,0:T(8,128)(2,1)S(1)}) custom-call(bf16[256,2,4096]{2,1,0:T(2,128)(2,1)S(1)} %near.1.train, bf16[16,4096]{1,0:T(8,128)(2,1)S(1)} %collective-permute-done.2.refs_0_, bf16[16,4096]{1,0:T(8,128)(2,1)S(1)} %collective-permute-done.4.refs_1_, ...), custom_call_target="tpu_custom_call" | custom-call | flops 536870912 | bytes 4194304 | tf_op jit(solution)/shard_map/scores_sent/pallas_call | solution.py:214
  27.3 1.6 %collective-permute-start.14 = (f32[128,128]{1,0:T(8,128)S(1)}, f32[128,128]{1,0:T(8,128)S(1)}, u32[]{:S(2)}, u32[]{:S(2)}) collective-permute-start(f32[128,128]{1,0:T(8,128)S(1)} %get-tuple-element.24), channel_id=1, source_target_pairs={{0,1},{1,0},{2,3},{3,2},{4,5},{5,4},{6,7},{7,6},{8,9},{9,8},{10,11... | collective-permute-start | bytes 196616 | tf_op jit(solution)/shard_map/ppermute | solution.py:258
  28.9 0.8 %scores_kept.1 = f32[128,128]{1,0:T(8,128)S(1)} custom-call(bf16[256,2,4096]{2,1,0:T(2,128)(2,1)S(1)} %near.1.train, bf16[2,128,4096]{2,1,0:T(8,128)(2,1)S(1)} %get-tuple-element.23.table), custom_call_target="tpu_custom_call" | custom-call | flops 536870912 | bytes 4194304 | tf_op jit(solution)/shard_map/scores_kept/pallas_call | solution.py:214
  29.7 2.0 %collective-permute-done.14 = f32[128,128]{1,0:T(8,128)S(1)} collective-permute-done((f32[128,128]{1,0:T(8,128)S(1)}, f32[128,128]{1,0:T(8,128)S(1)}, u32[]{:S(2)}, u32[]{:S(2)}) %collective-permute-start.14) | collective-permute-done | bytes 65568 | tf_op jit(solution)/shard_map/ppermute | solution.py:258
  31.7 0.6 %add.3 = f32[128,128]{1,0:T(8,128)} add(f32[128,128]{1,0:T(8,128)S(1)} %scores_kept.1, f32[128,128]{1,0:T(8,128)S(1)} %collective-permute-done.14) | non-fusion elementwise | flops 16384 | bytes 196608 | tf_op jit(solution)/shard_map/add | solution.py:260
Async XLA Ops:
  1.8 9.5 %collective-permute-start.1 = (bf16[16,4096]{1,0:T(8,128)(2,1)S(1)}, bf16[16,4096]{1,0:T(8,128)(2,1)S(1)}, u32[]{:S(2)}, u32[]{:S(2)}) collective-permute-start(bf16[16,4096]{1,0:T(8,128)(2,1)S(1)} %condition_mine.1.refs_4_), channel_id=1, source_target_pairs={{0,12},{2,14},{4,8},{6,10},{8,4},{10,6},{12,0},{14,2},{1,13},{3,15... | collective-permute-start | bytes 393224 | tf_op jit(solution)/shard_map/ppermute | solution.py:128
  6.9 6.4 %collective-permute-start = (bf16[16,4096]{1,0:T(8,128)(2,1)S(1)}, bf16[16,4096]{1,0:T(8,128)(2,1)S(1)}, u32[]{:S(2)}, u32[]{:S(2)}) collective-permute-start(bf16[16,4096]{1,0:T(8,128)(2,1)S(1)} %condition_mine.1.refs_4_), channel_id=1, source_target_pairs={{0,4},{2,6},{4,0},{6,2},{8,12},{10,14},{12,8},{14,10},{1,5},{3,7},... | collective-permute-start | bytes 393224 | tf_op jit(solution)/shard_map/ppermute | solution.py:128
  13.3 8.8 %collective-permute-start.11 = (bf16[16,4096]{1,0:T(8,128)(2,1)S(1)}, bf16[16,4096]{1,0:T(8,128)(2,1)S(1)}, u32[]{:S(2)}, u32[]{:S(2)}) collective-permute-start(bf16[16,4096]{1,0:T(8,128)(2,1)S(1)} %condition_other.1.refs_6_), channel_id=1, source_target_pairs={{0,8},{2,10},{4,12},{6,14},{8,0},{10,2},{12,4},{14,6},{1,9},{3,11}... | collective-permute-start | bytes 393224 | tf_op jit(solution)/shard_map/ppermute | solution.py:128
  13.8 8.3 %collective-permute-start.10 = (bf16[16,4096]{1,0:T(8,128)(2,1)S(1)}, bf16[16,4096]{1,0:T(8,128)(2,1)S(1)}, u32[]{:S(2)}, u32[]{:S(2)}) collective-permute-start(bf16[16,4096]{1,0:T(8,128)(2,1)S(1)} %collective-permute-done.1.refs_10_), channel_id=1, source_target_pairs={{0,4},{2,6},{4,0},{6,2},{8,12},{10,14},{12,8},{14,10},{1,5},{3,7},... | collective-permute-start | bytes 393224 | tf_op jit(solution)/shard_map/ppermute | solution.py:128
  15.6 7.0 %collective-permute-start.2 = (bf16[16,4096]{1,0:T(8,128)(2,1)S(1)}, bf16[16,4096]{1,0:T(8,128)(2,1)S(1)}, u32[]{:S(2)}, u32[]{:S(2)}) collective-permute-start(bf16[16,4096]{1,0:T(8,128)(2,1)S(1)} %collective-permute-done.refs_8_), channel_id=1, source_target_pairs={{0,18},{2,16},{4,22},{6,20},{8,26},{10,24},{12,30},{14,28},{16,2},... | collective-permute-start | bytes 393224 | tf_op jit(solution)/shard_map/ppermute | solution.py:138
  15.6 8.6 %collective-permute-start.3 = (bf16[16,4096]{1,0:T(8,128)(2,1)S(1)}, bf16[16,4096]{1,0:T(8,128)(2,1)S(1)}, u32[]{:S(2)}, u32[]{:S(2)}) collective-permute-start(bf16[16,4096]{1,0:T(8,128)(2,1)S(1)} %collective-permute-done.1.refs_10_), channel_id=1, source_target_pairs={{0,16},{2,18},{4,20},{6,22},{8,24},{10,26},{12,28},{14,30},{16,0},... | collective-permute-start | bytes 393224 | tf_op jit(solution)/shard_map/ppermute | solution.py:138
  17.2 7.1 %collective-permute-start.6 = (bf16[16,4096]{1,0:T(8,128)(2,1)S(1)}, bf16[16,4096]{1,0:T(8,128)(2,1)S(1)}, u32[]{:S(2)}, u32[]{:S(2)}) collective-permute-start(bf16[16,4096]{1,0:T(8,128)(2,1)S(1)} %condition_mine.1.refs_4_), channel_id=1, source_target_pairs={{0,2},{2,0},{4,6},{6,4},{8,10},{10,8},{12,14},{14,12},{1,3},{3,1},... | collective-permute-start | bytes 393224 | tf_op jit(solution)/shard_map/ppermute | solution.py:132
  22.1 2.7 %collective-permute-start.8 = (bf16[16,4096]{1,0:T(8,128)(2,1)S(1)}, bf16[16,4096]{1,0:T(8,128)(2,1)S(1)}, u32[]{:S(2)}, u32[]{:S(2)}) collective-permute-start(bf16[16,4096]{1,0:T(8,128)(2,1)S(1)} %collective-permute-done.refs_8_), channel_id=1, source_target_pairs={{0,2},{2,0},{4,6},{6,4},{8,10},{10,8},{12,14},{14,12},{1,3},{3,1},... | collective-permute-start | bytes 393224 | tf_op jit(solution)/shard_map/ppermute | solution.py:132
  22.1 2.7 %collective-permute-start.7 = (bf16[16,4096]{1,0:T(8,128)(2,1)S(1)}, bf16[16,4096]{1,0:T(8,128)(2,1)S(1)}, u32[]{:S(2)}, u32[]{:S(2)}) collective-permute-start(bf16[16,4096]{1,0:T(8,128)(2,1)S(1)} %condition_other.1.refs_6_), channel_id=1, source_target_pairs={{0,2},{2,0},{4,6},{6,4},{8,10},{10,8},{12,14},{14,12},{1,3},{3,1},... | collective-permute-start | bytes 393224 | tf_op jit(solution)/shard_map/ppermute | solution.py:132
  22.6 2.7 %collective-permute-start.9 = (bf16[16,4096]{1,0:T(8,128)(2,1)S(1)}, bf16[16,4096]{1,0:T(8,128)(2,1)S(1)}, u32[]{:S(2)}, u32[]{:S(2)}) collective-permute-start(bf16[16,4096]{1,0:T(8,128)(2,1)S(1)} %collective-permute-done.1.refs_10_), channel_id=1, source_target_pairs={{0,2},{2,0},{4,6},{6,4},{8,10},{10,8},{12,14},{14,12},{1,3},{3,1},... | collective-permute-start | bytes 393224 | tf_op jit(solution)/shard_map/ppermute | solution.py:132
  24.2 1.3 %collective-permute-start.12 = (bf16[16,4096]{1,0:T(8,128)(2,1)S(1)}, bf16[16,4096]{1,0:T(8,128)(2,1)S(1)}, u32[]{:S(2)}, u32[]{:S(2)}) collective-permute-start(bf16[16,4096]{1,0:T(8,128)(2,1)S(1)} %collective-permute-done.10.refs_12_), channel_id=1, source_target_pairs={{0,2},{2,0},{4,6},{6,4},{8,10},{10,8},{12,14},{14,12},{1,3},{3,1},... | collective-permute-start | bytes 393224 | tf_op jit(solution)/shard_map/ppermute | solution.py:132
  24.3 1.5 %collective-permute-start.13 = (bf16[16,4096]{1,0:T(8,128)(2,1)S(1)}, bf16[16,4096]{1,0:T(8,128)(2,1)S(1)}, u32[]{:S(2)}, u32[]{:S(2)}) collective-permute-start(bf16[16,4096]{1,0:T(8,128)(2,1)S(1)} %collective-permute-done.11.refs_14_), channel_id=1, source_target_pairs={{0,2},{2,0},{4,6},{6,4},{8,10},{10,8},{12,14},{14,12},{1,3},{3,1},... | collective-permute-start | bytes 393224 | tf_op jit(solution)/shard_map/ppermute | solution.py:132
  24.8 1.3 %collective-permute-start.4 = (bf16[16,4096]{1,0:T(8,128)(2,1)S(1)}, bf16[16,4096]{1,0:T(8,128)(2,1)S(1)}, u32[]{:S(2)}, u32[]{:S(2)}) collective-permute-start(bf16[16,4096]{1,0:T(8,128)(2,1)S(1)} %collective-permute-done.2.refs_0_), channel_id=1, source_target_pairs={{0,2},{2,0},{4,6},{6,4},{8,10},{10,8},{12,14},{14,12},{1,3},{3,1},... | collective-permute-start | bytes 393224 | tf_op jit(solution)/shard_map/ppermute | solution.py:132
  24.8 1.5 %collective-permute-start.5 = (bf16[16,4096]{1,0:T(8,128)(2,1)S(1)}, bf16[16,4096]{1,0:T(8,128)(2,1)S(1)}, u32[]{:S(2)}, u32[]{:S(2)}) collective-permute-start(bf16[16,4096]{1,0:T(8,128)(2,1)S(1)} %collective-permute-done.3.refs_2_), channel_id=1, source_target_pairs={{0,2},{2,0},{4,6},{6,4},{8,10},{10,8},{12,14},{14,12},{1,3},{3,1},... | collective-permute-start | bytes 393224 | tf_op jit(solution)/shard_map/ppermute | solution.py:132
  27.3 4.4 %collective-permute-start.14 = (f32[128,128]{1,0:T(8,128)S(1)}, f32[128,128]{1,0:T(8,128)S(1)}, u32[]{:S(2)}, u32[]{:S(2)}) collective-permute-start(f32[128,128]{1,0:T(8,128)S(1)} %get-tuple-element.24), channel_id=1, source_target_pairs={{0,1},{1,0},{2,3},{3,2},{4,5},{5,4},{6,7},{7,6},{8,9},{9,8},{10,11... | collective-permute-start | bytes 196616 | tf_op jit(solution)/shard_map/ppermute | solution.py:258

commit v20 on v18

--- a/solution.py
+++ b/solution.py
@@ -157,56 +157,37 @@
     )(pltpu.with_memory_space_constraint(value, pltpu.HBM))
 
 
-def place():
-    member = lax.axis_index("train")
-    return member // PAIR, lax.rem(member, PAIR)
-
-
-def row_scores(train, table, owner, terms, scores):
-    share = scores.shape[0]
-    rows, layer_count, width = train.shape
-    queries = table.shape[1]
-    first = pl.multiple_of(owner * share * layer_count, share * layer_count)
+def scores_kernel(away, train, *refs):
+    blocks, (scores, terms) = refs[:-2], refs[-2:]
+    part, here = lax.axis_index("parts"), lax.axis_index("layer")
+    count, width = blocks[0].shape
+    rows, layer_count, _ = train.shape
+    share, queries = scores.shape
+
+    mine, other, s2, s1, s3, t2, y1, y3 = (blocks[k : k + PAIR] for k in range(0, len(blocks), PAIR))
+    order = [*mine, *s1, *s2, *s3, *other, *y1[::-1], *t2, *y3]
+    first = pl.multiple_of((1 - here if away else here) * share * layer_count, share * layer_count)
     both = lax.dot_general(
         train.reshape(rows * layer_count, width)[pl.ds(first, share * layer_count), :],
-        table[...].reshape(layer_count * queries, width),
+        jnp.concatenate([block[...] for block in order], axis=0),
         LANES_LAST,
         preferred_element_type=jnp.float32,
     )
-    for layer in range(layer_count):
-        terms[layer] = both[:, layer * queries : (layer + 1) * queries]
-    scores[...] = sum(terms[layer, pl.ds(layer, share, stride=layer_count), :] for layer in range(layer_count))
-
-
-def sent_kernel(train, *refs):
-    blocks, (scores, table, terms) = refs[:-3], refs[-3:]
-    part = lax.axis_index("parts")
-    column, core = place()
-    count = blocks[0].shape[0]
-
-    def put(layer, flip, other, block):
-        member = (column ^ flip) * PAIR + (core ^ other)
-        table[layer, pl.ds(pl.multiple_of(member * count, count), count), :] = block
-
-    for twin in range(PAIR):
-        for k, (layer, flip, cross) in enumerate(
-            (
-                (part, 0, 0),
-                (1 - part, 0, 0),
-                (part, 2, 0),
-                (part, 1, 0),
-                (part, 3, 0),
-                (1 - part, 2, 0),
-                (1 - part, 1, 1),
-                (1 - part, 3, 0),
-            )
-        ):
-            put(layer, flip, twin ^ cross, blocks[PAIR * k + twin][...])
-    row_scores(train, table, 1 - lax.axis_index("layer"), terms, scores)
-
-
-def kept_kernel(train, table, scores, terms):
-    row_scores(train, table, lax.axis_index("layer"), terms, scores)
+    for k in range(layer_count):
+        terms[k] = both[:, k * queries : (k + 1) * queries]
+    total = (
+        terms[0, pl.ds(part, share, stride=layer_count), :] + terms[1, pl.ds(1 - part, share, stride=layer_count), :]
+    )
+
+    place = lax.axis_index("train")
+    lane = lax.broadcasted_iota(jnp.int32, (share, queries), 1)
+    span = count
+    while span < queries:
+        swapped = jnp.where((lane & span) == 0, pltpu.roll(total, queries - span, 1), pltpu.roll(total, span, 1))
+        odd = jnp.full((share, queries), place & (span // count), jnp.int32) != 0
+        total = jnp.where(odd, swapped, total)
+        span *= 2
+    scores[...] = total
 
 
 def local_call(kernel, name, out_shape, scratch_shapes, *operands):
@@ -244,19 +225,18 @@
     blocks = []
     for block in (mine, other, s2, s1, s3, t2, y1, y3):
         blocks += [block, other_core(block)]
-    f32 = functools.partial(jax.ShapeDtypeStruct, dtype=jnp.float32)
-    terms = [pltpu.VMEM((layer_count, share * layer_count, total), jnp.float32)]
-    sent, table = local_call(
-        sent_kernel,
-        "scores_sent",
-        [f32((share, total)), jax.ShapeDtypeStruct((layer_count, total, width), jnp.bfloat16)],
-        terms,
-        near,
-        *blocks,
-    )
-    received = lax.ppermute(sent, "layer", [(0, 1), (1, 0)])
-    kept = local_call(kept_kernel, "scores_kept", f32((share, total)), terms, near, table)
-    return kept + received
+    def scores(away):
+        return local_call(
+            functools.partial(scores_kernel, away),
+            "scores_sent" if away else "scores_kept",
+            jax.ShapeDtypeStruct((share, total), jnp.float32),
+            [pltpu.VMEM((layer_count, share * layer_count, total), jnp.float32)],
+            near,
+            *blocks,
+        )
+
+    received = lax.ppermute(scores(True), "layer", [(0, 1), (1, 0)])
+    return scores(False) + received
 
 
 def general(shape, train_grads, queries, left_factor, right_factor):

time: 30 us -> 30.1 us (level)
  transfers between devices with their start and end apart: 15 -> 15, of which waited for: 8 -> 8; matrix products, arithmetic and copies ran while one was open for 0% -> 0% of each run, Pallas kernels for 16% -> 17%
where the time goes in v20:
time: 30.1 us; the launch traced here: 29.9 us
  starting transfers between devices  13.6 us (45%)
  waiting for transfers between devices  7.83 us (26%)
  Pallas kernels  7.81 us (26%)
  other arithmetic  0.64 us (2%)
    ppermute x4, starting transfers between devices, along_columns(): lax.ppermute(value, 'train', [(k, k ^ flip * PAIR) for k in range(COLUMNS...  8.4 us
    ppermute x4, waiting for transfers between devices, along_columns(): lax.ppermute(value, 'train', [(k, k ^ flip * PAIR) for k in range(COLUMNS...  5.02 us
    pallas_call x2, Pallas kernels, condition_layer(): pl.pallas_call(functools.partial(condition_kernel, other), out_shape=jax....  3.53 us
    pallas_call x1, Pallas kernels, copy_near(): pl.pallas_call(copy_kernel, out_shape=jax.ShapeDtypeStruct(value.shape, v...  2.2 us
    pallas_call x2, Pallas kernels, local_call(): pl.pallas_call(kernel, out_shape=out_shape, in_specs=[spec] * len(operand...  2.08 us
    ppermute x2, starting transfers between devices, other_part(): return lax.ppermute(value, ('parts', 'train'), pairs)  1.92 us
    ppermute x1, waiting for transfers between devices, direct(): received = lax.ppermute(scores(True), 'layer', [(0, 1), (1, 0)])  1.78 us
    ppermute x8, starting transfers between devices, other_core(): lax.ppermute(value, 'train', [(k, k ^ 1) for k in range(COLUMNS * PAIR)])  1.69 us
  transfers between devices with their start and end apart: 15, of which 8 were waited for; matrix products, arithmetic and copies ran while one was open for 0% of the time, Pallas kernels for 17%

profile of v20, /device:TPU:0, one launch (start us, length us, event | category | flops | bytes accessed | tf_op | source)
XLA Modules:
  0.0 29.9 jit_solution(8472811659853718526)
XLA Ops:
  0.0 1.8 %condition_mine.1.refs_0_ = bf16[16,4096]{1,0:T(8,128)(2,1)S(1)} custom-call(bf16[2,1,16,4096]{3,2,1,0:T(8,128)(2,1)} %queries.3, f32[2,64,64]{2,1,0:T(8,128)} %left.3, f32[2,64,64]{2,1,0:T(8,128)} %right.3), custom_call_target="tpu_custom_call" | custom-call | flops 134217728 | bytes 524288 | tf_op jit(solution)/shard_map/condition_mine/pallas_call | solution.py:107
  1.8 3.1 %collective-permute-start.4 = (bf16[16,4096]{1,0:T(8,128)(2,1)S(1)}, bf16[16,4096]{1,0:T(8,128)(2,1)S(1)}, u32[]{:S(2)}, u32[]{:S(2)}) collective-permute-start(bf16[16,4096]{1,0:T(8,128)(2,1)S(1)} %condition_mine.1.refs_0_), channel_id=1, source_target_pairs={{0,4},{2,6},{4,0},{6,2},{8,12},{10,14},{12,8},{14,10},{1,5},{3,7},... | collective-permute-start | bytes 393224 | tf_op jit(solution)/shard_map/ppermute | solution.py:128
  4.9 2.5 %collective-permute-start = (bf16[16,4096]{1,0:T(8,128)(2,1)S(1)}, bf16[16,4096]{1,0:T(8,128)(2,1)S(1)}, u32[]{:S(2)}, u32[]{:S(2)}) collective-permute-start(bf16[16,4096]{1,0:T(8,128)(2,1)S(1)} %condition_mine.1.refs_0_), channel_id=1, source_target_pairs={{0,12},{2,14},{4,8},{6,10},{8,4},{10,6},{12,0},{14,2},{1,13},{3,15... | collective-permute-start | bytes 393224 | tf_op jit(solution)/shard_map/ppermute | solution.py:128
  7.3 1.8 %condition_other.1.refs_2_ = bf16[16,4096]{1,0:T(8,128)(2,1)S(1)} custom-call(bf16[2,1,16,4096]{3,2,1,0:T(8,128)(2,1)} %queries.3, f32[2,64,64]{2,1,0:T(8,128)} %left.3, f32[2,64,64]{2,1,0:T(8,128)} %right.3), custom_call_target="tpu_custom_call" | custom-call | flops 134217728 | bytes 524288 | tf_op jit(solution)/shard_map/condition_other/pallas_call | solution.py:107
  9.1 0.2 collective-permute-start.7
  9.3 0.0 collective-permute-done.4.refs_6_
  9.3 0.4 %collective-permute-start.5 = (bf16[16,4096]{1,0:T(8,128)(2,1)S(1)}, bf16[16,4096]{1,0:T(8,128)(2,1)S(1)}, u32[]{:S(2)}, u32[]{:S(2)}) collective-permute-start(bf16[16,4096]{1,0:T(8,128)(2,1)S(1)} %collective-permute-done.4.refs_6_), channel_id=1, source_target_pairs={{0,18},{2,16},{4,22},{6,20},{8,26},{10,24},{12,30},{14,28},{16,2},... | collective-permute-start | bytes 393224 | tf_op jit(solution)/shard_map/ppermute | solution.py:138
  9.7 2.2 %near.1.train = bf16[256,2,4096]{2,1,0:T(2,128)(2,1)S(1)} custom-call(bf16[256,2,4096]{2,1,0:T(2,128)(2,1)} %source.1), custom_call_target="tpu_custom_call" | custom-call | bytes 8388608 | tf_op jit(solution)/shard_map/near/pallas_call | solution.py:148
  11.9 2.7 %collective-permute-done.refs_8_ = bf16[16,4096]{1,0:T(8,128)(2,1)S(1)} collective-permute-done((bf16[16,4096]{1,0:T(8,128)(2,1)S(1)}, bf16[16,4096]{1,0:T(8,128)(2,1)S(1)}, u32[]{:S(2)}, u32[]{:S(2)}) %collective-permute-start) | collective-permute-done | bytes 131104 | tf_op jit(solution)/shard_map/ppermute | solution.py:128
  14.6 1.5 %collective-permute-start.6 = (bf16[16,4096]{1,0:T(8,128)(2,1)S(1)}, bf16[16,4096]{1,0:T(8,128)(2,1)S(1)}, u32[]{:S(2)}, u32[]{:S(2)}) collective-permute-start(bf16[16,4096]{1,0:T(8,128)(2,1)S(1)} %collective-permute-done.refs_8_), channel_id=1, source_target_pairs={{0,16},{2,18},{4,20},{6,22},{8,24},{10,26},{12,28},{14,30},{16,0},... | collective-permute-start | bytes 393224 | tf_op jit(solution)/shard_map/ppermute | solution.py:138
  16.1 2.7 %collective-permute-start.3 = (bf16[16,4096]{1,0:T(8,128)(2,1)S(1)}, bf16[16,4096]{1,0:T(8,128)(2,1)S(1)}, u32[]{:S(2)}, u32[]{:S(2)}) collective-permute-start(bf16[16,4096]{1,0:T(8,128)(2,1)S(1)} %collective-permute-done.refs_8_), channel_id=1, source_target_pairs={{0,4},{2,6},{4,0},{6,2},{8,12},{10,14},{12,8},{14,10},{1,5},{3,7},... | collective-permute-start | bytes 393224 | tf_op jit(solution)/shard_map/ppermute | solution.py:128
  18.8 0.0 collective-permute-start.2
  18.8 0.4 %collective-permute-done.7.refs_10_ = bf16[16,4096]{1,0:T(8,128)(2,1)S(1)} collective-permute-done((bf16[16,4096]{1,0:T(8,128)(2,1)S(1)}, bf16[16,4096]{1,0:T(8,128)(2,1)S(1)}, u32[]{:S(2)}, u32[]{:S(2)}) %collective-permute-start.7) | collective-permute-done | bytes 131104 | tf_op jit(solution)/shard_map/ppermute | solution.py:128
  19.1 0.2 collective-permute-start.1
  19.3 0.0 collective-permute-done.5.refs_12_
  19.3 0.4 %collective-permute-start.9 = (bf16[16,4096]{1,0:T(8,128)(2,1)S(1)}, bf16[16,4096]{1,0:T(8,128)(2,1)S(1)}, u32[]{:S(2)}, u32[]{:S(2)}) collective-permute-start(bf16[16,4096]{1,0:T(8,128)(2,1)S(1)} %collective-permute-done.4.refs_6_), channel_id=1, source_target_pairs={{0,2},{2,0},{4,6},{6,4},{8,10},{10,8},{12,14},{14,12},{1,3},{3,1},... | collective-permute-start | bytes 393224 | tf_op jit(solution)/shard_map/ppermute | solution.py:132
  19.7 0.0 collective-permute-done.6.refs_14_
  19.7 0.2 collective-permute-start.10
  19.8 2.0 %collective-permute-done.3.refs_4_ = bf16[16,4096]{1,0:T(8,128)(2,1)S(1)} collective-permute-done((bf16[16,4096]{1,0:T(8,128)(2,1)S(1)}, bf16[16,4096]{1,0:T(8,128)(2,1)S(1)}, u32[]{:S(2)}, u32[]{:S(2)}) %collective-permute-start.3) | collective-permute-done | bytes 131104 | tf_op jit(solution)/shard_map/ppermute | solution.py:128
  21.8 0.0 collective-permute-start.8
  21.8 0.0 collective-permute-done.2.refs_3_
  21.8 0.5 %collective-permute-start.11 = (bf16[16,4096]{1,0:T(8,128)(2,1)S(1)}, bf16[16,4096]{1,0:T(8,128)(2,1)S(1)}, u32[]{:S(2)}, u32[]{:S(2)}) collective-permute-start(bf16[16,4096]{1,0:T(8,128)(2,1)S(1)} %collective-permute-done.7.refs_10_), channel_id=1, source_target_pairs={{0,2},{2,0},{4,6},{6,4},{8,10},{10,8},{12,14},{14,12},{1,3},{3,1},... | collective-permute-start | bytes 393224 | tf_op jit(solution)/shard_map/ppermute | solution.py:132
  22.3 0.0 collective-permute-done.1.refs_1_
  22.3 0.1 collective-permute-start.12
  22.4 0.0 collective-permute-done.9.refs_7_
  22.4 0.4 %collective-permute-start.13 = (bf16[16,4096]{1,0:T(8,128)(2,1)S(1)}, bf16[16,4096]{1,0:T(8,128)(2,1)S(1)}, u32[]{:S(2)}, u32[]{:S(2)}) collective-permute-start(bf16[16,4096]{1,0:T(8,128)(2,1)S(1)} %collective-permute-done.6.refs_14_), channel_id=1, source_target_pairs={{0,2},{2,0},{4,6},{6,4},{8,10},{10,8},{12,14},{14,12},{1,3},{3,1},... | collective-permute-start | bytes 393224 | tf_op jit(solution)/shard_map/ppermute | solution.py:132
  22.8 0.0 collective-permute-done.10.refs_9_
  22.8 0.3 %collective-permute-done.8.refs_5_ = bf16[16,4096]{1,0:T(8,128)(2,1)S(1)} collective-permute-done((bf16[16,4096]{1,0:T(8,128)(2,1)S(1)}, bf16[16,4096]{1,0:T(8,128)(2,1)S(1)}, u32[]{:S(2)}, u32[]{:S(2)}) %collective-permute-start.8) | collective-permute-done | bytes 131104 | tf_op jit(solution)/shard_map/ppermute | solution.py:132
  23.1 0.2 collective-permute-done.11.refs_11_
  23.3 0.3 %collective-permute-done.12.refs_13_ = bf16[16,4096]{1,0:T(8,128)(2,1)S(1)} collective-permute-done((bf16[16,4096]{1,0:T(8,128)(2,1)S(1)}, bf16[16,4096]{1,0:T(8,128)(2,1)S(1)}, u32[]{:S(2)}, u32[]{:S(2)}) %collective-permute-start.12) | collective-permute-done | bytes 131104 | tf_op jit(solution)/shard_map/ppermute | solution.py:132
  23.6 0.2 collective-permute-done.13.refs_15_
  23.8 1.0 %scores_sent.1 = f32[128,128]{1,0:T(8,128)S(1)} custom-call(bf16[256,2,4096]{2,1,0:T(2,128)(2,1)S(1)} %near.1.train, bf16[16,4096]{1,0:T(8,128)(2,1)S(1)} %condition_mine.1.refs_0_, bf16[16,4096]{1,0:T(8,128)(2,1)S(1)} %collective-permute-done.1.refs_1_, bf16[16,4096]{1,0:T(8,128)(2,1)S(1)} %condition_other.1.refs_2_, ...), custom_call_target="tpu_custom_call" | custom-call | flops 536870912 | bytes 4194304 | tf_op jit(solution)/shard_map/scores_sent/pallas_call | solution.py:195
  24.9 1.6 %collective-permute-start.14 = (f32[128,128]{1,0:T(8,128)S(1)}, f32[128,128]{1,0:T(8,128)S(1)}, u32[]{:S(2)}, u32[]{:S(2)}) collective-permute-start(f32[128,128]{1,0:T(8,128)S(1)} %scores_sent.1), channel_id=1, source_target_pairs={{0,1},{1,0},{2,3},{3,2},{4,5},{5,4},{6,7},{7,6},{8,9},{9,8},{10,11... | collective-permute-start | bytes 196616 | tf_op jit(solution)/shard_map/ppermute | solution.py:238
  26.4 1.0 %scores_kept.1 = f32[128,128]{1,0:T(8,128)S(1)} custom-call(bf16[256,2,4096]{2,1,0:T(2,128)(2,1)S(1)} %near.1.train, bf16[16,4096]{1,0:T(8,128)(2,1)S(1)} %condition_mine.1.refs_0_, bf16[16,4096]{1,0:T(8,128)(2,1)S(1)} %collective-permute-done.1.refs_1_, bf16[16,4096]{1,0:T(8,128)(2,1)S(1)} %condition_other.1.refs_2_, ...), custom_call_target="tpu_custom_call" | custom-call | flops 536870912 | bytes 4194304 | tf_op jit(solution)/shard_map/scores_kept/pallas_call | solution.py:195
  27.5 1.8 %collective-permute-done.14 = f32[128,128]{1,0:T(8,128)S(1)} collective-permute-done((f32[128,128]{1,0:T(8,128)S(1)}, f32[128,128]{1,0:T(8,128)S(1)}, u32[]{:S(2)}, u32[]{:S(2)}) %collective-permute-start.14) | collective-permute-done | bytes 65568 | tf_op jit(solution)/shard_map/ppermute | solution.py:238
  29.2 0.6 %add.3 = f32[128,128]{1,0:T(8,128)} add(f32[128,128]{1,0:T(8,128)S(1)} %scores_kept.1, f32[128,128]{1,0:T(8,128)S(1)} %collective-permute-done.14) | non-fusion elementwise | flops 16384 | bytes 196608 | tf_op jit(solution)/shard_map/add | solution.py:239
Async XLA Ops:
  1.8 7.5 %collective-permute-start.4 = (bf16[16,4096]{1,0:T(8,128)(2,1)S(1)}, bf16[16,4096]{1,0:T(8,128)(2,1)S(1)}, u32[]{:S(2)}, u32[]{:S(2)}) collective-permute-start(bf16[16,4096]{1,0:T(8,128)(2,1)S(1)} %condition_mine.1.refs_0_), channel_id=1, source_target_pairs={{0,4},{2,6},{4,0},{6,2},{8,12},{10,14},{12,8},{14,10},{1,5},{3,7},... | collective-permute-start | bytes 393224 | tf_op jit(solution)/shard_map/ppermute | solution.py:128
  4.9 9.7 %collective-permute-start = (bf16[16,4096]{1,0:T(8,128)(2,1)S(1)}, bf16[16,4096]{1,0:T(8,128)(2,1)S(1)}, u32[]{:S(2)}, u32[]{:S(2)}) collective-permute-start(bf16[16,4096]{1,0:T(8,128)(2,1)S(1)} %condition_mine.1.refs_0_), channel_id=1, source_target_pairs={{0,12},{2,14},{4,8},{6,10},{8,4},{10,6},{12,0},{14,2},{1,13},{3,15... | collective-permute-start | bytes 393224 | tf_op jit(solution)/shard_map/ppermute | solution.py:128
  9.1 10.0 %collective-permute-start.7 = (bf16[16,4096]{1,0:T(8,128)(2,1)S(1)}, bf16[16,4096]{1,0:T(8,128)(2,1)S(1)}, u32[]{:S(2)}, u32[]{:S(2)}) collective-permute-start(bf16[16,4096]{1,0:T(8,128)(2,1)S(1)} %condition_other.1.refs_2_), channel_id=1, source_target_pairs={{0,8},{2,10},{4,12},{6,14},{8,0},{10,2},{12,4},{14,6},{1,9},{3,11}... | collective-permute-start | bytes 393224 | tf_op jit(solution)/shard_map/ppermute | solution.py:128
  9.3 10.0 %collective-permute-start.5 = (bf16[16,4096]{1,0:T(8,128)(2,1)S(1)}, bf16[16,4096]{1,0:T(8,128)(2,1)S(1)}, u32[]{:S(2)}, u32[]{:S(2)}) collective-permute-start(bf16[16,4096]{1,0:T(8,128)(2,1)S(1)} %collective-permute-done.4.refs_6_), channel_id=1, source_target_pairs={{0,18},{2,16},{4,22},{6,20},{8,26},{10,24},{12,30},{14,28},{16,2},... | collective-permute-start | bytes 393224 | tf_op jit(solution)/shard_map/ppermute | solution.py:138
  14.6 5.1 %collective-permute-start.6 = (bf16[16,4096]{1,0:T(8,128)(2,1)S(1)}, bf16[16,4096]{1,0:T(8,128)(2,1)S(1)}, u32[]{:S(2)}, u32[]{:S(2)}) collective-permute-start(bf16[16,4096]{1,0:T(8,128)(2,1)S(1)} %collective-permute-done.refs_8_), channel_id=1, source_target_pairs={{0,16},{2,18},{4,20},{6,22},{8,24},{10,26},{12,28},{14,30},{16,0},... | collective-permute-start | bytes 393224 | tf_op jit(solution)/shard_map/ppermute | solution.py:138
  16.1 5.6 %collective-permute-start.3 = (bf16[16,4096]{1,0:T(8,128)(2,1)S(1)}, bf16[16,4096]{1,0:T(8,128)(2,1)S(1)}, u32[]{:S(2)}, u32[]{:S(2)}) collective-permute-start(bf16[16,4096]{1,0:T(8,128)(2,1)S(1)} %collective-permute-done.refs_8_), channel_id=1, source_target_pairs={{0,4},{2,6},{4,0},{6,2},{8,12},{10,14},{12,8},{14,10},{1,5},{3,7},... | collective-permute-start | bytes 393224 | tf_op jit(solution)/shard_map/ppermute | solution.py:128
  18.8 3.0 %collective-permute-start.2 = (bf16[16,4096]{1,0:T(8,128)(2,1)S(1)}, bf16[16,4096]{1,0:T(8,128)(2,1)S(1)}, u32[]{:S(2)}, u32[]{:S(2)}) collective-permute-start(bf16[16,4096]{1,0:T(8,128)(2,1)S(1)} %condition_other.1.refs_2_), channel_id=1, source_target_pairs={{0,2},{2,0},{4,6},{6,4},{8,10},{10,8},{12,14},{14,12},{1,3},{3,1},... | collective-permute-start | bytes 393224 | tf_op jit(solution)/shard_map/ppermute | solution.py:132
  19.1 3.1 %collective-permute-start.1 = (bf16[16,4096]{1,0:T(8,128)(2,1)S(1)}, bf16[16,4096]{1,0:T(8,128)(2,1)S(1)}, u32[]{:S(2)}, u32[]{:S(2)}) collective-permute-start(bf16[16,4096]{1,0:T(8,128)(2,1)S(1)} %condition_mine.1.refs_0_), channel_id=1, source_target_pairs={{0,2},{2,0},{4,6},{6,4},{8,10},{10,8},{12,14},{14,12},{1,3},{3,1},... | collective-permute-start | bytes 393224 | tf_op jit(solution)/shard_map/ppermute | solution.py:132
  19.3 3.1 %collective-permute-start.9 = (bf16[16,4096]{1,0:T(8,128)(2,1)S(1)}, bf16[16,4096]{1,0:T(8,128)(2,1)S(1)}, u32[]{:S(2)}, u32[]{:S(2)}) collective-permute-start(bf16[16,4096]{1,0:T(8,128)(2,1)S(1)} %collective-permute-done.4.refs_6_), channel_id=1, source_target_pairs={{0,2},{2,0},{4,6},{6,4},{8,10},{10,8},{12,14},{14,12},{1,3},{3,1},... | collective-permute-start | bytes 393224 | tf_op jit(solution)/shard_map/ppermute | solution.py:132
  19.7 3.1 %collective-permute-start.10 = (bf16[16,4096]{1,0:T(8,128)(2,1)S(1)}, bf16[16,4096]{1,0:T(8,128)(2,1)S(1)}, u32[]{:S(2)}, u32[]{:S(2)}) collective-permute-start(bf16[16,4096]{1,0:T(8,128)(2,1)S(1)} %collective-permute-done.refs_8_), channel_id=1, source_target_pairs={{0,2},{2,0},{4,6},{6,4},{8,10},{10,8},{12,14},{14,12},{1,3},{3,1},... | collective-permute-start | bytes 393224 | tf_op jit(solution)/shard_map/ppermute | solution.py:132
  21.8 1.3 %collective-permute-start.8 = (bf16[16,4096]{1,0:T(8,128)(2,1)S(1)}, bf16[16,4096]{1,0:T(8,128)(2,1)S(1)}, u32[]{:S(2)}, u32[]{:S(2)}) collective-permute-start(bf16[16,4096]{1,0:T(8,128)(2,1)S(1)} %collective-permute-done.3.refs_4_), channel_id=1, source_target_pairs={{0,2},{2,0},{4,6},{6,4},{8,10},{10,8},{12,14},{14,12},{1,3},{3,1},... | collective-permute-start | bytes 393224 | tf_op jit(solution)/shard_map/ppermute | solution.py:132
  21.8 1.5 %collective-permute-start.11 = (bf16[16,4096]{1,0:T(8,128)(2,1)S(1)}, bf16[16,4096]{1,0:T(8,128)(2,1)S(1)}, u32[]{:S(2)}, u32[]{:S(2)}) collective-permute-start(bf16[16,4096]{1,0:T(8,128)(2,1)S(1)} %collective-permute-done.7.refs_10_), channel_id=1, source_target_pairs={{0,2},{2,0},{4,6},{6,4},{8,10},{10,8},{12,14},{14,12},{1,3},{3,1},... | collective-permute-start | bytes 393224 | tf_op jit(solution)/shard_map/ppermute | solution.py:132
  22.3 1.3 %collective-permute-start.12 = (bf16[16,4096]{1,0:T(8,128)(2,1)S(1)}, bf16[16,4096]{1,0:T(8,128)(2,1)S(1)}, u32[]{:S(2)}, u32[]{:S(2)}) collective-permute-start(bf16[16,4096]{1,0:T(8,128)(2,1)S(1)} %collective-permute-done.5.refs_12_), channel_id=1, source_target_pairs={{0,2},{2,0},{4,6},{6,4},{8,10},{10,8},{12,14},{14,12},{1,3},{3,1},... | collective-permute-start | bytes 393224 | tf_op jit(solution)/shard_map/ppermute | solution.py:132
  22.4 1.5 %collective-permute-start.13 = (bf16[16,4096]{1,0:T(8,128)(2,1)S(1)}, bf16[16,4096]{1,0:T(8,128)(2,1)S(1)}, u32[]{:S(2)}, u32[]{:S(2)}) collective-permute-start(bf16[16,4096]{1,0:T(8,128)(2,1)S(1)} %collective-permute-done.6.refs_14_), channel_id=1, source_target_pairs={{0,2},{2,0},{4,6},{6,4},{8,10},{10,8},{12,14},{14,12},{1,3},{3,1},... | collective-permute-start | bytes 393224 | tf_op jit(solution)/shard_map/ppermute | solution.py:132
  24.9 4.4 %collective-permute-start.14 = (f32[128,128]{1,0:T(8,128)S(1)}, f32[128,128]{1,0:T(8,128)S(1)}, u32[]{:S(2)}, u32[]{:S(2)}) collective-permute-start(f32[128,128]{1,0:T(8,128)S(1)} %scores_sent.1), channel_id=1, source_target_pairs={{0,1},{1,0},{2,3},{3,2},{4,5},{5,4},{6,7},{7,6},{8,9},{9,8},{10,11... | collective-permute-start | bytes 196616 | tf_op jit(solution)/shard_map/ppermute | solution.py:238

commit v21 on v18

--- a/solution.py
+++ b/solution.py
@@ -239,11 +239,19 @@
     t2 = along_columns(other, 2)
     y1 = other_part(s1, cross=True)
     y3 = other_part(s3)
-    s2, y1, y3, t2 = lax.optimization_barrier((s2, y1, y3, t2))
-
-    blocks = []
-    for block in (mine, other, s2, s1, s3, t2, y1, y3):
-        blocks += [block, other_core(block)]
+    y1_c = other_core(y1)
+    s2, y3, y1_c = lax.optimization_barrier((s2, y3, y1_c))
+
+    blocks = [
+        mine, other_core(mine),
+        other, other_core(other),
+        s2, other_core(s2),
+        s1, other_core(s1),
+        s3, other_core(s3),
+        t2, other_core(t2),
+        y1, y1_c,
+        y3, other_core(y3),
+    ]
     f32 = functools.partial(jax.ShapeDtypeStruct, dtype=jnp.float32)
     terms = [pltpu.VMEM((layer_count, share * layer_count, total), jnp.float32)]
     sent, table = local_call(

time: 30 us -> 33.1 us (1.10)
  starting transfers between devices: 13.6 us -> 17.9 us
  waiting for transfers between devices: 8.03 us -> 6.84 us
    ppermute x4, starting transfers between devices: 8.4 us -> 12.5 us  [along_columns(): lax.ppermute(value, 'train', [(k, k ^ flip * PAIR) for k in range(COLUMNS...]
    ppermute x4, waiting for transfers between devices: 5.02 us -> 3.01 us  [along_columns(): lax.ppermute(value, 'train', [(k, k ^ flip * PAIR) for k in range(COLUMNS...]
    ppermute x2, waiting for transfers between devices: 0.01 us -> 0.8 us  [other_part(): return lax.ppermute(value, ('parts', 'train'), pairs)]
  transfers between devices with their start and end apart: 15 -> 15, of which waited for: 8 -> 7; matrix products, arithmetic and copies ran while one was open for 0% -> 0% of each run, Pallas kernels for 16% -> 15%
where the time goes in v21:
time: 33.1 us; the launch traced here: 32.9 us
  starting transfers between devices  17.9 us (54%)
  Pallas kernels  7.56 us (23%)
  waiting for transfers between devices  6.84 us (21%)
  other arithmetic  0.64 us (2%)
    ppermute x4, starting transfers between devices, along_columns(): lax.ppermute(value, 'train', [(k, k ^ flip * PAIR) for k in range(COLUMNS...  12.5 us
    pallas_call x2, Pallas kernels, condition_layer(): pl.pallas_call(functools.partial(condition_kernel, other), out_shape=jax....  3.54 us
    ppermute x4, waiting for transfers between devices, along_columns(): lax.ppermute(value, 'train', [(k, k ^ flip * PAIR) for k in range(COLUMNS...  3.01 us
    pallas_call x1, Pallas kernels, copy_near(): pl.pallas_call(copy_kernel, out_shape=jax.ShapeDtypeStruct(value.shape, v...  2.2 us
    ppermute x1, waiting for transfers between devices, direct(): received = lax.ppermute(sent, 'layer', [(0, 1), (1, 0)])  2 us
    ppermute x8, starting transfers between devices, other_core(): lax.ppermute(value, 'train', [(k, k ^ 1) for k in range(COLUMNS * PAIR)])  1.95 us
    ppermute x2, starting transfers between devices, other_part(): return lax.ppermute(value, ('parts', 'train'), pairs)  1.84 us
    pallas_call x2, Pallas kernels, local_call(): pl.pallas_call(kernel, out_shape=out_shape, in_specs=[spec] * len(operand...  1.83 us
  transfers between devices with their start and end apart: 15, of which 7 were waited for; matrix products, arithmetic and copies ran while one was open for 0% of the time, Pallas kernels for 15%

profile of v21, /device:TPU:0, one launch (start us, length us, event | category | flops | bytes accessed | tf_op | source)
XLA Modules:
  0.0 32.9 jit_solution(4709222229009955140)
XLA Ops:
  0.0 1.8 %condition_mine.1.refs_0_ = bf16[16,4096]{1,0:T(8,128)(2,1)S(1)} custom-call(bf16[2,1,16,4096]{3,2,1,0:T(8,128)(2,1)} %queries.3, f32[2,64,64]{2,1,0:T(8,128)} %left.3, f32[2,64,64]{2,1,0:T(8,128)} %right.3), custom_call_target="tpu_custom_call" | custom-call | flops 134217728 | bytes 524288 | tf_op jit(solution)/shard_map/condition_mine/pallas_call | solution.py:107
  1.8 3.1 %collective-permute-start.5 = (bf16[16,4096]{1,0:T(8,128)(2,1)S(1)}, bf16[16,4096]{1,0:T(8,128)(2,1)S(1)}, u32[]{:S(2)}, u32[]{:S(2)}) collective-permute-start(bf16[16,4096]{1,0:T(8,128)(2,1)S(1)} %condition_mine.1.refs_0_), channel_id=1, source_target_pairs={{0,4},{2,6},{4,0},{6,2},{8,12},{10,14},{12,8},{14,10},{1,5},{3,7},... | collective-permute-start | bytes 393224 | tf_op jit(solution)/shard_map/ppermute | solution.py:128
  4.9 2.5 %collective-permute-start = (bf16[16,4096]{1,0:T(8,128)(2,1)S(1)}, bf16[16,4096]{1,0:T(8,128)(2,1)S(1)}, u32[]{:S(2)}, u32[]{:S(2)}) collective-permute-start(bf16[16,4096]{1,0:T(8,128)(2,1)S(1)} %condition_mine.1.refs_0_), channel_id=1, source_target_pairs={{0,12},{2,14},{4,8},{6,10},{8,4},{10,6},{12,0},{14,2},{1,13},{3,15... | collective-permute-start | bytes 393224 | tf_op jit(solution)/shard_map/ppermute | solution.py:128
  7.3 1.0 %collective-permute-done.5.refs_6_ = bf16[16,4096]{1,0:T(8,128)(2,1)S(1)} collective-permute-done((bf16[16,4096]{1,0:T(8,128)(2,1)S(1)}, bf16[16,4096]{1,0:T(8,128)(2,1)S(1)}, u32[]{:S(2)}, u32[]{:S(2)}) %collective-permute-start.5) | collective-permute-done | bytes 131104 | tf_op jit(solution)/shard_map/ppermute | solution.py:128
  8.4 0.3 collective-permute-start.6
  8.6 1.8 %condition_other.1.refs_2_ = bf16[16,4096]{1,0:T(8,128)(2,1)S(1)} custom-call(bf16[2,1,16,4096]{3,2,1,0:T(8,128)(2,1)} %queries.3, f32[2,64,64]{2,1,0:T(8,128)} %left.3, f32[2,64,64]{2,1,0:T(8,128)} %right.3), custom_call_target="tpu_custom_call" | custom-call | flops 134217728 | bytes 524288 | tf_op jit(solution)/shard_map/condition_other/pallas_call | solution.py:107
  10.4 3.7 %collective-permute-start.11 = (bf16[16,4096]{1,0:T(8,128)(2,1)S(1)}, bf16[16,4096]{1,0:T(8,128)(2,1)S(1)}, u32[]{:S(2)}, u32[]{:S(2)}) collective-permute-start(bf16[16,4096]{1,0:T(8,128)(2,1)S(1)} %condition_other.1.refs_2_), channel_id=1, source_target_pairs={{0,8},{2,10},{4,12},{6,14},{8,0},{10,2},{12,4},{14,6},{1,9},{3,11}... | collective-permute-start | bytes 393224 | tf_op jit(solution)/shard_map/ppermute | solution.py:128
  14.1 2.2 %near.1.train = bf16[256,2,4096]{2,1,0:T(2,128)(2,1)S(1)} custom-call(bf16[256,2,4096]{2,1,0:T(2,128)(2,1)} %source.1), custom_call_target="tpu_custom_call" | custom-call | bytes 8388608 | tf_op jit(solution)/shard_map/near/pallas_call | solution.py:148
  16.3 0.0 collective-permute-done.refs_8_
  16.3 1.6 %collective-permute-start.4 = (bf16[16,4096]{1,0:T(8,128)(2,1)S(1)}, bf16[16,4096]{1,0:T(8,128)(2,1)S(1)}, u32[]{:S(2)}, u32[]{:S(2)}) collective-permute-start(bf16[16,4096]{1,0:T(8,128)(2,1)S(1)} %collective-permute-done.refs_8_), channel_id=1, source_target_pairs={{0,16},{2,18},{4,20},{6,22},{8,24},{10,26},{12,28},{14,30},{16,0},... | collective-permute-start | bytes 393224 | tf_op jit(solution)/shard_map/ppermute | solution.py:138
  17.9 3.2 %collective-permute-start.3 = (bf16[16,4096]{1,0:T(8,128)(2,1)S(1)}, bf16[16,4096]{1,0:T(8,128)(2,1)S(1)}, u32[]{:S(2)}, u32[]{:S(2)}) collective-permute-start(bf16[16,4096]{1,0:T(8,128)(2,1)S(1)} %collective-permute-done.refs_8_), channel_id=1, source_target_pairs={{0,4},{2,6},{4,0},{6,2},{8,12},{10,14},{12,8},{14,10},{1,5},{3,7},... | collective-permute-start | bytes 393224 | tf_op jit(solution)/shard_map/ppermute | solution.py:128
  21.1 0.0 collective-permute-done.6.refs_12_
  21.1 0.0 collective-permute-start.7
  21.1 0.5 %collective-permute-start.2 = (bf16[16,4096]{1,0:T(8,128)(2,1)S(1)}, bf16[16,4096]{1,0:T(8,128)(2,1)S(1)}, u32[]{:S(2)}, u32[]{:S(2)}) collective-permute-start(bf16[16,4096]{1,0:T(8,128)(2,1)S(1)} %condition_other.1.refs_2_), channel_id=1, source_target_pairs={{0,2},{2,0},{4,6},{6,4},{8,10},{10,8},{12,14},{14,12},{1,3},{3,1},... | collective-permute-start | bytes 393224 | tf_op jit(solution)/shard_map/ppermute | solution.py:132
  21.7 0.0 collective-permute-done.11.refs_10_
  21.7 0.0 collective-permute-start.1
  21.7 0.8 %collective-permute-done.4.refs_14_ = bf16[16,4096]{1,0:T(8,128)(2,1)S(1)} collective-permute-done((bf16[16,4096]{1,0:T(8,128)(2,1)S(1)}, bf16[16,4096]{1,0:T(8,128)(2,1)S(1)}, u32[]{:S(2)}, u32[]{:S(2)}) %collective-permute-start.4) | collective-permute-done | bytes 131104 | tf_op jit(solution)/shard_map/ppermute | solution.py:138
  22.5 0.4 %collective-permute-start.10 = (bf16[16,4096]{1,0:T(8,128)(2,1)S(1)}, bf16[16,4096]{1,0:T(8,128)(2,1)S(1)}, u32[]{:S(2)}, u32[]{:S(2)}) collective-permute-start(bf16[16,4096]{1,0:T(8,128)(2,1)S(1)} %collective-permute-done.refs_8_), channel_id=1, source_target_pairs={{0,2},{2,0},{4,6},{6,4},{8,10},{10,8},{12,14},{14,12},{1,3},{3,1},... | collective-permute-start | bytes 393224 | tf_op jit(solution)/shard_map/ppermute | solution.py:132
  22.9 2.0 %collective-permute-done.3.refs_4_ = bf16[16,4096]{1,0:T(8,128)(2,1)S(1)} collective-permute-done((bf16[16,4096]{1,0:T(8,128)(2,1)S(1)}, bf16[16,4096]{1,0:T(8,128)(2,1)S(1)}, u32[]{:S(2)}, u32[]{:S(2)}) %collective-permute-start.3) | collective-permute-done | bytes 131104 | tf_op jit(solution)/shard_map/ppermute | solution.py:128
  24.9 0.0 collective-permute-start.9
  24.9 0.0 collective-permute-done.7.refs_13_
  24.9 0.5 %collective-permute-start.12 = (bf16[16,4096]{1,0:T(8,128)(2,1)S(1)}, bf16[16,4096]{1,0:T(8,128)(2,1)S(1)}, u32[]{:S(2)}, u32[]{:S(2)}) collective-permute-start(bf16[16,4096]{1,0:T(8,128)(2,1)S(1)} %collective-permute-done.11.refs_10_), channel_id=1, source_target_pairs={{0,2},{2,0},{4,6},{6,4},{8,10},{10,8},{12,14},{14,12},{1,3},{3,1},... | collective-permute-start | bytes 393224 | tf_op jit(solution)/shard_map/ppermute | solution.py:132
  25.4 0.0 collective-permute-done.2.refs_3_
  25.4 0.1 collective-permute-start.8
  25.5 0.0 collective-permute-done.1.refs_1_
  25.5 0.4 %collective-permute-start.13 = (bf16[16,4096]{1,0:T(8,128)(2,1)S(1)}, bf16[16,4096]{1,0:T(8,128)(2,1)S(1)}, u32[]{:S(2)}, u32[]{:S(2)}) collective-permute-start(bf16[16,4096]{1,0:T(8,128)(2,1)S(1)} %collective-permute-done.4.refs_14_), channel_id=1, source_target_pairs={{0,2},{2,0},{4,6},{6,4},{8,10},{10,8},{12,14},{14,12},{1,3},{3,1},... | collective-permute-start | bytes 393224 | tf_op jit(solution)/shard_map/ppermute | solution.py:132
  25.9 0.5 %collective-permute-done.12.refs_11_ = bf16[16,4096]{1,0:T(8,128)(2,1)S(1)} collective-permute-done((bf16[16,4096]{1,0:T(8,128)(2,1)S(1)}, bf16[16,4096]{1,0:T(8,128)(2,1)S(1)}, u32[]{:S(2)}, u32[]{:S(2)}) %collective-permute-start.12) | collective-permute-done | bytes 131104 | tf_op jit(solution)/shard_map/ppermute | solution.py:132
  26.4 0.0 collective-permute-done.9.refs_7_
  26.4 0.0 collective-permute-done.10.refs_9_
  26.4 0.3 collective-permute-done.8.refs_5_
  26.7 0.2 collective-permute-done.13.refs_15_
  26.9 1.0 %scores_sent.1 = (f32[128,128]{1,0:T(8,128)S(1)}, bf16[2,128,4096]{2,1,0:T(8,128)(2,1)S(1)}) custom-call(bf16[256,2,4096]{2,1,0:T(2,128)(2,1)S(1)} %near.1.train, bf16[16,4096]{1,0:T(8,128)(2,1)S(1)} %condition_mine.1.refs_0_, bf16[16,4096]{1,0:T(8,128)(2,1)S(1)} %collective-permute-done.1.refs_1_, bf16[16,4096]{1,0:T(8,128)(2,1)S(1)} %condition_other.1.refs_2_, ...), custom_call_target="tpu_custom_call" | custom-call | flops 536870912 | bytes 4194304 | tf_op jit(solution)/shard_map/scores_sent/pallas_call | solution.py:214
  27.9 1.6 %collective-permute-start.14 = (f32[128,128]{1,0:T(8,128)S(1)}, f32[128,128]{1,0:T(8,128)S(1)}, u32[]{:S(2)}, u32[]{:S(2)}) collective-permute-start(f32[128,128]{1,0:T(8,128)S(1)} %get-tuple-element.18), channel_id=1, source_target_pairs={{0,1},{1,0},{2,3},{3,2},{4,5},{5,4},{6,7},{7,6},{8,9},{9,8},{10,11... | collective-permute-start | bytes 196616 | tf_op jit(solution)/shard_map/ppermute | solution.py:265
  29.5 0.8 %scores_kept.1 = f32[128,128]{1,0:T(8,128)S(1)} custom-call(bf16[256,2,4096]{2,1,0:T(2,128)(2,1)S(1)} %near.1.train, bf16[2,128,4096]{2,1,0:T(8,128)(2,1)S(1)} %get-tuple-element.17.table), custom_call_target="tpu_custom_call" | custom-call | flops 536870912 | bytes 4194304 | tf_op jit(solution)/shard_map/scores_kept/pallas_call | solution.py:214
  30.3 2.0 %collective-permute-done.14 = f32[128,128]{1,0:T(8,128)S(1)} collective-permute-done((f32[128,128]{1,0:T(8,128)S(1)}, f32[128,128]{1,0:T(8,128)S(1)}, u32[]{:S(2)}, u32[]{:S(2)}) %collective-permute-start.14) | collective-permute-done | bytes 65568 | tf_op jit(solution)/shard_map/ppermute | solution.py:265
  32.3 0.6 %add.3 = f32[128,128]{1,0:T(8,128)} add(f32[128,128]{1,0:T(8,128)S(1)} %scores_kept.1, f32[128,128]{1,0:T(8,128)S(1)} %collective-permute-done.14) | non-fusion elementwise | flops 16384 | bytes 196608 | tf_op jit(solution)/shard_map/add | solution.py:267
Async XLA Ops:
  1.8 6.6 %collective-permute-start.5 = (bf16[16,4096]{1,0:T(8,128)(2,1)S(1)}, bf16[16,4096]{1,0:T(8,128)(2,1)S(1)}, u32[]{:S(2)}, u32[]{:S(2)}) collective-permute-start(bf16[16,4096]{1,0:T(8,128)(2,1)S(1)} %condition_mine.1.refs_0_), channel_id=1, source_target_pairs={{0,4},{2,6},{4,0},{6,2},{8,12},{10,14},{12,8},{14,10},{1,5},{3,7},... | collective-permute-start | bytes 393224 | tf_op jit(solution)/shard_map/ppermute | solution.py:128
  4.9 11.4 %collective-permute-start = (bf16[16,4096]{1,0:T(8,128)(2,1)S(1)}, bf16[16,4096]{1,0:T(8,128)(2,1)S(1)}, u32[]{:S(2)}, u32[]{:S(2)}) collective-permute-start(bf16[16,4096]{1,0:T(8,128)(2,1)S(1)} %condition_mine.1.refs_0_), channel_id=1, source_target_pairs={{0,12},{2,14},{4,8},{6,10},{8,4},{10,6},{12,0},{14,2},{1,13},{3,15... | collective-permute-start | bytes 393224 | tf_op jit(solution)/shard_map/ppermute | solution.py:128
  8.4 12.8 %collective-permute-start.6 = (bf16[16,4096]{1,0:T(8,128)(2,1)S(1)}, bf16[16,4096]{1,0:T(8,128)(2,1)S(1)}, u32[]{:S(2)}, u32[]{:S(2)}) collective-permute-start(bf16[16,4096]{1,0:T(8,128)(2,1)S(1)} %collective-permute-done.5.refs_6_), channel_id=1, source_target_pairs={{0,18},{2,16},{4,22},{6,20},{8,26},{10,24},{12,30},{14,28},{16,2},... | collective-permute-start | bytes 393224 | tf_op jit(solution)/shard_map/ppermute | solution.py:138
  10.4 11.3 %collective-permute-start.11 = (bf16[16,4096]{1,0:T(8,128)(2,1)S(1)}, bf16[16,4096]{1,0:T(8,128)(2,1)S(1)}, u32[]{:S(2)}, u32[]{:S(2)}) collective-permute-start(bf16[16,4096]{1,0:T(8,128)(2,1)S(1)} %condition_other.1.refs_2_), channel_id=1, source_target_pairs={{0,8},{2,10},{4,12},{6,14},{8,0},{10,2},{12,4},{14,6},{1,9},{3,11}... | collective-permute-start | bytes 393224 | tf_op jit(solution)/shard_map/ppermute | solution.py:128
  16.3 6.1 %collective-permute-start.4 = (bf16[16,4096]{1,0:T(8,128)(2,1)S(1)}, bf16[16,4096]{1,0:T(8,128)(2,1)S(1)}, u32[]{:S(2)}, u32[]{:S(2)}) collective-permute-start(bf16[16,4096]{1,0:T(8,128)(2,1)S(1)} %collective-permute-done.refs_8_), channel_id=1, source_target_pairs={{0,16},{2,18},{4,20},{6,22},{8,24},{10,26},{12,28},{14,30},{16,0},... | collective-permute-start | bytes 393224 | tf_op jit(solution)/shard_map/ppermute | solution.py:138
  17.9 7.0 %collective-permute-start.3 = (bf16[16,4096]{1,0:T(8,128)(2,1)S(1)}, bf16[16,4096]{1,0:T(8,128)(2,1)S(1)}, u32[]{:S(2)}, u32[]{:S(2)}) collective-permute-start(bf16[16,4096]{1,0:T(8,128)(2,1)S(1)} %collective-permute-done.refs_8_), channel_id=1, source_target_pairs={{0,4},{2,6},{4,0},{6,2},{8,12},{10,14},{12,8},{14,10},{1,5},{3,7},... | collective-permute-start | bytes 393224 | tf_op jit(solution)/shard_map/ppermute | solution.py:128
  21.1 3.7 %collective-permute-start.7 = (bf16[16,4096]{1,0:T(8,128)(2,1)S(1)}, bf16[16,4096]{1,0:T(8,128)(2,1)S(1)}, u32[]{:S(2)}, u32[]{:S(2)}) collective-permute-start(bf16[16,4096]{1,0:T(8,128)(2,1)S(1)} %collective-permute-done.6.refs_12_), channel_id=1, source_target_pairs={{0,2},{2,0},{4,6},{6,4},{8,10},{10,8},{12,14},{14,12},{1,3},{3,1},... | collective-permute-start | bytes 393224 | tf_op jit(solution)/shard_map/ppermute | solution.py:132
  21.1 4.2 %collective-permute-start.2 = (bf16[16,4096]{1,0:T(8,128)(2,1)S(1)}, bf16[16,4096]{1,0:T(8,128)(2,1)S(1)}, u32[]{:S(2)}, u32[]{:S(2)}) collective-permute-start(bf16[16,4096]{1,0:T(8,128)(2,1)S(1)} %condition_other.1.refs_2_), channel_id=1, source_target_pairs={{0,2},{2,0},{4,6},{6,4},{8,10},{10,8},{12,14},{14,12},{1,3},{3,1},... | collective-permute-start | bytes 393224 | tf_op jit(solution)/shard_map/ppermute | solution.py:132
  21.7 3.8 %collective-permute-start.1 = (bf16[16,4096]{1,0:T(8,128)(2,1)S(1)}, bf16[16,4096]{1,0:T(8,128)(2,1)S(1)}, u32[]{:S(2)}, u32[]{:S(2)}) collective-permute-start(bf16[16,4096]{1,0:T(8,128)(2,1)S(1)} %condition_mine.1.refs_0_), channel_id=1, source_target_pairs={{0,2},{2,0},{4,6},{6,4},{8,10},{10,8},{12,14},{14,12},{1,3},{3,1},... | collective-permute-start | bytes 393224 | tf_op jit(solution)/shard_map/ppermute | solution.py:132
  22.5 3.9 %collective-permute-start.10 = (bf16[16,4096]{1,0:T(8,128)(2,1)S(1)}, bf16[16,4096]{1,0:T(8,128)(2,1)S(1)}, u32[]{:S(2)}, u32[]{:S(2)}) collective-permute-start(bf16[16,4096]{1,0:T(8,128)(2,1)S(1)} %collective-permute-done.refs_8_), channel_id=1, source_target_pairs={{0,2},{2,0},{4,6},{6,4},{8,10},{10,8},{12,14},{14,12},{1,3},{3,1},... | collective-permute-start | bytes 393224 | tf_op jit(solution)/shard_map/ppermute | solution.py:132
  24.9 1.5 %collective-permute-start.9 = (bf16[16,4096]{1,0:T(8,128)(2,1)S(1)}, bf16[16,4096]{1,0:T(8,128)(2,1)S(1)}, u32[]{:S(2)}, u32[]{:S(2)}) collective-permute-start(bf16[16,4096]{1,0:T(8,128)(2,1)S(1)} %collective-permute-done.5.refs_6_), channel_id=1, source_target_pairs={{0,2},{2,0},{4,6},{6,4},{8,10},{10,8},{12,14},{14,12},{1,3},{3,1},... | collective-permute-start | bytes 393224 | tf_op jit(solution)/shard_map/ppermute | solution.py:132
  24.9 1.5 %collective-permute-start.12 = (bf16[16,4096]{1,0:T(8,128)(2,1)S(1)}, bf16[16,4096]{1,0:T(8,128)(2,1)S(1)}, u32[]{:S(2)}, u32[]{:S(2)}) collective-permute-start(bf16[16,4096]{1,0:T(8,128)(2,1)S(1)} %collective-permute-done.11.refs_10_), channel_id=1, source_target_pairs={{0,2},{2,0},{4,6},{6,4},{8,10},{10,8},{12,14},{14,12},{1,3},{3,1},... | collective-permute-start | bytes 393224 | tf_op jit(solution)/shard_map/ppermute | solution.py:132
  25.4 1.3 %collective-permute-start.8 = (bf16[16,4096]{1,0:T(8,128)(2,1)S(1)}, bf16[16,4096]{1,0:T(8,128)(2,1)S(1)}, u32[]{:S(2)}, u32[]{:S(2)}) collective-permute-start(bf16[16,4096]{1,0:T(8,128)(2,1)S(1)} %collective-permute-done.3.refs_4_), channel_id=1, source_target_pairs={{0,2},{2,0},{4,6},{6,4},{8,10},{10,8},{12,14},{14,12},{1,3},{3,1},... | collective-permute-start | bytes 393224 | tf_op jit(solution)/shard_map/ppermute | solution.py:132
  25.5 1.5 %collective-permute-start.13 = (bf16[16,4096]{1,0:T(8,128)(2,1)S(1)}, bf16[16,4096]{1,0:T(8,128)(2,1)S(1)}, u32[]{:S(2)}, u32[]{:S(2)}) collective-permute-start(bf16[16,4096]{1,0:T(8,128)(2,1)S(1)} %collective-permute-done.4.refs_14_), channel_id=1, source_target_pairs={{0,2},{2,0},{4,6},{6,4},{8,10},{10,8},{12,14},{14,12},{1,3},{3,1},... | collective-permute-start | bytes 393224 | tf_op jit(solution)/shard_map/ppermute | solution.py:132
  27.9 4.4 %collective-permute-start.14 = (f32[128,128]{1,0:T(8,128)S(1)}, f32[128,128]{1,0:T(8,128)S(1)}, u32[]{:S(2)}, u32[]{:S(2)}) collective-permute-start(f32[128,128]{1,0:T(8,128)S(1)} %get-tuple-element.18), channel_id=1, source_target_pairs={{0,1},{1,0},{2,3},{3,2},{4,5},{5,4},{6,7},{7,6},{8,9},{9,8},{10,11... | collective-permute-start | bytes 196616 | tf_op jit(solution)/shard_map/ppermute | solution.py:265

commit v22 on v18

--- a/solution.py
+++ b/solution.py
@@ -234,7 +234,7 @@
     near = copy_near(train_grads)
     s1 = along_columns(mine, 1)
     s3 = along_columns(mine, 3)
-    s3, near = lax.optimization_barrier((s3, near))
+    s1, s3, near = lax.optimization_barrier((s1, s3, near))
     s2 = along_columns(s3, 1)
     t2 = along_columns(other, 2)
     y1 = other_part(s1, cross=True)

time: 30 us -> 31.4 us (1.047)
  waiting for transfers between devices: 8.03 us -> 10.7 us
  starting transfers between devices: 13.6 us -> 12.3 us
    ppermute x2, waiting for transfers between devices: 0.01 us -> 4.48 us  [other_part(): return lax.ppermute(value, ('parts', 'train'), pairs)]
    ppermute x4, waiting for transfers between devices: 5.02 us -> 3 us  [along_columns(): lax.ppermute(value, 'train', [(k, k ^ flip * PAIR) for k in range(COLUMNS...]
    ppermute x4, starting transfers between devices: 8.4 us -> 7.62 us  [along_columns(): lax.ppermute(value, 'train', [(k, k ^ flip * PAIR) for k in range(COLUMNS...]
    ppermute x2, starting transfers between devices: 1.92 us -> 1.56 us  [other_part(): return lax.ppermute(value, ('parts', 'train'), pairs)]
  transfers between devices with their start and end apart: 15 -> 15, of which waited for: 8 -> 10; matrix products, arithmetic and copies ran while one was open for 0% -> 0% of each run, Pallas kernels for 16% -> 15%
where the time goes in v22:
time: 31.4 us; the launch traced here: 31.2 us
  starting transfers between devices  12.3 us (39%)
  waiting for transfers between devices  10.7 us (34%)
  Pallas kernels  7.57 us (24%)
  other arithmetic  0.64 us (2%)
    ppermute x4, starting transfers between devices, along_columns(): lax.ppermute(value, 'train', [(k, k ^ flip * PAIR) for k in range(COLUMNS...  7.62 us
    ppermute x2, waiting for transfers between devices, other_part(): return lax.ppermute(value, ('parts', 'train'), pairs)  4.48 us
    pallas_call x2, Pallas kernels, condition_layer(): pl.pallas_call(functools.partial(condition_kernel, other), out_shape=jax....  3.53 us
    ppermute x4, waiting for transfers between devices, along_columns(): lax.ppermute(value, 'train', [(k, k ^ flip * PAIR) for k in range(COLUMNS...  3 us
    pallas_call x1, Pallas kernels, copy_near(): pl.pallas_call(copy_kernel, out_shape=jax.ShapeDtypeStruct(value.shape, v...  2.2 us
    ppermute x1, waiting for transfers between devices, direct(): received = lax.ppermute(sent, 'layer', [(0, 1), (1, 0)])  1.92 us
    pallas_call x2, Pallas kernels, local_call(): pl.pallas_call(kernel, out_shape=out_shape, in_specs=[spec] * len(operand...  1.84 us
    ppermute x8, starting transfers between devices, other_core(): lax.ppermute(value, 'train', [(k, k ^ 1) for k in range(COLUMNS * PAIR)])  1.57 us
  transfers between devices with their start and end apart: 15, of which 10 were waited for; matrix products, arithmetic and copies ran while one was open for 0% of the time, Pallas kernels for 15%

profile of v22, /device:TPU:0, one launch (start us, length us, event | category | flops | bytes accessed | tf_op | source)
XLA Modules:
  0.0 31.2 jit_solution(10520117629750107499)
XLA Ops:
  0.0 1.8 %condition_mine.1.refs_0_ = bf16[16,4096]{1,0:T(8,128)(2,1)S(1)} custom-call(bf16[2,1,16,4096]{3,2,1,0:T(8,128)(2,1)} %queries.3, f32[2,64,64]{2,1,0:T(8,128)} %left.3, f32[2,64,64]{2,1,0:T(8,128)} %right.3), custom_call_target="tpu_custom_call" | custom-call | flops 134217728 | bytes 524288 | tf_op jit(solution)/shard_map/condition_mine/pallas_call | solution.py:107
  1.8 5.1 %collective-permute-start.1 = (bf16[16,4096]{1,0:T(8,128)(2,1)S(1)}, bf16[16,4096]{1,0:T(8,128)(2,1)S(1)}, u32[]{:S(2)}, u32[]{:S(2)}) collective-permute-start(bf16[16,4096]{1,0:T(8,128)(2,1)S(1)} %condition_mine.1.refs_0_), channel_id=1, source_target_pairs={{0,12},{2,14},{4,8},{6,10},{8,4},{10,6},{12,0},{14,2},{1,13},{3,15... | collective-permute-start | bytes 393224 | tf_op jit(solution)/shard_map/ppermute | solution.py:128
  6.9 0.0 collective-permute-start
  6.9 1.8 %condition_other.1.refs_2_ = bf16[16,4096]{1,0:T(8,128)(2,1)S(1)} custom-call(bf16[2,1,16,4096]{3,2,1,0:T(8,128)(2,1)} %queries.3, f32[2,64,64]{2,1,0:T(8,128)} %left.3, f32[2,64,64]{2,1,0:T(8,128)} %right.3), custom_call_target="tpu_custom_call" | custom-call | flops 134217728 | bytes 524288 | tf_op jit(solution)/shard_map/condition_other/pallas_call | solution.py:107
  8.7 0.7 %collective-permute-start.7 = (bf16[16,4096]{1,0:T(8,128)(2,1)S(1)}, bf16[16,4096]{1,0:T(8,128)(2,1)S(1)}, u32[]{:S(2)}, u32[]{:S(2)}) collective-permute-start(bf16[16,4096]{1,0:T(8,128)(2,1)S(1)} %condition_other.1.refs_2_), channel_id=1, source_target_pairs={{0,8},{2,10},{4,12},{6,14},{8,0},{10,2},{12,4},{14,6},{1,9},{3,11}... | collective-permute-start | bytes 393224 | tf_op jit(solution)/shard_map/ppermute | solution.py:128
  9.4 2.2 %near.1.train = bf16[256,2,4096]{2,1,0:T(2,128)(2,1)S(1)} custom-call(bf16[256,2,4096]{2,1,0:T(2,128)(2,1)} %source.1), custom_call_target="tpu_custom_call" | custom-call | bytes 8388608 | tf_op jit(solution)/shard_map/near/pallas_call | solution.py:148
  11.6 0.0 collective-permute-done.1.refs_8_
  11.6 2.7 %collective-permute-done.refs_6_ = bf16[16,4096]{1,0:T(8,128)(2,1)S(1)} collective-permute-done((bf16[16,4096]{1,0:T(8,128)(2,1)S(1)}, bf16[16,4096]{1,0:T(8,128)(2,1)S(1)}, u32[]{:S(2)}, u32[]{:S(2)}) %collective-permute-start) | collective-permute-done | bytes 131104 | tf_op jit(solution)/shard_map/ppermute | solution.py:128
  14.3 0.7 %collective-permute-start.5 = (bf16[16,4096]{1,0:T(8,128)(2,1)S(1)}, bf16[16,4096]{1,0:T(8,128)(2,1)S(1)}, u32[]{:S(2)}, u32[]{:S(2)}) collective-permute-start(bf16[16,4096]{1,0:T(8,128)(2,1)S(1)} %collective-permute-done.refs_6_), channel_id=1, source_target_pairs={{0,18},{2,16},{4,22},{6,20},{8,26},{10,24},{12,30},{14,28},{16,2},... | collective-permute-start | bytes 393224 | tf_op jit(solution)/shard_map/ppermute | solution.py:138
  15.0 0.8 %collective-permute-start.6 = (bf16[16,4096]{1,0:T(8,128)(2,1)S(1)}, bf16[16,4096]{1,0:T(8,128)(2,1)S(1)}, u32[]{:S(2)}, u32[]{:S(2)}) collective-permute-start(bf16[16,4096]{1,0:T(8,128)(2,1)S(1)} %collective-permute-done.1.refs_8_), channel_id=1, source_target_pairs={{0,16},{2,18},{4,20},{6,22},{8,24},{10,26},{12,28},{14,30},{16,0},... | collective-permute-start | bytes 393224 | tf_op jit(solution)/shard_map/ppermute | solution.py:138
  15.8 1.8 %collective-permute-start.4 = (bf16[16,4096]{1,0:T(8,128)(2,1)S(1)}, bf16[16,4096]{1,0:T(8,128)(2,1)S(1)}, u32[]{:S(2)}, u32[]{:S(2)}) collective-permute-start(bf16[16,4096]{1,0:T(8,128)(2,1)S(1)} %collective-permute-done.1.refs_8_), channel_id=1, source_target_pairs={{0,4},{2,6},{4,0},{6,2},{8,12},{10,14},{12,8},{14,10},{1,5},{3,7},... | collective-permute-start | bytes 393224 | tf_op jit(solution)/shard_map/ppermute | solution.py:128
  17.6 0.0 collective-permute-start.3
  17.7 0.3 collective-permute-done.7.refs_10_
  18.0 0.2 collective-permute-start.2
  18.2 1.9 %collective-permute-done.5.refs_12_ = bf16[16,4096]{1,0:T(8,128)(2,1)S(1)} collective-permute-done((bf16[16,4096]{1,0:T(8,128)(2,1)S(1)}, bf16[16,4096]{1,0:T(8,128)(2,1)S(1)}, u32[]{:S(2)}, u32[]{:S(2)}) %collective-permute-start.5) | collective-permute-done | bytes 131104 | tf_op jit(solution)/shard_map/ppermute | solution.py:138
  20.0 0.3 collective-permute-start.9
  20.3 2.6 %collective-permute-done.6.refs_14_ = bf16[16,4096]{1,0:T(8,128)(2,1)S(1)} collective-permute-done((bf16[16,4096]{1,0:T(8,128)(2,1)S(1)}, bf16[16,4096]{1,0:T(8,128)(2,1)S(1)}, u32[]{:S(2)}, u32[]{:S(2)}) %collective-permute-start.6) | collective-permute-done | bytes 131104 | tf_op jit(solution)/shard_map/ppermute | solution.py:138
  22.9 0.0 collective-permute-start.10
  22.9 0.0 collective-permute-done.4.refs_4_
  22.9 0.5 %collective-permute-start.8 = (bf16[16,4096]{1,0:T(8,128)(2,1)S(1)}, bf16[16,4096]{1,0:T(8,128)(2,1)S(1)}, u32[]{:S(2)}, u32[]{:S(2)}) collective-permute-start(bf16[16,4096]{1,0:T(8,128)(2,1)S(1)} %collective-permute-done.4.refs_4_), channel_id=1, source_target_pairs={{0,2},{2,0},{4,6},{6,4},{8,10},{10,8},{12,14},{14,12},{1,3},{3,1},... | collective-permute-start | bytes 393224 | tf_op jit(solution)/shard_map/ppermute | solution.py:132
  23.4 0.0 collective-permute-done.3.refs_3_
  23.4 0.1 collective-permute-start.11
  23.5 0.0 collective-permute-done.2.refs_1_
  23.5 0.4 %collective-permute-start.12 = (bf16[16,4096]{1,0:T(8,128)(2,1)S(1)}, bf16[16,4096]{1,0:T(8,128)(2,1)S(1)}, u32[]{:S(2)}, u32[]{:S(2)}) collective-permute-start(bf16[16,4096]{1,0:T(8,128)(2,1)S(1)} %collective-permute-done.5.refs_12_), channel_id=1, source_target_pairs={{0,2},{2,0},{4,6},{6,4},{8,10},{10,8},{12,14},{14,12},{1,3},{3,1},... | collective-permute-start | bytes 393224 | tf_op jit(solution)/shard_map/ppermute | solution.py:132
  23.9 0.0 collective-permute-done.9.refs_7_
  23.9 0.1 collective-permute-start.13
  24.0 0.2 collective-permute-done.10.refs_9_
  24.2 0.2 collective-permute-done.8.refs_5_
  24.4 0.3 %collective-permute-done.11.refs_11_ = bf16[16,4096]{1,0:T(8,128)(2,1)S(1)} collective-permute-done((bf16[16,4096]{1,0:T(8,128)(2,1)S(1)}, bf16[16,4096]{1,0:T(8,128)(2,1)S(1)}, u32[]{:S(2)}, u32[]{:S(2)}) %collective-permute-start.11) | collective-permute-done | bytes 131104 | tf_op jit(solution)/shard_map/ppermute | solution.py:132
  24.8 0.2 collective-permute-done.12.refs_13_
  24.9 0.3 %collective-permute-done.13.refs_15_ = bf16[16,4096]{1,0:T(8,128)(2,1)S(1)} collective-permute-done((bf16[16,4096]{1,0:T(8,128)(2,1)S(1)}, bf16[16,4096]{1,0:T(8,128)(2,1)S(1)}, u32[]{:S(2)}, u32[]{:S(2)}) %collective-permute-start.13) | collective-permute-done | bytes 131104 | tf_op jit(solution)/shard_map/ppermute | solution.py:132
  25.3 1.0 %scores_sent.1 = (f32[128,128]{1,0:T(8,128)S(1)}, bf16[2,128,4096]{2,1,0:T(8,128)(2,1)S(1)}) custom-call(bf16[256,2,4096]{2,1,0:T(2,128)(2,1)S(1)} %near.1.train, bf16[16,4096]{1,0:T(8,128)(2,1)S(1)} %condition_mine.1.refs_0_, bf16[16,4096]{1,0:T(8,128)(2,1)S(1)} %collective-permute-done.2.refs_1_, bf16[16,4096]{1,0:T(8,128)(2,1)S(1)} %condition_other.1.refs_2_, ...), custom_call_target="tpu_custom_call" | custom-call | flops 536870912 | bytes 4194304 | tf_op jit(solution)/shard_map/scores_sent/pallas_call | solution.py:214
  26.3 1.6 %collective-permute-start.14 = (f32[128,128]{1,0:T(8,128)S(1)}, f32[128,128]{1,0:T(8,128)S(1)}, u32[]{:S(2)}, u32[]{:S(2)}) collective-permute-start(f32[128,128]{1,0:T(8,128)S(1)} %get-tuple-element.22), channel_id=1, source_target_pairs={{0,1},{1,0},{2,3},{3,2},{4,5},{5,4},{6,7},{7,6},{8,9},{9,8},{10,11... | collective-permute-start | bytes 196616 | tf_op jit(solution)/shard_map/ppermute | solution.py:257
  27.8 0.8 %scores_kept.1 = f32[128,128]{1,0:T(8,128)S(1)} custom-call(bf16[256,2,4096]{2,1,0:T(2,128)(2,1)S(1)} %near.1.train, bf16[2,128,4096]{2,1,0:T(8,128)(2,1)S(1)} %get-tuple-element.21.table), custom_call_target="tpu_custom_call" | custom-call | flops 536870912 | bytes 4194304 | tf_op jit(solution)/shard_map/scores_kept/pallas_call | solution.py:214
  28.7 1.9 %collective-permute-done.14 = f32[128,128]{1,0:T(8,128)S(1)} collective-permute-done((f32[128,128]{1,0:T(8,128)S(1)}, f32[128,128]{1,0:T(8,128)S(1)}, u32[]{:S(2)}, u32[]{:S(2)}) %collective-permute-start.14) | collective-permute-done | bytes 65568 | tf_op jit(solution)/shard_map/ppermute | solution.py:257
  30.6 0.6 %add.3 = f32[128,128]{1,0:T(8,128)} add(f32[128,128]{1,0:T(8,128)S(1)} %scores_kept.1, f32[128,128]{1,0:T(8,128)S(1)} %collective-permute-done.14) | non-fusion elementwise | flops 16384 | bytes 196608 | tf_op jit(solution)/shard_map/add | solution.py:259
Async XLA Ops:
  1.8 9.8 %collective-permute-start.1 = (bf16[16,4096]{1,0:T(8,128)(2,1)S(1)}, bf16[16,4096]{1,0:T(8,128)(2,1)S(1)}, u32[]{:S(2)}, u32[]{:S(2)}) collective-permute-start(bf16[16,4096]{1,0:T(8,128)(2,1)S(1)} %condition_mine.1.refs_0_), channel_id=1, source_target_pairs={{0,12},{2,14},{4,8},{6,10},{8,4},{10,6},{12,0},{14,2},{1,13},{3,15... | collective-permute-start | bytes 393224 | tf_op jit(solution)/shard_map/ppermute | solution.py:128
  6.9 7.4 %collective-permute-start = (bf16[16,4096]{1,0:T(8,128)(2,1)S(1)}, bf16[16,4096]{1,0:T(8,128)(2,1)S(1)}, u32[]{:S(2)}, u32[]{:S(2)}) collective-permute-start(bf16[16,4096]{1,0:T(8,128)(2,1)S(1)} %condition_mine.1.refs_0_), channel_id=1, source_target_pairs={{0,4},{2,6},{4,0},{6,2},{8,12},{10,14},{12,8},{14,10},{1,5},{3,7},... | collective-permute-start | bytes 393224 | tf_op jit(solution)/shard_map/ppermute | solution.py:128
  8.7 9.3 %collective-permute-start.7 = (bf16[16,4096]{1,0:T(8,128)(2,1)S(1)}, bf16[16,4096]{1,0:T(8,128)(2,1)S(1)}, u32[]{:S(2)}, u32[]{:S(2)}) collective-permute-start(bf16[16,4096]{1,0:T(8,128)(2,1)S(1)} %condition_other.1.refs_2_), channel_id=1, source_target_pairs={{0,8},{2,10},{4,12},{6,14},{8,0},{10,2},{12,4},{14,6},{1,9},{3,11}... | collective-permute-start | bytes 393224 | tf_op jit(solution)/shard_map/ppermute | solution.py:128
  14.3 5.7 %collective-permute-start.5 = (bf16[16,4096]{1,0:T(8,128)(2,1)S(1)}, bf16[16,4096]{1,0:T(8,128)(2,1)S(1)}, u32[]{:S(2)}, u32[]{:S(2)}) collective-permute-start(bf16[16,4096]{1,0:T(8,128)(2,1)S(1)} %collective-permute-done.refs_6_), channel_id=1, source_target_pairs={{0,18},{2,16},{4,22},{6,20},{8,26},{10,24},{12,30},{14,28},{16,2},... | collective-permute-start | bytes 393224 | tf_op jit(solution)/shard_map/ppermute | solution.py:138
  15.0 7.9 %collective-permute-start.6 = (bf16[16,4096]{1,0:T(8,128)(2,1)S(1)}, bf16[16,4096]{1,0:T(8,128)(2,1)S(1)}, u32[]{:S(2)}, u32[]{:S(2)}) collective-permute-start(bf16[16,4096]{1,0:T(8,128)(2,1)S(1)} %collective-permute-done.1.refs_8_), channel_id=1, source_target_pairs={{0,16},{2,18},{4,20},{6,22},{8,24},{10,26},{12,28},{14,30},{16,0},... | collective-permute-start | bytes 393224 | tf_op jit(solution)/shard_map/ppermute | solution.py:138
  15.8 7.1 %collective-permute-start.4 = (bf16[16,4096]{1,0:T(8,128)(2,1)S(1)}, bf16[16,4096]{1,0:T(8,128)(2,1)S(1)}, u32[]{:S(2)}, u32[]{:S(2)}) collective-permute-start(bf16[16,4096]{1,0:T(8,128)(2,1)S(1)} %collective-permute-done.1.refs_8_), channel_id=1, source_target_pairs={{0,4},{2,6},{4,0},{6,2},{8,12},{10,14},{12,8},{14,10},{1,5},{3,7},... | collective-permute-start | bytes 393224 | tf_op jit(solution)/shard_map/ppermute | solution.py:128
  17.6 5.8 %collective-permute-start.3 = (bf16[16,4096]{1,0:T(8,128)(2,1)S(1)}, bf16[16,4096]{1,0:T(8,128)(2,1)S(1)}, u32[]{:S(2)}, u32[]{:S(2)}) collective-permute-start(bf16[16,4096]{1,0:T(8,128)(2,1)S(1)} %condition_other.1.refs_2_), channel_id=1, source_target_pairs={{0,2},{2,0},{4,6},{6,4},{8,10},{10,8},{12,14},{14,12},{1,3},{3,1},... | collective-permute-start | bytes 393224 | tf_op jit(solution)/shard_map/ppermute | solution.py:132
  18.0 5.5 %collective-permute-start.2 = (bf16[16,4096]{1,0:T(8,128)(2,1)S(1)}, bf16[16,4096]{1,0:T(8,128)(2,1)S(1)}, u32[]{:S(2)}, u32[]{:S(2)}) collective-permute-start(bf16[16,4096]{1,0:T(8,128)(2,1)S(1)} %condition_mine.1.refs_0_), channel_id=1, source_target_pairs={{0,2},{2,0},{4,6},{6,4},{8,10},{10,8},{12,14},{14,12},{1,3},{3,1},... | collective-permute-start | bytes 393224 | tf_op jit(solution)/shard_map/ppermute | solution.py:132
  20.0 3.9 %collective-permute-start.9 = (bf16[16,4096]{1,0:T(8,128)(2,1)S(1)}, bf16[16,4096]{1,0:T(8,128)(2,1)S(1)}, u32[]{:S(2)}, u32[]{:S(2)}) collective-permute-start(bf16[16,4096]{1,0:T(8,128)(2,1)S(1)} %collective-permute-done.refs_6_), channel_id=1, source_target_pairs={{0,2},{2,0},{4,6},{6,4},{8,10},{10,8},{12,14},{14,12},{1,3},{3,1},... | collective-permute-start | bytes 393224 | tf_op jit(solution)/shard_map/ppermute | solution.py:132
  22.9 1.3 %collective-permute-start.10 = (bf16[16,4096]{1,0:T(8,128)(2,1)S(1)}, bf16[16,4096]{1,0:T(8,128)(2,1)S(1)}, u32[]{:S(2)}, u32[]{:S(2)}) collective-permute-start(bf16[16,4096]{1,0:T(8,128)(2,1)S(1)} %collective-permute-done.1.refs_8_), channel_id=1, source_target_pairs={{0,2},{2,0},{4,6},{6,4},{8,10},{10,8},{12,14},{14,12},{1,3},{3,1},... | collective-permute-start | bytes 393224 | tf_op jit(solution)/shard_map/ppermute | solution.py:132
  22.9 1.5 %collective-permute-start.8 = (bf16[16,4096]{1,0:T(8,128)(2,1)S(1)}, bf16[16,4096]{1,0:T(8,128)(2,1)S(1)}, u32[]{:S(2)}, u32[]{:S(2)}) collective-permute-start(bf16[16,4096]{1,0:T(8,128)(2,1)S(1)} %collective-permute-done.4.refs_4_), channel_id=1, source_target_pairs={{0,2},{2,0},{4,6},{6,4},{8,10},{10,8},{12,14},{14,12},{1,3},{3,1},... | collective-permute-start | bytes 393224 | tf_op jit(solution)/shard_map/ppermute | solution.py:132
  23.4 1.3 %collective-permute-start.11 = (bf16[16,4096]{1,0:T(8,128)(2,1)S(1)}, bf16[16,4096]{1,0:T(8,128)(2,1)S(1)}, u32[]{:S(2)}, u32[]{:S(2)}) collective-permute-start(bf16[16,4096]{1,0:T(8,128)(2,1)S(1)} %collective-permute-done.7.refs_10_), channel_id=1, source_target_pairs={{0,2},{2,0},{4,6},{6,4},{8,10},{10,8},{12,14},{14,12},{1,3},{3,1},... | collective-permute-start | bytes 393224 | tf_op jit(solution)/shard_map/ppermute | solution.py:132
  23.5 1.5 %collective-permute-start.12 = (bf16[16,4096]{1,0:T(8,128)(2,1)S(1)}, bf16[16,4096]{1,0:T(8,128)(2,1)S(1)}, u32[]{:S(2)}, u32[]{:S(2)}) collective-permute-start(bf16[16,4096]{1,0:T(8,128)(2,1)S(1)} %collective-permute-done.5.refs_12_), channel_id=1, source_target_pairs={{0,2},{2,0},{4,6},{6,4},{8,10},{10,8},{12,14},{14,12},{1,3},{3,1},... | collective-permute-start | bytes 393224 | tf_op jit(solution)/shard_map/ppermute | solution.py:132
  23.9 1.3 %collective-permute-start.13 = (bf16[16,4096]{1,0:T(8,128)(2,1)S(1)}, bf16[16,4096]{1,0:T(8,128)(2,1)S(1)}, u32[]{:S(2)}, u32[]{:S(2)}) collective-permute-start(bf16[16,4096]{1,0:T(8,128)(2,1)S(1)} %collective-permute-done.6.refs_14_), channel_id=1, source_target_pairs={{0,2},{2,0},{4,6},{6,4},{8,10},{10,8},{12,14},{14,12},{1,3},{3,1},... | collective-permute-start | bytes 393224 | tf_op jit(solution)/shard_map/ppermute | solution.py:132
  26.3 4.3 %collective-permute-start.14 = (f32[128,128]{1,0:T(8,128)S(1)}, f32[128,128]{1,0:T(8,128)S(1)}, u32[]{:S(2)}, u32[]{:S(2)}) collective-permute-start(f32[128,128]{1,0:T(8,128)S(1)} %get-tuple-element.22), channel_id=1, source_target_pairs={{0,1},{1,0},{2,3},{3,2},{4,5},{5,4},{6,7},{7,6},{8,9},{9,8},{10,11... | collective-permute-start | bytes 196616 | tf_op jit(solution)/shard_map/ppermute | solution.py:257

commit v23 on v18

--- a/solution.py
+++ b/solution.py
@@ -179,7 +179,11 @@
 
 
 def sent_kernel(train, *refs):
-    blocks, (scores, table, terms) = refs[:-3], refs[-3:]
+    other, other_c, mine, s1, s3, first_c, s2, y3, last_c, t2, y1, middle_c, scores, table, terms = refs
+    blocks = [other, other_c]
+    for group, swapped in (((mine, s1, s3), first_c), ((s2, y3), last_c), ((t2, y1), middle_c)):
+        for k, block in enumerate(group):
+            blocks += [block, swapped.at[k]]
     part = lax.axis_index("parts")
     column, core = place()
     count = blocks[0].shape[0]
@@ -191,14 +195,14 @@
     for twin in range(PAIR):
         for k, (layer, flip, cross) in enumerate(
             (
+                (1 - part, 0, 0),
                 (part, 0, 0),
-                (1 - part, 0, 0),
-                (part, 2, 0),
                 (part, 1, 0),
                 (part, 3, 0),
+                (part, 2, 0),
+                (1 - part, 3, 0),
                 (1 - part, 2, 0),
                 (1 - part, 1, 1),
-                (1 - part, 3, 0),
             )
         ):
             put(layer, flip, twin ^ cross, blocks[PAIR * k + twin][...])
@@ -239,11 +243,10 @@
     t2 = along_columns(other, 2)
     y1 = other_part(s1, cross=True)
     y3 = other_part(s3)
-    s2, y1, y3, t2 = lax.optimization_barrier((s2, y1, y3, t2))
-
-    blocks = []
-    for block in (mine, other, s2, s1, s3, t2, y1, y3):
-        blocks += [block, other_core(block)]
+
+    blocks = [other, other_core(other)]
+    for group in ((mine, s1, s3), (s2, y3), (t2, y1)):
+        blocks += [*group, other_core(jnp.stack(group))]
     f32 = functools.partial(jax.ShapeDtypeStruct, dtype=jnp.float32)
     terms = [pltpu.VMEM((layer_count, share * layer_count, total), jnp.float32)]
     sent, table = local_call(

time: 30 us -> 29 us (0.967)
  starting transfers between devices: 13.6 us -> 13 us
  waiting for transfers between devices: 8.03 us -> 7.47 us
    ppermute x4, waiting for transfers between devices: 5.02 us -> 1.52 us  [along_columns(): lax.ppermute(value, 'train', [(k, k ^ flip * PAIR) for k in range(COLUMNS...]
    ppermute x2, waiting for transfers between devices: 0.01 us -> 2.61 us  [other_part(): return lax.ppermute(value, ('parts', 'train'), pairs)]
    ppermute x4, starting transfers between devices: 8.4 us -> 7.44 us  [along_columns(): lax.ppermute(value, 'train', [(k, k ^ flip * PAIR) for k in range(COLUMNS...]
    ppermute x8 -> x4, starting transfers between devices: 1.69 us -> 2.23 us  [other_core(): lax.ppermute(value, 'train', [(k, k ^ 1) for k in range(COLUMNS * PAIR)])]
    ppermute x8 -> x4, waiting for transfers between devices: 1.03 us -> 1.41 us  [other_core(): lax.ppermute(value, 'train', [(k, k ^ 1) for k in range(COLUMNS * PAIR)])]
  transfers between devices with their start and end apart: 15 -> 11, of which waited for: 8 -> 4; matrix products, arithmetic and copies ran while one was open for 0% -> 0% of each run, Pallas kernels for 16% -> 17%
where the time goes in v23:
time: 29 us; the launch traced here: 28.9 us
  starting transfers between devices  13 us (45%)
  Pallas kernels  7.57 us (26%)
  waiting for transfers between devices  7.47 us (26%)
  other arithmetic  0.73 us (3%)
    ppermute x4, starting transfers between devices, along_columns(): lax.ppermute(value, 'train', [(k, k ^ flip * PAIR) for k in range(COLUMNS...  7.44 us
    pallas_call x2, Pallas kernels, condition_layer(): pl.pallas_call(functools.partial(condition_kernel, other), out_shape=jax....  3.53 us
    ppermute x2, waiting for transfers between devices, other_part(): return lax.ppermute(value, ('parts', 'train'), pairs)  2.61 us
    ppermute x4, starting transfers between devices, other_core(): lax.ppermute(value, 'train', [(k, k ^ 1) for k in range(COLUMNS * PAIR)])  2.23 us
    pallas_call x1, Pallas kernels, copy_near(): pl.pallas_call(copy_kernel, out_shape=jax.ShapeDtypeStruct(value.shape, v...  2.2 us
    ppermute x1, waiting for transfers between devices, direct(): received = lax.ppermute(sent, 'layer', [(0, 1), (1, 0)])  1.92 us
    pallas_call x2, Pallas kernels, local_call(): pl.pallas_call(kernel, out_shape=out_shape, in_specs=[spec] * len(operand...  1.84 us
    ppermute x2, starting transfers between devices, other_part(): return lax.ppermute(value, ('parts', 'train'), pairs)  1.8 us
  transfers between devices with their start and end apart: 11, of which 4 were waited for; matrix products, arithmetic and copies ran while one was open for 0% of the time, Pallas kernels for 17%

profile of v23, /device:TPU:0, one launch (start us, length us, event | category | flops | bytes accessed | tf_op | source)
XLA Modules:
  0.0 28.9 jit_solution(2450779533126013390)
XLA Ops:
  0.0 1.8 %condition_mine.1.refs_2_ = bf16[16,4096]{1,0:T(8,128)(2,1)S(1)} custom-call(bf16[2,1,16,4096]{3,2,1,0:T(8,128)(2,1)} %queries.3, f32[2,64,64]{2,1,0:T(8,128)} %left.3, f32[2,64,64]{2,1,0:T(8,128)} %right.3), custom_call_target="tpu_custom_call" | custom-call | flops 134217728 | bytes 524288 | tf_op jit(solution)/shard_map/condition_mine/pallas_call | solution.py:107
  1.8 5.1 %collective-permute-start = (bf16[16,4096]{1,0:T(8,128)(2,1)S(1)}, bf16[16,4096]{1,0:T(8,128)(2,1)S(1)}, u32[]{:S(2)}, u32[]{:S(2)}) collective-permute-start(bf16[16,4096]{1,0:T(8,128)(2,1)S(1)} %condition_mine.1.refs_2_), channel_id=1, source_target_pairs={{0,12},{2,14},{4,8},{6,10},{8,4},{10,6},{12,0},{14,2},{1,13},{3,15... | collective-permute-start | bytes 393224 | tf_op jit(solution)/shard_map/ppermute | solution.py:128
  6.9 0.0 collective-permute-start.2
  6.9 1.8 %condition_other.1.refs_0_ = bf16[16,4096]{1,0:T(8,128)(2,1)S(1)} custom-call(bf16[2,1,16,4096]{3,2,1,0:T(8,128)(2,1)} %queries.3, f32[2,64,64]{2,1,0:T(8,128)} %left.3, f32[2,64,64]{2,1,0:T(8,128)} %right.3), custom_call_target="tpu_custom_call" | custom-call | flops 134217728 | bytes 524288 | tf_op jit(solution)/shard_map/condition_other/pallas_call | solution.py:107
  8.7 0.7 %collective-permute-start.7 = (bf16[16,4096]{1,0:T(8,128)(2,1)S(1)}, bf16[16,4096]{1,0:T(8,128)(2,1)S(1)}, u32[]{:S(2)}, u32[]{:S(2)}) collective-permute-start(bf16[16,4096]{1,0:T(8,128)(2,1)S(1)} %condition_other.1.refs_0_), channel_id=1, source_target_pairs={{0,8},{2,10},{4,12},{6,14},{8,0},{10,2},{12,4},{14,6},{1,9},{3,11}... | collective-permute-start | bytes 393224 | tf_op jit(solution)/shard_map/ppermute | solution.py:128
  9.4 2.2 %near.1.train = bf16[256,2,4096]{2,1,0:T(2,128)(2,1)S(1)} custom-call(bf16[256,2,4096]{2,1,0:T(2,128)(2,1)} %source.1), custom_call_target="tpu_custom_call" | custom-call | bytes 8388608 | tf_op jit(solution)/shard_map/near/pallas_call | solution.py:148
  11.6 0.0 collective-permute-done.refs_4_
  11.6 1.7 %collective-permute-start.5 = (bf16[16,4096]{1,0:T(8,128)(2,1)S(1)}, bf16[16,4096]{1,0:T(8,128)(2,1)S(1)}, u32[]{:S(2)}, u32[]{:S(2)}) collective-permute-start(bf16[16,4096]{1,0:T(8,128)(2,1)S(1)} %collective-permute-done.refs_4_), channel_id=1, source_target_pairs={{0,16},{2,18},{4,20},{6,22},{8,24},{10,26},{12,28},{14,30},{16,0},... | collective-permute-start | bytes 393224 | tf_op jit(solution)/shard_map/ppermute | solution.py:138
  13.3 1.6 %collective-permute-start.4 = (bf16[16,4096]{1,0:T(8,128)(2,1)S(1)}, bf16[16,4096]{1,0:T(8,128)(2,1)S(1)}, u32[]{:S(2)}, u32[]{:S(2)}) collective-permute-start(bf16[16,4096]{1,0:T(8,128)(2,1)S(1)} %collective-permute-done.refs_4_), channel_id=1, source_target_pairs={{0,4},{2,6},{4,0},{6,2},{8,12},{10,14},{12,8},{14,10},{1,5},{3,7},... | collective-permute-start | bytes 393224 | tf_op jit(solution)/shard_map/ppermute | solution.py:128
  14.9 0.0 collective-permute-done.2.refs_3_
  14.9 0.1 collective-permute-start.8
  15.1 1.5 %collective-permute-start.3 = (bf16[3,16,4096]{2,1,0:T(8,128)(2,1)S(1)}, bf16[3,16,4096]{2,1,0:T(8,128)(2,1)S(1)}, u32[]{:S(2)}, u32[]{:S(2)}) collective-permute-start(bf16[3,16,4096]{2,1,0:T(8,128)(2,1)S(1)} %pad_maximum_fusion), channel_id=1, source_target_pairs={{0,2},{2,0},{4,6},{6,4},{8,10},{10,8},{12,14},{14,12},{1,3},{3,1},... | collective-permute-start | bytes 1179656 | tf_op jit(solution)/shard_map/ppermute | solution.py:132
  16.6 1.5 %collective-permute-done.7.refs_9_ = bf16[16,4096]{1,0:T(8,128)(2,1)S(1)} collective-permute-done((bf16[16,4096]{1,0:T(8,128)(2,1)S(1)}, bf16[16,4096]{1,0:T(8,128)(2,1)S(1)}, u32[]{:S(2)}, u32[]{:S(2)}) %collective-permute-start.7) | collective-permute-done | bytes 131104 | tf_op jit(solution)/shard_map/ppermute | solution.py:128
  18.1 2.6 %collective-permute-done.8.refs_10_ = bf16[16,4096]{1,0:T(8,128)(2,1)S(1)} collective-permute-done((bf16[16,4096]{1,0:T(8,128)(2,1)S(1)}, bf16[16,4096]{1,0:T(8,128)(2,1)S(1)}, u32[]{:S(2)}, u32[]{:S(2)}) %collective-permute-start.8) | collective-permute-done | bytes 131104 | tf_op jit(solution)/shard_map/ppermute | solution.py:138
  20.7 0.1 collective-permute-start.9
  20.8 0.0 collective-permute-done.5.refs_7_
  20.8 0.0 collective-permute-done.4.refs_6_
  20.9 0.5 %collective-permute-start.6 = (bf16[2,16,4096]{2,1,0:T(8,128)(2,1)S(1)}, bf16[2,16,4096]{2,1,0:T(8,128)(2,1)S(1)}, u32[]{:S(2)}, u32[]{:S(2)}) collective-permute-start(bf16[2,16,4096]{2,1,0:T(8,128)(2,1)S(1)} %pad_maximum_fusion.1), channel_id=1, source_target_pairs={{0,2},{2,0},{4,6},{6,4},{8,10},{10,8},{12,14},{14,12},{1,3},{3,1},... | collective-permute-start | bytes 786440 | tf_op jit(solution)/shard_map/ppermute | solution.py:132
  21.4 0.1 collective-permute-start.1
  21.5 1.4 %collective-permute-done.1.refs_1_ = bf16[16,4096]{1,0:T(8,128)(2,1)S(1)} collective-permute-done((bf16[16,4096]{1,0:T(8,128)(2,1)S(1)}, bf16[16,4096]{1,0:T(8,128)(2,1)S(1)}, u32[]{:S(2)}, u32[]{:S(2)}) %collective-permute-start.1) | collective-permute-done | bytes 131104 | tf_op jit(solution)/shard_map/ppermute | solution.py:132
  22.9 0.0 collective-permute-done.9.refs_11_
  22.9 0.0 collective-permute-done.6.refs_8_
  22.9 0.0 collective-permute-done.3.refs_5_
  22.9 1.0 %scores_sent.1 = (f32[128,128]{1,0:T(8,128)S(1)}, bf16[2,128,4096]{2,1,0:T(8,128)(2,1)S(1)}) custom-call(bf16[256,2,4096]{2,1,0:T(2,128)(2,1)S(1)} %near.1.train, bf16[16,4096]{1,0:T(8,128)(2,1)S(1)} %condition_other.1.refs_0_, bf16[16,4096]{1,0:T(8,128)(2,1)S(1)} %collective-permute-done.1.refs_1_, bf16[16,4096]{1,0:T(8,128)(2,1)S(1)} %condition_mine.1.refs_2_, ...), custom_call_target="tpu_custom_call" | custom-call | flops 536870912 | bytes 4194304 | tf_op jit(solution)/shard_map/scores_sent/pallas_call | solution.py:218
  23.9 1.6 %collective-permute-start.10 = (f32[128,128]{1,0:T(8,128)S(1)}, f32[128,128]{1,0:T(8,128)S(1)}, u32[]{:S(2)}, u32[]{:S(2)}) collective-permute-start(f32[128,128]{1,0:T(8,128)S(1)} %get-tuple-element.12), channel_id=1, source_target_pairs={{0,1},{1,0},{2,3},{3,2},{4,5},{5,4},{6,7},{7,6},{8,9},{9,8},{10,11... | collective-permute-start | bytes 196616 | tf_op jit(solution)/shard_map/ppermute | solution.py:260
  25.5 0.8 %scores_kept.1 = f32[128,128]{1,0:T(8,128)S(1)} custom-call(bf16[256,2,4096]{2,1,0:T(2,128)(2,1)S(1)} %near.1.train, bf16[2,128,4096]{2,1,0:T(8,128)(2,1)S(1)} %get-tuple-element.11.table), custom_call_target="tpu_custom_call" | custom-call | flops 536870912 | bytes 4194304 | tf_op jit(solution)/shard_map/scores_kept/pallas_call | solution.py:218
  26.3 1.9 %collective-permute-done.10 = f32[128,128]{1,0:T(8,128)S(1)} collective-permute-done((f32[128,128]{1,0:T(8,128)S(1)}, f32[128,128]{1,0:T(8,128)S(1)}, u32[]{:S(2)}, u32[]{:S(2)}) %collective-permute-start.10) | collective-permute-done | bytes 65568 | tf_op jit(solution)/shard_map/ppermute | solution.py:260
  28.2 0.6 %add.3 = f32[128,128]{1,0:T(8,128)} add(f32[128,128]{1,0:T(8,128)S(1)} %scores_kept.1, f32[128,128]{1,0:T(8,128)S(1)} %collective-permute-done.10) | non-fusion elementwise | flops 16384 | bytes 196608 | tf_op jit(solution)/shard_map/add | solution.py:262
  (3 shorter events, 0.1 us)
Async XLA Ops:
  1.8 9.8 %collective-permute-start = (bf16[16,4096]{1,0:T(8,128)(2,1)S(1)}, bf16[16,4096]{1,0:T(8,128)(2,1)S(1)}, u32[]{:S(2)}, u32[]{:S(2)}) collective-permute-start(bf16[16,4096]{1,0:T(8,128)(2,1)S(1)} %condition_mine.1.refs_2_), channel_id=1, source_target_pairs={{0,12},{2,14},{4,8},{6,10},{8,4},{10,6},{12,0},{14,2},{1,13},{3,15... | collective-permute-start | bytes 393224 | tf_op jit(solution)/shard_map/ppermute | solution.py:128
  6.9 8.0 %collective-permute-start.2 = (bf16[16,4096]{1,0:T(8,128)(2,1)S(1)}, bf16[16,4096]{1,0:T(8,128)(2,1)S(1)}, u32[]{:S(2)}, u32[]{:S(2)}) collective-permute-start(bf16[16,4096]{1,0:T(8,128)(2,1)S(1)} %condition_mine.1.refs_2_), channel_id=1, source_target_pairs={{0,4},{2,6},{4,0},{6,2},{8,12},{10,14},{12,8},{14,10},{1,5},{3,7},... | collective-permute-start | bytes 393224 | tf_op jit(solution)/shard_map/ppermute | solution.py:128
  8.7 9.4 %collective-permute-start.7 = (bf16[16,4096]{1,0:T(8,128)(2,1)S(1)}, bf16[16,4096]{1,0:T(8,128)(2,1)S(1)}, u32[]{:S(2)}, u32[]{:S(2)}) collective-permute-start(bf16[16,4096]{1,0:T(8,128)(2,1)S(1)} %condition_other.1.refs_0_), channel_id=1, source_target_pairs={{0,8},{2,10},{4,12},{6,14},{8,0},{10,2},{12,4},{14,6},{1,9},{3,11}... | collective-permute-start | bytes 393224 | tf_op jit(solution)/shard_map/ppermute | solution.py:128
  11.6 9.3 %collective-permute-start.5 = (bf16[16,4096]{1,0:T(8,128)(2,1)S(1)}, bf16[16,4096]{1,0:T(8,128)(2,1)S(1)}, u32[]{:S(2)}, u32[]{:S(2)}) collective-permute-start(bf16[16,4096]{1,0:T(8,128)(2,1)S(1)} %collective-permute-done.refs_4_), channel_id=1, source_target_pairs={{0,16},{2,18},{4,20},{6,22},{8,24},{10,26},{12,28},{14,30},{16,0},... | collective-permute-start | bytes 393224 | tf_op jit(solution)/shard_map/ppermute | solution.py:138
  13.3 7.5 %collective-permute-start.4 = (bf16[16,4096]{1,0:T(8,128)(2,1)S(1)}, bf16[16,4096]{1,0:T(8,128)(2,1)S(1)}, u32[]{:S(2)}, u32[]{:S(2)}) collective-permute-start(bf16[16,4096]{1,0:T(8,128)(2,1)S(1)} %collective-permute-done.refs_4_), channel_id=1, source_target_pairs={{0,4},{2,6},{4,0},{6,2},{8,12},{10,14},{12,8},{14,10},{1,5},{3,7},... | collective-permute-start | bytes 393224 | tf_op jit(solution)/shard_map/ppermute | solution.py:128
  14.9 5.7 %collective-permute-start.8 = (bf16[16,4096]{1,0:T(8,128)(2,1)S(1)}, bf16[16,4096]{1,0:T(8,128)(2,1)S(1)}, u32[]{:S(2)}, u32[]{:S(2)}) collective-permute-start(bf16[16,4096]{1,0:T(8,128)(2,1)S(1)} %collective-permute-done.2.refs_3_), channel_id=1, source_target_pairs={{0,18},{2,16},{4,22},{6,20},{8,26},{10,24},{12,30},{14,28},{16,2},... | collective-permute-start | bytes 393224 | tf_op jit(solution)/shard_map/ppermute | solution.py:138
  15.1 7.8 %collective-permute-start.3 = (bf16[3,16,4096]{2,1,0:T(8,128)(2,1)S(1)}, bf16[3,16,4096]{2,1,0:T(8,128)(2,1)S(1)}, u32[]{:S(2)}, u32[]{:S(2)}) collective-permute-start(bf16[3,16,4096]{2,1,0:T(8,128)(2,1)S(1)} %pad_maximum_fusion), channel_id=1, source_target_pairs={{0,2},{2,0},{4,6},{6,4},{8,10},{10,8},{12,14},{14,12},{1,3},{3,1},... | collective-permute-start | bytes 1179656 | tf_op jit(solution)/shard_map/ppermute | solution.py:132
  20.7 2.2 %collective-permute-start.9 = (bf16[2,16,4096]{2,1,0:T(8,128)(2,1)S(1)}, bf16[2,16,4096]{2,1,0:T(8,128)(2,1)S(1)}, u32[]{:S(2)}, u32[]{:S(2)}) collective-permute-start(bf16[2,16,4096]{2,1,0:T(8,128)(2,1)S(1)} %pad_maximum_fusion.2), channel_id=1, source_target_pairs={{0,2},{2,0},{4,6},{6,4},{8,10},{10,8},{12,14},{14,12},{1,3},{3,1},... | collective-permute-start | bytes 786440 | tf_op jit(solution)/shard_map/ppermute | solution.py:132
  20.9 2.0 %collective-permute-start.6 = (bf16[2,16,4096]{2,1,0:T(8,128)(2,1)S(1)}, bf16[2,16,4096]{2,1,0:T(8,128)(2,1)S(1)}, u32[]{:S(2)}, u32[]{:S(2)}) collective-permute-start(bf16[2,16,4096]{2,1,0:T(8,128)(2,1)S(1)} %pad_maximum_fusion.1), channel_id=1, source_target_pairs={{0,2},{2,0},{4,6},{6,4},{8,10},{10,8},{12,14},{14,12},{1,3},{3,1},... | collective-permute-start | bytes 786440 | tf_op jit(solution)/shard_map/ppermute | solution.py:132
  21.4 1.5 %collective-permute-start.1 = (bf16[16,4096]{1,0:T(8,128)(2,1)S(1)}, bf16[16,4096]{1,0:T(8,128)(2,1)S(1)}, u32[]{:S(2)}, u32[]{:S(2)}) collective-permute-start(bf16[16,4096]{1,0:T(8,128)(2,1)S(1)} %condition_other.1.refs_0_), channel_id=1, source_target_pairs={{0,2},{2,0},{4,6},{6,4},{8,10},{10,8},{12,14},{14,12},{1,3},{3,1},... | collective-permute-start | bytes 393224 | tf_op jit(solution)/shard_map/ppermute | solution.py:132
  23.9 4.3 %collective-permute-start.10 = (f32[128,128]{1,0:T(8,128)S(1)}, f32[128,128]{1,0:T(8,128)S(1)}, u32[]{:S(2)}, u32[]{:S(2)}) collective-permute-start(f32[128,128]{1,0:T(8,128)S(1)} %get-tuple-element.12), channel_id=1, source_target_pairs={{0,1},{1,0},{2,3},{3,2},{4,5},{5,4},{6,7},{7,6},{8,9},{9,8},{10,11... | collective-permute-start | bytes 196616 | tf_op jit(solution)/shard_map/ppermute | solution.py:260

commit v24 on v23

--- a/solution.py
+++ b/solution.py
@@ -179,9 +179,9 @@
 
 
 def sent_kernel(train, *refs):
-    other, other_c, mine, s1, s3, first_c, s2, y3, last_c, t2, y1, middle_c, scores, table, terms = refs
-    blocks = [other, other_c]
-    for group, swapped in (((mine, s1, s3), first_c), ((s2, y3), last_c), ((t2, y1), middle_c)):
+    mine, other, s1, s3, first_c, s2, y3, last_c, t2, y1, middle_c, scores, table, terms = refs
+    blocks = []
+    for group, swapped in (((mine, other, s1, s3), first_c), ((s2, y3), last_c), ((t2, y1), middle_c)):
         for k, block in enumerate(group):
             blocks += [block, swapped.at[k]]
     part = lax.axis_index("parts")
@@ -195,8 +195,8 @@
     for twin in range(PAIR):
         for k, (layer, flip, cross) in enumerate(
             (
+                (part, 0, 0),
                 (1 - part, 0, 0),
-                (part, 0, 0),
                 (part, 1, 0),
                 (part, 3, 0),
                 (part, 2, 0),
@@ -244,8 +244,8 @@
     y1 = other_part(s1, cross=True)
     y3 = other_part(s3)
 
-    blocks = [other, other_core(other)]
-    for group in ((mine, s1, s3), (s2, y3), (t2, y1)):
+    blocks = []
+    for group in ((mine, other, s1, s3), (s2, y3), (t2, y1)):
         blocks += [*group, other_core(jnp.stack(group))]
     f32 = functools.partial(jax.ShapeDtypeStruct, dtype=jnp.float32)
     terms = [pltpu.VMEM((layer_count, share * layer_count, total), jnp.float32)]

time: 29 us -> 28.8 us (level)
    ppermute x4 -> x3, waiting for transfers between devices: 1.41 us -> 1.3 us  [other_core(): lax.ppermute(value, 'train', [(k, k ^ 1) for k in range(COLUMNS * PAIR)])]
    ppermute x4 -> x3, starting transfers between devices: 2.23 us -> 2.15 us  [other_core(): lax.ppermute(value, 'train', [(k, k ^ 1) for k in range(COLUMNS * PAIR)])]
  transfers between devices with their start and end apart: 11 -> 10, of which waited for: 4 -> 5; matrix products, arithmetic and copies ran while one was open for 0% -> 0% of each run, Pallas kernels for 17% -> 17%
where the time goes in v24:
time: 28.8 us; the launch traced here: 28.7 us
  starting transfers between devices  12.9 us (45%)
  Pallas kernels  7.57 us (26%)
  waiting for transfers between devices  7.33 us (25%)
  other arithmetic  0.76 us (3%)
    ppermute x4, starting transfers between devices, along_columns(): lax.ppermute(value, 'train', [(k, k ^ flip * PAIR) for k in range(COLUMNS...  7.44 us
    pallas_call x2, Pallas kernels, condition_layer(): pl.pallas_call(functools.partial(condition_kernel, other), out_shape=jax....  3.53 us
    ppermute x2, waiting for transfers between devices, other_part(): return lax.ppermute(value, ('parts', 'train'), pairs)  2.61 us
    pallas_call x1, Pallas kernels, copy_near(): pl.pallas_call(copy_kernel, out_shape=jax.ShapeDtypeStruct(value.shape, v...  2.2 us
    ppermute x3, starting transfers between devices, other_core(): lax.ppermute(value, 'train', [(k, k ^ 1) for k in range(COLUMNS * PAIR)])  2.15 us
    ppermute x1, waiting for transfers between devices, direct(): received = lax.ppermute(sent, 'layer', [(0, 1), (1, 0)])  1.92 us
    pallas_call x2, Pallas kernels, local_call(): pl.pallas_call(kernel, out_shape=out_shape, in_specs=[spec] * len(operand...  1.84 us
    ppermute x2, starting transfers between devices, other_part(): return lax.ppermute(value, ('parts', 'train'), pairs)  1.8 us
  transfers between devices with their start and end apart: 10, of which 5 were waited for; matrix products, arithmetic and copies ran while one was open for 0% of the time, Pallas kernels for 17%

profile of v24, /device:TPU:0, one launch (start us, length us, event | category | flops | bytes accessed | tf_op | source)
XLA Modules:
  0.0 28.7 jit_solution(12051281254144403883)
XLA Ops:
  0.0 1.8 %condition_mine.1.refs_0_ = bf16[16,4096]{1,0:T(8,128)(2,1)S(1)} custom-call(bf16[2,1,16,4096]{3,2,1,0:T(8,128)(2,1)} %queries.3, f32[2,64,64]{2,1,0:T(8,128)} %left.3, f32[2,64,64]{2,1,0:T(8,128)} %right.3), custom_call_target="tpu_custom_call" | custom-call | flops 134217728 | bytes 524288 | tf_op jit(solution)/shard_map/condition_mine/pallas_call | solution.py:107
  1.8 5.1 %collective-permute-start = (bf16[16,4096]{1,0:T(8,128)(2,1)S(1)}, bf16[16,4096]{1,0:T(8,128)(2,1)S(1)}, u32[]{:S(2)}, u32[]{:S(2)}) collective-permute-start(bf16[16,4096]{1,0:T(8,128)(2,1)S(1)} %condition_mine.1.refs_0_), channel_id=1, source_target_pairs={{0,12},{2,14},{4,8},{6,10},{8,4},{10,6},{12,0},{14,2},{1,13},{3,15... | collective-permute-start | bytes 393224 | tf_op jit(solution)/shard_map/ppermute | solution.py:128
  6.9 0.0 collective-permute-start.1
  6.9 1.8 %condition_other.1.refs_1_ = bf16[16,4096]{1,0:T(8,128)(2,1)S(1)} custom-call(bf16[2,1,16,4096]{3,2,1,0:T(8,128)(2,1)} %queries.3, f32[2,64,64]{2,1,0:T(8,128)} %left.3, f32[2,64,64]{2,1,0:T(8,128)} %right.3), custom_call_target="tpu_custom_call" | custom-call | flops 134217728 | bytes 524288 | tf_op jit(solution)/shard_map/condition_other/pallas_call | solution.py:107
  8.7 0.7 %collective-permute-start.6 = (bf16[16,4096]{1,0:T(8,128)(2,1)S(1)}, bf16[16,4096]{1,0:T(8,128)(2,1)S(1)}, u32[]{:S(2)}, u32[]{:S(2)}) collective-permute-start(bf16[16,4096]{1,0:T(8,128)(2,1)S(1)} %condition_other.1.refs_1_), channel_id=1, source_target_pairs={{0,8},{2,10},{4,12},{6,14},{8,0},{10,2},{12,4},{14,6},{1,9},{3,11}... | collective-permute-start | bytes 393224 | tf_op jit(solution)/shard_map/ppermute | solution.py:128
  9.4 2.2 %near.1.train = bf16[256,2,4096]{2,1,0:T(2,128)(2,1)S(1)} custom-call(bf16[256,2,4096]{2,1,0:T(2,128)(2,1)} %source.1), custom_call_target="tpu_custom_call" | custom-call | bytes 8388608 | tf_op jit(solution)/shard_map/near/pallas_call | solution.py:148
  11.6 0.0 collective-permute-done.refs_3_
  11.6 1.7 %collective-permute-start.4 = (bf16[16,4096]{1,0:T(8,128)(2,1)S(1)}, bf16[16,4096]{1,0:T(8,128)(2,1)S(1)}, u32[]{:S(2)}, u32[]{:S(2)}) collective-permute-start(bf16[16,4096]{1,0:T(8,128)(2,1)S(1)} %collective-permute-done.refs_3_), channel_id=1, source_target_pairs={{0,16},{2,18},{4,20},{6,22},{8,24},{10,26},{12,28},{14,30},{16,0},... | collective-permute-start | bytes 393224 | tf_op jit(solution)/shard_map/ppermute | solution.py:138
  13.3 1.6 %collective-permute-start.3 = (bf16[16,4096]{1,0:T(8,128)(2,1)S(1)}, bf16[16,4096]{1,0:T(8,128)(2,1)S(1)}, u32[]{:S(2)}, u32[]{:S(2)}) collective-permute-start(bf16[16,4096]{1,0:T(8,128)(2,1)S(1)} %collective-permute-done.refs_3_), channel_id=1, source_target_pairs={{0,4},{2,6},{4,0},{6,2},{8,12},{10,14},{12,8},{14,10},{1,5},{3,7},... | collective-permute-start | bytes 393224 | tf_op jit(solution)/shard_map/ppermute | solution.py:128
  14.9 0.0 collective-permute-done.1.refs_2_
  14.9 0.1 collective-permute-start.7
  15.0 0.1 pad_maximum_fusion
  15.1 1.5 %collective-permute-start.2 = (bf16[4,16,4096]{2,1,0:T(8,128)(2,1)S(1)}, bf16[4,16,4096]{2,1,0:T(8,128)(2,1)S(1)}, u32[]{:S(2)}, u32[]{:S(2)}) collective-permute-start(bf16[4,16,4096]{2,1,0:T(8,128)(2,1)S(1)} %pad_maximum_fusion), channel_id=1, source_target_pairs={{0,2},{2,0},{4,6},{6,4},{8,10},{10,8},{12,14},{14,12},{1,3},{3,1},... | collective-permute-start | bytes 1572872 | tf_op jit(solution)/shard_map/ppermute | solution.py:132
  16.6 1.5 %collective-permute-done.6.refs_8_ = bf16[16,4096]{1,0:T(8,128)(2,1)S(1)} collective-permute-done((bf16[16,4096]{1,0:T(8,128)(2,1)S(1)}, bf16[16,4096]{1,0:T(8,128)(2,1)S(1)}, u32[]{:S(2)}, u32[]{:S(2)}) %collective-permute-start.6) | collective-permute-done | bytes 131104 | tf_op jit(solution)/shard_map/ppermute | solution.py:128
  18.1 2.6 %collective-permute-done.7.refs_9_ = bf16[16,4096]{1,0:T(8,128)(2,1)S(1)} collective-permute-done((bf16[16,4096]{1,0:T(8,128)(2,1)S(1)}, bf16[16,4096]{1,0:T(8,128)(2,1)S(1)}, u32[]{:S(2)}, u32[]{:S(2)}) %collective-permute-start.7) | collective-permute-done | bytes 131104 | tf_op jit(solution)/shard_map/ppermute | solution.py:138
  20.7 0.1 collective-permute-start.8
  20.8 0.0 collective-permute-done.4.refs_6_
  20.8 0.0 collective-permute-done.3.refs_5_
  20.9 0.5 %collective-permute-start.5 = (bf16[2,16,4096]{2,1,0:T(8,128)(2,1)S(1)}, bf16[2,16,4096]{2,1,0:T(8,128)(2,1)S(1)}, u32[]{:S(2)}, u32[]{:S(2)}) collective-permute-start(bf16[2,16,4096]{2,1,0:T(8,128)(2,1)S(1)} %pad_maximum_fusion.1), channel_id=1, source_target_pairs={{0,2},{2,0},{4,6},{6,4},{8,10},{10,8},{12,14},{14,12},{1,3},{3,1},... | collective-permute-start | bytes 786440 | tf_op jit(solution)/shard_map/ppermute | solution.py:132
  21.4 0.9 %collective-permute-done.8.refs_10_ = bf16[2,16,4096]{2,1,0:T(8,128)(2,1)S(1)} collective-permute-done((bf16[2,16,4096]{2,1,0:T(8,128)(2,1)S(1)}, bf16[2,16,4096]{2,1,0:T(8,128)(2,1)S(1)}, u32[]{:S(2)}, u32[]{:S(2)}) %collective-permute-start.8) | collective-permute-done | bytes 262176 | tf_op jit(solution)/shard_map/ppermute | solution.py:132
  22.3 0.4 %collective-permute-done.5.refs_7_ = bf16[2,16,4096]{2,1,0:T(8,128)(2,1)S(1)} collective-permute-done((bf16[2,16,4096]{2,1,0:T(8,128)(2,1)S(1)}, bf16[2,16,4096]{2,1,0:T(8,128)(2,1)S(1)}, u32[]{:S(2)}, u32[]{:S(2)}) %collective-permute-start.5) | collective-permute-done | bytes 262176 | tf_op jit(solution)/shard_map/ppermute | solution.py:132
  22.7 0.0 collective-permute-done.2.refs_4_
  22.7 1.0 %scores_sent.1 = (f32[128,128]{1,0:T(8,128)S(1)}, bf16[2,128,4096]{2,1,0:T(8,128)(2,1)S(1)}) custom-call(bf16[256,2,4096]{2,1,0:T(2,128)(2,1)S(1)} %near.1.train, bf16[16,4096]{1,0:T(8,128)(2,1)S(1)} %condition_mine.1.refs_0_, bf16[16,4096]{1,0:T(8,128)(2,1)S(1)} %condition_other.1.refs_1_, bf16[16,4096]{1,0:T(8,128)(2,1)S(1)} %collective-permute-done.1.refs_2_, ...), custom_call_target="tpu_custom_call" | custom-call | flops 536870912 | bytes 4194304 | tf_op jit(solution)/shard_map/scores_sent/pallas_call | solution.py:218
  23.7 1.6 %collective-permute-start.9 = (f32[128,128]{1,0:T(8,128)S(1)}, f32[128,128]{1,0:T(8,128)S(1)}, u32[]{:S(2)}, u32[]{:S(2)}) collective-permute-start(f32[128,128]{1,0:T(8,128)S(1)} %get-tuple-element.12), channel_id=1, source_target_pairs={{0,1},{1,0},{2,3},{3,2},{4,5},{5,4},{6,7},{7,6},{8,9},{9,8},{10,11... | collective-permute-start | bytes 196616 | tf_op jit(solution)/shard_map/ppermute | solution.py:260
  25.3 0.8 %scores_kept.1 = f32[128,128]{1,0:T(8,128)S(1)} custom-call(bf16[256,2,4096]{2,1,0:T(2,128)(2,1)S(1)} %near.1.train, bf16[2,128,4096]{2,1,0:T(8,128)(2,1)S(1)} %get-tuple-element.11.table), custom_call_target="tpu_custom_call" | custom-call | flops 536870912 | bytes 4194304 | tf_op jit(solution)/shard_map/scores_kept/pallas_call | solution.py:218
  26.1 1.9 %collective-permute-done.9 = f32[128,128]{1,0:T(8,128)S(1)} collective-permute-done((f32[128,128]{1,0:T(8,128)S(1)}, f32[128,128]{1,0:T(8,128)S(1)}, u32[]{:S(2)}, u32[]{:S(2)}) %collective-permute-start.9) | collective-permute-done | bytes 65568 | tf_op jit(solution)/shard_map/ppermute | solution.py:260
  28.0 0.6 %add.3 = f32[128,128]{1,0:T(8,128)} add(f32[128,128]{1,0:T(8,128)S(1)} %scores_kept.1, f32[128,128]{1,0:T(8,128)S(1)} %collective-permute-done.9) | non-fusion elementwise | flops 16384 | bytes 196608 | tf_op jit(solution)/shard_map/add | solution.py:262
  (2 shorter events, 0.1 us)
Async XLA Ops:
  1.8 9.8 %collective-permute-start = (bf16[16,4096]{1,0:T(8,128)(2,1)S(1)}, bf16[16,4096]{1,0:T(8,128)(2,1)S(1)}, u32[]{:S(2)}, u32[]{:S(2)}) collective-permute-start(bf16[16,4096]{1,0:T(8,128)(2,1)S(1)} %condition_mine.1.refs_0_), channel_id=1, source_target_pairs={{0,12},{2,14},{4,8},{6,10},{8,4},{10,6},{12,0},{14,2},{1,13},{3,15... | collective-permute-start | bytes 393224 | tf_op jit(solution)/shard_map/ppermute | solution.py:128
  6.9 8.0 %collective-permute-start.1 = (bf16[16,4096]{1,0:T(8,128)(2,1)S(1)}, bf16[16,4096]{1,0:T(8,128)(2,1)S(1)}, u32[]{:S(2)}, u32[]{:S(2)}) collective-permute-start(bf16[16,4096]{1,0:T(8,128)(2,1)S(1)} %condition_mine.1.refs_0_), channel_id=1, source_target_pairs={{0,4},{2,6},{4,0},{6,2},{8,12},{10,14},{12,8},{14,10},{1,5},{3,7},... | collective-permute-start | bytes 393224 | tf_op jit(solution)/shard_map/ppermute | solution.py:128
  8.7 9.4 %collective-permute-start.6 = (bf16[16,4096]{1,0:T(8,128)(2,1)S(1)}, bf16[16,4096]{1,0:T(8,128)(2,1)S(1)}, u32[]{:S(2)}, u32[]{:S(2)}) collective-permute-start(bf16[16,4096]{1,0:T(8,128)(2,1)S(1)} %condition_other.1.refs_1_), channel_id=1, source_target_pairs={{0,8},{2,10},{4,12},{6,14},{8,0},{10,2},{12,4},{14,6},{1,9},{3,11}... | collective-permute-start | bytes 393224 | tf_op jit(solution)/shard_map/ppermute | solution.py:128
  11.6 9.3 %collective-permute-start.4 = (bf16[16,4096]{1,0:T(8,128)(2,1)S(1)}, bf16[16,4096]{1,0:T(8,128)(2,1)S(1)}, u32[]{:S(2)}, u32[]{:S(2)}) collective-permute-start(bf16[16,4096]{1,0:T(8,128)(2,1)S(1)} %collective-permute-done.refs_3_), channel_id=1, source_target_pairs={{0,16},{2,18},{4,20},{6,22},{8,24},{10,26},{12,28},{14,30},{16,0},... | collective-permute-start | bytes 393224 | tf_op jit(solution)/shard_map/ppermute | solution.py:138
  13.3 7.5 %collective-permute-start.3 = (bf16[16,4096]{1,0:T(8,128)(2,1)S(1)}, bf16[16,4096]{1,0:T(8,128)(2,1)S(1)}, u32[]{:S(2)}, u32[]{:S(2)}) collective-permute-start(bf16[16,4096]{1,0:T(8,128)(2,1)S(1)} %collective-permute-done.refs_3_), channel_id=1, source_target_pairs={{0,4},{2,6},{4,0},{6,2},{8,12},{10,14},{12,8},{14,10},{1,5},{3,7},... | collective-permute-start | bytes 393224 | tf_op jit(solution)/shard_map/ppermute | solution.py:128
  14.9 5.7 %collective-permute-start.7 = (bf16[16,4096]{1,0:T(8,128)(2,1)S(1)}, bf16[16,4096]{1,0:T(8,128)(2,1)S(1)}, u32[]{:S(2)}, u32[]{:S(2)}) collective-permute-start(bf16[16,4096]{1,0:T(8,128)(2,1)S(1)} %collective-permute-done.1.refs_2_), channel_id=1, source_target_pairs={{0,18},{2,16},{4,22},{6,20},{8,26},{10,24},{12,30},{14,28},{16,2},... | collective-permute-start | bytes 393224 | tf_op jit(solution)/shard_map/ppermute | solution.py:138
  15.1 7.6 %collective-permute-start.2 = (bf16[4,16,4096]{2,1,0:T(8,128)(2,1)S(1)}, bf16[4,16,4096]{2,1,0:T(8,128)(2,1)S(1)}, u32[]{:S(2)}, u32[]{:S(2)}) collective-permute-start(bf16[4,16,4096]{2,1,0:T(8,128)(2,1)S(1)} %pad_maximum_fusion), channel_id=1, source_target_pairs={{0,2},{2,0},{4,6},{6,4},{8,10},{10,8},{12,14},{14,12},{1,3},{3,1},... | collective-permute-start | bytes 1572872 | tf_op jit(solution)/shard_map/ppermute | solution.py:132
  20.7 1.6 %collective-permute-start.8 = (bf16[2,16,4096]{2,1,0:T(8,128)(2,1)S(1)}, bf16[2,16,4096]{2,1,0:T(8,128)(2,1)S(1)}, u32[]{:S(2)}, u32[]{:S(2)}) collective-permute-start(bf16[2,16,4096]{2,1,0:T(8,128)(2,1)S(1)} %pad_maximum_fusion.2), channel_id=1, source_target_pairs={{0,2},{2,0},{4,6},{6,4},{8,10},{10,8},{12,14},{14,12},{1,3},{3,1},... | collective-permute-start | bytes 786440 | tf_op jit(solution)/shard_map/ppermute | solution.py:132
  20.9 1.8 %collective-permute-start.5 = (bf16[2,16,4096]{2,1,0:T(8,128)(2,1)S(1)}, bf16[2,16,4096]{2,1,0:T(8,128)(2,1)S(1)}, u32[]{:S(2)}, u32[]{:S(2)}) collective-permute-start(bf16[2,16,4096]{2,1,0:T(8,128)(2,1)S(1)} %pad_maximum_fusion.1), channel_id=1, source_target_pairs={{0,2},{2,0},{4,6},{6,4},{8,10},{10,8},{12,14},{14,12},{1,3},{3,1},... | collective-permute-start | bytes 786440 | tf_op jit(solution)/shard_map/ppermute | solution.py:132
  23.7 4.3 %collective-permute-start.9 = (f32[128,128]{1,0:T(8,128)S(1)}, f32[128,128]{1,0:T(8,128)S(1)}, u32[]{:S(2)}, u32[]{:S(2)}) collective-permute-start(f32[128,128]{1,0:T(8,128)S(1)} %get-tuple-element.12), channel_id=1, source_target_pairs={{0,1},{1,0},{2,3},{3,2},{4,5},{5,4},{6,7},{7,6},{8,9},{9,8},{10,11... | collective-permute-start | bytes 196616 | tf_op jit(solution)/shard_map/ppermute | solution.py:260

commit v25 on v24

--- a/solution.py
+++ b/solution.py
@@ -179,9 +179,9 @@
 
 
 def sent_kernel(train, *refs):
-    mine, other, s1, s3, first_c, s2, y3, last_c, t2, y1, middle_c, scores, table, terms = refs
+    mine, other, s1, s3, first_c, s2, y1, last_c, t2, y3, middle_c, scores, table, terms = refs
     blocks = []
-    for group, swapped in (((mine, other, s1, s3), first_c), ((s2, y3), last_c), ((t2, y1), middle_c)):
+    for group, swapped in (((mine, other, s1, s3), first_c), ((s2, y1), last_c), ((t2, y3), middle_c)):
         for k, block in enumerate(group):
             blocks += [block, swapped.at[k]]
     part = lax.axis_index("parts")
@@ -200,9 +200,9 @@
                 (part, 1, 0),
                 (part, 3, 0),
                 (part, 2, 0),
+                (1 - part, 1, 1),
+                (1 - part, 2, 0),
                 (1 - part, 3, 0),
-                (1 - part, 2, 0),
-                (1 - part, 1, 1),
             )
         ):
             put(layer, flip, twin ^ cross, blocks[PAIR * k + twin][...])
@@ -245,7 +245,7 @@
     y3 = other_part(s3)
 
     blocks = []
-    for group in ((mine, other, s1, s3), (s2, y3), (t2, y1)):
+    for group in ((mine, other, s1, s3), (s2, y1), (t2, y3)):
         blocks += [*group, other_core(jnp.stack(group))]
     f32 = functools.partial(jax.ShapeDtypeStruct, dtype=jnp.float32)
     terms = [pltpu.VMEM((layer_count, share * layer_count, total), jnp.float32)]

time: 28.8 us -> 28.3 us (0.983)
  waiting for transfers between devices: 7.33 us -> 6.87 us
    ppermute x3, starting transfers between devices: 2.15 us -> 0.6 us  [other_core(): lax.ppermute(value, 'train', [(k, k ^ 1) for k in range(COLUMNS * PAIR)])]
    ppermute x2, starting transfers between devices: 1.8 us -> 3.24 us  [other_part(): return lax.ppermute(value, ('parts', 'train'), pairs)]
    ppermute x2, waiting for transfers between devices: 2.61 us -> 2.2 us  [other_part(): return lax.ppermute(value, ('parts', 'train'), pairs)]
  transfers between devices with their start and end apart: 10 -> 10, of which waited for: 5 -> 4; matrix products, arithmetic and copies ran while one was open for 0% -> 0% of each run, Pallas kernels for 17% -> 17%
where the time goes in v25:
time: 28.3 us; the launch traced here: 28.1 us
  starting transfers between devices  12.8 us (45%)
  Pallas kernels  7.57 us (27%)
  waiting for transfers between devices  6.87 us (24%)
  other arithmetic  0.76 us (3%)
    ppermute x4, starting transfers between devices, along_columns(): lax.ppermute(value, 'train', [(k, k ^ flip * PAIR) for k in range(COLUMNS...  7.44 us
    pallas_call x2, Pallas kernels, condition_layer(): pl.pallas_call(functools.partial(condition_kernel, other), out_shape=jax....  3.53 us
    ppermute x2, starting transfers between devices, other_part(): return lax.ppermute(value, ('parts', 'train'), pairs)  3.24 us
    ppermute x2, waiting for transfers between devices, other_part(): return lax.ppermute(value, ('parts', 'train'), pairs)  2.2 us
    pallas_call x1, Pallas kernels, copy_near(): pl.pallas_call(copy_kernel, out_shape=jax.ShapeDtypeStruct(value.shape, v...  2.2 us
    ppermute x1, waiting for transfers between devices, direct(): received = lax.ppermute(sent, 'layer', [(0, 1), (1, 0)])  2.03 us
    pallas_call x2, Pallas kernels, local_call(): pl.pallas_call(kernel, out_shape=out_shape, in_specs=[spec] * len(operand...  1.84 us
    ppermute x1, starting transfers between devices, direct(): received = lax.ppermute(sent, 'layer', [(0, 1), (1, 0)])  1.56 us
  transfers between devices with their start and end apart: 10, of which 4 were waited for; matrix products, arithmetic and copies ran while one was open for 0% of the time, Pallas kernels for 17%

profile of v25, /device:TPU:0, one launch (start us, length us, event | category | flops | bytes accessed | tf_op | source)
XLA Modules:
  0.0 28.1 jit_solution(10216372113985168980)
XLA Ops:
  0.0 1.8 %condition_mine.1.refs_0_ = bf16[16,4096]{1,0:T(8,128)(2,1)S(1)} custom-call(bf16[2,1,16,4096]{3,2,1,0:T(8,128)(2,1)} %queries.3, f32[2,64,64]{2,1,0:T(8,128)} %left.3, f32[2,64,64]{2,1,0:T(8,128)} %right.3), custom_call_target="tpu_custom_call" | custom-call | flops 134217728 | bytes 524288 | tf_op jit(solution)/shard_map/condition_mine/pallas_call | solution.py:107
  1.8 5.1 %collective-permute-start = (bf16[16,4096]{1,0:T(8,128)(2,1)S(1)}, bf16[16,4096]{1,0:T(8,128)(2,1)S(1)}, u32[]{:S(2)}, u32[]{:S(2)}) collective-permute-start(bf16[16,4096]{1,0:T(8,128)(2,1)S(1)} %condition_mine.1.refs_0_), channel_id=1, source_target_pairs={{0,12},{2,14},{4,8},{6,10},{8,4},{10,6},{12,0},{14,2},{1,13},{3,15... | collective-permute-start | bytes 393224 | tf_op jit(solution)/shard_map/ppermute | solution.py:128
  6.9 0.0 collective-permute-start.1
  6.9 1.8 %condition_other.1.refs_1_ = bf16[16,4096]{1,0:T(8,128)(2,1)S(1)} custom-call(bf16[2,1,16,4096]{3,2,1,0:T(8,128)(2,1)} %queries.3, f32[2,64,64]{2,1,0:T(8,128)} %left.3, f32[2,64,64]{2,1,0:T(8,128)} %right.3), custom_call_target="tpu_custom_call" | custom-call | flops 134217728 | bytes 524288 | tf_op jit(solution)/shard_map/condition_other/pallas_call | solution.py:107
  8.7 0.7 %collective-permute-start.6 = (bf16[16,4096]{1,0:T(8,128)(2,1)S(1)}, bf16[16,4096]{1,0:T(8,128)(2,1)S(1)}, u32[]{:S(2)}, u32[]{:S(2)}) collective-permute-start(bf16[16,4096]{1,0:T(8,128)(2,1)S(1)} %condition_other.1.refs_1_), channel_id=1, source_target_pairs={{0,8},{2,10},{4,12},{6,14},{8,0},{10,2},{12,4},{14,6},{1,9},{3,11}... | collective-permute-start | bytes 393224 | tf_op jit(solution)/shard_map/ppermute | solution.py:128
  9.4 2.2 %near.1.train = bf16[256,2,4096]{2,1,0:T(2,128)(2,1)S(1)} custom-call(bf16[256,2,4096]{2,1,0:T(2,128)(2,1)} %source.1), custom_call_target="tpu_custom_call" | custom-call | bytes 8388608 | tf_op jit(solution)/shard_map/near/pallas_call | solution.py:148
  11.6 0.0 collective-permute-done.refs_3_
  11.6 1.7 %collective-permute-start.7 = (bf16[16,4096]{1,0:T(8,128)(2,1)S(1)}, bf16[16,4096]{1,0:T(8,128)(2,1)S(1)}, u32[]{:S(2)}, u32[]{:S(2)}) collective-permute-start(bf16[16,4096]{1,0:T(8,128)(2,1)S(1)} %collective-permute-done.refs_3_), channel_id=1, source_target_pairs={{0,16},{2,18},{4,20},{6,22},{8,24},{10,26},{12,28},{14,30},{16,0},... | collective-permute-start | bytes 393224 | tf_op jit(solution)/shard_map/ppermute | solution.py:138
  13.3 1.6 %collective-permute-start.3 = (bf16[16,4096]{1,0:T(8,128)(2,1)S(1)}, bf16[16,4096]{1,0:T(8,128)(2,1)S(1)}, u32[]{:S(2)}, u32[]{:S(2)}) collective-permute-start(bf16[16,4096]{1,0:T(8,128)(2,1)S(1)} %collective-permute-done.refs_3_), channel_id=1, source_target_pairs={{0,4},{2,6},{4,0},{6,2},{8,12},{10,14},{12,8},{14,10},{1,5},{3,7},... | collective-permute-start | bytes 393224 | tf_op jit(solution)/shard_map/ppermute | solution.py:128
  14.9 0.0 collective-permute-done.1.refs_2_
  14.9 0.1 pad_maximum_fusion
  15.0 0.1 collective-permute-start.2
  15.1 1.5 %collective-permute-start.4 = (bf16[16,4096]{1,0:T(8,128)(2,1)S(1)}, bf16[16,4096]{1,0:T(8,128)(2,1)S(1)}, u32[]{:S(2)}, u32[]{:S(2)}) collective-permute-start(bf16[16,4096]{1,0:T(8,128)(2,1)S(1)} %collective-permute-done.1.refs_2_), channel_id=1, source_target_pairs={{0,18},{2,16},{4,22},{6,20},{8,26},{10,24},{12,30},{14,28},{16,2},... | collective-permute-start | bytes 393224 | tf_op jit(solution)/shard_map/ppermute | solution.py:138
  16.6 1.5 %collective-permute-done.6.refs_8_ = bf16[16,4096]{1,0:T(8,128)(2,1)S(1)} collective-permute-done((bf16[16,4096]{1,0:T(8,128)(2,1)S(1)}, bf16[16,4096]{1,0:T(8,128)(2,1)S(1)}, u32[]{:S(2)}, u32[]{:S(2)}) %collective-permute-start.6) | collective-permute-done | bytes 131104 | tf_op jit(solution)/shard_map/ppermute | solution.py:128
  18.1 0.0 collective-permute-done.7.refs_9_
  18.1 0.1 collective-permute-start.8
  18.2 2.2 %collective-permute-done.4.refs_6_ = bf16[16,4096]{1,0:T(8,128)(2,1)S(1)} collective-permute-done((bf16[16,4096]{1,0:T(8,128)(2,1)S(1)}, bf16[16,4096]{1,0:T(8,128)(2,1)S(1)}, u32[]{:S(2)}, u32[]{:S(2)}) %collective-permute-start.4) | collective-permute-done | bytes 131104 | tf_op jit(solution)/shard_map/ppermute | solution.py:138
  20.4 0.0 collective-permute-done.3.refs_5_
  20.4 0.5 %collective-permute-start.5 = (bf16[2,16,4096]{2,1,0:T(8,128)(2,1)S(1)}, bf16[2,16,4096]{2,1,0:T(8,128)(2,1)S(1)}, u32[]{:S(2)}, u32[]{:S(2)}) collective-permute-start(bf16[2,16,4096]{2,1,0:T(8,128)(2,1)S(1)} %pad_maximum_fusion.1), channel_id=1, source_target_pairs={{0,2},{2,0},{4,6},{6,4},{8,10},{10,8},{12,14},{14,12},{1,3},{3,1},... | collective-permute-start | bytes 786440 | tf_op jit(solution)/shard_map/ppermute | solution.py:132
  20.9 0.0 collective-permute-done.8.refs_10_
  20.9 1.2 %collective-permute-done.5.refs_7_ = bf16[2,16,4096]{2,1,0:T(8,128)(2,1)S(1)} collective-permute-done((bf16[2,16,4096]{2,1,0:T(8,128)(2,1)S(1)}, bf16[2,16,4096]{2,1,0:T(8,128)(2,1)S(1)}, u32[]{:S(2)}, u32[]{:S(2)}) %collective-permute-start.5) | collective-permute-done | bytes 262176 | tf_op jit(solution)/shard_map/ppermute | solution.py:132
  22.0 0.0 collective-permute-done.2.refs_4_
  22.0 1.0 %scores_sent.1 = (f32[128,128]{1,0:T(8,128)S(1)}, bf16[2,128,4096]{2,1,0:T(8,128)(2,1)S(1)}) custom-call(bf16[256,2,4096]{2,1,0:T(2,128)(2,1)S(1)} %near.1.train, bf16[16,4096]{1,0:T(8,128)(2,1)S(1)} %condition_mine.1.refs_0_, bf16[16,4096]{1,0:T(8,128)(2,1)S(1)} %condition_other.1.refs_1_, bf16[16,4096]{1,0:T(8,128)(2,1)S(1)} %collective-permute-done.1.refs_2_, ...), custom_call_target="tpu_custom_call" | custom-call | flops 536870912 | bytes 4194304 | tf_op jit(solution)/shard_map/scores_sent/pallas_call | solution.py:218
  23.0 1.6 %collective-permute-start.9 = (f32[128,128]{1,0:T(8,128)S(1)}, f32[128,128]{1,0:T(8,128)S(1)}, u32[]{:S(2)}, u32[]{:S(2)}) collective-permute-start(f32[128,128]{1,0:T(8,128)S(1)} %get-tuple-element.12), channel_id=1, source_target_pairs={{0,1},{1,0},{2,3},{3,2},{4,5},{5,4},{6,7},{7,6},{8,9},{9,8},{10,11... | collective-permute-start | bytes 196616 | tf_op jit(solution)/shard_map/ppermute | solution.py:260
  24.6 0.8 %scores_kept.1 = f32[128,128]{1,0:T(8,128)S(1)} custom-call(bf16[256,2,4096]{2,1,0:T(2,128)(2,1)S(1)} %near.1.train, bf16[2,128,4096]{2,1,0:T(8,128)(2,1)S(1)} %get-tuple-element.11.table), custom_call_target="tpu_custom_call" | custom-call | flops 536870912 | bytes 4194304 | tf_op jit(solution)/shard_map/scores_kept/pallas_call | solution.py:218
  25.4 2.0 %collective-permute-done.9 = f32[128,128]{1,0:T(8,128)S(1)} collective-permute-done((f32[128,128]{1,0:T(8,128)S(1)}, f32[128,128]{1,0:T(8,128)S(1)}, u32[]{:S(2)}, u32[]{:S(2)}) %collective-permute-start.9) | collective-permute-done | bytes 65568 | tf_op jit(solution)/shard_map/ppermute | solution.py:260
  27.5 0.6 %add.3 = f32[128,128]{1,0:T(8,128)} add(f32[128,128]{1,0:T(8,128)S(1)} %scores_kept.1, f32[128,128]{1,0:T(8,128)S(1)} %collective-permute-done.9) | non-fusion elementwise | flops 16384 | bytes 196608 | tf_op jit(solution)/shard_map/add | solution.py:262
  (2 shorter events, 0.1 us)
Async XLA Ops:
  1.8 9.8 %collective-permute-start = (bf16[16,4096]{1,0:T(8,128)(2,1)S(1)}, bf16[16,4096]{1,0:T(8,128)(2,1)S(1)}, u32[]{:S(2)}, u32[]{:S(2)}) collective-permute-start(bf16[16,4096]{1,0:T(8,128)(2,1)S(1)} %condition_mine.1.refs_0_), channel_id=1, source_target_pairs={{0,12},{2,14},{4,8},{6,10},{8,4},{10,6},{12,0},{14,2},{1,13},{3,15... | collective-permute-start | bytes 393224 | tf_op jit(solution)/shard_map/ppermute | solution.py:128
  6.9 8.0 %collective-permute-start.1 = (bf16[16,4096]{1,0:T(8,128)(2,1)S(1)}, bf16[16,4096]{1,0:T(8,128)(2,1)S(1)}, u32[]{:S(2)}, u32[]{:S(2)}) collective-permute-start(bf16[16,4096]{1,0:T(8,128)(2,1)S(1)} %condition_mine.1.refs_0_), channel_id=1, source_target_pairs={{0,4},{2,6},{4,0},{6,2},{8,12},{10,14},{12,8},{14,10},{1,5},{3,7},... | collective-permute-start | bytes 393224 | tf_op jit(solution)/shard_map/ppermute | solution.py:128
  8.7 9.4 %collective-permute-start.6 = (bf16[16,4096]{1,0:T(8,128)(2,1)S(1)}, bf16[16,4096]{1,0:T(8,128)(2,1)S(1)}, u32[]{:S(2)}, u32[]{:S(2)}) collective-permute-start(bf16[16,4096]{1,0:T(8,128)(2,1)S(1)} %condition_other.1.refs_1_), channel_id=1, source_target_pairs={{0,8},{2,10},{4,12},{6,14},{8,0},{10,2},{12,4},{14,6},{1,9},{3,11}... | collective-permute-start | bytes 393224 | tf_op jit(solution)/shard_map/ppermute | solution.py:128
  11.6 6.5 %collective-permute-start.7 = (bf16[16,4096]{1,0:T(8,128)(2,1)S(1)}, bf16[16,4096]{1,0:T(8,128)(2,1)S(1)}, u32[]{:S(2)}, u32[]{:S(2)}) collective-permute-start(bf16[16,4096]{1,0:T(8,128)(2,1)S(1)} %collective-permute-done.refs_3_), channel_id=1, source_target_pairs={{0,16},{2,18},{4,20},{6,22},{8,24},{10,26},{12,28},{14,30},{16,0},... | collective-permute-start | bytes 393224 | tf_op jit(solution)/shard_map/ppermute | solution.py:138
  13.3 7.1 %collective-permute-start.3 = (bf16[16,4096]{1,0:T(8,128)(2,1)S(1)}, bf16[16,4096]{1,0:T(8,128)(2,1)S(1)}, u32[]{:S(2)}, u32[]{:S(2)}) collective-permute-start(bf16[16,4096]{1,0:T(8,128)(2,1)S(1)} %collective-permute-done.refs_3_), channel_id=1, source_target_pairs={{0,4},{2,6},{4,0},{6,2},{8,12},{10,14},{12,8},{14,10},{1,5},{3,7},... | collective-permute-start | bytes 393224 | tf_op jit(solution)/shard_map/ppermute | solution.py:128
  15.0 7.0 %collective-permute-start.2 = (bf16[4,16,4096]{2,1,0:T(8,128)(2,1)S(1)}, bf16[4,16,4096]{2,1,0:T(8,128)(2,1)S(1)}, u32[]{:S(2)}, u32[]{:S(2)}) collective-permute-start(bf16[4,16,4096]{2,1,0:T(8,128)(2,1)S(1)} %pad_maximum_fusion), channel_id=1, source_target_pairs={{0,2},{2,0},{4,6},{6,4},{8,10},{10,8},{12,14},{14,12},{1,3},{3,1},... | collective-permute-start | bytes 1572872 | tf_op jit(solution)/shard_map/ppermute | solution.py:132
  15.1 5.3 %collective-permute-start.4 = (bf16[16,4096]{1,0:T(8,128)(2,1)S(1)}, bf16[16,4096]{1,0:T(8,128)(2,1)S(1)}, u32[]{:S(2)}, u32[]{:S(2)}) collective-permute-start(bf16[16,4096]{1,0:T(8,128)(2,1)S(1)} %collective-permute-done.1.refs_2_), channel_id=1, source_target_pairs={{0,18},{2,16},{4,22},{6,20},{8,26},{10,24},{12,30},{14,28},{16,2},... | collective-permute-start | bytes 393224 | tf_op jit(solution)/shard_map/ppermute | solution.py:138
  18.1 2.8 %collective-permute-start.8 = (bf16[2,16,4096]{2,1,0:T(8,128)(2,1)S(1)}, bf16[2,16,4096]{2,1,0:T(8,128)(2,1)S(1)}, u32[]{:S(2)}, u32[]{:S(2)}) collective-permute-start(bf16[2,16,4096]{2,1,0:T(8,128)(2,1)S(1)} %pad_maximum_fusion.2), channel_id=1, source_target_pairs={{0,2},{2,0},{4,6},{6,4},{8,10},{10,8},{12,14},{14,12},{1,3},{3,1},... | collective-permute-start | bytes 786440 | tf_op jit(solution)/shard_map/ppermute | solution.py:132
  20.4 1.6 %collective-permute-start.5 = (bf16[2,16,4096]{2,1,0:T(8,128)(2,1)S(1)}, bf16[2,16,4096]{2,1,0:T(8,128)(2,1)S(1)}, u32[]{:S(2)}, u32[]{:S(2)}) collective-permute-start(bf16[2,16,4096]{2,1,0:T(8,128)(2,1)S(1)} %pad_maximum_fusion.1), channel_id=1, source_target_pairs={{0,2},{2,0},{4,6},{6,4},{8,10},{10,8},{12,14},{14,12},{1,3},{3,1},... | collective-permute-start | bytes 786440 | tf_op jit(solution)/shard_map/ppermute | solution.py:132
  23.0 4.4 %collective-permute-start.9 = (f32[128,128]{1,0:T(8,128)S(1)}, f32[128,128]{1,0:T(8,128)S(1)}, u32[]{:S(2)}, u32[]{:S(2)}) collective-permute-start(f32[128,128]{1,0:T(8,128)S(1)} %get-tuple-element.12), channel_id=1, source_target_pairs={{0,1},{1,0},{2,3},{3,2},{4,5},{5,4},{6,7},{7,6},{8,9},{9,8},{10,11... | collective-permute-start | bytes 196616 | tf_op jit(solution)/shard_map/ppermute | solution.py:260
